TPU v7x, 32 devices: a whole 2x2x4 slice. The times are simulated.
32 devices in a mesh: dp: 8 (over y, x, core), shard: 4 (over z).
Axes of the slice: x: 2, y: 2, z: 4, core: 2. Of those that a mesh axis runs over, the one named last changes fastest.
Arguments:
- queries: bfloat16 [4096, 2048], P(('dp', 'shard')), may hold values from -6 to 6
- keys_in: bfloat16 [4096, 2048], P(('dp', 'shard')), may hold values from -6 to 6
- values: bfloat16 [4096, 2048], P(('dp', 'shard')), may hold values from -6 to 6
- out_grad: bfloat16 [4096, 2048], P(('dp', 'shard')), may hold values from -48 to 48
- out_weight: bfloat16 [2048, 2048], P('shard'), may hold values from -0.125 to 0.125
- block_lists: int32 [8, 4, 4], P('dp'), may hold values from 0 to 3, as said below
- voxel_count: int32 [8], P('dp'), may hold values from 256 to 512
Outputs:
- grad_query: bfloat16 [4096, 2048], P(('dp', 'shard'))
- grad_key: bfloat16 [4096, 2048], P(('dp', 'shard'))
- grad_value: bfloat16 [4096, 2048], P(('dp', 'shard'))
- grad_weight: bfloat16 [2048, 2048], P('shard')
Inputs may be any that keep to these rules, and one draw needn't show every extreme that they name: `block_lists`: entry 0 of row b of a scene's list is b itself; the 4 entries of a row are different blocks of that scene.
All inputs are finite; a program needn't handle non-finite values.
Results may differ from a plain program's by a relative error of at most 0.0095.
Values may be sent and summed in bfloat16 or wider, within the bound.
No kernel may reach another device: no remote copies, remote signals or barrier semaphores. Data moves between devices by JAX's collectives and lax.ppermute only.
A program may use at most 128 MiB of HBM per device.

v0:
```python
import functools
import math

import jax
import jax.numpy as jnp
from jax import lax
from jax.experimental import pallas as pl
from jax.experimental.pallas import tpu as pltpu
from jax.sharding import PartitionSpec as P

HDIM = 128
BLOCK = 128
NB = 4
MIB = 1024 * 1024
DP = ("chips", "core")

Z, COUNT, CORE, CHIP = range(4)

EARLY = 3

NO_COST = pl.CostEstimate(flops=0, bytes_accessed=1024, transcendentals=0)

f32 = jnp.float32
bf16 = jnp.bfloat16


def dot(a, b, ca, cb):
    return lax.dot_general(a, b, (((ca,), (cb,)), ((), ())), preferred_element_type=f32)


def sds(shape, dtype):
    return jax.ShapeDtypeStruct(shape, dtype)


def params(mib=2):
    return pltpu.CompilerParams(vmem_limit_bytes=mib * MIB)


def swap(x, axis, size, flip):
    return lax.ppermute(x, axis, [(i, i ^ flip) for i in range(size)])


def after(x, *earlier):
    return lax.optimization_barrier((x, *earlier))[0]


def run_all(copies):
    for copy in copies:
        copy.start()
    for copy in copies:
        copy.wait()


def whole(kernel, out_shape, operands, name, scalars=0, mib=2, scratch=()):
    return pl.pallas_call(
        kernel,
        out_shape=out_shape,
        in_specs=[pl.BlockSpec(memory_space=pltpu.SMEM)] * scalars
        + [pl.BlockSpec(memory_space=pltpu.VMEM)] * (len(operands) - scalars),
        out_specs=jax.tree.map(lambda _: pl.BlockSpec(memory_space=pltpu.VMEM), out_shape),
        scratch_shapes=scratch,
        compiler_params=params(mib),
        cost_estimate=NO_COST,
        name=name,
    )(*operands)


def pack_kernel(meta, q_ref, k_ref, v_ref, grad_ref, mine_ref, *refs):
    *outs, sems = refs
    width = outs[0].shape[2]
    copies = [pltpu.make_async_copy(grad_ref, mine_ref, sems.at[3 * len(outs)])]
    for n, out_ref in enumerate(outs):
        k, first = (n, 0) if n < 2 else (n // 2 + 1, n % 2 * EARLY * HDIM)
        start = pl.multiple_of((meta[Z] ^ k) * width + first, 128)
        for i, ref in enumerate((q_ref, k_ref, v_ref)):
            part = ref.at[:, pl.ds(start, out_ref.shape[2])]
            copies.append(pltpu.make_async_copy(part, out_ref.at[i], sems.at[3 * n + i]))
    run_all(copies)


def pack(meta, queries, keys_in, values, grad):
    rows, width = queries.shape
    part, early = width // 4, EARLY * HDIM
    shapes = [sds((3, rows, n), bf16) for n in (part, part, early, part - early, early, part - early)]
    shapes = [sds(grad.shape, bf16)] + shapes
    return pl.pallas_call(
        pack_kernel,
        out_shape=shapes,
        in_specs=[pl.BlockSpec(memory_space=pltpu.SMEM)] + [pl.BlockSpec(memory_space=pl.ANY)] * 4,
        out_specs=[pl.BlockSpec(memory_space=pltpu.VMEM)] * len(shapes),
        scratch_shapes=[pltpu.SemaphoreType.DMA((3 * len(shapes),))],
        compiler_params=params(),
        cost_estimate=NO_COST,
        name="pack_heads",
    )(meta, queries, keys_in, values, grad)


def token_pos(shape, dim, z, start=0):
    return (lax.broadcasted_iota(jnp.int32, shape, dim) + start) ^ (z * BLOCK)


def grad_attn_kernel(start, meta, *refs):
    *grads, w_ref, out_ref = refs
    grad = jnp.concatenate([g[...] for g in grads], axis=0)
    live = token_pos((grad.shape[0], 1), 0, meta[Z], start) < meta[COUNT]
    tile = 2 * HDIM

    @pl.loop(0, w_ref.shape[0] // tile)
    def _(i):
        part = pl.ds(pl.multiple_of(i * tile, tile), tile)
        out_ref[:, part] = jnp.where(live, dot(grad, w_ref[part, :], 1, 1), 0.0).astype(bf16)


def grad_attn(meta, grads, weight, start):
    shape = (sum(g.shape[0] for g in grads), weight.shape[0])
    kernel = functools.partial(grad_attn_kernel, start)
    return whole(kernel, sds(shape, bf16), (meta, *grads, weight), "grad_attn", 1, 6)


def head_of(pieces, group, h):
    part = pieces[-1].shape[2]
    parts = []
    for p in pieces:
        start = (group * EARLY * HDIM if p.shape[2] > part else 0) + h * HDIM
        parts.append([p[i, :, start : start + HDIM] for i in range(3)])
    return (jnp.concatenate(x, axis=0) for x in zip(*parts))


def forward_kernel(group, meta, p0, p1, p2, p3, weight_ref, inverse_ref, out_ref, heads_ref, bias_ref):
    pieces = (p0, p1, p2, p3)
    rows = p0.shape[1]
    total = 4 * rows
    tile = 2 * rows
    to_power = math.log2(math.e) / math.sqrt(HDIM)
    query_live = token_pos((1, total), 1, meta[Z]) < meta[COUNT]
    key_live = token_pos((total, 1), 0, meta[Z]) < meta[COUNT]
    bias_ref[...] = jnp.where(key_live | ~query_live, 0.0, -jnp.inf)
    for h in range(p3.shape[2] // HDIM):
        cols = slice(h * HDIM, (h + 1) * HDIM)
        query, key, value = head_of(pieces, group, h)
        for t in range(2):
            part = slice(t * tile, (t + 1) * tile)
            scores = dot(key, query[part], 1, 1) + bias_ref[:, part]
            peak = jnp.max(scores, axis=0, keepdims=True)
            weights = jnp.exp2((scores - peak) * to_power).astype(bf16)
            weight_ref[h, :, part] = weights
            inverse = 1.0 / jnp.sum(weights.astype(f32), axis=0, keepdims=True)
            inverse_ref[h, :, part] = inverse
            heads = dot(value, weights, 0, 0) * inverse
            out_ref[cols, part] = heads
            heads_ref[cols, part] = jnp.where(query_live[:, part], heads, 0.0).astype(bf16)


def forward(meta, pieces, group):
    _, rows, width = pieces[-1].shape
    total = 4 * rows
    shapes = [
        sds((width // HDIM, total, total), bf16),
        sds((width // HDIM, 1, total), f32),
        sds((width, total), f32),
        sds((width, total), bf16),
    ]
    scratch = [pltpu.VMEM((total, total), f32)]
    kernel = functools.partial(forward_kernel, group)
    return whole(kernel, shapes, (meta, *pieces), "attend_forward", 1, 8, scratch)


def span_gradients(query, key, value, grad, weights, inverse, outs):
    turned = grad.astype(f32).T
    row_delta = jnp.sum(outs * turned, axis=0, keepdims=True)
    grad_prob = dot(value, grad, 1, 1)
    factor = inverse * (1.0 / math.sqrt(HDIM))
    dscore = (weights.astype(f32) * ((grad_prob - row_delta) * factor)).astype(bf16)
    grad_query = dot(key, dscore, 0, 0).T.astype(bf16)
    grad_value = dot(weights, (turned * inverse).T.astype(bf16), 1, 0)
    return grad_query, dot(dscore, query, 1, 0), grad_value


def backward_early_kernel(*refs):
    pieces, (grad_ref, weight_ref, inverse_ref, out_ref, query_out, key_out, value_out) = refs[:4], refs[4:]
    early = grad_ref.shape[0]
    for h in range(pieces[-1].shape[2] // HDIM):
        cols = slice(h * HDIM, (h + 1) * HDIM)
        query, key, value = head_of(pieces, 0, h)
        grad_key = grad_value = 0.0
        for span in (slice(0, 2 * BLOCK), slice(2 * BLOCK, early)):
            grad_query, add_key, add_value = span_gradients(
                query[span], key, value, grad_ref[span, cols],
                weight_ref[h, :, span], inverse_ref[h, :, span], out_ref[cols, span],
            )
            query_out[span, cols] = grad_query
            grad_key += add_key
            grad_value += add_value
        key_out[:, cols] = grad_key
        value_out[:, cols] = grad_value


def backward_early(pieces, grad, saved):
    _, rows, part = pieces[-1].shape
    shapes = [sds((grad.shape[0], part), bf16), sds((4 * rows, part), f32), sds((4 * rows, part), f32)]
    return whole(backward_early_kernel, shapes, (*pieces, grad, *saved), "backward_early", 0, 8)


def backward_kernel(own, near, far2a, far3a, far2b, far3b, early_ref, late_ref, *refs):
    saved, done, backs = (refs[:3], refs[3:6]), refs[6:9], refs[9:]
    rows = own.shape[1]
    early, total = early_ref.shape[0], 4 * rows
    for n in range(own.shape[2] // HDIM):
        group, h = divmod(n, EARLY)
        query, key, value = head_of(((own, near, far2a, far3a), (own, near, far2b, far3b))[group], group, h)
        weight_ref, inverse_ref, out_ref = saved[group]
        here = slice(h * HDIM, (h + 1) * HDIM)
        cols = slice(n * HDIM, (n + 1) * HDIM)
        if group == 0:
            spans = ((slice(early, total), late_ref[:, cols]),)
            grad_key, grad_value = done[1][:, here], done[2][:, here]
            for k in range(early // rows):
                backs[k][0, :, cols] = done[0][k * rows : (k + 1) * rows, here]
        else:
            grad = jnp.concatenate([early_ref[:, cols], late_ref[:, cols]], axis=0)
            spans = [(slice(t, t + 2 * rows), grad[t : t + 2 * rows]) for t in (0, 2 * rows)]
            grad_key = grad_value = 0.0
        for span, grad in spans:
            grad_query, add_key, add_value = span_gradients(
                query[span], key, value, grad, weight_ref[h, :, span], inverse_ref[h, :, span], out_ref[here, span]
            )
            for k in range(span.start // rows, span.stop // rows):
                at = k * rows - span.start
                backs[k][0, :, cols] = grad_query[at : at + rows]
            grad_key += add_key
            grad_value += add_value
        for k in range(4):
            mine = slice(k * rows, (k + 1) * rows)
            backs[k][1, :, cols] = grad_key[mine].astype(bf16)
            backs[k][2, :, cols] = grad_value[mine].astype(bf16)


def backward(pieces, grads, saved, done):
    shapes = [sds(pieces[0].shape, bf16)] * 4
    return whole(backward_kernel, shapes, (*pieces, *grads, *saved, *done), "attend_backward", 0, 8)


LINE = HDIM // 8


def line_at(meta, head, other, j):
    at = head * HDIM + ((meta[CORE] ^ other) * 4 + (meta[CHIP] ^ j)) * LINE
    return pl.ds(pl.multiple_of(at, LINE), LINE)


def weight_kernel(meta, heads_a, heads_b, *refs):
    *grads, send_ref, keep_ref = refs
    width = heads_a.shape[0] + heads_b.shape[0]
    lines = []
    for other in (1, 0):
        for j in range(4):
            for ref in (heads_a, heads_b):
                lines += [ref[line_at(meta, h, other, j), :] for h in range(ref.shape[0] // HDIM)]
    lines = jnp.concatenate(lines, axis=0)
    tile = 4 * HDIM

    @pl.loop(0, send_ref.shape[1] // tile)
    def _(i):
        part = pl.ds(pl.multiple_of(i * tile, tile), tile)
        product = dot(lines, jnp.concatenate([g[:, part] for g in grads], axis=0), 1, 0)
        send_ref[:, part] = product[: width // 2].astype(bf16)
        keep_ref[:, part] = product[width // 2 :]


def weight_halves(meta, heads, grads):
    shape = (sum(x.shape[0] for x in heads) // 2, grads[0].shape[1])
    return whole(weight_kernel, [sds(shape, bf16), sds(shape, f32)], (meta, *heads, *grads), "weight_halves", 1, 6)


def add_kernel(keep_ref, recv_ref, *outs):
    size = outs[0].shape[0]
    for j, out_ref in enumerate(outs):
        part = slice(j * size, (j + 1) * size)
        out_ref[...] = (keep_ref[part, :] + recv_ref[part, :].astype(f32)).astype(out_ref.dtype)


def add_parts(keep, recv):
    shape = (keep.shape[0] // 4, keep.shape[1])
    return whole(add_kernel, [sds(shape, f32)] + [sds(shape, bf16)] * 3, (keep, recv), "add_parts")


def total_kernel(scale, own_ref, r1, r2, r3, out_ref):
    total = own_ref[...] + r1[...].astype(f32) + r2[...].astype(f32) + r3[...].astype(f32)
    out_ref[...] = (total * scale).astype(bf16)


def total_of(own, recvs, scale):
    return whole(functools.partial(total_kernel, scale), sds(own.shape, bf16), (own, *recvs), "scene_mean")


def weight_copies(meta, parts, first, out_ref, sems):
    copies = []
    for p, ref in enumerate(parts, first):
        for h in range(ref.shape[0] // LINE):
            line = out_ref.at[line_at(meta, h, p // 4, p % 4), :]
            copies.append(pltpu.make_async_copy(ref.at[pl.ds(h * LINE, LINE), :], line, sems.at[len(copies)]))
    return copies


def head_copies(meta, pieces, outs, sems):
    copies = []
    for k, ref in pieces.items():
        width = ref.shape[2]
        start = pl.multiple_of((meta[Z] ^ k) * width, 128)
        for i, out_ref in enumerate(outs):
            part = out_ref.at[:, pl.ds(start, width)]
            copies.append(pltpu.make_async_copy(ref.at[i], part, sems.at[len(copies)]))
    return copies


def join(kernel, meta, parts, shapes, copies, name, outs=()):
    return pl.pallas_call(
        kernel,
        out_shape=shapes,
        in_specs=[pl.BlockSpec(memory_space=pltpu.SMEM)]
        + [pl.BlockSpec(memory_space=pltpu.VMEM)] * len(parts)
        + [pl.BlockSpec(memory_space=pl.ANY)] * len(outs),
        out_specs=[pl.BlockSpec(memory_space=pl.ANY)] * len(shapes),
        scratch_shapes=[pltpu.SemaphoreType.DMA((n,)) for n in copies],
        input_output_aliases={1 + len(parts) + i: i for i in range(len(outs))},
        compiler_params=params(),
        cost_estimate=NO_COST,
        name=name,
    )(meta, *parts, *outs)


def join_weight_kernel(meta, *refs):
    run_all(weight_copies(meta, refs[:4], 0, refs[4], refs[5]))


def join_weight(meta, near):
    size, outw = near[0].shape
    return join(join_weight_kernel, meta, near, [sds((8 * size, outw), bf16)], [4 * size // LINE], "join_weight")[0]


def join_heads_kernel(meta, own, back2, back3, *refs):
    run_all(head_copies(meta, {0: own, 2: back2, 3: back3}, refs[:3], refs[3]))


def join_heads(meta, own, back2, back3):
    _, rows, width = own.shape
    shapes = [sds((rows, 4 * width), bf16)] * 3
    return join(join_heads_kernel, meta, (own, back2, back3), shapes, [9], "join_heads")


def join_last_kernel(meta, *refs):
    far, back1, outs, sems = refs[:4], refs[4], refs[9:13], refs[13:]
    run_all(weight_copies(meta, far, 4, outs[3], sems[0]) + head_copies(meta, {1: back1}, outs[:3], sems[1]))


def join_last(meta, far, back1, outs):
    shapes = [sds(x.shape, x.dtype) for x in outs]
    return join(join_last_kernel, meta, (*far, back1), shapes, [4 * far[0].shape[0] // LINE, 3], "join_last", outs)


def dense_body(queries, keys_in, values, out_grad, out_weight, voxel_count):
    meta = jnp.stack([lax.axis_index("shard"), voxel_count[0], lax.axis_index("core"), lax.axis_index("chips")])
    meta = meta.astype(jnp.int32)

    def send(x, k, *earlier):
        return swap(after(x, *earlier) if earlier else x, "shard", 4, k)

    across = send(out_grad, 2)
    beside = send(out_grad, 1)
    mine, own, near1, far2a, far2b, far3a, far3b = pack(meta, queries, keys_in, values, out_grad)
    piece1 = send(near1, 1)
    piece3a = send(far3a, 3, beside)
    piece2a = send(far2a, 2, across)
    piece3b = send(far3b, 3, piece3a)
    piece2b = send(far2b, 2, piece2a)
    half = across.shape[0] // 2
    grad_early = grad_attn(meta, (mine, beside, across), out_weight, 0)
    corners = [send(across[:half], 1), send(after(across, piece1, grad_early)[half:], 1)]

    *saved_a, heads_a = forward(meta, (own, piece1, piece2a, piece3a), 0)
    early = backward_early((own, piece1, piece2a, piece3a), grad_early, saved_a)
    heads_a, *early, piece2b, piece3b = lax.optimization_barrier((heads_a, *early, piece2b, piece3b))
    *saved_b, heads_b = forward(meta, (own, piece1, piece2b, piece3b), 1)
    grad_early, heads_b, *corners = lax.optimization_barrier((grad_early, heads_b, *corners))
    grads = (mine, beside, across, *corners)

    out, keep = weight_halves(meta, (heads_a, heads_b), grads)
    recv = swap(out, "core", 2, 1)
    grad_late = grad_attn(meta, after(grads[3:], out), out_weight, 3 * BLOCK)
    pieces = (own, piece1, piece2a, piece3a, piece2b, piece3b)
    own0, *backs = backward(pieces, (grad_early, grad_late), (*saved_a, *saved_b), early)
    own_part, *sends = add_parts(after(keep, own0), recv)
    recvs = [swap(x, "chips", 4, j + 1) for j, x in enumerate(sends)]
    back3, back2 = send(backs[2], 3), send(backs[1], 2)
    done = total_of(own_part, recvs, 1.0 / 8)
    near = [done] + [swap(done, "chips", 4, j) for j in (1, 2, 3)]
    back1 = send(backs[0], 1, near[1])
    weight = join_weight(meta, near)
    weight, *near, back2, back3 = lax.optimization_barrier((weight, *near, back2, back3))
    far = [swap(x, "core", 2, 1) for x in near]
    heads = join_heads(meta, own0, back2, back3)
    return tuple(join_last(meta, far, back1, (*heads, weight)))


def attend_listed(queries, keys_in, values, block_ids, live_count):
    row_count, width_all = queries.shape
    head_count = width_all // HDIM
    block_count = row_count // BLOCK
    score_scale = 1.0 / math.sqrt(HDIM)
    query_blk = queries.reshape(block_count, BLOCK, head_count, HDIM)
    key_blk = keys_in.reshape(block_count, BLOCK, head_count, HDIM)[block_ids].reshape(
        block_count, NB * BLOCK, head_count, HDIM
    )
    value_blk = values.reshape(block_count, BLOCK, head_count, HDIM)[block_ids].reshape(
        block_count, NB * BLOCK, head_count, HDIM
    )
    query_pos = jnp.arange(row_count, dtype=jnp.int32).reshape(block_count, BLOCK)
    key_pos = (
        block_ids[:, :, None] * BLOCK + jnp.arange(BLOCK, dtype=jnp.int32)[None, None, :]
    ).reshape(block_count, NB * BLOCK)
    allowed = (key_pos[:, None, :] < live_count) | (query_pos[:, :, None] >= live_count)
    scores = (
        jnp.einsum("bqhd,bkhd->bhqk", query_blk, key_blk, preferred_element_type=jnp.float32)
        * score_scale
    )
    scores = jnp.where(allowed[:, None], scores, -jnp.inf)
    peak = jnp.max(scores, axis=-1, keepdims=True)
    weights = jnp.exp(scores - peak)
    probs = weights / jnp.sum(weights, axis=-1, keepdims=True)
    return (query_blk, key_blk, value_blk, probs)


def listed_body(queries, keys_in, values, out_grad, out_weight, block_lists, voxel_count):
    local_rows = queries.shape[0]
    live_count = voxel_count[0]
    block_ids = block_lists[0]
    positions = lax.axis_index("shard") * local_rows + jnp.arange(local_rows, dtype=jnp.int32)
    grad_live = jnp.where((positions < live_count)[:, None], out_grad, jnp.zeros_like(out_grad))
    query_head, key_head, value_head = (
        lax.all_to_all(queries, "shard", split_axis=1, concat_axis=0, tiled=True),
        lax.all_to_all(keys_in, "shard", split_axis=1, concat_axis=0, tiled=True),
        lax.all_to_all(values, "shard", split_axis=1, concat_axis=0, tiled=True),
    )
    row_count, width_all = query_head.shape
    head_count = width_all // HDIM
    block_count = row_count // BLOCK
    score_scale = 1.0 / math.sqrt(HDIM)
    query_blk, key_blk, value_blk, probs = attend_listed(
        query_head, key_head, value_head, block_ids, live_count
    )
    prob_bf = probs.astype(jnp.bfloat16)
    heads_out = (
        jnp.einsum("bhqk,bkhd->bqhd", prob_bf, value_blk, preferred_element_type=jnp.float32)
        .reshape(row_count, width_all)
        .astype(jnp.bfloat16)
    )
    row_piece = lax.all_gather(grad_live, "shard", axis=0, tiled=True)
    acc_now = jnp.einsum("rw,ro->wo", heads_out, row_piece, preferred_element_type=jnp.float32)
    product = jnp.einsum("ro,wo->rw", row_piece, out_weight, preferred_element_type=jnp.float32)
    grad_o = product.astype(jnp.bfloat16).reshape(block_count, BLOCK, head_count, HDIM)
    grad_prob = jnp.einsum("bqhd,bkhd->bhqk", grad_o, value_blk, preferred_element_type=jnp.float32)
    row_delta = jnp.sum(probs * grad_prob, axis=-1, keepdims=True)
    dscore = (probs * (grad_prob - row_delta) * score_scale).astype(jnp.bfloat16)
    grad_query = (
        jnp.einsum("bhqk,bkhd->bqhd", dscore, key_blk, preferred_element_type=jnp.float32)
        .reshape(row_count, width_all)
        .astype(jnp.bfloat16)
    )
    onehot = (
        block_ids[:, :, None] == jnp.arange(block_count, dtype=jnp.int32)[None, None, :]
    ).astype(jnp.float32)
    key_parts = jnp.einsum(
        "bhqk,bqhd->bkhd", dscore, query_blk, preferred_element_type=jnp.float32
    ).reshape(block_count, NB, BLOCK, width_all)
    value_parts = jnp.einsum(
        "bhqk,bqhd->bkhd", prob_bf, grad_o, preferred_element_type=jnp.float32
    ).reshape(block_count, NB, BLOCK, width_all)
    grad_key = (
        jnp.einsum("bjc,bjrx->crx", onehot, key_parts, precision=lax.Precision.HIGHEST)
        .reshape(row_count, width_all)
        .astype(jnp.bfloat16)
    )
    grad_value = (
        jnp.einsum("bjc,bjrx->crx", onehot, value_parts, precision=lax.Precision.HIGHEST)
        .reshape(row_count, width_all)
        .astype(jnp.bfloat16)
    )
    query_back, key_back, value_back = (
        lax.all_to_all(grad_query, "shard", split_axis=0, concat_axis=1, tiled=True),
        lax.all_to_all(grad_key, "shard", split_axis=0, concat_axis=1, tiled=True),
        lax.all_to_all(grad_value, "shard", split_axis=0, concat_axis=1, tiled=True),
    )
    scene_total = lax.axis_size(DP)
    summed = lax.psum(acc_now, DP)
    grad_weight = (summed / scene_total).astype(jnp.bfloat16)
    return (query_back, key_back, value_back, grad_weight)


def body(queries, keys_in, values, out_grad, out_weight, block_lists, voxel_count):
    dense = block_lists.shape[1] == NB and queries.shape[0] == BLOCK
    if dense and lax.axis_size("shard") == 4 and lax.axis_size("chips") == 4:
        return dense_body(queries, keys_in, values, out_grad, out_weight, voxel_count)
    return listed_body(queries, keys_in, values, out_grad, out_weight, block_lists, voxel_count)


def solution(mesh):
    chips = mesh.shape["dp"] // 2
    mesh = jax.sharding.Mesh(mesh.devices.reshape(chips, 2, -1), ("chips", "core", "shard"))
    return jax.shard_map(
        body,
        mesh=mesh,
        in_specs=(
            P((*DP, "shard"), None),
            P((*DP, "shard"), None),
            P((*DP, "shard"), None),
            P((*DP, "shard"), None),
            P("shard", None),
            P(DP, None, None),
            P(DP),
        ),
        out_specs=(
            P((*DP, "shard"), None),
            P((*DP, "shard"), None),
            P((*DP, "shard"), None),
            P("shard", None),
        ),
        check_vma=False,
    )
```

profile of v0, /device:TPU:0, one launch (start us, length us, event | category | flops | bytes accessed | tf_op | source)
XLA Modules:
  0.0 114.6 jit_solution(5150688084357618074)
XLA Ops:
  0.6 3.1 %collective-permute-start.3 = (bf16[128,2048]{1,0:T(8,128)(2,1)}, bf16[128,2048]{1,0:T(8,128)(2,1)S(1)}, u32[]{:S(2)}, u32[]{:S(2)}) collective-permute-start(bf16[128,2048]{1,0:T(8,128)(2,1)} %grad_ref.1), channel_id=1, source_target_pairs={{0,1},{1,0},{2,3},{3,2},{4,5},{5,4},{6,7},{7,6},{8,9},{9,8},{10,11... | collective-permute-start | bytes 1572872 | tf_op jit(solution)/shard_map/ppermute | solution.py:40
  3.7 2.6 %collective-permute-start.1 = (bf16[128,2048]{1,0:T(8,128)(2,1)}, bf16[128,2048]{1,0:T(8,128)(2,1)S(1)}, u32[]{:S(2)}, u32[]{:S(2)}) collective-permute-start(bf16[128,2048]{1,0:T(8,128)(2,1)} %grad_ref.1), channel_id=1, source_target_pairs={{0,2},{1,3},{2,0},{3,1},{4,6},{5,7},{6,4},{7,5},{8,10},{9,11},{10,... | collective-permute-start | bytes 1572872 | tf_op jit(solution)/shard_map/ppermute | solution.py:40
  7.0 0.1 pad_add_fusion.meta
  7.1 1.0 copy-done.1
  8.1 1.0 copy-done.2
  9.1 1.0 copy-done.3
  10.2 1.0 copy-done.4
  11.2 1.1 pack_heads.1
  12.3 0.5 collective-permute-start
  12.8 15.0 %collective-permute-done.3.refs_1_ = bf16[128,2048]{1,0:T(8,128)(2,1)S(1)} collective-permute-done((bf16[128,2048]{1,0:T(8,128)(2,1)}, bf16[128,2048]{1,0:T(8,128)(2,1)S(1)}, u32[]{:S(2)}, u32[]{:S(2)}) %collective-permute-start.3) | collective-permute-done | bytes 524320 | tf_op jit(solution)/shard_map/ppermute | solution.py:40
  27.8 3.6 %collective-permute-start.4 = (bf16[3,128,384]{2,1,0:T(8,128)(2,1)S(1)}, bf16[3,128,384]{2,1,0:T(8,128)(2,1)S(1)}, u32[]{:S(2)}, u32[]{:S(2)}) collective-permute-start(bf16[3,128,384]{2,1,0:T(8,128)(2,1)S(1)} %get-tuple-element.66), channel_id=1, source_target_pairs={{0,3},{1,2},{2,1},{3,0},{4,7},{5,6},{6,5},{7,4},{8,11},{9,10},{10,... | collective-permute-start | bytes 884744 | tf_op jit(solution)/shard_map/ppermute | solution.py:40
  31.4 0.0 collective-permute-done.1.refs_2_
  31.4 0.0 collective-permute-start.2
  31.4 2.1 %collective-permute-start.7 = (bf16[64,2048]{1,0:T(8,128)(2,1)S(1)}, bf16[64,2048]{1,0:T(8,128)(2,1)S(1)}, u32[]{:S(2)}, u32[]{:S(2)}) collective-permute-start(bf16[64,2048]{1,0:T(8,128)(2,1)S(1)} %slice.8), channel_id=1, source_target_pairs={{0,1},{1,0},{2,3},{3,2},{4,5},{5,4},{6,7},{7,6},{8,9},{9,8},{10,11... | collective-permute-start | bytes 786440 | tf_op jit(solution)/shard_map/ppermute | solution.py:40
  33.5 1.9 %grad_attn.2.refs_4_.early_ref = bf16[384,512]{1,0:T(8,128)(2,1)S(1)} custom-call(s32[4]{0:T(128)S(1)} %pad_add_fusion.meta, bf16[128,2048]{1,0:T(8,128)(2,1)S(1)} %get-tuple-element.68.refs_0_, bf16[128,2048]{1,0:T(8,128)(2,1)S(1)} %collective-permute-done.3.refs_1_, bf16[128,2048]{1,0:T(8,128)(2,1)S(1)} %collective-permute-done.1.refs_2_, ...), custom_call_target="tpu_custom_call" | custom-call | bytes 1024 | tf_op jit(solution)/shard_map/grad_attn/pallas_call | solution.py:55
  35.4 8.7 %collective-permute-done.p1.refs_1_.near = bf16[3,128,512]{2,1,0:T(8,128)(2,1)S(1)} collective-permute-done((bf16[3,128,512]{2,1,0:T(8,128)(2,1)S(1)}, bf16[3,128,512]{2,1,0:T(8,128)(2,1)S(1)}, u32[]{:S(2)}, u32[]{:S(2)}) %collective-permute-start) | collective-permute-done | bytes 393248 | tf_op jit(solution)/shard_map/ppermute | solution.py:40
  44.1 0.1 collective-permute-start.8
  44.2 1.2 %collective-permute-done.4.p3.refs_3_.far3a = bf16[3,128,384]{2,1,0:T(8,128)(2,1)S(1)} collective-permute-done((bf16[3,128,384]{2,1,0:T(8,128)(2,1)S(1)}, bf16[3,128,384]{2,1,0:T(8,128)(2,1)S(1)}, u32[]{:S(2)}, u32[]{:S(2)}) %collective-permute-start.4) | collective-permute-done | bytes 294944 | tf_op jit(solution)/shard_map/ppermute | solution.py:40
  45.3 3.0 %collective-permute-start.6 = (bf16[3,128,128]{2,1,0:T(8,128)(2,1)S(1)}, bf16[3,128,128]{2,1,0:T(8,128)(2,1)S(1)}, u32[]{:S(2)}, u32[]{:S(2)}) collective-permute-start(bf16[3,128,128]{2,1,0:T(8,128)(2,1)S(1)} %get-tuple-element.78), channel_id=1, source_target_pairs={{0,3},{1,2},{2,1},{3,0},{4,7},{5,6},{6,5},{7,4},{8,11},{9,10},{10,... | collective-permute-start | bytes 294920 | tf_op jit(solution)/shard_map/ppermute | solution.py:40
  48.3 7.6 %collective-permute-done.2.p2.refs_2_.far2a = bf16[3,128,384]{2,1,0:T(8,128)(2,1)S(1)} collective-permute-done((bf16[3,128,384]{2,1,0:T(8,128)(2,1)S(1)}, bf16[3,128,384]{2,1,0:T(8,128)(2,1)S(1)}, u32[]{:S(2)}, u32[]{:S(2)}) %collective-permute-start.2) | collective-permute-done | bytes 294944 | tf_op jit(solution)/shard_map/ppermute | solution.py:40
  55.9 0.0 collective-permute-start.5
  55.9 3.4 %attend_forward.2 = (bf16[3,512,512]{2,1,0:T(8,128)(2,1)S(1)}, f32[3,1,512]{2,1,0:T(1,128)S(1)}, f32[384,512]{1,0:T(8,128)S(1)}, bf16[384,512]{1,0:T(8,128)(2,1)S(1)}) custom-call(s32[4]{0:T(128)S(1)} %pad_add_fusion.meta, bf16[3,128,512]{2,1,0:T(8,128)(2,1)S(1)} %get-tuple-element.61.p0.refs_0_.own, ...), custom_call_target="tpu_custom_call" | custom-call | bytes 1024 | tf_op jit(solution)/shard_map/attend_forward/pallas_call | solution.py:55
  59.3 2.3 %backward_early.1 = (bf16[384,384]{1,0:T(8,128)(2,1)S(1)}, f32[512,384]{1,0:T(8,128)S(1)}, f32[512,384]{1,0:T(8,128)S(1)}) custom-call(bf16[3,128,512]{2,1,0:T(8,128)(2,1)S(1)} %get-tuple-element.61.p0.refs_0_.own, bf16[3,128,512]{2,1,0:T(8,128)(2,1)S(1)} %collective-permute-done.p1.refs_1_.near, ...), custom_call_target="tpu_custom_call" | custom-call | bytes 1024 | tf_op jit(solution)/shard_map/backward_early/pallas_call | solution.py:55
  61.6 3.2 %collective-permute-done.6.p3.far3b = bf16[3,128,128]{2,1,0:T(8,128)(2,1)S(1)} collective-permute-done((bf16[3,128,128]{2,1,0:T(8,128)(2,1)S(1)}, bf16[3,128,128]{2,1,0:T(8,128)(2,1)S(1)}, u32[]{:S(2)}, u32[]{:S(2)}) %collective-permute-start.6) | collective-permute-done | bytes 98336 | tf_op jit(solution)/shard_map/ppermute | solution.py:40
  64.8 0.0 collective-permute-done.5.p2.far2b
  64.8 1.6 %attend_forward.3 = (bf16[1,512,512]{2,1,0:T(8,128)(2,1)S(1)}, f32[1,1,512]{2,1,0:T(1,128)S(1)}, f32[128,512]{1,0:T(8,128)S(1)}, bf16[128,512]{1,0:T(8,128)(2,1)S(1)}) custom-call(s32[4]{0:T(128)S(1)} %pad_add_fusion.meta, bf16[3,128,512]{2,1,0:T(8,128)(2,1)S(1)} %get-tuple-element.61.p0.refs_0_.own, ...), custom_call_target="tpu_custom_call" | custom-call | bytes 1024 | tf_op jit(solution)/shard_map/attend_forward/pallas_call | solution.py:55
  66.5 0.0 collective-permute-done.7.refs_3_.refs_0_
  66.5 0.0 collective-permute-done.8.refs_4_.refs_1_
  66.5 2.4 %weight_halves.1 = (bf16[256,2048]{1,0:T(8,128)(2,1)S(1)}, f32[256,2048]{1,0:T(8,128)S(1)}) custom-call(s32[4]{0:T(128)S(1)} %pad_add_fusion.meta, bf16[384,512]{1,0:T(8,128)(2,1)S(1)} %get-tuple-element.79.heads_a, bf16[128,512]{1,0:T(8,128)(2,1)S(1)} %get-tuple-element.84.heads_b, bf16[128,2048]{1,0:T(8,128)(2,1)S(1)} %get-tuple-element.68.refs_0_, ...), custom_call_target="tpu_custom_call" | custom-call | bytes 1024 | tf_op jit(solution)/shard_map/weight_halves/pallas_call | solution.py:55
  68.9 0.1 collective-permute-start.9
  68.9 1.5 %grad_attn.3.late_ref = bf16[128,512]{1,0:T(8,128)(2,1)S(1)} custom-call(s32[4]{0:T(128)S(1)} %pad_add_fusion.meta, bf16[64,2048]{1,0:T(8,128)(2,1)S(1)} %collective-permute-done.7.refs_3_.refs_0_, bf16[64,2048]{1,0:T(8,128)(2,1)S(1)} %collective-permute-done.8.refs_4_.refs_1_, bf16[512,2048]{1,0:T(8,128)(2,1)S(1)} %copy-done), custom_call_target="tpu_custom_call" | custom-call | bytes 1024 | tf_op jit(solution)/shard_map/grad_attn/pallas_call | solution.py:55
  70.5 1.6 %attend_backward.1 = (bf16[3,128,512]{2,1,0:T(8,128)(2,1)S(1)}, bf16[3,128,512]{2,1,0:T(8,128)(2,1)S(1)}, bf16[3,128,512]{2,1,0:T(8,128)(2,1)S(1)}, bf16[3,128,512]{2,1,0:T(8,128)(2,1)S(1)}) custom-call(bf16[3,128,512]{2,1,0:T(8,128)(2,1)S(1)} %get-tuple-element.61.p0.refs_0_.own, bf16[3,128,512]{2,1,0:T(8,128)(2,1)S(1)} %collective-permute-done.p1.refs_1_.near, ...), custom_call_target="tpu_custom_call" | custom-call | bytes 1024 | tf_op jit(solution)/shard_map/attend_backward/pallas_call | solution.py:55
  72.1 0.0 collective-permute-done.9.recv_ref
  72.1 0.2 add_parts.1
  72.4 1.6 %collective-permute-start.10 = (bf16[64,2048]{1,0:T(8,128)(2,1)S(1)}, bf16[64,2048]{1,0:T(8,128)(2,1)S(1)}, u32[]{:S(2)}, u32[]{:S(2)}) collective-permute-start(bf16[64,2048]{1,0:T(8,128)(2,1)S(1)} %get-tuple-element.101), channel_id=1, source_target_pairs={{0,8},{8,0},{16,24},{24,16},{1,9},{9,1},{17,25},{25,17},{2,10},{10... | collective-permute-start | bytes 786440 | tf_op jit(solution)/shard_map/ppermute | solution.py:40
  73.9 1.5 %collective-permute-start.11 = (bf16[64,2048]{1,0:T(8,128)(2,1)S(1)}, bf16[64,2048]{1,0:T(8,128)(2,1)S(1)}, u32[]{:S(2)}, u32[]{:S(2)}) collective-permute-start(bf16[64,2048]{1,0:T(8,128)(2,1)S(1)} %get-tuple-element.102), channel_id=1, source_target_pairs={{0,16},{8,24},{16,0},{24,8},{1,17},{9,25},{17,1},{25,9},{2,18},{10... | collective-permute-start | bytes 786440 | tf_op jit(solution)/shard_map/ppermute | solution.py:40
  75.5 0.5 collective-permute-start.12
  75.9 1.5 %collective-permute-start.16 = (bf16[3,128,512]{2,1,0:T(8,128)(2,1)S(1)}, bf16[3,128,512]{2,1,0:T(8,128)(2,1)S(1)}, u32[]{:S(2)}, u32[]{:S(2)}) collective-permute-start(bf16[3,128,512]{2,1,0:T(8,128)(2,1)S(1)} %get-tuple-element.104), channel_id=1, source_target_pairs={{0,2},{1,3},{2,0},{3,1},{4,6},{5,7},{6,4},{7,5},{8,10},{9,11},{10,... | collective-permute-start | bytes 1179656 | tf_op jit(solution)/shard_map/ppermute | solution.py:40
  77.4 2.5 %collective-permute-start.17 = (bf16[3,128,512]{2,1,0:T(8,128)(2,1)S(1)}, bf16[3,128,512]{2,1,0:T(8,128)(2,1)S(1)}, u32[]{:S(2)}, u32[]{:S(2)}) collective-permute-start(bf16[3,128,512]{2,1,0:T(8,128)(2,1)S(1)} %get-tuple-element.105), channel_id=1, source_target_pairs={{0,3},{1,2},{2,1},{3,0},{4,7},{5,6},{6,5},{7,4},{8,11},{9,10},{10,... | collective-permute-start | bytes 1179656 | tf_op jit(solution)/shard_map/ppermute | solution.py:40
  79.9 1.6 %collective-permute-done.10.r1 = bf16[64,2048]{1,0:T(8,128)(2,1)S(1)} collective-permute-done((bf16[64,2048]{1,0:T(8,128)(2,1)S(1)}, bf16[64,2048]{1,0:T(8,128)(2,1)S(1)}, u32[]{:S(2)}, u32[]{:S(2)}) %collective-permute-start.10) | collective-permute-done | bytes 262176 | tf_op jit(solution)/shard_map/ppermute | solution.py:40
  81.5 6.4 %collective-permute-done.11.r2 = bf16[64,2048]{1,0:T(8,128)(2,1)S(1)} collective-permute-done((bf16[64,2048]{1,0:T(8,128)(2,1)S(1)}, bf16[64,2048]{1,0:T(8,128)(2,1)S(1)}, u32[]{:S(2)}, u32[]{:S(2)}) %collective-permute-start.11) | collective-permute-done | bytes 262176 | tf_op jit(solution)/shard_map/ppermute | solution.py:40
  88.0 0.0 collective-permute-done.12.r3
  88.0 0.1 scene_mean.1.refs_0_
  88.1 1.3 %collective-permute-start.13 = (bf16[64,2048]{1,0:T(8,128)(2,1)S(1)}, bf16[64,2048]{1,0:T(8,128)(2,1)S(1)}, u32[]{:S(2)}, u32[]{:S(2)}) collective-permute-start(bf16[64,2048]{1,0:T(8,128)(2,1)S(1)} %scene_mean.1.refs_0_), channel_id=1, source_target_pairs={{0,8},{8,0},{16,24},{24,16},{1,9},{9,1},{17,25},{25,17},{2,10},{10... | collective-permute-start | bytes 786440 | tf_op jit(solution)/shard_map/ppermute | solution.py:40
  89.4 1.8 %collective-permute-start.15 = (bf16[64,2048]{1,0:T(8,128)(2,1)S(1)}, bf16[64,2048]{1,0:T(8,128)(2,1)S(1)}, u32[]{:S(2)}, u32[]{:S(2)}) collective-permute-start(bf16[64,2048]{1,0:T(8,128)(2,1)S(1)} %scene_mean.1.refs_0_), channel_id=1, source_target_pairs={{0,24},{8,16},{16,8},{24,0},{1,25},{9,17},{17,9},{25,1},{2,26},{10... | collective-permute-start | bytes 786440 | tf_op jit(solution)/shard_map/ppermute | solution.py:40
  91.2 0.5 collective-permute-start.14
  91.7 5.8 %collective-permute-done.13.refs_1_ = bf16[64,2048]{1,0:T(8,128)(2,1)S(1)} collective-permute-done((bf16[64,2048]{1,0:T(8,128)(2,1)S(1)}, bf16[64,2048]{1,0:T(8,128)(2,1)S(1)}, u32[]{:S(2)}, u32[]{:S(2)}) %collective-permute-start.13) | collective-permute-done | bytes 262176 | tf_op jit(solution)/shard_map/ppermute | solution.py:40
  97.4 1.6 %collective-permute-start.22 = (bf16[3,128,512]{2,1,0:T(8,128)(2,1)S(1)}, bf16[3,128,512]{2,1,0:T(8,128)(2,1)S(1)}, u32[]{:S(2)}, u32[]{:S(2)}) collective-permute-start(bf16[3,128,512]{2,1,0:T(8,128)(2,1)S(1)} %get-tuple-element.111), channel_id=1, source_target_pairs={{0,1},{1,0},{2,3},{3,2},{4,5},{5,4},{6,7},{7,6},{8,9},{9,8},{10,11... | collective-permute-start | bytes 1179656 | tf_op jit(solution)/shard_map/ppermute | solution.py:40
  99.1 3.4 %collective-permute-done.15.refs_3_ = bf16[64,2048]{1,0:T(8,128)(2,1)S(1)} collective-permute-done((bf16[64,2048]{1,0:T(8,128)(2,1)S(1)}, bf16[64,2048]{1,0:T(8,128)(2,1)S(1)}, u32[]{:S(2)}, u32[]{:S(2)}) %collective-permute-start.15) | collective-permute-done | bytes 262176 | tf_op jit(solution)/shard_map/ppermute | solution.py:40
  102.5 1.4 %collective-permute-done.14.refs_2_ = bf16[64,2048]{1,0:T(8,128)(2,1)S(1)} collective-permute-done((bf16[64,2048]{1,0:T(8,128)(2,1)S(1)}, bf16[64,2048]{1,0:T(8,128)(2,1)S(1)}, u32[]{:S(2)}, u32[]{:S(2)}) %collective-permute-start.14) | collective-permute-done | bytes 262176 | tf_op jit(solution)/shard_map/ppermute | solution.py:40
  103.8 1.6 %join_weight.1.refs_8_ = bf16[512,2048]{1,0:T(8,128)(2,1)} custom-call(s32[4]{0:T(128)S(1)} %pad_add_fusion.meta, bf16[64,2048]{1,0:T(8,128)(2,1)S(1)} %scene_mean.1.refs_0_, bf16[64,2048]{1,0:T(8,128)(2,1)S(1)} %collective-permute-done.13.refs_1_, bf16[64,2048]{1,0:T(8,128)(2,1)S(1)} %collective-permute-done.14.refs_2_, ...), custom_call_target="tpu_custom_call" | custom-call | bytes 1024 | tf_op jit(solution)/shard_map/join_weight/pallas_call | solution.py:317
  105.5 0.1 collective-permute-done.16.back2
  105.6 0.0 collective-permute-done.17.back3
  105.6 0.0 collective-permute-start.18
  105.6 0.5 collective-permute-start.19
  106.1 0.1 collective-permute-start.20
  106.2 0.5 collective-permute-start.21
  106.6 1.6 %join_heads.1 = (bf16[128,2048]{1,0:T(8,128)(2,1)}, bf16[128,2048]{1,0:T(8,128)(2,1)}, bf16[128,2048]{1,0:T(8,128)(2,1)}) custom-call(s32[4]{0:T(128)S(1)} %pad_add_fusion.meta, bf16[3,128,512]{2,1,0:T(8,128)(2,1)S(1)} %get-tuple-element.98.own, bf16[3,128,512]{2,1,0:T(8,128)(2,1)S(1)} %collective-permute-done.16.back2, ...), custom_call_target="tpu_custom_call" | custom-call | bytes 1024 | tf_op jit(solution)/shard_map/join_heads/pallas_call | solution.py:317
  108.2 0.0 collective-permute-done.18.refs_0_
  108.3 0.0 collective-permute-done.19.refs_1_
  108.3 0.0 collective-permute-done.20.refs_2_
  108.3 0.0 collective-permute-done.21.refs_3_
  108.3 4.5 %collective-permute-done.22.refs_4_ = bf16[3,128,512]{2,1,0:T(8,128)(2,1)S(1)} collective-permute-done((bf16[3,128,512]{2,1,0:T(8,128)(2,1)S(1)}, bf16[3,128,512]{2,1,0:T(8,128)(2,1)S(1)}, u32[]{:S(2)}, u32[]{:S(2)}) %collective-permute-start.22) | collective-permute-done | bytes 393248 | tf_op jit(solution)/shard_map/ppermute | solution.py:40
  112.8 1.8 %join_last.1 = (bf16[128,2048]{1,0:T(8,128)(2,1)}, bf16[128,2048]{1,0:T(8,128)(2,1)}, bf16[128,2048]{1,0:T(8,128)(2,1)}, bf16[512,2048]{1,0:T(8,128)(2,1)}) custom-call(s32[4]{0:T(128)S(1)} %pad_add_fusion.meta, bf16[64,2048]{1,0:T(8,128)(2,1)S(1)} %collective-permute-done.18.refs_0_, ...), custom_call_target="tpu_custom_call", output_to_operand_aliasing={{0}: (6, {}), {1}: (7, {}), {2}: (8, {}), {3}: (9, {})} | custom-call | bytes 1024 | tf_op jit(solution)/shard_map/join_last/pallas_call | solution.py:317
  (8 shorter events, 0.0 us)
Async XLA Ops:
  0.6 32.9 %copy-start = (bf16[512,2048]{1,0:T(8,128)(2,1)S(1)}, bf16[512,2048]{1,0:T(8,128)(2,1)}, u32[]{:S(2)}) copy-start(bf16[512,2048]{1,0:T(8,128)(2,1)} %refs_2_.1) | copy-start | bytes 6291460
  0.6 27.2 %collective-permute-start.3 = (bf16[128,2048]{1,0:T(8,128)(2,1)}, bf16[128,2048]{1,0:T(8,128)(2,1)S(1)}, u32[]{:S(2)}, u32[]{:S(2)}) collective-permute-start(bf16[128,2048]{1,0:T(8,128)(2,1)} %grad_ref.1), channel_id=1, source_target_pairs={{0,1},{1,0},{2,3},{3,2},{4,5},{5,4},{6,7},{7,6},{8,9},{9,8},{10,11... | collective-permute-start | bytes 1572872 | tf_op jit(solution)/shard_map/ppermute | solution.py:40
  3.7 27.7 %collective-permute-start.1 = (bf16[128,2048]{1,0:T(8,128)(2,1)}, bf16[128,2048]{1,0:T(8,128)(2,1)S(1)}, u32[]{:S(2)}, u32[]{:S(2)}) collective-permute-start(bf16[128,2048]{1,0:T(8,128)(2,1)} %grad_ref.1), channel_id=1, source_target_pairs={{0,2},{1,3},{2,0},{3,1},{4,6},{5,7},{6,4},{7,5},{8,10},{9,11},{10,... | collective-permute-start | bytes 1572872 | tf_op jit(solution)/shard_map/ppermute | solution.py:40
  7.0 1.0 copy-start.1
  8.1 1.0 copy-start.2
  9.1 1.0 copy-start.3
  10.2 1.0 copy-start.4
  12.3 31.8 %collective-permute-start = (bf16[3,128,512]{2,1,0:T(8,128)(2,1)S(1)}, bf16[3,128,512]{2,1,0:T(8,128)(2,1)S(1)}, u32[]{:S(2)}, u32[]{:S(2)}) collective-permute-start(bf16[3,128,512]{2,1,0:T(8,128)(2,1)S(1)} %get-tuple-element.62), channel_id=1, source_target_pairs={{0,1},{1,0},{2,3},{3,2},{4,5},{5,4},{6,7},{7,6},{8,9},{9,8},{10,11... | collective-permute-start | bytes 1179656 | tf_op jit(solution)/shard_map/ppermute | solution.py:40
  27.8 17.5 %collective-permute-start.4 = (bf16[3,128,384]{2,1,0:T(8,128)(2,1)S(1)}, bf16[3,128,384]{2,1,0:T(8,128)(2,1)S(1)}, u32[]{:S(2)}, u32[]{:S(2)}) collective-permute-start(bf16[3,128,384]{2,1,0:T(8,128)(2,1)S(1)} %get-tuple-element.66), channel_id=1, source_target_pairs={{0,3},{1,2},{2,1},{3,0},{4,7},{5,6},{6,5},{7,4},{8,11},{9,10},{10,... | collective-permute-start | bytes 884744 | tf_op jit(solution)/shard_map/ppermute | solution.py:40
  31.4 24.5 %collective-permute-start.2 = (bf16[3,128,384]{2,1,0:T(8,128)(2,1)S(1)}, bf16[3,128,384]{2,1,0:T(8,128)(2,1)S(1)}, u32[]{:S(2)}, u32[]{:S(2)}) collective-permute-start(bf16[3,128,384]{2,1,0:T(8,128)(2,1)S(1)} %get-tuple-element.64), channel_id=1, source_target_pairs={{0,2},{1,3},{2,0},{3,1},{4,6},{5,7},{6,4},{7,5},{8,10},{9,11},{10,... | collective-permute-start | bytes 884744 | tf_op jit(solution)/shard_map/ppermute | solution.py:40
  31.4 35.1 %collective-permute-start.7 = (bf16[64,2048]{1,0:T(8,128)(2,1)S(1)}, bf16[64,2048]{1,0:T(8,128)(2,1)S(1)}, u32[]{:S(2)}, u32[]{:S(2)}) collective-permute-start(bf16[64,2048]{1,0:T(8,128)(2,1)S(1)} %slice.8), channel_id=1, source_target_pairs={{0,1},{1,0},{2,3},{3,2},{4,5},{5,4},{6,7},{7,6},{8,9},{9,8},{10,11... | collective-permute-start | bytes 786440 | tf_op jit(solution)/shard_map/ppermute | solution.py:40
  44.1 22.4 %collective-permute-start.8 = (bf16[64,2048]{1,0:T(8,128)(2,1)S(1)}, bf16[64,2048]{1,0:T(8,128)(2,1)S(1)}, u32[]{:S(2)}, u32[]{:S(2)}) collective-permute-start(bf16[64,2048]{1,0:T(8,128)(2,1)S(1)} %slice.7), channel_id=1, source_target_pairs={{0,1},{1,0},{2,3},{3,2},{4,5},{5,4},{6,7},{7,6},{8,9},{9,8},{10,11... | collective-permute-start | bytes 786440 | tf_op jit(solution)/shard_map/ppermute | solution.py:40
  45.3 19.5 %collective-permute-start.6 = (bf16[3,128,128]{2,1,0:T(8,128)(2,1)S(1)}, bf16[3,128,128]{2,1,0:T(8,128)(2,1)S(1)}, u32[]{:S(2)}, u32[]{:S(2)}) collective-permute-start(bf16[3,128,128]{2,1,0:T(8,128)(2,1)S(1)} %get-tuple-element.78), channel_id=1, source_target_pairs={{0,3},{1,2},{2,1},{3,0},{4,7},{5,6},{6,5},{7,4},{8,11},{9,10},{10,... | collective-permute-start | bytes 294920 | tf_op jit(solution)/shard_map/ppermute | solution.py:40
  55.9 8.9 %collective-permute-start.5 = (bf16[3,128,128]{2,1,0:T(8,128)(2,1)S(1)}, bf16[3,128,128]{2,1,0:T(8,128)(2,1)S(1)}, u32[]{:S(2)}, u32[]{:S(2)}) collective-permute-start(bf16[3,128,128]{2,1,0:T(8,128)(2,1)S(1)} %get-tuple-element.76), channel_id=1, source_target_pairs={{0,2},{1,3},{2,0},{3,1},{4,6},{5,7},{6,4},{7,5},{8,10},{9,11},{10,... | collective-permute-start | bytes 294920 | tf_op jit(solution)/shard_map/ppermute | solution.py:40
  68.9 3.3 %collective-permute-start.9 = (bf16[256,2048]{1,0:T(8,128)(2,1)S(1)}, bf16[256,2048]{1,0:T(8,128)(2,1)S(1)}, u32[]{:S(2)}, u32[]{:S(2)}) collective-permute-start(bf16[256,2048]{1,0:T(8,128)(2,1)S(1)} %get-tuple-element.89), channel_id=1, source_target_pairs={{0,4},{4,0},{1,5},{5,1},{2,6},{6,2},{3,7},{7,3},{8,12},{12,8},{9,1... | collective-permute-start | bytes 3145736 | tf_op jit(solution)/shard_map/ppermute | solution.py:40
  72.4 9.2 %collective-permute-start.10 = (bf16[64,2048]{1,0:T(8,128)(2,1)S(1)}, bf16[64,2048]{1,0:T(8,128)(2,1)S(1)}, u32[]{:S(2)}, u32[]{:S(2)}) collective-permute-start(bf16[64,2048]{1,0:T(8,128)(2,1)S(1)} %get-tuple-element.101), channel_id=1, source_target_pairs={{0,8},{8,0},{16,24},{24,16},{1,9},{9,1},{17,25},{25,17},{2,10},{10... | collective-permute-start | bytes 786440 | tf_op jit(solution)/shard_map/ppermute | solution.py:40
  73.9 14.0 %collective-permute-start.11 = (bf16[64,2048]{1,0:T(8,128)(2,1)S(1)}, bf16[64,2048]{1,0:T(8,128)(2,1)S(1)}, u32[]{:S(2)}, u32[]{:S(2)}) collective-permute-start(bf16[64,2048]{1,0:T(8,128)(2,1)S(1)} %get-tuple-element.102), channel_id=1, source_target_pairs={{0,16},{8,24},{16,0},{24,8},{1,17},{9,25},{17,1},{25,9},{2,18},{10... | collective-permute-start | bytes 786440 | tf_op jit(solution)/shard_map/ppermute | solution.py:40
  75.5 12.5 %collective-permute-start.12 = (bf16[64,2048]{1,0:T(8,128)(2,1)S(1)}, bf16[64,2048]{1,0:T(8,128)(2,1)S(1)}, u32[]{:S(2)}, u32[]{:S(2)}) collective-permute-start(bf16[64,2048]{1,0:T(8,128)(2,1)S(1)} %get-tuple-element.103), channel_id=1, source_target_pairs={{0,24},{8,16},{16,8},{24,0},{1,25},{9,17},{17,9},{25,1},{2,26},{10... | collective-permute-start | bytes 786440 | tf_op jit(solution)/shard_map/ppermute | solution.py:40
  75.9 29.7 %collective-permute-start.16 = (bf16[3,128,512]{2,1,0:T(8,128)(2,1)S(1)}, bf16[3,128,512]{2,1,0:T(8,128)(2,1)S(1)}, u32[]{:S(2)}, u32[]{:S(2)}) collective-permute-start(bf16[3,128,512]{2,1,0:T(8,128)(2,1)S(1)} %get-tuple-element.104), channel_id=1, source_target_pairs={{0,2},{1,3},{2,0},{3,1},{4,6},{5,7},{6,4},{7,5},{8,10},{9,11},{10,... | collective-permute-start | bytes 1179656 | tf_op jit(solution)/shard_map/ppermute | solution.py:40
  77.4 28.2 %collective-permute-start.17 = (bf16[3,128,512]{2,1,0:T(8,128)(2,1)S(1)}, bf16[3,128,512]{2,1,0:T(8,128)(2,1)S(1)}, u32[]{:S(2)}, u32[]{:S(2)}) collective-permute-start(bf16[3,128,512]{2,1,0:T(8,128)(2,1)S(1)} %get-tuple-element.105), channel_id=1, source_target_pairs={{0,3},{1,2},{2,1},{3,0},{4,7},{5,6},{6,5},{7,4},{8,11},{9,10},{10,... | collective-permute-start | bytes 1179656 | tf_op jit(solution)/shard_map/ppermute | solution.py:40
  88.1 9.3 %collective-permute-start.13 = (bf16[64,2048]{1,0:T(8,128)(2,1)S(1)}, bf16[64,2048]{1,0:T(8,128)(2,1)S(1)}, u32[]{:S(2)}, u32[]{:S(2)}) collective-permute-start(bf16[64,2048]{1,0:T(8,128)(2,1)S(1)} %scene_mean.1.refs_0_), channel_id=1, source_target_pairs={{0,8},{8,0},{16,24},{24,16},{1,9},{9,1},{17,25},{25,17},{2,10},{10... | collective-permute-start | bytes 786440 | tf_op jit(solution)/shard_map/ppermute | solution.py:40
  89.4 13.1 %collective-permute-start.15 = (bf16[64,2048]{1,0:T(8,128)(2,1)S(1)}, bf16[64,2048]{1,0:T(8,128)(2,1)S(1)}, u32[]{:S(2)}, u32[]{:S(2)}) collective-permute-start(bf16[64,2048]{1,0:T(8,128)(2,1)S(1)} %scene_mean.1.refs_0_), channel_id=1, source_target_pairs={{0,24},{8,16},{16,8},{24,0},{1,25},{9,17},{17,9},{25,1},{2,26},{10... | collective-permute-start | bytes 786440 | tf_op jit(solution)/shard_map/ppermute | solution.py:40
  91.2 12.7 %collective-permute-start.14 = (bf16[64,2048]{1,0:T(8,128)(2,1)S(1)}, bf16[64,2048]{1,0:T(8,128)(2,1)S(1)}, u32[]{:S(2)}, u32[]{:S(2)}) collective-permute-start(bf16[64,2048]{1,0:T(8,128)(2,1)S(1)} %scene_mean.1.refs_0_), channel_id=1, source_target_pairs={{0,16},{8,24},{16,0},{24,8},{1,17},{9,25},{17,1},{25,9},{2,18},{10... | collective-permute-start | bytes 786440 | tf_op jit(solution)/shard_map/ppermute | solution.py:40
  97.4 15.4 %collective-permute-start.22 = (bf16[3,128,512]{2,1,0:T(8,128)(2,1)S(1)}, bf16[3,128,512]{2,1,0:T(8,128)(2,1)S(1)}, u32[]{:S(2)}, u32[]{:S(2)}) collective-permute-start(bf16[3,128,512]{2,1,0:T(8,128)(2,1)S(1)} %get-tuple-element.111), channel_id=1, source_target_pairs={{0,1},{1,0},{2,3},{3,2},{4,5},{5,4},{6,7},{7,6},{8,9},{9,8},{10,11... | collective-permute-start | bytes 1179656 | tf_op jit(solution)/shard_map/ppermute | solution.py:40
  105.6 2.7 %collective-permute-start.18 = (bf16[64,2048]{1,0:T(8,128)(2,1)S(1)}, bf16[64,2048]{1,0:T(8,128)(2,1)S(1)}, u32[]{:S(2)}, u32[]{:S(2)}) collective-permute-start(bf16[64,2048]{1,0:T(8,128)(2,1)S(1)} %scene_mean.1.refs_0_), channel_id=1, source_target_pairs={{0,4},{4,0},{1,5},{5,1},{2,6},{6,2},{3,7},{7,3},{8,12},{12,8},{9,1... | collective-permute-start | bytes 786440 | tf_op jit(solution)/shard_map/ppermute | solution.py:40
  105.6 2.7 %collective-permute-start.19 = (bf16[64,2048]{1,0:T(8,128)(2,1)S(1)}, bf16[64,2048]{1,0:T(8,128)(2,1)S(1)}, u32[]{:S(2)}, u32[]{:S(2)}) collective-permute-start(bf16[64,2048]{1,0:T(8,128)(2,1)S(1)} %collective-permute-done.13.refs_1_), channel_id=1, source_target_pairs={{0,4},{4,0},{1,5},{5,1},{2,6},{6,2},{3,7},{7,3},{8,12},{12,8},{9,1... | collective-permute-start | bytes 786440 | tf_op jit(solution)/shard_map/ppermute | solution.py:40
  106.1 2.2 %collective-permute-start.20 = (bf16[64,2048]{1,0:T(8,128)(2,1)S(1)}, bf16[64,2048]{1,0:T(8,128)(2,1)S(1)}, u32[]{:S(2)}, u32[]{:S(2)}) collective-permute-start(bf16[64,2048]{1,0:T(8,128)(2,1)S(1)} %collective-permute-done.14.refs_2_), channel_id=1, source_target_pairs={{0,4},{4,0},{1,5},{5,1},{2,6},{6,2},{3,7},{7,3},{8,12},{12,8},{9,1... | collective-permute-start | bytes 786440 | tf_op jit(solution)/shard_map/ppermute | solution.py:40
  106.2 2.1 %collective-permute-start.21 = (bf16[64,2048]{1,0:T(8,128)(2,1)S(1)}, bf16[64,2048]{1,0:T(8,128)(2,1)S(1)}, u32[]{:S(2)}, u32[]{:S(2)}) collective-permute-start(bf16[64,2048]{1,0:T(8,128)(2,1)S(1)} %collective-permute-done.15.refs_3_), channel_id=1, source_target_pairs={{0,4},{4,0},{1,5},{5,1},{2,6},{6,2},{3,7},{7,3},{8,12},{12,8},{9,1... | collective-permute-start | bytes 786440 | tf_op jit(solution)/shard_map/ppermute | solution.py:40
where the time goes:
time: 115 us
  waiting for transfers between devices  58.9 us (51%)
  starting transfers between devices  28.7 us (25%)
  Pallas kernels  21.2 us (18%)
  local copies, waits for them, and re-layouts  4.21 us (4%)
  between operations  1.47 us (1%)
    ppermute x23, waiting for transfers between devices, swap(): return lax.ppermute(x, axis, [(i, i ^ flip) for i in range(size)])  58.9 us
    ppermute x23, starting transfers between devices, swap(): return lax.ppermute(x, axis, [(i, i ^ flip) for i in range(size)])  28.7 us
    pallas_call x9, Pallas kernels, whole(): pl.pallas_call(kernel, out_shape=out_shape, in_specs=[pl.BlockSpec(memory...  15.1 us
    pallas_call x3, Pallas kernels, join(): pl.pallas_call(kernel, out_shape=shapes, in_specs=[pl.BlockSpec(memory_sp...  5.04 us
    unnamed x10, local copies, waits for them, and re-layouts  4.17 us
  transfers between devices with their start and end apart: 23, of which 12 were waited for; matrix products, arithmetic and copies ran while one was open for 0% of the time, Pallas kernels for 15%

commit v1 on v0

--- a/solution.py
+++ b/solution.py
@@ -338,24 +338,26 @@
     return join(join_weight_kernel, meta, near, [sds((8 * size, outw), bf16)], [4 * size // LINE], "join_weight")[0]
 
 
-def join_heads_kernel(meta, own, back2, back3, *refs):
-    run_all(head_copies(meta, {0: own, 2: back2, 3: back3}, refs[:3], refs[3]))
-
-
-def join_heads(meta, own, back2, back3):
+def join_heads_kernel(meta, own, back2, *refs):
+    run_all(head_copies(meta, {0: own, 2: back2}, refs[:3], refs[3]))
+
+
+def join_heads(meta, own, back2):
     _, rows, width = own.shape
     shapes = [sds((rows, 4 * width), bf16)] * 3
-    return join(join_heads_kernel, meta, (own, back2, back3), shapes, [9], "join_heads")
+    return join(join_heads_kernel, meta, (own, back2), shapes, [6], "join_heads")
 
 
 def join_last_kernel(meta, *refs):
-    far, back1, outs, sems = refs[:4], refs[4], refs[9:13], refs[13:]
-    run_all(weight_copies(meta, far, 4, outs[3], sems[0]) + head_copies(meta, {1: back1}, outs[:3], sems[1]))
-
-
-def join_last(meta, far, back1, outs):
+    far, back1, back3, outs, sems = refs[:4], refs[4], refs[5], refs[10:14], refs[14:]
+    heads = head_copies(meta, {1: back1, 3: back3}, outs[:3], sems[1])
+    run_all(weight_copies(meta, far, 4, outs[3], sems[0]) + heads)
+
+
+def join_last(meta, far, back1, back3, outs):
     shapes = [sds(x.shape, x.dtype) for x in outs]
-    return join(join_last_kernel, meta, (*far, back1), shapes, [4 * far[0].shape[0] // LINE, 3], "join_last", outs)
+    parts = (*far, back1, back3)
+    return join(join_last_kernel, meta, parts, shapes, [4 * far[0].shape[0] // LINE, 6], "join_last", outs)
 
 
 def dense_body(queries, keys_in, values, out_grad, out_weight, voxel_count):
@@ -369,7 +371,7 @@
     beside = send(out_grad, 1)
     mine, own, near1, far2a, far2b, far3a, far3b = pack(meta, queries, keys_in, values, out_grad)
     piece1 = send(near1, 1)
-    piece3a = send(far3a, 3, beside)
+    piece3a = send(far3a, 3, across)
     piece2a = send(far2a, 2, across)
     piece3b = send(far3b, 3, piece3a)
     piece2b = send(far2b, 2, piece2a)
@@ -395,11 +397,10 @@
     done = total_of(own_part, recvs, 1.0 / 8)
     near = [done] + [swap(done, "chips", 4, j) for j in (1, 2, 3)]
     back1 = send(backs[0], 1, near[1])
-    weight = join_weight(meta, near)
-    weight, *near, back2, back3 = lax.optimization_barrier((weight, *near, back2, back3))
-    far = [swap(x, "core", 2, 1) for x in near]
-    heads = join_heads(meta, own0, back2, back3)
-    return tuple(join_last(meta, far, back1, (*heads, weight)))
+    outs = (*join_heads(meta, own0, back2), join_weight(meta, near))
+    *outs, near1, back2, back3 = lax.optimization_barrier((*outs, near[1], back2, back3))
+    far = [swap(x, "core", 2, 1) for x in (near[0], near1, *near[2:])]
+    return tuple(join_last(meta, far, back1, back3, outs))
 
 
 def attend_listed(queries, keys_in, values, block_ids, live_count):

time: 115 us -> 116 us (level)
  waiting for transfers between devices: 58.9 us -> 63.7 us
  starting transfers between devices: 28.7 us -> 25 us
    ppermute x23, waiting for transfers between devices: 58.9 us -> 63.7 us  [swap(): return lax.ppermute(x, axis, [(i, i ^ flip) for i in range(size)])]
    ppermute x23, starting transfers between devices: 28.7 us -> 25 us  [swap(): return lax.ppermute(x, axis, [(i, i ^ flip) for i in range(size)])]
  transfers between devices with their start and end apart: 23 -> 23, of which waited for: 12 -> 13; matrix products, arithmetic and copies ran while one was open for 0% -> 0% of each run, Pallas kernels for 15% -> 14%
where the time goes in v1:
time: 116 us
  waiting for transfers between devices  63.7 us (55%)
  starting transfers between devices  25 us (22%)
  Pallas kernels  21.2 us (18%)
  local copies, waits for them, and re-layouts  4.21 us (4%)
  between operations  1.47 us (1%)
    ppermute x23, waiting for transfers between devices, swap(): return lax.ppermute(x, axis, [(i, i ^ flip) for i in range(size)])  63.7 us
    ppermute x23, starting transfers between devices, swap(): return lax.ppermute(x, axis, [(i, i ^ flip) for i in range(size)])  25 us
    pallas_call x9, Pallas kernels, whole(): pl.pallas_call(kernel, out_shape=out_shape, in_specs=[pl.BlockSpec(memory...  15.1 us
    pallas_call x3, Pallas kernels, join(): pl.pallas_call(kernel, out_shape=shapes, in_specs=[pl.BlockSpec(memory_sp...  5.05 us
    unnamed x10, local copies, waits for them, and re-layouts  4.17 us
  transfers between devices with their start and end apart: 23, of which 13 were waited for; matrix products, arithmetic and copies ran while one was open for 0% of the time, Pallas kernels for 14%

profile of v1, /device:TPU:0, one launch (start us, length us, event | category | flops | bytes accessed | tf_op | source)
XLA Modules:
  0.0 115.8 jit_solution(15992291783330643388)
XLA Ops:
  0.6 4.1 %collective-permute-start.1 = (bf16[128,2048]{1,0:T(8,128)(2,1)}, bf16[128,2048]{1,0:T(8,128)(2,1)S(1)}, u32[]{:S(2)}, u32[]{:S(2)}) collective-permute-start(bf16[128,2048]{1,0:T(8,128)(2,1)} %grad_ref.1), channel_id=1, source_target_pairs={{0,2},{1,3},{2,0},{3,1},{4,6},{5,7},{6,4},{7,5},{8,10},{9,11},{10,... | collective-permute-start | bytes 1572872 | tf_op jit(solution)/shard_map/ppermute | solution.py:40
  4.7 1.6 %collective-permute-start.4 = (bf16[128,2048]{1,0:T(8,128)(2,1)}, bf16[128,2048]{1,0:T(8,128)(2,1)S(1)}, u32[]{:S(2)}, u32[]{:S(2)}) collective-permute-start(bf16[128,2048]{1,0:T(8,128)(2,1)} %grad_ref.1), channel_id=1, source_target_pairs={{0,1},{1,0},{2,3},{3,2},{4,5},{5,4},{6,7},{7,6},{8,9},{9,8},{10,11... | collective-permute-start | bytes 1572872 | tf_op jit(solution)/shard_map/ppermute | solution.py:40
  7.0 0.1 pad_add_fusion.meta
  7.1 1.0 copy-done.1
  8.1 1.0 copy-done.2
  9.1 1.0 copy-done.3
  10.2 1.0 copy-done.4
  11.2 1.1 pack_heads.1
  12.3 0.5 collective-permute-start
  12.8 15.4 %collective-permute-done.1.refs_2_ = bf16[128,2048]{1,0:T(8,128)(2,1)S(1)} collective-permute-done((bf16[128,2048]{1,0:T(8,128)(2,1)}, bf16[128,2048]{1,0:T(8,128)(2,1)S(1)}, u32[]{:S(2)}, u32[]{:S(2)}) %collective-permute-start.1) | collective-permute-done | bytes 524320 | tf_op jit(solution)/shard_map/ppermute | solution.py:40
  28.2 3.5 %collective-permute-start.3 = (bf16[3,128,384]{2,1,0:T(8,128)(2,1)S(1)}, bf16[3,128,384]{2,1,0:T(8,128)(2,1)S(1)}, u32[]{:S(2)}, u32[]{:S(2)}) collective-permute-start(bf16[3,128,384]{2,1,0:T(8,128)(2,1)S(1)} %get-tuple-element.65), channel_id=1, source_target_pairs={{0,3},{1,2},{2,1},{3,0},{4,7},{5,6},{6,5},{7,4},{8,11},{9,10},{10,... | collective-permute-start | bytes 884744 | tf_op jit(solution)/shard_map/ppermute | solution.py:40
  31.8 0.0 collective-permute-start.2
  31.8 0.9 collective-permute-start.7
  32.7 0.0 collective-permute-done.4.refs_1_
  32.7 1.9 %grad_attn.2.refs_4_.early_ref = bf16[384,512]{1,0:T(8,128)(2,1)S(1)} custom-call(s32[4]{0:T(128)S(1)} %pad_add_fusion.meta, bf16[128,2048]{1,0:T(8,128)(2,1)S(1)} %get-tuple-element.67.refs_0_, bf16[128,2048]{1,0:T(8,128)(2,1)S(1)} %collective-permute-done.4.refs_1_, bf16[128,2048]{1,0:T(8,128)(2,1)S(1)} %collective-permute-done.1.refs_2_, ...), custom_call_target="tpu_custom_call" | custom-call | bytes 1024 | tf_op jit(solution)/shard_map/grad_attn/pallas_call | solution.py:55
  34.6 10.7 %collective-permute-done.p1.refs_1_.near = bf16[3,128,512]{2,1,0:T(8,128)(2,1)S(1)} collective-permute-done((bf16[3,128,512]{2,1,0:T(8,128)(2,1)S(1)}, bf16[3,128,512]{2,1,0:T(8,128)(2,1)S(1)}, u32[]{:S(2)}, u32[]{:S(2)}) %collective-permute-start) | collective-permute-done | bytes 393248 | tf_op jit(solution)/shard_map/ppermute | solution.py:40
  45.3 0.1 collective-permute-start.8
  45.4 0.0 collective-permute-done.3.p3.refs_3_.far3a
  45.4 3.5 %collective-permute-start.6 = (bf16[3,128,128]{2,1,0:T(8,128)(2,1)S(1)}, bf16[3,128,128]{2,1,0:T(8,128)(2,1)S(1)}, u32[]{:S(2)}, u32[]{:S(2)}) collective-permute-start(bf16[3,128,128]{2,1,0:T(8,128)(2,1)S(1)} %get-tuple-element.77), channel_id=1, source_target_pairs={{0,3},{1,2},{2,1},{3,0},{4,7},{5,6},{6,5},{7,4},{8,11},{9,10},{10,... | collective-permute-start | bytes 294920 | tf_op jit(solution)/shard_map/ppermute | solution.py:40
  48.9 8.4 %collective-permute-done.2.p2.refs_2_.far2a = bf16[3,128,384]{2,1,0:T(8,128)(2,1)S(1)} collective-permute-done((bf16[3,128,384]{2,1,0:T(8,128)(2,1)S(1)}, bf16[3,128,384]{2,1,0:T(8,128)(2,1)S(1)}, u32[]{:S(2)}, u32[]{:S(2)}) %collective-permute-start.2) | collective-permute-done | bytes 294944 | tf_op jit(solution)/shard_map/ppermute | solution.py:40
  57.3 0.0 collective-permute-start.5
  57.3 3.4 %attend_forward.2 = (bf16[3,512,512]{2,1,0:T(8,128)(2,1)S(1)}, f32[3,1,512]{2,1,0:T(1,128)S(1)}, f32[384,512]{1,0:T(8,128)S(1)}, bf16[384,512]{1,0:T(8,128)(2,1)S(1)}) custom-call(s32[4]{0:T(128)S(1)} %pad_add_fusion.meta, bf16[3,128,512]{2,1,0:T(8,128)(2,1)S(1)} %get-tuple-element.60.p0.refs_0_.own, ...), custom_call_target="tpu_custom_call" | custom-call | bytes 1024 | tf_op jit(solution)/shard_map/attend_forward/pallas_call | solution.py:55
  60.7 2.3 %backward_early.1 = (bf16[384,384]{1,0:T(8,128)(2,1)S(1)}, f32[512,384]{1,0:T(8,128)S(1)}, f32[512,384]{1,0:T(8,128)S(1)}) custom-call(bf16[3,128,512]{2,1,0:T(8,128)(2,1)S(1)} %get-tuple-element.60.p0.refs_0_.own, bf16[3,128,512]{2,1,0:T(8,128)(2,1)S(1)} %collective-permute-done.p1.refs_1_.near, ...), custom_call_target="tpu_custom_call" | custom-call | bytes 1024 | tf_op jit(solution)/shard_map/backward_early/pallas_call | solution.py:55
  63.0 1.8 %collective-permute-done.6.p3.far3b = bf16[3,128,128]{2,1,0:T(8,128)(2,1)S(1)} collective-permute-done((bf16[3,128,128]{2,1,0:T(8,128)(2,1)S(1)}, bf16[3,128,128]{2,1,0:T(8,128)(2,1)S(1)}, u32[]{:S(2)}, u32[]{:S(2)}) %collective-permute-start.6) | collective-permute-done | bytes 98336 | tf_op jit(solution)/shard_map/ppermute | solution.py:40
  64.8 1.6 %collective-permute-done.5.p2.far2b = bf16[3,128,128]{2,1,0:T(8,128)(2,1)S(1)} collective-permute-done((bf16[3,128,128]{2,1,0:T(8,128)(2,1)S(1)}, bf16[3,128,128]{2,1,0:T(8,128)(2,1)S(1)}, u32[]{:S(2)}, u32[]{:S(2)}) %collective-permute-start.5) | collective-permute-done | bytes 98336 | tf_op jit(solution)/shard_map/ppermute | solution.py:40
  66.4 1.6 %attend_forward.3 = (bf16[1,512,512]{2,1,0:T(8,128)(2,1)S(1)}, f32[1,1,512]{2,1,0:T(1,128)S(1)}, f32[128,512]{1,0:T(8,128)S(1)}, bf16[128,512]{1,0:T(8,128)(2,1)S(1)}) custom-call(s32[4]{0:T(128)S(1)} %pad_add_fusion.meta, bf16[3,128,512]{2,1,0:T(8,128)(2,1)S(1)} %get-tuple-element.60.p0.refs_0_.own, ...), custom_call_target="tpu_custom_call" | custom-call | bytes 1024 | tf_op jit(solution)/shard_map/attend_forward/pallas_call | solution.py:55
  68.0 0.0 collective-permute-done.7.refs_3_.refs_0_
  68.0 0.0 collective-permute-done.8.refs_4_.refs_1_
  68.0 2.4 %weight_halves.1 = (bf16[256,2048]{1,0:T(8,128)(2,1)S(1)}, f32[256,2048]{1,0:T(8,128)S(1)}) custom-call(s32[4]{0:T(128)S(1)} %pad_add_fusion.meta, bf16[384,512]{1,0:T(8,128)(2,1)S(1)} %get-tuple-element.78.heads_a, bf16[128,512]{1,0:T(8,128)(2,1)S(1)} %get-tuple-element.83.heads_b, bf16[128,2048]{1,0:T(8,128)(2,1)S(1)} %get-tuple-element.67.refs_0_, ...), custom_call_target="tpu_custom_call" | custom-call | bytes 1024 | tf_op jit(solution)/shard_map/weight_halves/pallas_call | solution.py:55
  70.4 0.1 collective-permute-start.9
  70.5 1.5 %grad_attn.3.late_ref = bf16[128,512]{1,0:T(8,128)(2,1)S(1)} custom-call(s32[4]{0:T(128)S(1)} %pad_add_fusion.meta, bf16[64,2048]{1,0:T(8,128)(2,1)S(1)} %collective-permute-done.7.refs_3_.refs_0_, bf16[64,2048]{1,0:T(8,128)(2,1)S(1)} %collective-permute-done.8.refs_4_.refs_1_, bf16[512,2048]{1,0:T(8,128)(2,1)S(1)} %copy-done), custom_call_target="tpu_custom_call" | custom-call | bytes 1024 | tf_op jit(solution)/shard_map/grad_attn/pallas_call | solution.py:55
  72.0 1.6 %attend_backward.1 = (bf16[3,128,512]{2,1,0:T(8,128)(2,1)S(1)}, bf16[3,128,512]{2,1,0:T(8,128)(2,1)S(1)}, bf16[3,128,512]{2,1,0:T(8,128)(2,1)S(1)}, bf16[3,128,512]{2,1,0:T(8,128)(2,1)S(1)}) custom-call(bf16[3,128,512]{2,1,0:T(8,128)(2,1)S(1)} %get-tuple-element.60.p0.refs_0_.own, bf16[3,128,512]{2,1,0:T(8,128)(2,1)S(1)} %collective-permute-done.p1.refs_1_.near, ...), custom_call_target="tpu_custom_call" | custom-call | bytes 1024 | tf_op jit(solution)/shard_map/attend_backward/pallas_call | solution.py:55
  73.7 0.0 collective-permute-done.9.recv_ref
  73.7 0.2 add_parts.1
  73.9 1.6 %collective-permute-start.10 = (bf16[64,2048]{1,0:T(8,128)(2,1)S(1)}, bf16[64,2048]{1,0:T(8,128)(2,1)S(1)}, u32[]{:S(2)}, u32[]{:S(2)}) collective-permute-start(bf16[64,2048]{1,0:T(8,128)(2,1)S(1)} %get-tuple-element.100), channel_id=1, source_target_pairs={{0,8},{8,0},{16,24},{24,16},{1,9},{9,1},{17,25},{25,17},{2,10},{10... | collective-permute-start | bytes 786440 | tf_op jit(solution)/shard_map/ppermute | solution.py:40
  75.5 1.5 %collective-permute-start.11 = (bf16[64,2048]{1,0:T(8,128)(2,1)S(1)}, bf16[64,2048]{1,0:T(8,128)(2,1)S(1)}, u32[]{:S(2)}, u32[]{:S(2)}) collective-permute-start(bf16[64,2048]{1,0:T(8,128)(2,1)S(1)} %get-tuple-element.101), channel_id=1, source_target_pairs={{0,16},{8,24},{16,0},{24,8},{1,17},{9,25},{17,1},{25,9},{2,18},{10... | collective-permute-start | bytes 786440 | tf_op jit(solution)/shard_map/ppermute | solution.py:40
  77.0 0.5 collective-permute-start.12
  77.5 1.0 collective-permute-start.14
  78.5 1.4 %collective-permute-start.18 = (bf16[3,128,512]{2,1,0:T(8,128)(2,1)S(1)}, bf16[3,128,512]{2,1,0:T(8,128)(2,1)S(1)}, u32[]{:S(2)}, u32[]{:S(2)}) collective-permute-start(bf16[3,128,512]{2,1,0:T(8,128)(2,1)S(1)} %get-tuple-element.107), channel_id=1, source_target_pairs={{0,3},{1,2},{2,1},{3,0},{4,7},{5,6},{6,5},{7,4},{8,11},{9,10},{10,... | collective-permute-start | bytes 1179656 | tf_op jit(solution)/shard_map/ppermute | solution.py:40
  79.9 3.2 %collective-permute-done.10.r1 = bf16[64,2048]{1,0:T(8,128)(2,1)S(1)} collective-permute-done((bf16[64,2048]{1,0:T(8,128)(2,1)S(1)}, bf16[64,2048]{1,0:T(8,128)(2,1)S(1)}, u32[]{:S(2)}, u32[]{:S(2)}) %collective-permute-start.10) | collective-permute-done | bytes 262176 | tf_op jit(solution)/shard_map/ppermute | solution.py:40
  83.1 6.4 %collective-permute-done.11.r2 = bf16[64,2048]{1,0:T(8,128)(2,1)S(1)} collective-permute-done((bf16[64,2048]{1,0:T(8,128)(2,1)S(1)}, bf16[64,2048]{1,0:T(8,128)(2,1)S(1)}, u32[]{:S(2)}, u32[]{:S(2)}) %collective-permute-start.11) | collective-permute-done | bytes 262176 | tf_op jit(solution)/shard_map/ppermute | solution.py:40
  89.5 0.0 collective-permute-done.12.r3
  89.5 0.1 scene_mean.1.refs_0_
  89.7 1.3 %collective-permute-start.15 = (bf16[64,2048]{1,0:T(8,128)(2,1)S(1)}, bf16[64,2048]{1,0:T(8,128)(2,1)S(1)}, u32[]{:S(2)}, u32[]{:S(2)}) collective-permute-start(bf16[64,2048]{1,0:T(8,128)(2,1)S(1)} %scene_mean.1.refs_0_), channel_id=1, source_target_pairs={{0,8},{8,0},{16,24},{24,16},{1,9},{9,1},{17,25},{25,17},{2,10},{10... | collective-permute-start | bytes 786440 | tf_op jit(solution)/shard_map/ppermute | solution.py:40
  91.0 1.8 %collective-permute-start.17 = (bf16[64,2048]{1,0:T(8,128)(2,1)S(1)}, bf16[64,2048]{1,0:T(8,128)(2,1)S(1)}, u32[]{:S(2)}, u32[]{:S(2)}) collective-permute-start(bf16[64,2048]{1,0:T(8,128)(2,1)S(1)} %scene_mean.1.refs_0_), channel_id=1, source_target_pairs={{0,24},{8,16},{16,8},{24,0},{1,25},{9,17},{17,9},{25,1},{2,26},{10... | collective-permute-start | bytes 786440 | tf_op jit(solution)/shard_map/ppermute | solution.py:40
  92.7 0.5 collective-permute-start.16
  93.2 5.8 %collective-permute-done.15.refs_1_ = bf16[64,2048]{1,0:T(8,128)(2,1)S(1)} collective-permute-done((bf16[64,2048]{1,0:T(8,128)(2,1)S(1)}, bf16[64,2048]{1,0:T(8,128)(2,1)S(1)}, u32[]{:S(2)}, u32[]{:S(2)}) %collective-permute-start.15) | collective-permute-done | bytes 262176 | tf_op jit(solution)/shard_map/ppermute | solution.py:40
  99.0 0.1 collective-permute-start.22
  99.0 6.5 %collective-permute-done.14.back2 = bf16[3,128,512]{2,1,0:T(8,128)(2,1)S(1)} collective-permute-done((bf16[3,128,512]{2,1,0:T(8,128)(2,1)S(1)}, bf16[3,128,512]{2,1,0:T(8,128)(2,1)S(1)}, u32[]{:S(2)}, u32[]{:S(2)}) %collective-permute-start.14) | collective-permute-done | bytes 393248 | tf_op jit(solution)/shard_map/ppermute | solution.py:40
  105.5 1.5 %join_heads.1 = (bf16[128,2048]{1,0:T(8,128)(2,1)}, bf16[128,2048]{1,0:T(8,128)(2,1)}, bf16[128,2048]{1,0:T(8,128)(2,1)}) custom-call(s32[4]{0:T(128)S(1)} %pad_add_fusion.meta, bf16[3,128,512]{2,1,0:T(8,128)(2,1)S(1)} %get-tuple-element.97.own, bf16[3,128,512]{2,1,0:T(8,128)(2,1)S(1)} %collective-permute-done.14.back2), custom_call_target="tpu_custom_call" | custom-call | bytes 1024 | tf_op jit(solution)/shard_map/join_heads/pallas_call | solution.py:317
  107.0 0.1 collective-permute-start.13
  107.1 0.0 collective-permute-done.17.refs_3_
  107.1 0.0 collective-permute-done.16.refs_2_
  107.1 1.6 %join_weight.1.refs_9_ = bf16[512,2048]{1,0:T(8,128)(2,1)} custom-call(s32[4]{0:T(128)S(1)} %pad_add_fusion.meta, bf16[64,2048]{1,0:T(8,128)(2,1)S(1)} %scene_mean.1.refs_0_, bf16[64,2048]{1,0:T(8,128)(2,1)S(1)} %collective-permute-done.15.refs_1_, bf16[64,2048]{1,0:T(8,128)(2,1)S(1)} %collective-permute-done.16.refs_2_, ...), custom_call_target="tpu_custom_call" | custom-call | bytes 1024 | tf_op jit(solution)/shard_map/join_weight/pallas_call | solution.py:317
  108.8 0.0 collective-permute-done.18.refs_5_
  108.8 0.5 collective-permute-start.21
  109.3 0.1 collective-permute-start.20
  109.4 0.4 collective-permute-start.19
  109.8 0.0 collective-permute-done.13.refs_0_
  109.8 0.6 collective-permute-done.21.refs_3_
  110.5 0.4 collective-permute-done.20.refs_2_
  110.9 0.4 collective-permute-done.19.refs_1_
  111.2 2.6 %collective-permute-done.22.refs_4_ = bf16[3,128,512]{2,1,0:T(8,128)(2,1)S(1)} collective-permute-done((bf16[3,128,512]{2,1,0:T(8,128)(2,1)S(1)}, bf16[3,128,512]{2,1,0:T(8,128)(2,1)S(1)}, u32[]{:S(2)}, u32[]{:S(2)}) %collective-permute-start.22) | collective-permute-done | bytes 393248 | tf_op jit(solution)/shard_map/ppermute | solution.py:40
  113.8 1.9 %join_last.1 = (bf16[128,2048]{1,0:T(8,128)(2,1)}, bf16[128,2048]{1,0:T(8,128)(2,1)}, bf16[128,2048]{1,0:T(8,128)(2,1)}, bf16[512,2048]{1,0:T(8,128)(2,1)}) custom-call(s32[4]{0:T(128)S(1)} %pad_add_fusion.meta, bf16[64,2048]{1,0:T(8,128)(2,1)S(1)} %collective-permute-done.13.refs_0_, ...), custom_call_target="tpu_custom_call", output_to_operand_aliasing={{0}: (7, {}), {1}: (8, {}), {2}: (9, {}), {3}: (10, {})} | custom-call | bytes 1024 | tf_op jit(solution)/shard_map/join_last/pallas_call | solution.py:317
  (8 shorter events, 0.0 us)
Async XLA Ops:
  0.6 32.1 %copy-start = (bf16[512,2048]{1,0:T(8,128)(2,1)S(1)}, bf16[512,2048]{1,0:T(8,128)(2,1)}, u32[]{:S(2)}) copy-start(bf16[512,2048]{1,0:T(8,128)(2,1)} %refs_2_.1) | copy-start | bytes 6291460
  0.6 27.6 %collective-permute-start.1 = (bf16[128,2048]{1,0:T(8,128)(2,1)}, bf16[128,2048]{1,0:T(8,128)(2,1)S(1)}, u32[]{:S(2)}, u32[]{:S(2)}) collective-permute-start(bf16[128,2048]{1,0:T(8,128)(2,1)} %grad_ref.1), channel_id=1, source_target_pairs={{0,2},{1,3},{2,0},{3,1},{4,6},{5,7},{6,4},{7,5},{8,10},{9,11},{10,... | collective-permute-start | bytes 1572872 | tf_op jit(solution)/shard_map/ppermute | solution.py:40
  4.7 28.0 %collective-permute-start.4 = (bf16[128,2048]{1,0:T(8,128)(2,1)}, bf16[128,2048]{1,0:T(8,128)(2,1)S(1)}, u32[]{:S(2)}, u32[]{:S(2)}) collective-permute-start(bf16[128,2048]{1,0:T(8,128)(2,1)} %grad_ref.1), channel_id=1, source_target_pairs={{0,1},{1,0},{2,3},{3,2},{4,5},{5,4},{6,7},{7,6},{8,9},{9,8},{10,11... | collective-permute-start | bytes 1572872 | tf_op jit(solution)/shard_map/ppermute | solution.py:40
  7.0 1.0 copy-start.1
  8.1 1.0 copy-start.2
  9.1 1.0 copy-start.3
  10.2 1.0 copy-start.4
  12.3 33.0 %collective-permute-start = (bf16[3,128,512]{2,1,0:T(8,128)(2,1)S(1)}, bf16[3,128,512]{2,1,0:T(8,128)(2,1)S(1)}, u32[]{:S(2)}, u32[]{:S(2)}) collective-permute-start(bf16[3,128,512]{2,1,0:T(8,128)(2,1)S(1)} %get-tuple-element.61), channel_id=1, source_target_pairs={{0,1},{1,0},{2,3},{3,2},{4,5},{5,4},{6,7},{7,6},{8,9},{9,8},{10,11... | collective-permute-start | bytes 1179656 | tf_op jit(solution)/shard_map/ppermute | solution.py:40
  28.2 17.2 %collective-permute-start.3 = (bf16[3,128,384]{2,1,0:T(8,128)(2,1)S(1)}, bf16[3,128,384]{2,1,0:T(8,128)(2,1)S(1)}, u32[]{:S(2)}, u32[]{:S(2)}) collective-permute-start(bf16[3,128,384]{2,1,0:T(8,128)(2,1)S(1)} %get-tuple-element.65), channel_id=1, source_target_pairs={{0,3},{1,2},{2,1},{3,0},{4,7},{5,6},{6,5},{7,4},{8,11},{9,10},{10,... | collective-permute-start | bytes 884744 | tf_op jit(solution)/shard_map/ppermute | solution.py:40
  31.8 25.5 %collective-permute-start.2 = (bf16[3,128,384]{2,1,0:T(8,128)(2,1)S(1)}, bf16[3,128,384]{2,1,0:T(8,128)(2,1)S(1)}, u32[]{:S(2)}, u32[]{:S(2)}) collective-permute-start(bf16[3,128,384]{2,1,0:T(8,128)(2,1)S(1)} %get-tuple-element.63), channel_id=1, source_target_pairs={{0,2},{1,3},{2,0},{3,1},{4,6},{5,7},{6,4},{7,5},{8,10},{9,11},{10,... | collective-permute-start | bytes 884744 | tf_op jit(solution)/shard_map/ppermute | solution.py:40
  31.8 36.2 %collective-permute-start.7 = (bf16[64,2048]{1,0:T(8,128)(2,1)S(1)}, bf16[64,2048]{1,0:T(8,128)(2,1)S(1)}, u32[]{:S(2)}, u32[]{:S(2)}) collective-permute-start(bf16[64,2048]{1,0:T(8,128)(2,1)S(1)} %slice.8), channel_id=1, source_target_pairs={{0,1},{1,0},{2,3},{3,2},{4,5},{5,4},{6,7},{7,6},{8,9},{9,8},{10,11... | collective-permute-start | bytes 786440 | tf_op jit(solution)/shard_map/ppermute | solution.py:40
  45.3 22.7 %collective-permute-start.8 = (bf16[64,2048]{1,0:T(8,128)(2,1)S(1)}, bf16[64,2048]{1,0:T(8,128)(2,1)S(1)}, u32[]{:S(2)}, u32[]{:S(2)}) collective-permute-start(bf16[64,2048]{1,0:T(8,128)(2,1)S(1)} %slice.7), channel_id=1, source_target_pairs={{0,1},{1,0},{2,3},{3,2},{4,5},{5,4},{6,7},{7,6},{8,9},{9,8},{10,11... | collective-permute-start | bytes 786440 | tf_op jit(solution)/shard_map/ppermute | solution.py:40
  45.4 19.4 %collective-permute-start.6 = (bf16[3,128,128]{2,1,0:T(8,128)(2,1)S(1)}, bf16[3,128,128]{2,1,0:T(8,128)(2,1)S(1)}, u32[]{:S(2)}, u32[]{:S(2)}) collective-permute-start(bf16[3,128,128]{2,1,0:T(8,128)(2,1)S(1)} %get-tuple-element.77), channel_id=1, source_target_pairs={{0,3},{1,2},{2,1},{3,0},{4,7},{5,6},{6,5},{7,4},{8,11},{9,10},{10,... | collective-permute-start | bytes 294920 | tf_op jit(solution)/shard_map/ppermute | solution.py:40
  57.3 9.1 %collective-permute-start.5 = (bf16[3,128,128]{2,1,0:T(8,128)(2,1)S(1)}, bf16[3,128,128]{2,1,0:T(8,128)(2,1)S(1)}, u32[]{:S(2)}, u32[]{:S(2)}) collective-permute-start(bf16[3,128,128]{2,1,0:T(8,128)(2,1)S(1)} %get-tuple-element.75), channel_id=1, source_target_pairs={{0,2},{1,3},{2,0},{3,1},{4,6},{5,7},{6,4},{7,5},{8,10},{9,11},{10,... | collective-permute-start | bytes 294920 | tf_op jit(solution)/shard_map/ppermute | solution.py:40
  70.4 3.3 %collective-permute-start.9 = (bf16[256,2048]{1,0:T(8,128)(2,1)S(1)}, bf16[256,2048]{1,0:T(8,128)(2,1)S(1)}, u32[]{:S(2)}, u32[]{:S(2)}) collective-permute-start(bf16[256,2048]{1,0:T(8,128)(2,1)S(1)} %get-tuple-element.88), channel_id=1, source_target_pairs={{0,4},{4,0},{1,5},{5,1},{2,6},{6,2},{3,7},{7,3},{8,12},{12,8},{9,1... | collective-permute-start | bytes 3145736 | tf_op jit(solution)/shard_map/ppermute | solution.py:40
  73.9 9.2 %collective-permute-start.10 = (bf16[64,2048]{1,0:T(8,128)(2,1)S(1)}, bf16[64,2048]{1,0:T(8,128)(2,1)S(1)}, u32[]{:S(2)}, u32[]{:S(2)}) collective-permute-start(bf16[64,2048]{1,0:T(8,128)(2,1)S(1)} %get-tuple-element.100), channel_id=1, source_target_pairs={{0,8},{8,0},{16,24},{24,16},{1,9},{9,1},{17,25},{25,17},{2,10},{10... | collective-permute-start | bytes 786440 | tf_op jit(solution)/shard_map/ppermute | solution.py:40
  75.5 14.0 %collective-permute-start.11 = (bf16[64,2048]{1,0:T(8,128)(2,1)S(1)}, bf16[64,2048]{1,0:T(8,128)(2,1)S(1)}, u32[]{:S(2)}, u32[]{:S(2)}) collective-permute-start(bf16[64,2048]{1,0:T(8,128)(2,1)S(1)} %get-tuple-element.101), channel_id=1, source_target_pairs={{0,16},{8,24},{16,0},{24,8},{1,17},{9,25},{17,1},{25,9},{2,18},{10... | collective-permute-start | bytes 786440 | tf_op jit(solution)/shard_map/ppermute | solution.py:40
  77.0 12.5 %collective-permute-start.12 = (bf16[64,2048]{1,0:T(8,128)(2,1)S(1)}, bf16[64,2048]{1,0:T(8,128)(2,1)S(1)}, u32[]{:S(2)}, u32[]{:S(2)}) collective-permute-start(bf16[64,2048]{1,0:T(8,128)(2,1)S(1)} %get-tuple-element.102), channel_id=1, source_target_pairs={{0,24},{8,16},{16,8},{24,0},{1,25},{9,17},{17,9},{25,1},{2,26},{10... | collective-permute-start | bytes 786440 | tf_op jit(solution)/shard_map/ppermute | solution.py:40
  77.5 28.1 %collective-permute-start.14 = (bf16[3,128,512]{2,1,0:T(8,128)(2,1)S(1)}, bf16[3,128,512]{2,1,0:T(8,128)(2,1)S(1)}, u32[]{:S(2)}, u32[]{:S(2)}) collective-permute-start(bf16[3,128,512]{2,1,0:T(8,128)(2,1)S(1)} %get-tuple-element.103), channel_id=1, source_target_pairs={{0,2},{1,3},{2,0},{3,1},{4,6},{5,7},{6,4},{7,5},{8,10},{9,11},{10,... | collective-permute-start | bytes 1179656 | tf_op jit(solution)/shard_map/ppermute | solution.py:40
  78.5 30.3 %collective-permute-start.18 = (bf16[3,128,512]{2,1,0:T(8,128)(2,1)S(1)}, bf16[3,128,512]{2,1,0:T(8,128)(2,1)S(1)}, u32[]{:S(2)}, u32[]{:S(2)}) collective-permute-start(bf16[3,128,512]{2,1,0:T(8,128)(2,1)S(1)} %get-tuple-element.107), channel_id=1, source_target_pairs={{0,3},{1,2},{2,1},{3,0},{4,7},{5,6},{6,5},{7,4},{8,11},{9,10},{10,... | collective-permute-start | bytes 1179656 | tf_op jit(solution)/shard_map/ppermute | solution.py:40
  89.7 9.3 %collective-permute-start.15 = (bf16[64,2048]{1,0:T(8,128)(2,1)S(1)}, bf16[64,2048]{1,0:T(8,128)(2,1)S(1)}, u32[]{:S(2)}, u32[]{:S(2)}) collective-permute-start(bf16[64,2048]{1,0:T(8,128)(2,1)S(1)} %scene_mean.1.refs_0_), channel_id=1, source_target_pairs={{0,8},{8,0},{16,24},{24,16},{1,9},{9,1},{17,25},{25,17},{2,10},{10... | collective-permute-start | bytes 786440 | tf_op jit(solution)/shard_map/ppermute | solution.py:40
  91.0 16.1 %collective-permute-start.17 = (bf16[64,2048]{1,0:T(8,128)(2,1)S(1)}, bf16[64,2048]{1,0:T(8,128)(2,1)S(1)}, u32[]{:S(2)}, u32[]{:S(2)}) collective-permute-start(bf16[64,2048]{1,0:T(8,128)(2,1)S(1)} %scene_mean.1.refs_0_), channel_id=1, source_target_pairs={{0,24},{8,16},{16,8},{24,0},{1,25},{9,17},{17,9},{25,1},{2,26},{10... | collective-permute-start | bytes 786440 | tf_op jit(solution)/shard_map/ppermute | solution.py:40
  92.7 14.4 %collective-permute-start.16 = (bf16[64,2048]{1,0:T(8,128)(2,1)S(1)}, bf16[64,2048]{1,0:T(8,128)(2,1)S(1)}, u32[]{:S(2)}, u32[]{:S(2)}) collective-permute-start(bf16[64,2048]{1,0:T(8,128)(2,1)S(1)} %scene_mean.1.refs_0_), channel_id=1, source_target_pairs={{0,16},{8,24},{16,0},{24,8},{1,17},{9,25},{17,1},{25,9},{2,18},{10... | collective-permute-start | bytes 786440 | tf_op jit(solution)/shard_map/ppermute | solution.py:40
  99.0 14.9 %collective-permute-start.22 = (bf16[3,128,512]{2,1,0:T(8,128)(2,1)S(1)}, bf16[3,128,512]{2,1,0:T(8,128)(2,1)S(1)}, u32[]{:S(2)}, u32[]{:S(2)}) collective-permute-start(bf16[3,128,512]{2,1,0:T(8,128)(2,1)S(1)} %get-tuple-element.110), channel_id=1, source_target_pairs={{0,1},{1,0},{2,3},{3,2},{4,5},{5,4},{6,7},{7,6},{8,9},{9,8},{10,11... | collective-permute-start | bytes 1179656 | tf_op jit(solution)/shard_map/ppermute | solution.py:40
  107.0 2.8 %collective-permute-start.13 = (bf16[64,2048]{1,0:T(8,128)(2,1)S(1)}, bf16[64,2048]{1,0:T(8,128)(2,1)S(1)}, u32[]{:S(2)}, u32[]{:S(2)}) collective-permute-start(bf16[64,2048]{1,0:T(8,128)(2,1)S(1)} %scene_mean.1.refs_0_), channel_id=1, source_target_pairs={{0,4},{4,0},{1,5},{5,1},{2,6},{6,2},{3,7},{7,3},{8,12},{12,8},{9,1... | collective-permute-start | bytes 786440 | tf_op jit(solution)/shard_map/ppermute | solution.py:40
  108.8 1.7 %collective-permute-start.21 = (bf16[64,2048]{1,0:T(8,128)(2,1)S(1)}, bf16[64,2048]{1,0:T(8,128)(2,1)S(1)}, u32[]{:S(2)}, u32[]{:S(2)}) collective-permute-start(bf16[64,2048]{1,0:T(8,128)(2,1)S(1)} %collective-permute-done.17.refs_3_), channel_id=1, source_target_pairs={{0,4},{4,0},{1,5},{5,1},{2,6},{6,2},{3,7},{7,3},{8,12},{12,8},{9,1... | collective-permute-start | bytes 786440 | tf_op jit(solution)/shard_map/ppermute | solution.py:40
  109.3 1.5 %collective-permute-start.20 = (bf16[64,2048]{1,0:T(8,128)(2,1)S(1)}, bf16[64,2048]{1,0:T(8,128)(2,1)S(1)}, u32[]{:S(2)}, u32[]{:S(2)}) collective-permute-start(bf16[64,2048]{1,0:T(8,128)(2,1)S(1)} %collective-permute-done.16.refs_2_), channel_id=1, source_target_pairs={{0,4},{4,0},{1,5},{5,1},{2,6},{6,2},{3,7},{7,3},{8,12},{12,8},{9,1... | collective-permute-start | bytes 786440 | tf_op jit(solution)/shard_map/ppermute | solution.py:40
  109.4 1.8 %collective-permute-start.19 = (bf16[64,2048]{1,0:T(8,128)(2,1)S(1)}, bf16[64,2048]{1,0:T(8,128)(2,1)S(1)}, u32[]{:S(2)}, u32[]{:S(2)}) collective-permute-start(bf16[64,2048]{1,0:T(8,128)(2,1)S(1)} %collective-permute-done.15.refs_1_), channel_id=1, source_target_pairs={{0,4},{4,0},{1,5},{5,1},{2,6},{6,2},{3,7},{7,3},{8,12},{12,8},{9,1... | collective-permute-start | bytes 786440 | tf_op jit(solution)/shard_map/ppermute | solution.py:40

commit v2 on v0

--- a/solution.py
+++ b/solution.py
@@ -105,9 +105,8 @@
     live = token_pos((grad.shape[0], 1), 0, meta[Z], start) < meta[COUNT]
     tile = 2 * HDIM
 
-    @pl.loop(0, w_ref.shape[0] // tile)
-    def _(i):
-        part = pl.ds(pl.multiple_of(i * tile, tile), tile)
+    for i in range(w_ref.shape[0] // tile):
+        part = slice(i * tile, (i + 1) * tile)
         out_ref[:, part] = jnp.where(live, dot(grad, w_ref[part, :], 1, 1), 0.0).astype(bf16)
 
 
@@ -126,16 +125,18 @@
     return (jnp.concatenate(x, axis=0) for x in zip(*parts))
 
 
-def forward_kernel(group, meta, p0, p1, p2, p3, weight_ref, inverse_ref, out_ref, heads_ref, bias_ref):
-    pieces = (p0, p1, p2, p3)
-    rows = p0.shape[1]
+def forward_kernel(group, meta, *refs):
+    pieces, (weight_ref, inverse_ref, out_ref, heads_ref) = refs[:4], refs[-4:] if group else refs[4:8]
+    bias_ref = refs[4] if group else refs[8]
+    rows = pieces[0].shape[1]
     total = 4 * rows
     tile = 2 * rows
     to_power = math.log2(math.e) / math.sqrt(HDIM)
     query_live = token_pos((1, total), 1, meta[Z]) < meta[COUNT]
-    key_live = token_pos((total, 1), 0, meta[Z]) < meta[COUNT]
-    bias_ref[...] = jnp.where(key_live | ~query_live, 0.0, -jnp.inf)
-    for h in range(p3.shape[2] // HDIM):
+    if group == 0:
+        key_live = token_pos((total, 1), 0, meta[Z]) < meta[COUNT]
+        bias_ref[...] = jnp.where(key_live | ~query_live, 0.0, -jnp.inf)
+    for h in range(pieces[-1].shape[2] // HDIM):
         cols = slice(h * HDIM, (h + 1) * HDIM)
         query, key, value = head_of(pieces, group, h)
         for t in range(2):
@@ -151,7 +152,7 @@
             heads_ref[cols, part] = jnp.where(query_live[:, part], heads, 0.0).astype(bf16)
 
 
-def forward(meta, pieces, group):
+def forward(meta, pieces, group, *bias):
     _, rows, width = pieces[-1].shape
     total = 4 * rows
     shapes = [
@@ -159,10 +160,9 @@
         sds((width // HDIM, 1, total), f32),
         sds((width, total), f32),
         sds((width, total), bf16),
-    ]
-    scratch = [pltpu.VMEM((total, total), f32)]
+    ] + ([] if bias else [sds((total, total), f32)])
     kernel = functools.partial(forward_kernel, group)
-    return whole(kernel, shapes, (meta, *pieces), "attend_forward", 1, 8, scratch)
+    return whole(kernel, shapes, (meta, *pieces, *bias), "attend_forward", 1, 8)
 
 
 def span_gradients(query, key, value, grad, weights, inverse, outs):
@@ -259,9 +259,8 @@
     lines = jnp.concatenate(lines, axis=0)
     tile = 4 * HDIM
 
-    @pl.loop(0, send_ref.shape[1] // tile)
-    def _(i):
-        part = pl.ds(pl.multiple_of(i * tile, tile), tile)
+    for i in range(send_ref.shape[1] // tile):
+        part = slice(i * tile, (i + 1) * tile)
         product = dot(lines, jnp.concatenate([g[:, part] for g in grads], axis=0), 1, 0)
         send_ref[:, part] = product[: width // 2].astype(bf16)
         keep_ref[:, part] = product[width // 2 :]
@@ -377,10 +376,10 @@
     grad_early = grad_attn(meta, (mine, beside, across), out_weight, 0)
     corners = [send(across[:half], 1), send(after(across, piece1, grad_early)[half:], 1)]
 
-    *saved_a, heads_a = forward(meta, (own, piece1, piece2a, piece3a), 0)
+    *saved_a, heads_a, bias = forward(meta, (own, piece1, piece2a, piece3a), 0)
     early = backward_early((own, piece1, piece2a, piece3a), grad_early, saved_a)
     heads_a, *early, piece2b, piece3b = lax.optimization_barrier((heads_a, *early, piece2b, piece3b))
-    *saved_b, heads_b = forward(meta, (own, piece1, piece2b, piece3b), 1)
+    *saved_b, heads_b = forward(meta, (own, piece1, piece2b, piece3b), 1, bias)
     grad_early, heads_b, *corners = lax.optimization_barrier((grad_early, heads_b, *corners))
     grads = (mine, beside, across, *corners)
 

time: 115 us -> 115 us (level)
  Pallas kernels: 21.2 us -> 20 us
    pallas_call x9, Pallas kernels: 15.1 us -> 13.9 us  [whole(): pl.pallas_call(kernel, out_shape=out_shape, in_specs=[pl.BlockSpec(memory...]
  transfers between devices with their start and end apart: 23 -> 23, of which waited for: 12 -> 12; matrix products, arithmetic and copies ran while one was open for 0% -> 0% of each run, Pallas kernels for 15% -> 14%
where the time goes in v2:
time: 115 us; the launch traced here: 114 us
  waiting for transfers between devices  59.3 us (52%)
  starting transfers between devices  28.7 us (25%)
  Pallas kernels  20 us (17%)
  local copies, waits for them, and re-layouts  4.21 us (4%)
  between operations  1.47 us (1%)
    ppermute x23, waiting for transfers between devices, swap(): return lax.ppermute(x, axis, [(i, i ^ flip) for i in range(size)])  59.3 us
    ppermute x23, starting transfers between devices, swap(): return lax.ppermute(x, axis, [(i, i ^ flip) for i in range(size)])  28.7 us
    pallas_call x9, Pallas kernels, whole(): pl.pallas_call(kernel, out_shape=out_shape, in_specs=[pl.BlockSpec(memory...  13.9 us
    pallas_call x3, Pallas kernels, join(): pl.pallas_call(kernel, out_shape=shapes, in_specs=[pl.BlockSpec(memory_sp...  5.04 us
    unnamed x10, local copies, waits for them, and re-layouts  4.17 us
  transfers between devices with their start and end apart: 23, of which 12 were waited for; matrix products, arithmetic and copies ran while one was open for 0% of the time, Pallas kernels for 14%

profile of v2, /device:TPU:0, one launch (start us, length us, event | category | flops | bytes accessed | tf_op | source)
XLA Modules:
  0.0 113.8 jit_solution(18076512773249156195)
XLA Ops:
  0.6 3.1 %collective-permute-start.3 = (bf16[128,2048]{1,0:T(8,128)(2,1)}, bf16[128,2048]{1,0:T(8,128)(2,1)S(1)}, u32[]{:S(2)}, u32[]{:S(2)}) collective-permute-start(bf16[128,2048]{1,0:T(8,128)(2,1)} %grad_ref.1), channel_id=1, source_target_pairs={{0,1},{1,0},{2,3},{3,2},{4,5},{5,4},{6,7},{7,6},{8,9},{9,8},{10,11... | collective-permute-start | bytes 1572872 | tf_op jit(solution)/shard_map/ppermute | solution.py:40
  3.7 2.6 %collective-permute-start.1 = (bf16[128,2048]{1,0:T(8,128)(2,1)}, bf16[128,2048]{1,0:T(8,128)(2,1)S(1)}, u32[]{:S(2)}, u32[]{:S(2)}) collective-permute-start(bf16[128,2048]{1,0:T(8,128)(2,1)} %grad_ref.1), channel_id=1, source_target_pairs={{0,2},{1,3},{2,0},{3,1},{4,6},{5,7},{6,4},{7,5},{8,10},{9,11},{10,... | collective-permute-start | bytes 1572872 | tf_op jit(solution)/shard_map/ppermute | solution.py:40
  7.0 0.1 pad_add_fusion.meta
  7.1 1.0 copy-done.1
  8.1 1.0 copy-done.2
  9.1 1.0 copy-done.3
  10.2 1.0 copy-done.4
  11.2 1.1 pack_heads.1
  12.3 0.5 collective-permute-start
  12.8 15.0 %collective-permute-done.3.refs_1_ = bf16[128,2048]{1,0:T(8,128)(2,1)S(1)} collective-permute-done((bf16[128,2048]{1,0:T(8,128)(2,1)}, bf16[128,2048]{1,0:T(8,128)(2,1)S(1)}, u32[]{:S(2)}, u32[]{:S(2)}) %collective-permute-start.3) | collective-permute-done | bytes 524320 | tf_op jit(solution)/shard_map/ppermute | solution.py:40
  27.8 3.6 %collective-permute-start.4 = (bf16[3,128,384]{2,1,0:T(8,128)(2,1)S(1)}, bf16[3,128,384]{2,1,0:T(8,128)(2,1)S(1)}, u32[]{:S(2)}, u32[]{:S(2)}) collective-permute-start(bf16[3,128,384]{2,1,0:T(8,128)(2,1)S(1)} %get-tuple-element.67), channel_id=1, source_target_pairs={{0,3},{1,2},{2,1},{3,0},{4,7},{5,6},{6,5},{7,4},{8,11},{9,10},{10,... | collective-permute-start | bytes 884744 | tf_op jit(solution)/shard_map/ppermute | solution.py:40
  31.4 0.0 collective-permute-done.1.refs_2_
  31.4 0.0 collective-permute-start.2
  31.4 2.1 %collective-permute-start.7 = (bf16[64,2048]{1,0:T(8,128)(2,1)S(1)}, bf16[64,2048]{1,0:T(8,128)(2,1)S(1)}, u32[]{:S(2)}, u32[]{:S(2)}) collective-permute-start(bf16[64,2048]{1,0:T(8,128)(2,1)S(1)} %slice.8), channel_id=1, source_target_pairs={{0,1},{1,0},{2,3},{3,2},{4,5},{5,4},{6,7},{7,6},{8,9},{9,8},{10,11... | collective-permute-start | bytes 786440 | tf_op jit(solution)/shard_map/ppermute | solution.py:40
  33.5 1.6 %grad_attn.2.refs_4_.early_ref = bf16[384,512]{1,0:T(8,128)(2,1)S(1)} custom-call(s32[4]{0:T(128)S(1)} %pad_add_fusion.meta, bf16[128,2048]{1,0:T(8,128)(2,1)S(1)} %get-tuple-element.69.refs_0_, bf16[128,2048]{1,0:T(8,128)(2,1)S(1)} %collective-permute-done.3.refs_1_, bf16[128,2048]{1,0:T(8,128)(2,1)S(1)} %collective-permute-done.1.refs_2_, ...), custom_call_target="tpu_custom_call" | custom-call | bytes 1024 | tf_op jit(solution)/shard_map/grad_attn/pallas_call | solution.py:55
  35.0 9.0 %collective-permute-done.refs_1_.near = bf16[3,128,512]{2,1,0:T(8,128)(2,1)S(1)} collective-permute-done((bf16[3,128,512]{2,1,0:T(8,128)(2,1)S(1)}, bf16[3,128,512]{2,1,0:T(8,128)(2,1)S(1)}, u32[]{:S(2)}, u32[]{:S(2)}) %collective-permute-start) | collective-permute-done | bytes 393248 | tf_op jit(solution)/shard_map/ppermute | solution.py:40
  44.1 0.1 collective-permute-start.8
  44.2 1.2 %collective-permute-done.4.refs_3_.far3a = bf16[3,128,384]{2,1,0:T(8,128)(2,1)S(1)} collective-permute-done((bf16[3,128,384]{2,1,0:T(8,128)(2,1)S(1)}, bf16[3,128,384]{2,1,0:T(8,128)(2,1)S(1)}, u32[]{:S(2)}, u32[]{:S(2)}) %collective-permute-start.4) | collective-permute-done | bytes 294944 | tf_op jit(solution)/shard_map/ppermute | solution.py:40
  45.3 3.0 %collective-permute-start.6 = (bf16[3,128,128]{2,1,0:T(8,128)(2,1)S(1)}, bf16[3,128,128]{2,1,0:T(8,128)(2,1)S(1)}, u32[]{:S(2)}, u32[]{:S(2)}) collective-permute-start(bf16[3,128,128]{2,1,0:T(8,128)(2,1)S(1)} %get-tuple-element.79), channel_id=1, source_target_pairs={{0,3},{1,2},{2,1},{3,0},{4,7},{5,6},{6,5},{7,4},{8,11},{9,10},{10,... | collective-permute-start | bytes 294920 | tf_op jit(solution)/shard_map/ppermute | solution.py:40
  48.3 7.6 %collective-permute-done.2.refs_2_.far2a = bf16[3,128,384]{2,1,0:T(8,128)(2,1)S(1)} collective-permute-done((bf16[3,128,384]{2,1,0:T(8,128)(2,1)S(1)}, bf16[3,128,384]{2,1,0:T(8,128)(2,1)S(1)}, u32[]{:S(2)}, u32[]{:S(2)}) %collective-permute-start.2) | collective-permute-done | bytes 294944 | tf_op jit(solution)/shard_map/ppermute | solution.py:40
  55.9 0.0 collective-permute-start.5
  55.9 3.3 %attend_forward.2 = (bf16[3,512,512]{2,1,0:T(8,128)(2,1)S(1)}, f32[3,1,512]{2,1,0:T(1,128)S(1)}, f32[384,512]{1,0:T(8,128)S(1)}, bf16[384,512]{1,0:T(8,128)(2,1)S(1)}, f32[512,512]{1,0:T(8,128)S(1)}) custom-call(s32[4]{0:T(128)S(1)} %pad_add_fusion.meta, bf16[3,128,512]{2,1,0:T(8,128)(2,1)S(1)} %get-tuple-element.62.refs_0_.own, ...), custom_call_target="tpu_custom_call" | custom-call | bytes 1024 | tf_op jit(solution)/shard_map/attend_forward/pallas_call | solution.py:55
  59.3 2.3 %backward_early.1 = (bf16[384,384]{1,0:T(8,128)(2,1)S(1)}, f32[512,384]{1,0:T(8,128)S(1)}, f32[512,384]{1,0:T(8,128)S(1)}) custom-call(bf16[3,128,512]{2,1,0:T(8,128)(2,1)S(1)} %get-tuple-element.62.refs_0_.own, bf16[3,128,512]{2,1,0:T(8,128)(2,1)S(1)} %collective-permute-done.refs_1_.near, bf16[3,128,384]{2,1,0:T(8,128)(2,1)S(1)} %collective-permute-done.2.refs_2_.far2a, ...), custom_call_target="tpu_custom_call" | custom-call | bytes 1024 | tf_op jit(solution)/shard_map/backward_early/pallas_call | solution.py:55
  61.6 3.2 %collective-permute-done.6.refs_3_.far3b = bf16[3,128,128]{2,1,0:T(8,128)(2,1)S(1)} collective-permute-done((bf16[3,128,128]{2,1,0:T(8,128)(2,1)S(1)}, bf16[3,128,128]{2,1,0:T(8,128)(2,1)S(1)}, u32[]{:S(2)}, u32[]{:S(2)}) %collective-permute-start.6) | collective-permute-done | bytes 98336 | tf_op jit(solution)/shard_map/ppermute | solution.py:40
  64.8 0.0 collective-permute-done.5.refs_2_.far2b
  64.8 1.6 %attend_forward.3 = (bf16[1,512,512]{2,1,0:T(8,128)(2,1)S(1)}, f32[1,1,512]{2,1,0:T(1,128)S(1)}, f32[128,512]{1,0:T(8,128)S(1)}, bf16[128,512]{1,0:T(8,128)(2,1)S(1)}) custom-call(s32[4]{0:T(128)S(1)} %pad_add_fusion.meta, bf16[3,128,512]{2,1,0:T(8,128)(2,1)S(1)} %get-tuple-element.62.refs_0_.own, ...), custom_call_target="tpu_custom_call" | custom-call | bytes 1024 | tf_op jit(solution)/shard_map/attend_forward/pallas_call | solution.py:55
  66.4 0.0 collective-permute-done.7.refs_3_.refs_0_
  66.4 0.0 collective-permute-done.8.refs_4_.refs_1_
  66.4 1.8 %weight_halves.1 = (bf16[256,2048]{1,0:T(8,128)(2,1)S(1)}, f32[256,2048]{1,0:T(8,128)S(1)}) custom-call(s32[4]{0:T(128)S(1)} %pad_add_fusion.meta, bf16[384,512]{1,0:T(8,128)(2,1)S(1)} %get-tuple-element.80.heads_a, bf16[128,512]{1,0:T(8,128)(2,1)S(1)} %get-tuple-element.86.heads_b, bf16[128,2048]{1,0:T(8,128)(2,1)S(1)} %get-tuple-element.69.refs_0_, ...), custom_call_target="tpu_custom_call" | custom-call | bytes 1024 | tf_op jit(solution)/shard_map/weight_halves/pallas_call | solution.py:55
  68.2 0.1 collective-permute-start.9
  68.3 1.4 %grad_attn.3.late_ref = bf16[128,512]{1,0:T(8,128)(2,1)S(1)} custom-call(s32[4]{0:T(128)S(1)} %pad_add_fusion.meta, bf16[64,2048]{1,0:T(8,128)(2,1)S(1)} %collective-permute-done.7.refs_3_.refs_0_, bf16[64,2048]{1,0:T(8,128)(2,1)S(1)} %collective-permute-done.8.refs_4_.refs_1_, bf16[512,2048]{1,0:T(8,128)(2,1)S(1)} %copy-done), custom_call_target="tpu_custom_call" | custom-call | bytes 1024 | tf_op jit(solution)/shard_map/grad_attn/pallas_call | solution.py:55
  69.7 1.6 %attend_backward.1 = (bf16[3,128,512]{2,1,0:T(8,128)(2,1)S(1)}, bf16[3,128,512]{2,1,0:T(8,128)(2,1)S(1)}, bf16[3,128,512]{2,1,0:T(8,128)(2,1)S(1)}, bf16[3,128,512]{2,1,0:T(8,128)(2,1)S(1)}) custom-call(bf16[3,128,512]{2,1,0:T(8,128)(2,1)S(1)} %get-tuple-element.62.refs_0_.own, bf16[3,128,512]{2,1,0:T(8,128)(2,1)S(1)} %collective-permute-done.refs_1_.near, ...), custom_call_target="tpu_custom_call" | custom-call | bytes 1024 | tf_op jit(solution)/shard_map/attend_backward/pallas_call | solution.py:55
  71.3 0.0 collective-permute-done.9.recv_ref
  71.4 0.2 add_parts.1
  71.6 1.6 %collective-permute-start.10 = (bf16[64,2048]{1,0:T(8,128)(2,1)S(1)}, bf16[64,2048]{1,0:T(8,128)(2,1)S(1)}, u32[]{:S(2)}, u32[]{:S(2)}) collective-permute-start(bf16[64,2048]{1,0:T(8,128)(2,1)S(1)} %get-tuple-element.103), channel_id=1, source_target_pairs={{0,8},{8,0},{16,24},{24,16},{1,9},{9,1},{17,25},{25,17},{2,10},{10... | collective-permute-start | bytes 786440 | tf_op jit(solution)/shard_map/ppermute | solution.py:40
  73.1 1.5 %collective-permute-start.11 = (bf16[64,2048]{1,0:T(8,128)(2,1)S(1)}, bf16[64,2048]{1,0:T(8,128)(2,1)S(1)}, u32[]{:S(2)}, u32[]{:S(2)}) collective-permute-start(bf16[64,2048]{1,0:T(8,128)(2,1)S(1)} %get-tuple-element.104), channel_id=1, source_target_pairs={{0,16},{8,24},{16,0},{24,8},{1,17},{9,25},{17,1},{25,9},{2,18},{10... | collective-permute-start | bytes 786440 | tf_op jit(solution)/shard_map/ppermute | solution.py:40
  74.7 0.5 collective-permute-start.12
  75.1 1.5 %collective-permute-start.16 = (bf16[3,128,512]{2,1,0:T(8,128)(2,1)S(1)}, bf16[3,128,512]{2,1,0:T(8,128)(2,1)S(1)}, u32[]{:S(2)}, u32[]{:S(2)}) collective-permute-start(bf16[3,128,512]{2,1,0:T(8,128)(2,1)S(1)} %get-tuple-element.106), channel_id=1, source_target_pairs={{0,2},{1,3},{2,0},{3,1},{4,6},{5,7},{6,4},{7,5},{8,10},{9,11},{10,... | collective-permute-start | bytes 1179656 | tf_op jit(solution)/shard_map/ppermute | solution.py:40
  76.6 2.5 %collective-permute-start.17 = (bf16[3,128,512]{2,1,0:T(8,128)(2,1)S(1)}, bf16[3,128,512]{2,1,0:T(8,128)(2,1)S(1)}, u32[]{:S(2)}, u32[]{:S(2)}) collective-permute-start(bf16[3,128,512]{2,1,0:T(8,128)(2,1)S(1)} %get-tuple-element.107), channel_id=1, source_target_pairs={{0,3},{1,2},{2,1},{3,0},{4,7},{5,6},{6,5},{7,4},{8,11},{9,10},{10,... | collective-permute-start | bytes 1179656 | tf_op jit(solution)/shard_map/ppermute | solution.py:40
  79.1 1.6 %collective-permute-done.10.r1 = bf16[64,2048]{1,0:T(8,128)(2,1)S(1)} collective-permute-done((bf16[64,2048]{1,0:T(8,128)(2,1)S(1)}, bf16[64,2048]{1,0:T(8,128)(2,1)S(1)}, u32[]{:S(2)}, u32[]{:S(2)}) %collective-permute-start.10) | collective-permute-done | bytes 262176 | tf_op jit(solution)/shard_map/ppermute | solution.py:40
  80.8 6.4 %collective-permute-done.11.r2 = bf16[64,2048]{1,0:T(8,128)(2,1)S(1)} collective-permute-done((bf16[64,2048]{1,0:T(8,128)(2,1)S(1)}, bf16[64,2048]{1,0:T(8,128)(2,1)S(1)}, u32[]{:S(2)}, u32[]{:S(2)}) %collective-permute-start.11) | collective-permute-done | bytes 262176 | tf_op jit(solution)/shard_map/ppermute | solution.py:40
  87.2 0.0 collective-permute-done.12.r3
  87.2 0.1 scene_mean.1.refs_0_
  87.3 1.3 %collective-permute-start.13 = (bf16[64,2048]{1,0:T(8,128)(2,1)S(1)}, bf16[64,2048]{1,0:T(8,128)(2,1)S(1)}, u32[]{:S(2)}, u32[]{:S(2)}) collective-permute-start(bf16[64,2048]{1,0:T(8,128)(2,1)S(1)} %scene_mean.1.refs_0_), channel_id=1, source_target_pairs={{0,8},{8,0},{16,24},{24,16},{1,9},{9,1},{17,25},{25,17},{2,10},{10... | collective-permute-start | bytes 786440 | tf_op jit(solution)/shard_map/ppermute | solution.py:40
  88.6 1.8 %collective-permute-start.15 = (bf16[64,2048]{1,0:T(8,128)(2,1)S(1)}, bf16[64,2048]{1,0:T(8,128)(2,1)S(1)}, u32[]{:S(2)}, u32[]{:S(2)}) collective-permute-start(bf16[64,2048]{1,0:T(8,128)(2,1)S(1)} %scene_mean.1.refs_0_), channel_id=1, source_target_pairs={{0,24},{8,16},{16,8},{24,0},{1,25},{9,17},{17,9},{25,1},{2,26},{10... | collective-permute-start | bytes 786440 | tf_op jit(solution)/shard_map/ppermute | solution.py:40
  90.4 0.5 collective-permute-start.14
  90.9 5.8 %collective-permute-done.13.refs_1_ = bf16[64,2048]{1,0:T(8,128)(2,1)S(1)} collective-permute-done((bf16[64,2048]{1,0:T(8,128)(2,1)S(1)}, bf16[64,2048]{1,0:T(8,128)(2,1)S(1)}, u32[]{:S(2)}, u32[]{:S(2)}) %collective-permute-start.13) | collective-permute-done | bytes 262176 | tf_op jit(solution)/shard_map/ppermute | solution.py:40
  96.6 1.6 %collective-permute-start.22 = (bf16[3,128,512]{2,1,0:T(8,128)(2,1)S(1)}, bf16[3,128,512]{2,1,0:T(8,128)(2,1)S(1)}, u32[]{:S(2)}, u32[]{:S(2)}) collective-permute-start(bf16[3,128,512]{2,1,0:T(8,128)(2,1)S(1)} %get-tuple-element.113), channel_id=1, source_target_pairs={{0,1},{1,0},{2,3},{3,2},{4,5},{5,4},{6,7},{7,6},{8,9},{9,8},{10,11... | collective-permute-start | bytes 1179656 | tf_op jit(solution)/shard_map/ppermute | solution.py:40
  98.2 3.4 %collective-permute-done.15.refs_3_ = bf16[64,2048]{1,0:T(8,128)(2,1)S(1)} collective-permute-done((bf16[64,2048]{1,0:T(8,128)(2,1)S(1)}, bf16[64,2048]{1,0:T(8,128)(2,1)S(1)}, u32[]{:S(2)}, u32[]{:S(2)}) %collective-permute-start.15) | collective-permute-done | bytes 262176 | tf_op jit(solution)/shard_map/ppermute | solution.py:40
  101.7 1.4 %collective-permute-done.14.refs_2_ = bf16[64,2048]{1,0:T(8,128)(2,1)S(1)} collective-permute-done((bf16[64,2048]{1,0:T(8,128)(2,1)S(1)}, bf16[64,2048]{1,0:T(8,128)(2,1)S(1)}, u32[]{:S(2)}, u32[]{:S(2)}) %collective-permute-start.14) | collective-permute-done | bytes 262176 | tf_op jit(solution)/shard_map/ppermute | solution.py:40
  103.0 1.6 %join_weight.1.refs_8_ = bf16[512,2048]{1,0:T(8,128)(2,1)} custom-call(s32[4]{0:T(128)S(1)} %pad_add_fusion.meta, bf16[64,2048]{1,0:T(8,128)(2,1)S(1)} %scene_mean.1.refs_0_, bf16[64,2048]{1,0:T(8,128)(2,1)S(1)} %collective-permute-done.13.refs_1_, bf16[64,2048]{1,0:T(8,128)(2,1)S(1)} %collective-permute-done.14.refs_2_, ...), custom_call_target="tpu_custom_call" | custom-call | bytes 1024 | tf_op jit(solution)/shard_map/join_weight/pallas_call | solution.py:316
  104.7 0.1 collective-permute-done.16.back2
  104.8 0.0 collective-permute-done.17.back3
  104.8 0.0 collective-permute-start.18
  104.8 0.5 collective-permute-start.19
  105.3 0.1 collective-permute-start.20
  105.4 0.5 collective-permute-start.21
  105.8 1.6 %join_heads.1 = (bf16[128,2048]{1,0:T(8,128)(2,1)}, bf16[128,2048]{1,0:T(8,128)(2,1)}, bf16[128,2048]{1,0:T(8,128)(2,1)}) custom-call(s32[4]{0:T(128)S(1)} %pad_add_fusion.meta, bf16[3,128,512]{2,1,0:T(8,128)(2,1)S(1)} %get-tuple-element.100.own, bf16[3,128,512]{2,1,0:T(8,128)(2,1)S(1)} %collective-permute-done.16.back2, ...), custom_call_target="tpu_custom_call" | custom-call | bytes 1024 | tf_op jit(solution)/shard_map/join_heads/pallas_call | solution.py:316
  107.5 0.0 collective-permute-done.18.refs_0_
  107.5 0.0 collective-permute-done.19.refs_1_
  107.5 0.0 collective-permute-done.20.refs_2_
  107.5 0.0 collective-permute-done.21.refs_3_
  107.5 4.5 %collective-permute-done.22.refs_4_ = bf16[3,128,512]{2,1,0:T(8,128)(2,1)S(1)} collective-permute-done((bf16[3,128,512]{2,1,0:T(8,128)(2,1)S(1)}, bf16[3,128,512]{2,1,0:T(8,128)(2,1)S(1)}, u32[]{:S(2)}, u32[]{:S(2)}) %collective-permute-start.22) | collective-permute-done | bytes 393248 | tf_op jit(solution)/shard_map/ppermute | solution.py:40
  112.0 1.8 %join_last.1 = (bf16[128,2048]{1,0:T(8,128)(2,1)}, bf16[128,2048]{1,0:T(8,128)(2,1)}, bf16[128,2048]{1,0:T(8,128)(2,1)}, bf16[512,2048]{1,0:T(8,128)(2,1)}) custom-call(s32[4]{0:T(128)S(1)} %pad_add_fusion.meta, bf16[64,2048]{1,0:T(8,128)(2,1)S(1)} %collective-permute-done.18.refs_0_, ...), custom_call_target="tpu_custom_call", output_to_operand_aliasing={{0}: (6, {}), {1}: (7, {}), {2}: (8, {}), {3}: (9, {})} | custom-call | bytes 1024 | tf_op jit(solution)/shard_map/join_last/pallas_call | solution.py:316
  (8 shorter events, 0.0 us)
Async XLA Ops:
  0.6 32.9 %copy-start = (bf16[512,2048]{1,0:T(8,128)(2,1)S(1)}, bf16[512,2048]{1,0:T(8,128)(2,1)}, u32[]{:S(2)}) copy-start(bf16[512,2048]{1,0:T(8,128)(2,1)} %refs_2_.1) | copy-start | bytes 6291460
  0.6 27.2 %collective-permute-start.3 = (bf16[128,2048]{1,0:T(8,128)(2,1)}, bf16[128,2048]{1,0:T(8,128)(2,1)S(1)}, u32[]{:S(2)}, u32[]{:S(2)}) collective-permute-start(bf16[128,2048]{1,0:T(8,128)(2,1)} %grad_ref.1), channel_id=1, source_target_pairs={{0,1},{1,0},{2,3},{3,2},{4,5},{5,4},{6,7},{7,6},{8,9},{9,8},{10,11... | collective-permute-start | bytes 1572872 | tf_op jit(solution)/shard_map/ppermute | solution.py:40
  3.7 27.7 %collective-permute-start.1 = (bf16[128,2048]{1,0:T(8,128)(2,1)}, bf16[128,2048]{1,0:T(8,128)(2,1)S(1)}, u32[]{:S(2)}, u32[]{:S(2)}) collective-permute-start(bf16[128,2048]{1,0:T(8,128)(2,1)} %grad_ref.1), channel_id=1, source_target_pairs={{0,2},{1,3},{2,0},{3,1},{4,6},{5,7},{6,4},{7,5},{8,10},{9,11},{10,... | collective-permute-start | bytes 1572872 | tf_op jit(solution)/shard_map/ppermute | solution.py:40
  7.0 1.0 copy-start.1
  8.1 1.0 copy-start.2
  9.1 1.0 copy-start.3
  10.2 1.0 copy-start.4
  12.3 31.8 %collective-permute-start = (bf16[3,128,512]{2,1,0:T(8,128)(2,1)S(1)}, bf16[3,128,512]{2,1,0:T(8,128)(2,1)S(1)}, u32[]{:S(2)}, u32[]{:S(2)}) collective-permute-start(bf16[3,128,512]{2,1,0:T(8,128)(2,1)S(1)} %get-tuple-element.63), channel_id=1, source_target_pairs={{0,1},{1,0},{2,3},{3,2},{4,5},{5,4},{6,7},{7,6},{8,9},{9,8},{10,11... | collective-permute-start | bytes 1179656 | tf_op jit(solution)/shard_map/ppermute | solution.py:40
  27.8 17.5 %collective-permute-start.4 = (bf16[3,128,384]{2,1,0:T(8,128)(2,1)S(1)}, bf16[3,128,384]{2,1,0:T(8,128)(2,1)S(1)}, u32[]{:S(2)}, u32[]{:S(2)}) collective-permute-start(bf16[3,128,384]{2,1,0:T(8,128)(2,1)S(1)} %get-tuple-element.67), channel_id=1, source_target_pairs={{0,3},{1,2},{2,1},{3,0},{4,7},{5,6},{6,5},{7,4},{8,11},{9,10},{10,... | collective-permute-start | bytes 884744 | tf_op jit(solution)/shard_map/ppermute | solution.py:40
  31.4 24.5 %collective-permute-start.2 = (bf16[3,128,384]{2,1,0:T(8,128)(2,1)S(1)}, bf16[3,128,384]{2,1,0:T(8,128)(2,1)S(1)}, u32[]{:S(2)}, u32[]{:S(2)}) collective-permute-start(bf16[3,128,384]{2,1,0:T(8,128)(2,1)S(1)} %get-tuple-element.65), channel_id=1, source_target_pairs={{0,2},{1,3},{2,0},{3,1},{4,6},{5,7},{6,4},{7,5},{8,10},{9,11},{10,... | collective-permute-start | bytes 884744 | tf_op jit(solution)/shard_map/ppermute | solution.py:40
  31.4 35.0 %collective-permute-start.7 = (bf16[64,2048]{1,0:T(8,128)(2,1)S(1)}, bf16[64,2048]{1,0:T(8,128)(2,1)S(1)}, u32[]{:S(2)}, u32[]{:S(2)}) collective-permute-start(bf16[64,2048]{1,0:T(8,128)(2,1)S(1)} %slice.8), channel_id=1, source_target_pairs={{0,1},{1,0},{2,3},{3,2},{4,5},{5,4},{6,7},{7,6},{8,9},{9,8},{10,11... | collective-permute-start | bytes 786440 | tf_op jit(solution)/shard_map/ppermute | solution.py:40
  44.1 22.4 %collective-permute-start.8 = (bf16[64,2048]{1,0:T(8,128)(2,1)S(1)}, bf16[64,2048]{1,0:T(8,128)(2,1)S(1)}, u32[]{:S(2)}, u32[]{:S(2)}) collective-permute-start(bf16[64,2048]{1,0:T(8,128)(2,1)S(1)} %slice.7), channel_id=1, source_target_pairs={{0,1},{1,0},{2,3},{3,2},{4,5},{5,4},{6,7},{7,6},{8,9},{9,8},{10,11... | collective-permute-start | bytes 786440 | tf_op jit(solution)/shard_map/ppermute | solution.py:40
  45.3 19.5 %collective-permute-start.6 = (bf16[3,128,128]{2,1,0:T(8,128)(2,1)S(1)}, bf16[3,128,128]{2,1,0:T(8,128)(2,1)S(1)}, u32[]{:S(2)}, u32[]{:S(2)}) collective-permute-start(bf16[3,128,128]{2,1,0:T(8,128)(2,1)S(1)} %get-tuple-element.79), channel_id=1, source_target_pairs={{0,3},{1,2},{2,1},{3,0},{4,7},{5,6},{6,5},{7,4},{8,11},{9,10},{10,... | collective-permute-start | bytes 294920 | tf_op jit(solution)/shard_map/ppermute | solution.py:40
  55.9 8.9 %collective-permute-start.5 = (bf16[3,128,128]{2,1,0:T(8,128)(2,1)S(1)}, bf16[3,128,128]{2,1,0:T(8,128)(2,1)S(1)}, u32[]{:S(2)}, u32[]{:S(2)}) collective-permute-start(bf16[3,128,128]{2,1,0:T(8,128)(2,1)S(1)} %get-tuple-element.77), channel_id=1, source_target_pairs={{0,2},{1,3},{2,0},{3,1},{4,6},{5,7},{6,4},{7,5},{8,10},{9,11},{10,... | collective-permute-start | bytes 294920 | tf_op jit(solution)/shard_map/ppermute | solution.py:40
  68.2 3.1 %collective-permute-start.9 = (bf16[256,2048]{1,0:T(8,128)(2,1)S(1)}, bf16[256,2048]{1,0:T(8,128)(2,1)S(1)}, u32[]{:S(2)}, u32[]{:S(2)}) collective-permute-start(bf16[256,2048]{1,0:T(8,128)(2,1)S(1)} %get-tuple-element.91), channel_id=1, source_target_pairs={{0,4},{4,0},{1,5},{5,1},{2,6},{6,2},{3,7},{7,3},{8,12},{12,8},{9,1... | collective-permute-start | bytes 3145736 | tf_op jit(solution)/shard_map/ppermute | solution.py:40
  71.6 9.2 %collective-permute-start.10 = (bf16[64,2048]{1,0:T(8,128)(2,1)S(1)}, bf16[64,2048]{1,0:T(8,128)(2,1)S(1)}, u32[]{:S(2)}, u32[]{:S(2)}) collective-permute-start(bf16[64,2048]{1,0:T(8,128)(2,1)S(1)} %get-tuple-element.103), channel_id=1, source_target_pairs={{0,8},{8,0},{16,24},{24,16},{1,9},{9,1},{17,25},{25,17},{2,10},{10... | collective-permute-start | bytes 786440 | tf_op jit(solution)/shard_map/ppermute | solution.py:40
  73.1 14.0 %collective-permute-start.11 = (bf16[64,2048]{1,0:T(8,128)(2,1)S(1)}, bf16[64,2048]{1,0:T(8,128)(2,1)S(1)}, u32[]{:S(2)}, u32[]{:S(2)}) collective-permute-start(bf16[64,2048]{1,0:T(8,128)(2,1)S(1)} %get-tuple-element.104), channel_id=1, source_target_pairs={{0,16},{8,24},{16,0},{24,8},{1,17},{9,25},{17,1},{25,9},{2,18},{10... | collective-permute-start | bytes 786440 | tf_op jit(solution)/shard_map/ppermute | solution.py:40
  74.7 12.5 %collective-permute-start.12 = (bf16[64,2048]{1,0:T(8,128)(2,1)S(1)}, bf16[64,2048]{1,0:T(8,128)(2,1)S(1)}, u32[]{:S(2)}, u32[]{:S(2)}) collective-permute-start(bf16[64,2048]{1,0:T(8,128)(2,1)S(1)} %get-tuple-element.105), channel_id=1, source_target_pairs={{0,24},{8,16},{16,8},{24,0},{1,25},{9,17},{17,9},{25,1},{2,26},{10... | collective-permute-start | bytes 786440 | tf_op jit(solution)/shard_map/ppermute | solution.py:40
  75.1 29.7 %collective-permute-start.16 = (bf16[3,128,512]{2,1,0:T(8,128)(2,1)S(1)}, bf16[3,128,512]{2,1,0:T(8,128)(2,1)S(1)}, u32[]{:S(2)}, u32[]{:S(2)}) collective-permute-start(bf16[3,128,512]{2,1,0:T(8,128)(2,1)S(1)} %get-tuple-element.106), channel_id=1, source_target_pairs={{0,2},{1,3},{2,0},{3,1},{4,6},{5,7},{6,4},{7,5},{8,10},{9,11},{10,... | collective-permute-start | bytes 1179656 | tf_op jit(solution)/shard_map/ppermute | solution.py:40
  76.6 28.2 %collective-permute-start.17 = (bf16[3,128,512]{2,1,0:T(8,128)(2,1)S(1)}, bf16[3,128,512]{2,1,0:T(8,128)(2,1)S(1)}, u32[]{:S(2)}, u32[]{:S(2)}) collective-permute-start(bf16[3,128,512]{2,1,0:T(8,128)(2,1)S(1)} %get-tuple-element.107), channel_id=1, source_target_pairs={{0,3},{1,2},{2,1},{3,0},{4,7},{5,6},{6,5},{7,4},{8,11},{9,10},{10,... | collective-permute-start | bytes 1179656 | tf_op jit(solution)/shard_map/ppermute | solution.py:40
  87.3 9.3 %collective-permute-start.13 = (bf16[64,2048]{1,0:T(8,128)(2,1)S(1)}, bf16[64,2048]{1,0:T(8,128)(2,1)S(1)}, u32[]{:S(2)}, u32[]{:S(2)}) collective-permute-start(bf16[64,2048]{1,0:T(8,128)(2,1)S(1)} %scene_mean.1.refs_0_), channel_id=1, source_target_pairs={{0,8},{8,0},{16,24},{24,16},{1,9},{9,1},{17,25},{25,17},{2,10},{10... | collective-permute-start | bytes 786440 | tf_op jit(solution)/shard_map/ppermute | solution.py:40
  88.6 13.1 %collective-permute-start.15 = (bf16[64,2048]{1,0:T(8,128)(2,1)S(1)}, bf16[64,2048]{1,0:T(8,128)(2,1)S(1)}, u32[]{:S(2)}, u32[]{:S(2)}) collective-permute-start(bf16[64,2048]{1,0:T(8,128)(2,1)S(1)} %scene_mean.1.refs_0_), channel_id=1, source_target_pairs={{0,24},{8,16},{16,8},{24,0},{1,25},{9,17},{17,9},{25,1},{2,26},{10... | collective-permute-start | bytes 786440 | tf_op jit(solution)/shard_map/ppermute | solution.py:40
  90.4 12.7 %collective-permute-start.14 = (bf16[64,2048]{1,0:T(8,128)(2,1)S(1)}, bf16[64,2048]{1,0:T(8,128)(2,1)S(1)}, u32[]{:S(2)}, u32[]{:S(2)}) collective-permute-start(bf16[64,2048]{1,0:T(8,128)(2,1)S(1)} %scene_mean.1.refs_0_), channel_id=1, source_target_pairs={{0,16},{8,24},{16,0},{24,8},{1,17},{9,25},{17,1},{25,9},{2,18},{10... | collective-permute-start | bytes 786440 | tf_op jit(solution)/shard_map/ppermute | solution.py:40
  96.6 15.4 %collective-permute-start.22 = (bf16[3,128,512]{2,1,0:T(8,128)(2,1)S(1)}, bf16[3,128,512]{2,1,0:T(8,128)(2,1)S(1)}, u32[]{:S(2)}, u32[]{:S(2)}) collective-permute-start(bf16[3,128,512]{2,1,0:T(8,128)(2,1)S(1)} %get-tuple-element.113), channel_id=1, source_target_pairs={{0,1},{1,0},{2,3},{3,2},{4,5},{5,4},{6,7},{7,6},{8,9},{9,8},{10,11... | collective-permute-start | bytes 1179656 | tf_op jit(solution)/shard_map/ppermute | solution.py:40
  104.8 2.7 %collective-permute-start.18 = (bf16[64,2048]{1,0:T(8,128)(2,1)S(1)}, bf16[64,2048]{1,0:T(8,128)(2,1)S(1)}, u32[]{:S(2)}, u32[]{:S(2)}) collective-permute-start(bf16[64,2048]{1,0:T(8,128)(2,1)S(1)} %scene_mean.1.refs_0_), channel_id=1, source_target_pairs={{0,4},{4,0},{1,5},{5,1},{2,6},{6,2},{3,7},{7,3},{8,12},{12,8},{9,1... | collective-permute-start | bytes 786440 | tf_op jit(solution)/shard_map/ppermute | solution.py:40
  104.8 2.7 %collective-permute-start.19 = (bf16[64,2048]{1,0:T(8,128)(2,1)S(1)}, bf16[64,2048]{1,0:T(8,128)(2,1)S(1)}, u32[]{:S(2)}, u32[]{:S(2)}) collective-permute-start(bf16[64,2048]{1,0:T(8,128)(2,1)S(1)} %collective-permute-done.13.refs_1_), channel_id=1, source_target_pairs={{0,4},{4,0},{1,5},{5,1},{2,6},{6,2},{3,7},{7,3},{8,12},{12,8},{9,1... | collective-permute-start | bytes 786440 | tf_op jit(solution)/shard_map/ppermute | solution.py:40
  105.3 2.2 %collective-permute-start.20 = (bf16[64,2048]{1,0:T(8,128)(2,1)S(1)}, bf16[64,2048]{1,0:T(8,128)(2,1)S(1)}, u32[]{:S(2)}, u32[]{:S(2)}) collective-permute-start(bf16[64,2048]{1,0:T(8,128)(2,1)S(1)} %collective-permute-done.14.refs_2_), channel_id=1, source_target_pairs={{0,4},{4,0},{1,5},{5,1},{2,6},{6,2},{3,7},{7,3},{8,12},{12,8},{9,1... | collective-permute-start | bytes 786440 | tf_op jit(solution)/shard_map/ppermute | solution.py:40
  105.4 2.1 %collective-permute-start.21 = (bf16[64,2048]{1,0:T(8,128)(2,1)S(1)}, bf16[64,2048]{1,0:T(8,128)(2,1)S(1)}, u32[]{:S(2)}, u32[]{:S(2)}) collective-permute-start(bf16[64,2048]{1,0:T(8,128)(2,1)S(1)} %collective-permute-done.15.refs_3_), channel_id=1, source_target_pairs={{0,4},{4,0},{1,5},{5,1},{2,6},{6,2},{3,7},{7,3},{8,12},{12,8},{9,1... | collective-permute-start | bytes 786440 | tf_op jit(solution)/shard_map/ppermute | solution.py:40

commit v3 on v2

--- a/solution.py
+++ b/solution.py
@@ -241,6 +241,7 @@
 
 
 LINE = HDIM // 8
+WIDE = 14 * HDIM
 
 
 def line_at(meta, head, other, j):
@@ -283,20 +284,25 @@
     return whole(add_kernel, [sds(shape, f32)] + [sds(shape, bf16)] * 3, (keep, recv), "add_parts")
 
 
-def total_kernel(scale, own_ref, r1, r2, r3, out_ref):
+def total_kernel(scale, own_ref, r1, r2, r3, out_ref, wide_ref, rest_ref):
     total = own_ref[...] + r1[...].astype(f32) + r2[...].astype(f32) + r3[...].astype(f32)
-    out_ref[...] = (total * scale).astype(bf16)
+    total = (total * scale).astype(bf16)
+    out_ref[...] = total
+    wide_ref[...] = total[:, :WIDE].astype(f32)
+    rest_ref[...] = total[:, WIDE:]
 
 
 def total_of(own, recvs, scale):
-    return whole(functools.partial(total_kernel, scale), sds(own.shape, bf16), (own, *recvs), "scene_mean")
-
-
-def weight_copies(meta, parts, first, out_ref, sems):
+    rows, outw = own.shape
+    shapes = [sds(own.shape, bf16), sds((rows, WIDE), f32), sds((rows, outw - WIDE), bf16)]
+    return whole(functools.partial(total_kernel, scale), shapes, (own, *recvs), "scene_mean")
+
+
+def weight_copies(meta, parts, first, out_ref, sems, start=0):
     copies = []
     for p, ref in enumerate(parts, first):
         for h in range(ref.shape[0] // LINE):
-            line = out_ref.at[line_at(meta, h, p // 4, p % 4), :]
+            line = out_ref.at[line_at(meta, h, p // 4, p % 4), pl.ds(start, ref.shape[1])]
             copies.append(pltpu.make_async_copy(ref.at[pl.ds(h * LINE, LINE), :], line, sems.at[len(copies)]))
     return copies
 
@@ -312,49 +318,36 @@
     return copies
 
 
-def join(kernel, meta, parts, shapes, copies, name, outs=()):
+def join_kernel(meta, *refs):
+    near, (wide, rest), far, pieces = refs[:4], refs[4:6], refs[6:9], refs[9:13]
+    outs, weight, narrow, sems = refs[13:16], refs[16], refs[17], refs[18:]
+    copies = weight_copies(meta, near, 0, weight, sems[0]) + weight_copies(meta, far, 5, weight, sems[1])
+    copies += weight_copies(meta, (rest,), 4, weight, sems[2], WIDE)
+    copies += head_copies(meta, dict(enumerate(pieces)), outs, sems[3])
+    for copy in copies:
+        copy.start()
+    narrow[...] = wide[...].astype(bf16)
+    run_all(weight_copies(meta, (narrow,), 4, weight, sems[4]))
+    for copy in copies:
+        copy.wait()
+
+
+def join(meta, near, far, pieces):
+    size, outw = near[0].shape
+    _, rows, width = pieces[0].shape
+    parts = (*near, *far, *pieces)
+    lines = size // LINE
     return pl.pallas_call(
-        kernel,
-        out_shape=shapes,
-        in_specs=[pl.BlockSpec(memory_space=pltpu.SMEM)]
-        + [pl.BlockSpec(memory_space=pltpu.VMEM)] * len(parts)
-        + [pl.BlockSpec(memory_space=pl.ANY)] * len(outs),
-        out_specs=[pl.BlockSpec(memory_space=pl.ANY)] * len(shapes),
-        scratch_shapes=[pltpu.SemaphoreType.DMA((n,)) for n in copies],
-        input_output_aliases={1 + len(parts) + i: i for i in range(len(outs))},
+        join_kernel,
+        out_shape=[sds((rows, 4 * width), bf16)] * 3 + [sds((8 * size, outw), bf16)],
+        in_specs=[pl.BlockSpec(memory_space=pltpu.SMEM)] + [pl.BlockSpec(memory_space=pltpu.VMEM)] * len(parts),
+        out_specs=[pl.BlockSpec(memory_space=pl.ANY)] * 4,
+        scratch_shapes=[pltpu.VMEM(far[0].shape, bf16)]
+        + [pltpu.SemaphoreType.DMA((n,)) for n in (4 * lines, 3 * lines, lines, 12, lines)],
         compiler_params=params(),
         cost_estimate=NO_COST,
-        name=name,
-    )(meta, *parts, *outs)
-
-
-def join_weight_kernel(meta, *refs):
-    run_all(weight_copies(meta, refs[:4], 0, refs[4], refs[5]))
-
-
-def join_weight(meta, near):
-    size, outw = near[0].shape
-    return join(join_weight_kernel, meta, near, [sds((8 * size, outw), bf16)], [4 * size // LINE], "join_weight")[0]
-
-
-def join_heads_kernel(meta, own, back2, back3, *refs):
-    run_all(head_copies(meta, {0: own, 2: back2, 3: back3}, refs[:3], refs[3]))
-
-
-def join_heads(meta, own, back2, back3):
-    _, rows, width = own.shape
-    shapes = [sds((rows, 4 * width), bf16)] * 3
-    return join(join_heads_kernel, meta, (own, back2, back3), shapes, [9], "join_heads")
-
-
-def join_last_kernel(meta, *refs):
-    far, back1, outs, sems = refs[:4], refs[4], refs[9:13], refs[13:]
-    run_all(weight_copies(meta, far, 4, outs[3], sems[0]) + head_copies(meta, {1: back1}, outs[:3], sems[1]))
-
-
-def join_last(meta, far, back1, outs):
-    shapes = [sds(x.shape, x.dtype) for x in outs]
-    return join(join_last_kernel, meta, (*far, back1), shapes, [4 * far[0].shape[0] // LINE, 3], "join_last", outs)
+        name="join",
+    )(meta, *parts)
 
 
 def dense_body(queries, keys_in, values, out_grad, out_weight, voxel_count):
@@ -390,15 +383,14 @@
     own0, *backs = backward(pieces, (grad_early, grad_late), (*saved_a, *saved_b), early)
     own_part, *sends = add_parts(after(keep, own0), recv)
     recvs = [swap(x, "chips", 4, j + 1) for j, x in enumerate(sends)]
-    back3, back2 = send(backs[2], 3), send(backs[1], 2)
-    done = total_of(own_part, recvs, 1.0 / 8)
-    near = [done] + [swap(done, "chips", 4, j) for j in (1, 2, 3)]
-    back1 = send(backs[0], 1, near[1])
-    weight = join_weight(meta, near)
-    weight, *near, back2, back3 = lax.optimization_barrier((weight, *near, back2, back3))
-    far = [swap(x, "core", 2, 1) for x in near]
-    heads = join_heads(meta, own0, back2, back3)
-    return tuple(join_last(meta, far, back1, (*heads, weight)))
+    back3, back2, back1 = (send(backs[k - 1], k) for k in (3, 2, 1))
+    done, wide, rest = total_of(own_part, recvs, 1.0 / 8)
+    after_near = after(done, back1)
+    near = [swap(after_near if j == 3 else done, "chips", 4, j) for j in (1, 2, 3)]
+
+    wide, back2, back3 = lax.optimization_barrier((wide, back2, back3))
+    far = [swap(x, "core", 2, 1) for x in (wide, rest, *near)]
+    return tuple(join(meta, (done, *near), far, (own0, back1, back2, back3)))
 
 
 def attend_listed(queries, keys_in, values, block_ids, live_count):

time: 115 us -> 116 us (level)
  the two profiles are of different devices: /device:TPU:0 before, /device:TPU:13 now
where the time goes in v3:
time: 116 us
  waiting for transfers between devices  60.5 us (52%)
  starting transfers between devices  31.5 us (27%)
  Pallas kernels  17.9 us (15%)
  local copies, waits for them, and re-layouts  4.21 us (4%)
  between operations  1.43 us (1%)
    ppermute x24, waiting for transfers between devices, swap(): return lax.ppermute(x, axis, [(i, i ^ flip) for i in range(size)])  60.5 us
    ppermute x24, starting transfers between devices, swap(): return lax.ppermute(x, axis, [(i, i ^ flip) for i in range(size)])  31.5 us
    pallas_call x9, Pallas kernels, whole(): pl.pallas_call(kernel, out_shape=out_shape, in_specs=[pl.BlockSpec(memory...  14 us
    unnamed x10, local copies, waits for them, and re-layouts  4.17 us
    pallas_call x1, Pallas kernels, join(): pl.pallas_call(join_kernel, out_shape=[sds((rows, 4 * width), bf16)] * 3...  2.85 us
  transfers between devices with their start and end apart: 24, of which 12 were waited for; matrix products, arithmetic and copies ran while one was open for 0% of the time, Pallas kernels for 11%

profile of v3, /device:TPU:13, one launch (start us, length us, event | category | flops | bytes accessed | tf_op | source)
XLA Modules:
  0.0 115.6 jit_solution(8042544581937685410)
XLA Ops:
  0.6 0.2 collective-permute-start.3
  0.9 2.3 %collective-permute-start.1 = (bf16[128,2048]{1,0:T(8,128)(2,1)}, bf16[128,2048]{1,0:T(8,128)(2,1)S(1)}, u32[]{:S(2)}, u32[]{:S(2)}) collective-permute-start(bf16[128,2048]{1,0:T(8,128)(2,1)} %grad_ref.1), channel_id=1, source_target_pairs={{0,2},{1,3},{2,0},{3,1},{4,6},{5,7},{6,4},{7,5},{8,10},{9,11},{10,... | collective-permute-start | bytes 1572872 | tf_op jit(solution)/shard_map/ppermute | solution.py:40
  3.8 0.1 pad_add_fusion.meta
  3.9 1.0 copy-done.1
  5.0 1.0 copy-done.2
  6.0 1.0 copy-done.3
  7.0 1.0 copy-done.4
  8.1 1.1 pack_heads.1
  9.2 1.4 %collective-permute-start = (bf16[3,128,512]{2,1,0:T(8,128)(2,1)S(1)}, bf16[3,128,512]{2,1,0:T(8,128)(2,1)S(1)}, u32[]{:S(2)}, u32[]{:S(2)}) collective-permute-start(bf16[3,128,512]{2,1,0:T(8,128)(2,1)S(1)} %get-tuple-element.59), channel_id=1, source_target_pairs={{0,1},{1,0},{2,3},{3,2},{4,5},{5,4},{6,7},{7,6},{8,9},{9,8},{10,11... | collective-permute-start | bytes 1179656 | tf_op jit(solution)/shard_map/ppermute | solution.py:40
  10.5 12.4 %collective-permute-done.3.refs_1_ = bf16[128,2048]{1,0:T(8,128)(2,1)S(1)} collective-permute-done((bf16[128,2048]{1,0:T(8,128)(2,1)}, bf16[128,2048]{1,0:T(8,128)(2,1)S(1)}, u32[]{:S(2)}, u32[]{:S(2)}) %collective-permute-start.3) | collective-permute-done | bytes 524320 | tf_op jit(solution)/shard_map/ppermute | solution.py:40
  22.9 1.3 %collective-permute-start.4 = (bf16[3,128,384]{2,1,0:T(8,128)(2,1)S(1)}, bf16[3,128,384]{2,1,0:T(8,128)(2,1)S(1)}, u32[]{:S(2)}, u32[]{:S(2)}) collective-permute-start(bf16[3,128,384]{2,1,0:T(8,128)(2,1)S(1)} %get-tuple-element.63), channel_id=1, source_target_pairs={{0,3},{1,2},{2,1},{3,0},{4,7},{5,6},{6,5},{7,4},{8,11},{9,10},{10,... | collective-permute-start | bytes 884744 | tf_op jit(solution)/shard_map/ppermute | solution.py:40
  24.2 1.8 %collective-permute-done.1.refs_2_ = bf16[128,2048]{1,0:T(8,128)(2,1)S(1)} collective-permute-done((bf16[128,2048]{1,0:T(8,128)(2,1)}, bf16[128,2048]{1,0:T(8,128)(2,1)S(1)}, u32[]{:S(2)}, u32[]{:S(2)}) %collective-permute-start.1) | collective-permute-done | bytes 524320 | tf_op jit(solution)/shard_map/ppermute | solution.py:40
  26.0 1.1 collective-permute-start.2
  27.1 0.4 collective-permute-start.7
  27.4 1.6 %grad_attn.2.refs_4_.early_ref = bf16[384,512]{1,0:T(8,128)(2,1)S(1)} custom-call(s32[4]{0:T(128)S(1)} %pad_add_fusion.meta, bf16[128,2048]{1,0:T(8,128)(2,1)S(1)} %get-tuple-element.65.refs_0_, bf16[128,2048]{1,0:T(8,128)(2,1)S(1)} %collective-permute-done.3.refs_1_, bf16[128,2048]{1,0:T(8,128)(2,1)S(1)} %collective-permute-done.1.refs_2_, ...), custom_call_target="tpu_custom_call" | custom-call | bytes 1024 | tf_op jit(solution)/shard_map/grad_attn/pallas_call | solution.py:55
  29.0 4.4 %collective-permute-done.refs_1_.near = bf16[3,128,512]{2,1,0:T(8,128)(2,1)S(1)} collective-permute-done((bf16[3,128,512]{2,1,0:T(8,128)(2,1)S(1)}, bf16[3,128,512]{2,1,0:T(8,128)(2,1)S(1)}, u32[]{:S(2)}, u32[]{:S(2)}) %collective-permute-start) | collective-permute-done | bytes 393248 | tf_op jit(solution)/shard_map/ppermute | solution.py:40
  33.4 0.4 collective-permute-start.8
  33.8 0.0 collective-permute-done.4.refs_3_.far3a
  33.8 9.2 %collective-permute-start.6 = (bf16[3,128,128]{2,1,0:T(8,128)(2,1)S(1)}, bf16[3,128,128]{2,1,0:T(8,128)(2,1)S(1)}, u32[]{:S(2)}, u32[]{:S(2)}) collective-permute-start(bf16[3,128,128]{2,1,0:T(8,128)(2,1)S(1)} %get-tuple-element.75), channel_id=1, source_target_pairs={{0,3},{1,2},{2,1},{3,0},{4,7},{5,6},{6,5},{7,4},{8,11},{9,10},{10,... | collective-permute-start | bytes 294920 | tf_op jit(solution)/shard_map/ppermute | solution.py:40
  43.0 6.9 %collective-permute-done.2.refs_2_.far2a = bf16[3,128,384]{2,1,0:T(8,128)(2,1)S(1)} collective-permute-done((bf16[3,128,384]{2,1,0:T(8,128)(2,1)S(1)}, bf16[3,128,384]{2,1,0:T(8,128)(2,1)S(1)}, u32[]{:S(2)}, u32[]{:S(2)}) %collective-permute-start.2) | collective-permute-done | bytes 294944 | tf_op jit(solution)/shard_map/ppermute | solution.py:40
  49.9 3.1 %collective-permute-start.5 = (bf16[3,128,128]{2,1,0:T(8,128)(2,1)S(1)}, bf16[3,128,128]{2,1,0:T(8,128)(2,1)S(1)}, u32[]{:S(2)}, u32[]{:S(2)}) collective-permute-start(bf16[3,128,128]{2,1,0:T(8,128)(2,1)S(1)} %get-tuple-element.73), channel_id=1, source_target_pairs={{0,2},{1,3},{2,0},{3,1},{4,6},{5,7},{6,4},{7,5},{8,10},{9,11},{10,... | collective-permute-start | bytes 294920 | tf_op jit(solution)/shard_map/ppermute | solution.py:40
  53.0 3.3 %attend_forward.2 = (bf16[3,512,512]{2,1,0:T(8,128)(2,1)S(1)}, f32[3,1,512]{2,1,0:T(1,128)S(1)}, f32[384,512]{1,0:T(8,128)S(1)}, bf16[384,512]{1,0:T(8,128)(2,1)S(1)}, f32[512,512]{1,0:T(8,128)S(1)}) custom-call(s32[4]{0:T(128)S(1)} %pad_add_fusion.meta, bf16[3,128,512]{2,1,0:T(8,128)(2,1)S(1)} %get-tuple-element.58.refs_0_.own, ...), custom_call_target="tpu_custom_call" | custom-call | bytes 1024 | tf_op jit(solution)/shard_map/attend_forward/pallas_call | solution.py:55
  56.3 2.3 %backward_early.1 = (bf16[384,384]{1,0:T(8,128)(2,1)S(1)}, f32[512,384]{1,0:T(8,128)S(1)}, f32[512,384]{1,0:T(8,128)S(1)}) custom-call(bf16[3,128,512]{2,1,0:T(8,128)(2,1)S(1)} %get-tuple-element.58.refs_0_.own, bf16[3,128,512]{2,1,0:T(8,128)(2,1)S(1)} %collective-permute-done.refs_1_.near, bf16[3,128,384]{2,1,0:T(8,128)(2,1)S(1)} %collective-permute-done.2.refs_2_.far2a, ...), custom_call_target="tpu_custom_call" | custom-call | bytes 1024 | tf_op jit(solution)/shard_map/backward_early/pallas_call | solution.py:55
  58.6 0.0 collective-permute-done.6.refs_3_.far3b
  58.6 3.6 %collective-permute-done.5.refs_2_.far2b = bf16[3,128,128]{2,1,0:T(8,128)(2,1)S(1)} collective-permute-done((bf16[3,128,128]{2,1,0:T(8,128)(2,1)S(1)}, bf16[3,128,128]{2,1,0:T(8,128)(2,1)S(1)}, u32[]{:S(2)}, u32[]{:S(2)}) %collective-permute-start.5) | collective-permute-done | bytes 98336 | tf_op jit(solution)/shard_map/ppermute | solution.py:40
  62.3 1.6 %attend_forward.3 = (bf16[1,512,512]{2,1,0:T(8,128)(2,1)S(1)}, f32[1,1,512]{2,1,0:T(1,128)S(1)}, f32[128,512]{1,0:T(8,128)S(1)}, bf16[128,512]{1,0:T(8,128)(2,1)S(1)}) custom-call(s32[4]{0:T(128)S(1)} %pad_add_fusion.meta, bf16[3,128,512]{2,1,0:T(8,128)(2,1)S(1)} %get-tuple-element.58.refs_0_.own, ...), custom_call_target="tpu_custom_call" | custom-call | bytes 1024 | tf_op jit(solution)/shard_map/attend_forward/pallas_call | solution.py:55
  63.8 0.0 collective-permute-done.7.refs_3_.refs_0_
  63.9 0.0 collective-permute-done.8.refs_4_.refs_1_
  63.9 1.8 %weight_halves.1 = (bf16[256,2048]{1,0:T(8,128)(2,1)S(1)}, f32[256,2048]{1,0:T(8,128)S(1)}) custom-call(s32[4]{0:T(128)S(1)} %pad_add_fusion.meta, bf16[384,512]{1,0:T(8,128)(2,1)S(1)} %get-tuple-element.76.heads_a, bf16[128,512]{1,0:T(8,128)(2,1)S(1)} %get-tuple-element.82.heads_b, bf16[128,2048]{1,0:T(8,128)(2,1)S(1)} %get-tuple-element.65.refs_0_, ...), custom_call_target="tpu_custom_call" | custom-call | bytes 1024 | tf_op jit(solution)/shard_map/weight_halves/pallas_call | solution.py:55
  65.7 1.9 %collective-permute-start.9 = (bf16[256,2048]{1,0:T(8,128)(2,1)S(1)}, bf16[256,2048]{1,0:T(8,128)(2,1)S(1)}, u32[]{:S(2)}, u32[]{:S(2)}) collective-permute-start(bf16[256,2048]{1,0:T(8,128)(2,1)S(1)} %get-tuple-element.87), channel_id=1, source_target_pairs={{0,4},{4,0},{1,5},{5,1},{2,6},{6,2},{3,7},{7,3},{8,12},{12,8},{9,1... | collective-permute-start | bytes 3145736 | tf_op jit(solution)/shard_map/ppermute | solution.py:40
  67.6 1.4 %grad_attn.3.late_ref = bf16[128,512]{1,0:T(8,128)(2,1)S(1)} custom-call(s32[4]{0:T(128)S(1)} %pad_add_fusion.meta, bf16[64,2048]{1,0:T(8,128)(2,1)S(1)} %collective-permute-done.7.refs_3_.refs_0_, bf16[64,2048]{1,0:T(8,128)(2,1)S(1)} %collective-permute-done.8.refs_4_.refs_1_, bf16[512,2048]{1,0:T(8,128)(2,1)S(1)} %copy-done), custom_call_target="tpu_custom_call" | custom-call | bytes 1024 | tf_op jit(solution)/shard_map/grad_attn/pallas_call | solution.py:55
  69.0 1.6 %attend_backward.1 = (bf16[3,128,512]{2,1,0:T(8,128)(2,1)S(1)}, bf16[3,128,512]{2,1,0:T(8,128)(2,1)S(1)}, bf16[3,128,512]{2,1,0:T(8,128)(2,1)S(1)}, bf16[3,128,512]{2,1,0:T(8,128)(2,1)S(1)}) custom-call(bf16[3,128,512]{2,1,0:T(8,128)(2,1)S(1)} %get-tuple-element.58.refs_0_.own, bf16[3,128,512]{2,1,0:T(8,128)(2,1)S(1)} %collective-permute-done.refs_1_.near, ...), custom_call_target="tpu_custom_call" | custom-call | bytes 1024 | tf_op jit(solution)/shard_map/attend_backward/pallas_call | solution.py:55
  70.6 0.0 collective-permute-done.9.recv_ref
  70.6 0.2 add_parts.1
  70.8 1.3 %collective-permute-start.10 = (bf16[64,2048]{1,0:T(8,128)(2,1)S(1)}, bf16[64,2048]{1,0:T(8,128)(2,1)S(1)}, u32[]{:S(2)}, u32[]{:S(2)}) collective-permute-start(bf16[64,2048]{1,0:T(8,128)(2,1)S(1)} %get-tuple-element.99), channel_id=1, source_target_pairs={{0,8},{8,0},{16,24},{24,16},{1,9},{9,1},{17,25},{25,17},{2,10},{10... | collective-permute-start | bytes 786440 | tf_op jit(solution)/shard_map/ppermute | solution.py:40
  72.1 0.1 collective-permute-start.15
  72.3 1.4 %collective-permute-start.17 = (bf16[3,128,512]{2,1,0:T(8,128)(2,1)S(1)}, bf16[3,128,512]{2,1,0:T(8,128)(2,1)S(1)}, u32[]{:S(2)}, u32[]{:S(2)}) collective-permute-start(bf16[3,128,512]{2,1,0:T(8,128)(2,1)S(1)} %get-tuple-element.106), channel_id=1, source_target_pairs={{0,2},{1,3},{2,0},{3,1},{4,6},{5,7},{6,4},{7,5},{8,10},{9,11},{10,... | collective-permute-start | bytes 1179656 | tf_op jit(solution)/shard_map/ppermute | solution.py:40
  73.6 1.1 collective-permute-start.18
  74.8 0.2 collective-permute-start.11
  75.0 3.8 %collective-permute-done.10.r1 = bf16[64,2048]{1,0:T(8,128)(2,1)S(1)} collective-permute-done((bf16[64,2048]{1,0:T(8,128)(2,1)S(1)}, bf16[64,2048]{1,0:T(8,128)(2,1)S(1)}, u32[]{:S(2)}, u32[]{:S(2)}) %collective-permute-start.10) | collective-permute-done | bytes 262176 | tf_op jit(solution)/shard_map/ppermute | solution.py:40
  78.8 1.1 collective-permute-start.12
  80.0 1.4 %collective-permute-done.11.r2 = bf16[64,2048]{1,0:T(8,128)(2,1)S(1)} collective-permute-done((bf16[64,2048]{1,0:T(8,128)(2,1)S(1)}, bf16[64,2048]{1,0:T(8,128)(2,1)S(1)}, u32[]{:S(2)}, u32[]{:S(2)}) %collective-permute-start.11) | collective-permute-done | bytes 262176 | tf_op jit(solution)/shard_map/ppermute | solution.py:40
  81.4 5.4 %collective-permute-done.12.r3 = bf16[64,2048]{1,0:T(8,128)(2,1)S(1)} collective-permute-done((bf16[64,2048]{1,0:T(8,128)(2,1)S(1)}, bf16[64,2048]{1,0:T(8,128)(2,1)S(1)}, u32[]{:S(2)}, u32[]{:S(2)}) %collective-permute-start.12) | collective-permute-done | bytes 262176 | tf_op jit(solution)/shard_map/ppermute | solution.py:40
  86.9 0.2 scene_mean.1
  87.0 0.8 collective-permute-done.15.refs_10_
  87.8 0.4 collective-permute-start.16
  88.2 1.2 %collective-permute-start.14 = (bf16[64,2048]{1,0:T(8,128)(2,1)S(1)}, bf16[64,2048]{1,0:T(8,128)(2,1)S(1)}, u32[]{:S(2)}, u32[]{:S(2)}) collective-permute-start(bf16[64,2048]{1,0:T(8,128)(2,1)S(1)} %get-tuple-element.104.refs_0_), channel_id=1, source_target_pairs={{0,16},{8,24},{16,0},{24,8},{1,17},{9,25},{17,1},{25,9},{2,18},{10... | collective-permute-start | bytes 786440 | tf_op jit(solution)/shard_map/ppermute | solution.py:40
  89.4 1.0 collective-permute-start.13
  90.5 0.8 collective-permute-done.17.refs_11_
  91.2 17.5 %collective-permute-done.18.refs_12_ = bf16[3,128,512]{2,1,0:T(8,128)(2,1)S(1)} collective-permute-done((bf16[3,128,512]{2,1,0:T(8,128)(2,1)S(1)}, bf16[3,128,512]{2,1,0:T(8,128)(2,1)S(1)}, u32[]{:S(2)}, u32[]{:S(2)}) %collective-permute-start.18) | collective-permute-done | bytes 393248 | tf_op jit(solution)/shard_map/ppermute | solution.py:40
  108.8 1.4 %collective-permute-start.19 = (f32[64,1792]{1,0:T(8,128)S(1)}, f32[64,1792]{1,0:T(8,128)S(1)}, u32[]{:S(2)}, u32[]{:S(2)}) collective-permute-start(f32[64,1792]{1,0:T(8,128)S(1)} %get-tuple-element.108), channel_id=1, source_target_pairs={{0,4},{4,0},{1,5},{5,1},{2,6},{6,2},{3,7},{7,3},{8,12},{12,8},{9,1... | collective-permute-start | bytes 1376264 | tf_op jit(solution)/shard_map/ppermute | solution.py:40
  110.2 0.0 collective-permute-done.16.refs_3_
  110.2 0.0 collective-permute-start.23
  110.2 0.0 collective-permute-done.14.refs_2_
  110.2 0.5 collective-permute-start.22
  110.7 0.0 collective-permute-done.13.refs_1_
  110.7 0.1 collective-permute-start.21
  110.7 0.4 collective-permute-start.20
  111.2 1.6 %collective-permute-done.20.refs_5_ = bf16[64,256]{1,0:T(8,128)(2,1)S(1)} collective-permute-done((bf16[64,256]{1,0:T(8,128)(2,1)S(1)}, bf16[64,256]{1,0:T(8,128)(2,1)S(1)}, u32[]{:S(2)}, u32[]{:S(2)}) %collective-permute-start.20) | collective-permute-done | bytes 32800 | tf_op jit(solution)/shard_map/ppermute | solution.py:40
  112.8 0.0 collective-permute-done.19.refs_4_
  112.8 0.0 collective-permute-done.23.refs_8_
  112.8 0.0 collective-permute-done.22.refs_7_
  112.8 0.0 collective-permute-done.21.refs_6_
  112.8 2.9 %join.1 = (bf16[128,2048]{1,0:T(8,128)(2,1)}, bf16[128,2048]{1,0:T(8,128)(2,1)}, bf16[128,2048]{1,0:T(8,128)(2,1)}, bf16[512,2048]{1,0:T(8,128)(2,1)}) custom-call(s32[4]{0:T(128)S(1)} %pad_add_fusion.meta, bf16[64,2048]{1,0:T(8,128)(2,1)S(1)} %get-tuple-element.104.refs_0_, bf16[64,2048]{1,0:T(8,128)(2,1)S(1)} %collective-permute-done.13.refs_1_, ...), custom_call_target="tpu_custom_call" | custom-call | bytes 1024 | tf_op jit(solution)/shard_map/join/pallas_call | solution.py:340
  (8 shorter events, 0.0 us)
Async XLA Ops:
  0.6 26.8 %copy-start = (bf16[512,2048]{1,0:T(8,128)(2,1)S(1)}, bf16[512,2048]{1,0:T(8,128)(2,1)}, u32[]{:S(2)}) copy-start(bf16[512,2048]{1,0:T(8,128)(2,1)} %refs_2_.1) | copy-start | bytes 6291460
  0.6 22.2 %collective-permute-start.3 = (bf16[128,2048]{1,0:T(8,128)(2,1)}, bf16[128,2048]{1,0:T(8,128)(2,1)S(1)}, u32[]{:S(2)}, u32[]{:S(2)}) collective-permute-start(bf16[128,2048]{1,0:T(8,128)(2,1)} %grad_ref.1), channel_id=1, source_target_pairs={{0,1},{1,0},{2,3},{3,2},{4,5},{5,4},{6,7},{7,6},{8,9},{9,8},{10,11... | collective-permute-start | bytes 1572872 | tf_op jit(solution)/shard_map/ppermute | solution.py:40
  0.9 25.1 %collective-permute-start.1 = (bf16[128,2048]{1,0:T(8,128)(2,1)}, bf16[128,2048]{1,0:T(8,128)(2,1)S(1)}, u32[]{:S(2)}, u32[]{:S(2)}) collective-permute-start(bf16[128,2048]{1,0:T(8,128)(2,1)} %grad_ref.1), channel_id=1, source_target_pairs={{0,2},{1,3},{2,0},{3,1},{4,6},{5,7},{6,4},{7,5},{8,10},{9,11},{10,... | collective-permute-start | bytes 1572872 | tf_op jit(solution)/shard_map/ppermute | solution.py:40
  3.9 1.0 copy-start.1
  5.0 1.0 copy-start.2
  6.0 1.0 copy-start.3
  7.0 1.0 copy-start.4
  9.2 24.3 %collective-permute-start = (bf16[3,128,512]{2,1,0:T(8,128)(2,1)S(1)}, bf16[3,128,512]{2,1,0:T(8,128)(2,1)S(1)}, u32[]{:S(2)}, u32[]{:S(2)}) collective-permute-start(bf16[3,128,512]{2,1,0:T(8,128)(2,1)S(1)} %get-tuple-element.59), channel_id=1, source_target_pairs={{0,1},{1,0},{2,3},{3,2},{4,5},{5,4},{6,7},{7,6},{8,9},{9,8},{10,11... | collective-permute-start | bytes 1179656 | tf_op jit(solution)/shard_map/ppermute | solution.py:40
  22.9 10.9 %collective-permute-start.4 = (bf16[3,128,384]{2,1,0:T(8,128)(2,1)S(1)}, bf16[3,128,384]{2,1,0:T(8,128)(2,1)S(1)}, u32[]{:S(2)}, u32[]{:S(2)}) collective-permute-start(bf16[3,128,384]{2,1,0:T(8,128)(2,1)S(1)} %get-tuple-element.63), channel_id=1, source_target_pairs={{0,3},{1,2},{2,1},{3,0},{4,7},{5,6},{6,5},{7,4},{8,11},{9,10},{10,... | collective-permute-start | bytes 884744 | tf_op jit(solution)/shard_map/ppermute | solution.py:40
  26.0 23.9 %collective-permute-start.2 = (bf16[3,128,384]{2,1,0:T(8,128)(2,1)S(1)}, bf16[3,128,384]{2,1,0:T(8,128)(2,1)S(1)}, u32[]{:S(2)}, u32[]{:S(2)}) collective-permute-start(bf16[3,128,384]{2,1,0:T(8,128)(2,1)S(1)} %get-tuple-element.61), channel_id=1, source_target_pairs={{0,2},{1,3},{2,0},{3,1},{4,6},{5,7},{6,4},{7,5},{8,10},{9,11},{10,... | collective-permute-start | bytes 884744 | tf_op jit(solution)/shard_map/ppermute | solution.py:40
  27.1 36.8 %collective-permute-start.7 = (bf16[64,2048]{1,0:T(8,128)(2,1)S(1)}, bf16[64,2048]{1,0:T(8,128)(2,1)S(1)}, u32[]{:S(2)}, u32[]{:S(2)}) collective-permute-start(bf16[64,2048]{1,0:T(8,128)(2,1)S(1)} %slice.8), channel_id=1, source_target_pairs={{0,1},{1,0},{2,3},{3,2},{4,5},{5,4},{6,7},{7,6},{8,9},{9,8},{10,11... | collective-permute-start | bytes 786440 | tf_op jit(solution)/shard_map/ppermute | solution.py:40
  33.4 30.4 %collective-permute-start.8 = (bf16[64,2048]{1,0:T(8,128)(2,1)S(1)}, bf16[64,2048]{1,0:T(8,128)(2,1)S(1)}, u32[]{:S(2)}, u32[]{:S(2)}) collective-permute-start(bf16[64,2048]{1,0:T(8,128)(2,1)S(1)} %slice.7), channel_id=1, source_target_pairs={{0,1},{1,0},{2,3},{3,2},{4,5},{5,4},{6,7},{7,6},{8,9},{9,8},{10,11... | collective-permute-start | bytes 786440 | tf_op jit(solution)/shard_map/ppermute | solution.py:40
  33.8 24.8 %collective-permute-start.6 = (bf16[3,128,128]{2,1,0:T(8,128)(2,1)S(1)}, bf16[3,128,128]{2,1,0:T(8,128)(2,1)S(1)}, u32[]{:S(2)}, u32[]{:S(2)}) collective-permute-start(bf16[3,128,128]{2,1,0:T(8,128)(2,1)S(1)} %get-tuple-element.75), channel_id=1, source_target_pairs={{0,3},{1,2},{2,1},{3,0},{4,7},{5,6},{6,5},{7,4},{8,11},{9,10},{10,... | collective-permute-start | bytes 294920 | tf_op jit(solution)/shard_map/ppermute | solution.py:40
  49.9 12.4 %collective-permute-start.5 = (bf16[3,128,128]{2,1,0:T(8,128)(2,1)S(1)}, bf16[3,128,128]{2,1,0:T(8,128)(2,1)S(1)}, u32[]{:S(2)}, u32[]{:S(2)}) collective-permute-start(bf16[3,128,128]{2,1,0:T(8,128)(2,1)S(1)} %get-tuple-element.73), channel_id=1, source_target_pairs={{0,2},{1,3},{2,0},{3,1},{4,6},{5,7},{6,4},{7,5},{8,10},{9,11},{10,... | collective-permute-start | bytes 294920 | tf_op jit(solution)/shard_map/ppermute | solution.py:40
  65.7 4.9 %collective-permute-start.9 = (bf16[256,2048]{1,0:T(8,128)(2,1)S(1)}, bf16[256,2048]{1,0:T(8,128)(2,1)S(1)}, u32[]{:S(2)}, u32[]{:S(2)}) collective-permute-start(bf16[256,2048]{1,0:T(8,128)(2,1)S(1)} %get-tuple-element.87), channel_id=1, source_target_pairs={{0,4},{4,0},{1,5},{5,1},{2,6},{6,2},{3,7},{7,3},{8,12},{12,8},{9,1... | collective-permute-start | bytes 3145736 | tf_op jit(solution)/shard_map/ppermute | solution.py:40
  70.8 8.0 %collective-permute-start.10 = (bf16[64,2048]{1,0:T(8,128)(2,1)S(1)}, bf16[64,2048]{1,0:T(8,128)(2,1)S(1)}, u32[]{:S(2)}, u32[]{:S(2)}) collective-permute-start(bf16[64,2048]{1,0:T(8,128)(2,1)S(1)} %get-tuple-element.99), channel_id=1, source_target_pairs={{0,8},{8,0},{16,24},{24,16},{1,9},{9,1},{17,25},{25,17},{2,10},{10... | collective-permute-start | bytes 786440 | tf_op jit(solution)/shard_map/ppermute | solution.py:40
  72.1 15.7 %collective-permute-start.15 = (bf16[3,128,512]{2,1,0:T(8,128)(2,1)S(1)}, bf16[3,128,512]{2,1,0:T(8,128)(2,1)S(1)}, u32[]{:S(2)}, u32[]{:S(2)}) collective-permute-start(bf16[3,128,512]{2,1,0:T(8,128)(2,1)S(1)} %get-tuple-element.103), channel_id=1, source_target_pairs={{0,1},{1,0},{2,3},{3,2},{4,5},{5,4},{6,7},{7,6},{8,9},{9,8},{10,11... | collective-permute-start | bytes 1179656 | tf_op jit(solution)/shard_map/ppermute | solution.py:40
  72.3 19.0 %collective-permute-start.17 = (bf16[3,128,512]{2,1,0:T(8,128)(2,1)S(1)}, bf16[3,128,512]{2,1,0:T(8,128)(2,1)S(1)}, u32[]{:S(2)}, u32[]{:S(2)}) collective-permute-start(bf16[3,128,512]{2,1,0:T(8,128)(2,1)S(1)} %get-tuple-element.106), channel_id=1, source_target_pairs={{0,2},{1,3},{2,0},{3,1},{4,6},{5,7},{6,4},{7,5},{8,10},{9,11},{10,... | collective-permute-start | bytes 1179656 | tf_op jit(solution)/shard_map/ppermute | solution.py:40
  73.6 35.1 %collective-permute-start.18 = (bf16[3,128,512]{2,1,0:T(8,128)(2,1)S(1)}, bf16[3,128,512]{2,1,0:T(8,128)(2,1)S(1)}, u32[]{:S(2)}, u32[]{:S(2)}) collective-permute-start(bf16[3,128,512]{2,1,0:T(8,128)(2,1)S(1)} %get-tuple-element.107), channel_id=1, source_target_pairs={{0,3},{1,2},{2,1},{3,0},{4,7},{5,6},{6,5},{7,4},{8,11},{9,10},{10,... | collective-permute-start | bytes 1179656 | tf_op jit(solution)/shard_map/ppermute | solution.py:40
  74.8 6.7 %collective-permute-start.11 = (bf16[64,2048]{1,0:T(8,128)(2,1)S(1)}, bf16[64,2048]{1,0:T(8,128)(2,1)S(1)}, u32[]{:S(2)}, u32[]{:S(2)}) collective-permute-start(bf16[64,2048]{1,0:T(8,128)(2,1)S(1)} %get-tuple-element.100), channel_id=1, source_target_pairs={{0,16},{8,24},{16,0},{24,8},{1,17},{9,25},{17,1},{25,9},{2,18},{10... | collective-permute-start | bytes 786440 | tf_op jit(solution)/shard_map/ppermute | solution.py:40
  78.8 8.0 %collective-permute-start.12 = (bf16[64,2048]{1,0:T(8,128)(2,1)S(1)}, bf16[64,2048]{1,0:T(8,128)(2,1)S(1)}, u32[]{:S(2)}, u32[]{:S(2)}) collective-permute-start(bf16[64,2048]{1,0:T(8,128)(2,1)S(1)} %get-tuple-element.101), channel_id=1, source_target_pairs={{0,24},{8,16},{16,8},{24,0},{1,25},{9,17},{17,9},{25,1},{2,26},{10... | collective-permute-start | bytes 786440 | tf_op jit(solution)/shard_map/ppermute | solution.py:40
  87.8 22.3 %collective-permute-start.16 = (bf16[64,2048]{1,0:T(8,128)(2,1)S(1)}, bf16[64,2048]{1,0:T(8,128)(2,1)S(1)}, u32[]{:S(2)}, u32[]{:S(2)}) collective-permute-start(bf16[64,2048]{1,0:T(8,128)(2,1)S(1)} %get-tuple-element.104.refs_0_), channel_id=1, source_target_pairs={{0,24},{8,16},{16,8},{24,0},{1,25},{9,17},{17,9},{25,1},{2,26},{10... | collective-permute-start | bytes 786440 | tf_op jit(solution)/shard_map/ppermute | solution.py:40
  88.2 22.0 %collective-permute-start.14 = (bf16[64,2048]{1,0:T(8,128)(2,1)S(1)}, bf16[64,2048]{1,0:T(8,128)(2,1)S(1)}, u32[]{:S(2)}, u32[]{:S(2)}) collective-permute-start(bf16[64,2048]{1,0:T(8,128)(2,1)S(1)} %get-tuple-element.104.refs_0_), channel_id=1, source_target_pairs={{0,16},{8,24},{16,0},{24,8},{1,17},{9,25},{17,1},{25,9},{2,18},{10... | collective-permute-start | bytes 786440 | tf_op jit(solution)/shard_map/ppermute | solution.py:40
  89.4 21.3 %collective-permute-start.13 = (bf16[64,2048]{1,0:T(8,128)(2,1)S(1)}, bf16[64,2048]{1,0:T(8,128)(2,1)S(1)}, u32[]{:S(2)}, u32[]{:S(2)}) collective-permute-start(bf16[64,2048]{1,0:T(8,128)(2,1)S(1)} %get-tuple-element.104.refs_0_), channel_id=1, source_target_pairs={{0,8},{8,0},{16,24},{24,16},{1,9},{9,1},{17,25},{25,17},{2,10},{10... | collective-permute-start | bytes 786440 | tf_op jit(solution)/shard_map/ppermute | solution.py:40
  108.8 4.0 %collective-permute-start.19 = (f32[64,1792]{1,0:T(8,128)S(1)}, f32[64,1792]{1,0:T(8,128)S(1)}, u32[]{:S(2)}, u32[]{:S(2)}) collective-permute-start(f32[64,1792]{1,0:T(8,128)S(1)} %get-tuple-element.108), channel_id=1, source_target_pairs={{0,4},{4,0},{1,5},{5,1},{2,6},{6,2},{3,7},{7,3},{8,12},{12,8},{9,1... | collective-permute-start | bytes 1376264 | tf_op jit(solution)/shard_map/ppermute | solution.py:40
  110.2 2.6 %collective-permute-start.23 = (bf16[64,2048]{1,0:T(8,128)(2,1)S(1)}, bf16[64,2048]{1,0:T(8,128)(2,1)S(1)}, u32[]{:S(2)}, u32[]{:S(2)}) collective-permute-start(bf16[64,2048]{1,0:T(8,128)(2,1)S(1)} %collective-permute-done.16.refs_3_), channel_id=1, source_target_pairs={{0,4},{4,0},{1,5},{5,1},{2,6},{6,2},{3,7},{7,3},{8,12},{12,8},{9,1... | collective-permute-start | bytes 786440 | tf_op jit(solution)/shard_map/ppermute | solution.py:40
  110.2 2.6 %collective-permute-start.22 = (bf16[64,2048]{1,0:T(8,128)(2,1)S(1)}, bf16[64,2048]{1,0:T(8,128)(2,1)S(1)}, u32[]{:S(2)}, u32[]{:S(2)}) collective-permute-start(bf16[64,2048]{1,0:T(8,128)(2,1)S(1)} %collective-permute-done.14.refs_2_), channel_id=1, source_target_pairs={{0,4},{4,0},{1,5},{5,1},{2,6},{6,2},{3,7},{7,3},{8,12},{12,8},{9,1... | collective-permute-start | bytes 786440 | tf_op jit(solution)/shard_map/ppermute | solution.py:40
  110.7 2.1 %collective-permute-start.21 = (bf16[64,2048]{1,0:T(8,128)(2,1)S(1)}, bf16[64,2048]{1,0:T(8,128)(2,1)S(1)}, u32[]{:S(2)}, u32[]{:S(2)}) collective-permute-start(bf16[64,2048]{1,0:T(8,128)(2,1)S(1)} %collective-permute-done.13.refs_1_), channel_id=1, source_target_pairs={{0,4},{4,0},{1,5},{5,1},{2,6},{6,2},{3,7},{7,3},{8,12},{12,8},{9,1... | collective-permute-start | bytes 786440 | tf_op jit(solution)/shard_map/ppermute | solution.py:40
  110.7 2.0 %collective-permute-start.20 = (bf16[64,256]{1,0:T(8,128)(2,1)S(1)}, bf16[64,256]{1,0:T(8,128)(2,1)S(1)}, u32[]{:S(2)}, u32[]{:S(2)}) collective-permute-start(bf16[64,256]{1,0:T(8,128)(2,1)S(1)} %get-tuple-element.109), channel_id=1, source_target_pairs={{0,4},{4,0},{1,5},{5,1},{2,6},{6,2},{3,7},{7,3},{8,12},{12,8},{9,1... | collective-permute-start | bytes 98312 | tf_op jit(solution)/shard_map/ppermute | solution.py:40

commit v4 on v2

--- a/solution.py
+++ b/solution.py
@@ -125,44 +125,49 @@
     return (jnp.concatenate(x, axis=0) for x in zip(*parts))
 
 
-def forward_kernel(group, meta, *refs):
-    pieces, (weight_ref, inverse_ref, out_ref, heads_ref) = refs[:4], refs[-4:] if group else refs[4:8]
-    bias_ref = refs[4] if group else refs[8]
-    rows = pieces[0].shape[1]
-    total = 4 * rows
-    tile = 2 * rows
-    to_power = math.log2(math.e) / math.sqrt(HDIM)
-    query_live = token_pos((1, total), 1, meta[Z]) < meta[COUNT]
-    if group == 0:
-        key_live = token_pos((total, 1), 0, meta[Z]) < meta[COUNT]
-        bias_ref[...] = jnp.where(key_live | ~query_live, 0.0, -jnp.inf)
-    for h in range(pieces[-1].shape[2] // HDIM):
-        cols = slice(h * HDIM, (h + 1) * HDIM)
-        query, key, value = head_of(pieces, group, h)
-        for t in range(2):
-            part = slice(t * tile, (t + 1) * tile)
-            scores = dot(key, query[part], 1, 1) + bias_ref[:, part]
-            peak = jnp.max(scores, axis=0, keepdims=True)
-            weights = jnp.exp2((scores - peak) * to_power).astype(bf16)
-            weight_ref[h, :, part] = weights
-            inverse = 1.0 / jnp.sum(weights.astype(f32), axis=0, keepdims=True)
-            inverse_ref[h, :, part] = inverse
-            heads = dot(value, weights, 0, 0) * inverse
-            out_ref[cols, part] = heads
-            heads_ref[cols, part] = jnp.where(query_live[:, part], heads, 0.0).astype(bf16)
-
-
-def forward(meta, pieces, group, *bias):
+def span_forward(query, key, value, bias, live, weight_ref, inverse_ref, out_ref, heads_ref, h, span):
+    cols = slice(h * HDIM, (h + 1) * HDIM)
+    scores = dot(key, query[span], 1, 1) + bias
+    peak = jnp.max(scores, axis=0, keepdims=True)
+    weights = jnp.exp2((scores - peak) * (math.log2(math.e) / math.sqrt(HDIM))).astype(bf16)
+    weight_ref[h, :, span] = weights
+    inverse = 1.0 / jnp.sum(weights.astype(f32), axis=0, keepdims=True)
+    inverse_ref[h, :, span] = inverse
+    heads = dot(value, weights, 0, 0) * inverse
+    out_ref[cols, span] = heads
+    heads_ref[cols, span] = jnp.where(live, heads, 0.0).astype(bf16)
+
+
+def forward_shapes(pieces):
     _, rows, width = pieces[-1].shape
     total = 4 * rows
-    shapes = [
+    return [
         sds((width // HDIM, total, total), bf16),
         sds((width // HDIM, 1, total), f32),
         sds((width, total), f32),
         sds((width, total), bf16),
-    ] + ([] if bias else [sds((total, total), f32)])
-    kernel = functools.partial(forward_kernel, group)
-    return whole(kernel, shapes, (meta, *pieces, *bias), "attend_forward", 1, 8)
+    ]
+
+
+def forward_kernel(meta, p0, p1, p2, p3, weight_ref, inverse_ref, out_ref, heads_ref, bias_ref):
+    pieces = (p0, p1, p2, p3)
+    rows = p0.shape[1]
+    total = 4 * rows
+    query_live = token_pos((1, total), 1, meta[Z]) < meta[COUNT]
+    key_live = token_pos((total, 1), 0, meta[Z]) < meta[COUNT]
+    bias_ref[...] = jnp.where(key_live | ~query_live, 0.0, -jnp.inf)
+    for h in range(p3.shape[2] // HDIM):
+        query, key, value = head_of(pieces, 0, h)
+        for t in range(2):
+            span = slice(2 * rows * t, 2 * rows * (t + 1))
+            outs = (weight_ref, inverse_ref, out_ref, heads_ref, h, span)
+            span_forward(query, key, value, bias_ref[:, span], query_live[:, span], *outs)
+
+
+def forward(meta, pieces):
+    total = 4 * pieces[-1].shape[1]
+    shapes = forward_shapes(pieces) + [sds((total, total), f32)]
+    return whole(forward_kernel, shapes, (meta, *pieces), "attend_forward", 1, 8)
 
 
 def span_gradients(query, key, value, grad, weights, inverse, outs):
@@ -248,27 +253,55 @@
     return pl.ds(pl.multiple_of(at, LINE), LINE)
 
 
-def weight_kernel(meta, heads_a, heads_b, *refs):
-    *grads, send_ref, keep_ref = refs
-    width = heads_a.shape[0] + heads_b.shape[0]
+def lines_of(meta, heads_ref):
     lines = []
     for other in (1, 0):
         for j in range(4):
-            for ref in (heads_a, heads_b):
-                lines += [ref[line_at(meta, h, other, j), :] for h in range(ref.shape[0] // HDIM)]
-    lines = jnp.concatenate(lines, axis=0)
+            lines += [heads_ref[line_at(meta, h, other, j), :] for h in range(heads_ref.shape[0] // HDIM)]
+    return jnp.concatenate(lines, axis=0)
+
+
+def weight_kernel(meta, p0, p1, p2, p3, bias_ref, heads_a, *refs):
+    pieces, grads = (p0, p1, p2, p3), refs[:-6]
+    weight_ref, inverse_ref, out_ref, send_ref, keep_ref, heads_b = refs[-6:]
+    rows = p0.shape[1]
+    query_live = token_pos((1, 4 * rows), 1, meta[Z]) < meta[COUNT]
     tile = 4 * HDIM
-
-    for i in range(send_ref.shape[1] // tile):
-        part = slice(i * tile, (i + 1) * tile)
-        product = dot(lines, jnp.concatenate([g[:, part] for g in grads], axis=0), 1, 0)
-        send_ref[:, part] = product[: width // 2].astype(bf16)
-        keep_ref[:, part] = product[width // 2 :]
-
-
-def weight_halves(meta, heads, grads):
-    shape = (sum(x.shape[0] for x in heads) // 2, grads[0].shape[1])
-    return whole(weight_kernel, [sds(shape, bf16), sds(shape, f32)], (meta, *heads, *grads), "weight_halves", 1, 6)
+    tiles = send_ref.shape[1] // tile
+    whole_size = send_ref.shape[0] // 4
+
+    def product(lines, first, i):
+        cols = slice(i * tile, (i + 1) * tile)
+        result = dot(lines, jnp.concatenate([g[:, cols] for g in grads], axis=0), 1, 0)
+        size = lines.shape[0] // 8
+        for j in range(4):
+            at = slice(j * whole_size + first, j * whole_size + first + size)
+            send_ref[at, cols] = result[j * size : (j + 1) * size].astype(bf16)
+            keep_ref[at, cols] = result[(4 + j) * size : (5 + j) * size]
+
+    lines = lines_of(meta, heads_a)
+    count = p3.shape[2] // HDIM
+    for n in range(max(tiles, 2 * count)):
+        if n < 2 * count:
+            h, t = divmod(n, 2)
+            query, key, value = head_of(pieces, 1, h)
+            span = slice(2 * rows * t, 2 * rows * (t + 1))
+            outs = (weight_ref, inverse_ref, out_ref, heads_b, h, span)
+            span_forward(query, key, value, bias_ref[:, span], query_live[:, span], *outs)
+        if n < tiles:
+            product(lines, 0, n)
+    lines_b = lines_of(meta, heads_b)
+    for i in range(tiles):
+        product(lines_b, lines.shape[0] // 8, i)
+
+
+def weight_halves(meta, pieces, bias, heads, grads):
+    forward_out = forward_shapes(pieces)
+    width = heads.shape[0] + pieces[-1].shape[2]
+    shape = (width // 2, grads[0].shape[1])
+    shapes = forward_out[:3] + [sds(shape, bf16), sds(shape, f32)]
+    scratch = [pltpu.VMEM(forward_out[3].shape, bf16)]
+    return whole(weight_kernel, shapes, (meta, *pieces, bias, heads, *grads), "weight_halves", 1, 10, scratch)
 
 
 def add_kernel(keep_ref, recv_ref, *outs):
@@ -376,14 +409,13 @@
     grad_early = grad_attn(meta, (mine, beside, across), out_weight, 0)
     corners = [send(across[:half], 1), send(after(across, piece1, grad_early)[half:], 1)]
 
-    *saved_a, heads_a, bias = forward(meta, (own, piece1, piece2a, piece3a), 0)
+    *saved_a, heads_a, bias = forward(meta, (own, piece1, piece2a, piece3a))
     early = backward_early((own, piece1, piece2a, piece3a), grad_early, saved_a)
     heads_a, *early, piece2b, piece3b = lax.optimization_barrier((heads_a, *early, piece2b, piece3b))
-    *saved_b, heads_b = forward(meta, (own, piece1, piece2b, piece3b), 1, bias)
-    grad_early, heads_b, *corners = lax.optimization_barrier((grad_early, heads_b, *corners))
+    grad_early, piece2b, *corners = lax.optimization_barrier((grad_early, piece2b, *corners))
     grads = (mine, beside, across, *corners)
 
-    out, keep = weight_halves(meta, (heads_a, heads_b), grads)
+    *saved_b, out, keep = weight_halves(meta, (own, piece1, piece2b, piece3b), bias, heads_a, grads)
     recv = swap(out, "core", 2, 1)
     grad_late = grad_attn(meta, after(grads[3:], out), out_weight, 3 * BLOCK)
     pieces = (own, piece1, piece2a, piece3a, piece2b, piece3b)

time: 115 us -> 114 us (level)
    pallas_call x9 -> x8, Pallas kernels: 13.9 us -> 13.3 us  [whole(): pl.pallas_call(kernel, out_shape=out_shape, in_specs=[pl.BlockSpec(memory...]
  transfers between devices with their start and end apart: 23 -> 23, of which waited for: 12 -> 12; matrix products, arithmetic and copies ran while one was open for 0% -> 0% of each run, Pallas kernels for 14% -> 13%
where the time goes in v4:
time: 114 us; the launch traced here: 113 us
  waiting for transfers between devices  59.3 us (52%)
  starting transfers between devices  28.7 us (25%)
  Pallas kernels  19.5 us (17%)
  local copies, waits for them, and re-layouts  4.21 us (4%)
  between operations  1.45 us (1%)
    ppermute x23, waiting for transfers between devices, swap(): return lax.ppermute(x, axis, [(i, i ^ flip) for i in range(size)])  59.3 us
    ppermute x23, starting transfers between devices, swap(): return lax.ppermute(x, axis, [(i, i ^ flip) for i in range(size)])  28.7 us
    pallas_call x8, Pallas kernels, whole(): pl.pallas_call(kernel, out_shape=out_shape, in_specs=[pl.BlockSpec(memory...  13.3 us
    pallas_call x3, Pallas kernels, join(): pl.pallas_call(kernel, out_shape=shapes, in_specs=[pl.BlockSpec(memory_sp...  5.04 us
    unnamed x10, local copies, waits for them, and re-layouts  4.17 us
  transfers between devices with their start and end apart: 23, of which 12 were waited for; matrix products, arithmetic and copies ran while one was open for 0% of the time, Pallas kernels for 13%

profile of v4, /device:TPU:0, one launch (start us, length us, event | category | flops | bytes accessed | tf_op | source)
XLA Modules:
  0.0 113.2 jit_solution(7952966935967776938)
XLA Ops:
  0.6 0.0 copy-start
  0.6 3.1 %collective-permute-start.1 = (bf16[128,2048]{1,0:T(8,128)(2,1)}, bf16[128,2048]{1,0:T(8,128)(2,1)S(1)}, u32[]{:S(2)}, u32[]{:S(2)}) collective-permute-start(bf16[128,2048]{1,0:T(8,128)(2,1)} %grad_ref.1), channel_id=1, source_target_pairs={{0,1},{1,0},{2,3},{3,2},{4,5},{5,4},{6,7},{7,6},{8,9},{9,8},{10,11... | collective-permute-start | bytes 1572872 | tf_op jit(solution)/shard_map/ppermute | solution.py:40
  3.7 2.6 %collective-permute-start.2 = (bf16[128,2048]{1,0:T(8,128)(2,1)}, bf16[128,2048]{1,0:T(8,128)(2,1)S(1)}, u32[]{:S(2)}, u32[]{:S(2)}) collective-permute-start(bf16[128,2048]{1,0:T(8,128)(2,1)} %grad_ref.1), channel_id=1, source_target_pairs={{0,2},{1,3},{2,0},{3,1},{4,6},{5,7},{6,4},{7,5},{8,10},{9,11},{10,... | collective-permute-start | bytes 1572872 | tf_op jit(solution)/shard_map/ppermute | solution.py:40
  7.0 0.1 pad_add_fusion.meta
  7.1 1.0 copy-done.1
  8.1 1.0 copy-done.2
  9.1 1.0 copy-done.3
  10.2 1.0 copy-done.4
  11.2 1.1 pack_heads.1
  12.3 0.5 collective-permute-start
  12.8 15.0 %collective-permute-done.1.refs_1_ = bf16[128,2048]{1,0:T(8,128)(2,1)S(1)} collective-permute-done((bf16[128,2048]{1,0:T(8,128)(2,1)}, bf16[128,2048]{1,0:T(8,128)(2,1)S(1)}, u32[]{:S(2)}, u32[]{:S(2)}) %collective-permute-start.1) | collective-permute-done | bytes 524320 | tf_op jit(solution)/shard_map/ppermute | solution.py:40
  27.8 3.6 %collective-permute-start.4 = (bf16[3,128,384]{2,1,0:T(8,128)(2,1)S(1)}, bf16[3,128,384]{2,1,0:T(8,128)(2,1)S(1)}, u32[]{:S(2)}, u32[]{:S(2)}) collective-permute-start(bf16[3,128,384]{2,1,0:T(8,128)(2,1)S(1)} %get-tuple-element.67), channel_id=1, source_target_pairs={{0,3},{1,2},{2,1},{3,0},{4,7},{5,6},{6,5},{7,4},{8,11},{9,10},{10,... | collective-permute-start | bytes 884744 | tf_op jit(solution)/shard_map/ppermute | solution.py:40
  31.4 0.0 collective-permute-done.2.refs_2_
  31.4 0.0 collective-permute-start.3
  31.4 2.1 %collective-permute-start.7 = (bf16[64,2048]{1,0:T(8,128)(2,1)S(1)}, bf16[64,2048]{1,0:T(8,128)(2,1)S(1)}, u32[]{:S(2)}, u32[]{:S(2)}) collective-permute-start(bf16[64,2048]{1,0:T(8,128)(2,1)S(1)} %slice.8), channel_id=1, source_target_pairs={{0,1},{1,0},{2,3},{3,2},{4,5},{5,4},{6,7},{7,6},{8,9},{9,8},{10,11... | collective-permute-start | bytes 786440 | tf_op jit(solution)/shard_map/ppermute | solution.py:40
  33.5 1.5 %grad_attn.2.refs_4_.early_ref = bf16[384,512]{1,0:T(8,128)(2,1)S(1)} custom-call(s32[4]{0:T(128)S(1)} %pad_add_fusion.meta, bf16[128,2048]{1,0:T(8,128)(2,1)S(1)} %get-tuple-element.63.refs_0_, bf16[128,2048]{1,0:T(8,128)(2,1)S(1)} %collective-permute-done.1.refs_1_, bf16[128,2048]{1,0:T(8,128)(2,1)S(1)} %collective-permute-done.2.refs_2_, ...), custom_call_target="tpu_custom_call" | custom-call | bytes 1024 | tf_op jit(solution)/shard_map/grad_attn/pallas_call | solution.py:55
  35.0 9.0 %collective-permute-done.p1.refs_1_.near = bf16[3,128,512]{2,1,0:T(8,128)(2,1)S(1)} collective-permute-done((bf16[3,128,512]{2,1,0:T(8,128)(2,1)S(1)}, bf16[3,128,512]{2,1,0:T(8,128)(2,1)S(1)}, u32[]{:S(2)}, u32[]{:S(2)}) %collective-permute-start) | collective-permute-done | bytes 393248 | tf_op jit(solution)/shard_map/ppermute | solution.py:40
  44.1 0.1 collective-permute-start.8
  44.2 1.2 %collective-permute-done.4.p3.refs_3_.far3a = bf16[3,128,384]{2,1,0:T(8,128)(2,1)S(1)} collective-permute-done((bf16[3,128,384]{2,1,0:T(8,128)(2,1)S(1)}, bf16[3,128,384]{2,1,0:T(8,128)(2,1)S(1)}, u32[]{:S(2)}, u32[]{:S(2)}) %collective-permute-start.4) | collective-permute-done | bytes 294944 | tf_op jit(solution)/shard_map/ppermute | solution.py:40
  45.3 3.0 %collective-permute-start.6 = (bf16[3,128,128]{2,1,0:T(8,128)(2,1)S(1)}, bf16[3,128,128]{2,1,0:T(8,128)(2,1)S(1)}, u32[]{:S(2)}, u32[]{:S(2)}) collective-permute-start(bf16[3,128,128]{2,1,0:T(8,128)(2,1)S(1)} %get-tuple-element.78), channel_id=1, source_target_pairs={{0,3},{1,2},{2,1},{3,0},{4,7},{5,6},{6,5},{7,4},{8,11},{9,10},{10,... | collective-permute-start | bytes 294920 | tf_op jit(solution)/shard_map/ppermute | solution.py:40
  48.3 7.6 %collective-permute-done.3.p2.refs_2_.far2a = bf16[3,128,384]{2,1,0:T(8,128)(2,1)S(1)} collective-permute-done((bf16[3,128,384]{2,1,0:T(8,128)(2,1)S(1)}, bf16[3,128,384]{2,1,0:T(8,128)(2,1)S(1)}, u32[]{:S(2)}, u32[]{:S(2)}) %collective-permute-start.3) | collective-permute-done | bytes 294944 | tf_op jit(solution)/shard_map/ppermute | solution.py:40
  55.9 0.0 collective-permute-start.5
  55.9 3.3 %attend_forward.1 = (bf16[3,512,512]{2,1,0:T(8,128)(2,1)S(1)}, f32[3,1,512]{2,1,0:T(1,128)S(1)}, f32[384,512]{1,0:T(8,128)S(1)}, bf16[384,512]{1,0:T(8,128)(2,1)S(1)}, f32[512,512]{1,0:T(8,128)S(1)}) custom-call(s32[4]{0:T(128)S(1)} %pad_add_fusion.meta, bf16[3,128,512]{2,1,0:T(8,128)(2,1)S(1)} %get-tuple-element.61.p0.refs_0_.own, ...), custom_call_target="tpu_custom_call" | custom-call | bytes 1024 | tf_op jit(solution)/shard_map/attend_forward/pallas_call | solution.py:55
  59.3 2.3 %backward_early.1 = (bf16[384,384]{1,0:T(8,128)(2,1)S(1)}, f32[512,384]{1,0:T(8,128)S(1)}, f32[512,384]{1,0:T(8,128)S(1)}) custom-call(bf16[3,128,512]{2,1,0:T(8,128)(2,1)S(1)} %get-tuple-element.61.p0.refs_0_.own, bf16[3,128,512]{2,1,0:T(8,128)(2,1)S(1)} %collective-permute-done.p1.refs_1_.near, ...), custom_call_target="tpu_custom_call" | custom-call | bytes 1024 | tf_op jit(solution)/shard_map/backward_early/pallas_call | solution.py:55
  61.6 3.2 %collective-permute-done.6.p3.far3b = bf16[3,128,128]{2,1,0:T(8,128)(2,1)S(1)} collective-permute-done((bf16[3,128,128]{2,1,0:T(8,128)(2,1)S(1)}, bf16[3,128,128]{2,1,0:T(8,128)(2,1)S(1)}, u32[]{:S(2)}, u32[]{:S(2)}) %collective-permute-start.6) | collective-permute-done | bytes 98336 | tf_op jit(solution)/shard_map/ppermute | solution.py:40
  64.8 0.0 collective-permute-done.5.p2.far2b
  64.8 0.0 collective-permute-done.7.refs_3_.refs_0_
  64.8 0.0 collective-permute-done.8.refs_4_.refs_1_
  64.9 2.7 %weight_halves.1 = (bf16[1,512,512]{2,1,0:T(8,128)(2,1)S(1)}, f32[1,1,512]{2,1,0:T(1,128)S(1)}, f32[128,512]{1,0:T(8,128)S(1)}, bf16[256,2048]{1,0:T(8,128)(2,1)S(1)}, f32[256,2048]{1,0:T(8,128)S(1)}) custom-call(s32[4]{0:T(128)S(1)} %pad_add_fusion.meta, bf16[3,128,512]{2,1,0:T(8,128)(2,1)S(1)} %get-tuple-element.61.p0.refs_0_.own, ...), custom_call_target="tpu_custom_call" | custom-call | bytes 1024 | tf_op jit(solution)/shard_map/weight_halves/pallas_call | solution.py:55
  67.6 0.1 collective-permute-start.9
  67.7 1.4 %grad_attn.3.late_ref = bf16[128,512]{1,0:T(8,128)(2,1)S(1)} custom-call(s32[4]{0:T(128)S(1)} %pad_add_fusion.meta, bf16[64,2048]{1,0:T(8,128)(2,1)S(1)} %collective-permute-done.7.refs_3_.refs_0_, bf16[64,2048]{1,0:T(8,128)(2,1)S(1)} %collective-permute-done.8.refs_4_.refs_1_, bf16[512,2048]{1,0:T(8,128)(2,1)S(1)} %copy-done), custom_call_target="tpu_custom_call" | custom-call | bytes 1024 | tf_op jit(solution)/shard_map/grad_attn/pallas_call | solution.py:55
  69.0 1.7 %attend_backward.1 = (bf16[3,128,512]{2,1,0:T(8,128)(2,1)S(1)}, bf16[3,128,512]{2,1,0:T(8,128)(2,1)S(1)}, bf16[3,128,512]{2,1,0:T(8,128)(2,1)S(1)}, bf16[3,128,512]{2,1,0:T(8,128)(2,1)S(1)}) custom-call(bf16[3,128,512]{2,1,0:T(8,128)(2,1)S(1)} %get-tuple-element.61.p0.refs_0_.own, bf16[3,128,512]{2,1,0:T(8,128)(2,1)S(1)} %collective-permute-done.p1.refs_1_.near, ...), custom_call_target="tpu_custom_call" | custom-call | bytes 1024 | tf_op jit(solution)/shard_map/attend_backward/pallas_call | solution.py:55
  70.7 0.0 collective-permute-done.9.recv_ref
  70.7 0.3 add_parts.1
  71.0 1.6 %collective-permute-start.10 = (bf16[64,2048]{1,0:T(8,128)(2,1)S(1)}, bf16[64,2048]{1,0:T(8,128)(2,1)S(1)}, u32[]{:S(2)}, u32[]{:S(2)}) collective-permute-start(bf16[64,2048]{1,0:T(8,128)(2,1)S(1)} %get-tuple-element.101), channel_id=1, source_target_pairs={{0,8},{8,0},{16,24},{24,16},{1,9},{9,1},{17,25},{25,17},{2,10},{10... | collective-permute-start | bytes 786440 | tf_op jit(solution)/shard_map/ppermute | solution.py:40
  72.5 1.5 %collective-permute-start.11 = (bf16[64,2048]{1,0:T(8,128)(2,1)S(1)}, bf16[64,2048]{1,0:T(8,128)(2,1)S(1)}, u32[]{:S(2)}, u32[]{:S(2)}) collective-permute-start(bf16[64,2048]{1,0:T(8,128)(2,1)S(1)} %get-tuple-element.102), channel_id=1, source_target_pairs={{0,16},{8,24},{16,0},{24,8},{1,17},{9,25},{17,1},{25,9},{2,18},{10... | collective-permute-start | bytes 786440 | tf_op jit(solution)/shard_map/ppermute | solution.py:40
  74.0 0.5 collective-permute-start.12
  74.5 1.5 %collective-permute-start.16 = (bf16[3,128,512]{2,1,0:T(8,128)(2,1)S(1)}, bf16[3,128,512]{2,1,0:T(8,128)(2,1)S(1)}, u32[]{:S(2)}, u32[]{:S(2)}) collective-permute-start(bf16[3,128,512]{2,1,0:T(8,128)(2,1)S(1)} %get-tuple-element.104), channel_id=1, source_target_pairs={{0,2},{1,3},{2,0},{3,1},{4,6},{5,7},{6,4},{7,5},{8,10},{9,11},{10,... | collective-permute-start | bytes 1179656 | tf_op jit(solution)/shard_map/ppermute | solution.py:40
  76.0 2.5 %collective-permute-start.17 = (bf16[3,128,512]{2,1,0:T(8,128)(2,1)S(1)}, bf16[3,128,512]{2,1,0:T(8,128)(2,1)S(1)}, u32[]{:S(2)}, u32[]{:S(2)}) collective-permute-start(bf16[3,128,512]{2,1,0:T(8,128)(2,1)S(1)} %get-tuple-element.105), channel_id=1, source_target_pairs={{0,3},{1,2},{2,1},{3,0},{4,7},{5,6},{6,5},{7,4},{8,11},{9,10},{10,... | collective-permute-start | bytes 1179656 | tf_op jit(solution)/shard_map/ppermute | solution.py:40
  78.5 1.7 %collective-permute-done.10.r1 = bf16[64,2048]{1,0:T(8,128)(2,1)S(1)} collective-permute-done((bf16[64,2048]{1,0:T(8,128)(2,1)S(1)}, bf16[64,2048]{1,0:T(8,128)(2,1)S(1)}, u32[]{:S(2)}, u32[]{:S(2)}) %collective-permute-start.10) | collective-permute-done | bytes 262176 | tf_op jit(solution)/shard_map/ppermute | solution.py:40
  80.1 6.4 %collective-permute-done.11.r2 = bf16[64,2048]{1,0:T(8,128)(2,1)S(1)} collective-permute-done((bf16[64,2048]{1,0:T(8,128)(2,1)S(1)}, bf16[64,2048]{1,0:T(8,128)(2,1)S(1)}, u32[]{:S(2)}, u32[]{:S(2)}) %collective-permute-start.11) | collective-permute-done | bytes 262176 | tf_op jit(solution)/shard_map/ppermute | solution.py:40
  86.6 0.0 collective-permute-done.12.r3
  86.6 0.1 scene_mean.1.refs_0_
  86.7 1.3 %collective-permute-start.13 = (bf16[64,2048]{1,0:T(8,128)(2,1)S(1)}, bf16[64,2048]{1,0:T(8,128)(2,1)S(1)}, u32[]{:S(2)}, u32[]{:S(2)}) collective-permute-start(bf16[64,2048]{1,0:T(8,128)(2,1)S(1)} %scene_mean.1.refs_0_), channel_id=1, source_target_pairs={{0,8},{8,0},{16,24},{24,16},{1,9},{9,1},{17,25},{25,17},{2,10},{10... | collective-permute-start | bytes 786440 | tf_op jit(solution)/shard_map/ppermute | solution.py:40
  88.0 1.8 %collective-permute-start.15 = (bf16[64,2048]{1,0:T(8,128)(2,1)S(1)}, bf16[64,2048]{1,0:T(8,128)(2,1)S(1)}, u32[]{:S(2)}, u32[]{:S(2)}) collective-permute-start(bf16[64,2048]{1,0:T(8,128)(2,1)S(1)} %scene_mean.1.refs_0_), channel_id=1, source_target_pairs={{0,24},{8,16},{16,8},{24,0},{1,25},{9,17},{17,9},{25,1},{2,26},{10... | collective-permute-start | bytes 786440 | tf_op jit(solution)/shard_map/ppermute | solution.py:40
  89.8 0.5 collective-permute-start.14
  90.3 5.8 %collective-permute-done.13.refs_1_ = bf16[64,2048]{1,0:T(8,128)(2,1)S(1)} collective-permute-done((bf16[64,2048]{1,0:T(8,128)(2,1)S(1)}, bf16[64,2048]{1,0:T(8,128)(2,1)S(1)}, u32[]{:S(2)}, u32[]{:S(2)}) %collective-permute-start.13) | collective-permute-done | bytes 262176 | tf_op jit(solution)/shard_map/ppermute | solution.py:40
  96.0 1.6 %collective-permute-start.22 = (bf16[3,128,512]{2,1,0:T(8,128)(2,1)S(1)}, bf16[3,128,512]{2,1,0:T(8,128)(2,1)S(1)}, u32[]{:S(2)}, u32[]{:S(2)}) collective-permute-start(bf16[3,128,512]{2,1,0:T(8,128)(2,1)S(1)} %get-tuple-element.111), channel_id=1, source_target_pairs={{0,1},{1,0},{2,3},{3,2},{4,5},{5,4},{6,7},{7,6},{8,9},{9,8},{10,11... | collective-permute-start | bytes 1179656 | tf_op jit(solution)/shard_map/ppermute | solution.py:40
  97.6 3.4 %collective-permute-done.15.refs_3_ = bf16[64,2048]{1,0:T(8,128)(2,1)S(1)} collective-permute-done((bf16[64,2048]{1,0:T(8,128)(2,1)S(1)}, bf16[64,2048]{1,0:T(8,128)(2,1)S(1)}, u32[]{:S(2)}, u32[]{:S(2)}) %collective-permute-start.15) | collective-permute-done | bytes 262176 | tf_op jit(solution)/shard_map/ppermute | solution.py:40
  101.1 1.4 %collective-permute-done.14.refs_2_ = bf16[64,2048]{1,0:T(8,128)(2,1)S(1)} collective-permute-done((bf16[64,2048]{1,0:T(8,128)(2,1)S(1)}, bf16[64,2048]{1,0:T(8,128)(2,1)S(1)}, u32[]{:S(2)}, u32[]{:S(2)}) %collective-permute-start.14) | collective-permute-done | bytes 262176 | tf_op jit(solution)/shard_map/ppermute | solution.py:40
  102.4 1.6 %join_weight.1.refs_8_ = bf16[512,2048]{1,0:T(8,128)(2,1)} custom-call(s32[4]{0:T(128)S(1)} %pad_add_fusion.meta, bf16[64,2048]{1,0:T(8,128)(2,1)S(1)} %scene_mean.1.refs_0_, bf16[64,2048]{1,0:T(8,128)(2,1)S(1)} %collective-permute-done.13.refs_1_, bf16[64,2048]{1,0:T(8,128)(2,1)S(1)} %collective-permute-done.14.refs_2_, ...), custom_call_target="tpu_custom_call" | custom-call | bytes 1024 | tf_op jit(solution)/shard_map/join_weight/pallas_call | solution.py:349
  104.1 0.1 collective-permute-done.16.back2
  104.2 0.0 collective-permute-done.17.back3
  104.2 0.0 collective-permute-start.18
  104.2 0.5 collective-permute-start.19
  104.7 0.1 collective-permute-start.20
  104.7 0.4 collective-permute-start.21
  105.2 1.6 %join_heads.1 = (bf16[128,2048]{1,0:T(8,128)(2,1)}, bf16[128,2048]{1,0:T(8,128)(2,1)}, bf16[128,2048]{1,0:T(8,128)(2,1)}) custom-call(s32[4]{0:T(128)S(1)} %pad_add_fusion.meta, bf16[3,128,512]{2,1,0:T(8,128)(2,1)S(1)} %get-tuple-element.98.own, bf16[3,128,512]{2,1,0:T(8,128)(2,1)S(1)} %collective-permute-done.16.back2, ...), custom_call_target="tpu_custom_call" | custom-call | bytes 1024 | tf_op jit(solution)/shard_map/join_heads/pallas_call | solution.py:349
  106.8 0.0 collective-permute-done.18.refs_0_
  106.8 0.0 collective-permute-done.19.refs_1_
  106.8 0.0 collective-permute-done.20.refs_2_
  106.8 0.0 collective-permute-done.21.refs_3_
  106.9 4.5 %collective-permute-done.22.refs_4_ = bf16[3,128,512]{2,1,0:T(8,128)(2,1)S(1)} collective-permute-done((bf16[3,128,512]{2,1,0:T(8,128)(2,1)S(1)}, bf16[3,128,512]{2,1,0:T(8,128)(2,1)S(1)}, u32[]{:S(2)}, u32[]{:S(2)}) %collective-permute-start.22) | collective-permute-done | bytes 393248 | tf_op jit(solution)/shard_map/ppermute | solution.py:40
  111.4 1.8 %join_last.1 = (bf16[128,2048]{1,0:T(8,128)(2,1)}, bf16[128,2048]{1,0:T(8,128)(2,1)}, bf16[128,2048]{1,0:T(8,128)(2,1)}, bf16[512,2048]{1,0:T(8,128)(2,1)}) custom-call(s32[4]{0:T(128)S(1)} %pad_add_fusion.meta, bf16[64,2048]{1,0:T(8,128)(2,1)S(1)} %collective-permute-done.18.refs_0_, ...), custom_call_target="tpu_custom_call", output_to_operand_aliasing={{0}: (6, {}), {1}: (7, {}), {2}: (8, {}), {3}: (9, {})} | custom-call | bytes 1024 | tf_op jit(solution)/shard_map/join_last/pallas_call | solution.py:349
  (7 shorter events, 0.0 us)
Async XLA Ops:
  0.6 32.9 %copy-start = (bf16[512,2048]{1,0:T(8,128)(2,1)S(1)}, bf16[512,2048]{1,0:T(8,128)(2,1)}, u32[]{:S(2)}) copy-start(bf16[512,2048]{1,0:T(8,128)(2,1)} %refs_2_.1) | copy-start | bytes 6291460
  0.6 27.2 %collective-permute-start.1 = (bf16[128,2048]{1,0:T(8,128)(2,1)}, bf16[128,2048]{1,0:T(8,128)(2,1)S(1)}, u32[]{:S(2)}, u32[]{:S(2)}) collective-permute-start(bf16[128,2048]{1,0:T(8,128)(2,1)} %grad_ref.1), channel_id=1, source_target_pairs={{0,1},{1,0},{2,3},{3,2},{4,5},{5,4},{6,7},{7,6},{8,9},{9,8},{10,11... | collective-permute-start | bytes 1572872 | tf_op jit(solution)/shard_map/ppermute | solution.py:40
  3.7 27.7 %collective-permute-start.2 = (bf16[128,2048]{1,0:T(8,128)(2,1)}, bf16[128,2048]{1,0:T(8,128)(2,1)S(1)}, u32[]{:S(2)}, u32[]{:S(2)}) collective-permute-start(bf16[128,2048]{1,0:T(8,128)(2,1)} %grad_ref.1), channel_id=1, source_target_pairs={{0,2},{1,3},{2,0},{3,1},{4,6},{5,7},{6,4},{7,5},{8,10},{9,11},{10,... | collective-permute-start | bytes 1572872 | tf_op jit(solution)/shard_map/ppermute | solution.py:40
  7.0 1.0 copy-start.1
  8.1 1.0 copy-start.2
  9.1 1.0 copy-start.3
  10.2 1.0 copy-start.4
  12.3 31.8 %collective-permute-start = (bf16[3,128,512]{2,1,0:T(8,128)(2,1)S(1)}, bf16[3,128,512]{2,1,0:T(8,128)(2,1)S(1)}, u32[]{:S(2)}, u32[]{:S(2)}) collective-permute-start(bf16[3,128,512]{2,1,0:T(8,128)(2,1)S(1)} %get-tuple-element.62), channel_id=1, source_target_pairs={{0,1},{1,0},{2,3},{3,2},{4,5},{5,4},{6,7},{7,6},{8,9},{9,8},{10,11... | collective-permute-start | bytes 1179656 | tf_op jit(solution)/shard_map/ppermute | solution.py:40
  27.8 17.5 %collective-permute-start.4 = (bf16[3,128,384]{2,1,0:T(8,128)(2,1)S(1)}, bf16[3,128,384]{2,1,0:T(8,128)(2,1)S(1)}, u32[]{:S(2)}, u32[]{:S(2)}) collective-permute-start(bf16[3,128,384]{2,1,0:T(8,128)(2,1)S(1)} %get-tuple-element.67), channel_id=1, source_target_pairs={{0,3},{1,2},{2,1},{3,0},{4,7},{5,6},{6,5},{7,4},{8,11},{9,10},{10,... | collective-permute-start | bytes 884744 | tf_op jit(solution)/shard_map/ppermute | solution.py:40
  31.4 24.5 %collective-permute-start.3 = (bf16[3,128,384]{2,1,0:T(8,128)(2,1)S(1)}, bf16[3,128,384]{2,1,0:T(8,128)(2,1)S(1)}, u32[]{:S(2)}, u32[]{:S(2)}) collective-permute-start(bf16[3,128,384]{2,1,0:T(8,128)(2,1)S(1)} %get-tuple-element.65), channel_id=1, source_target_pairs={{0,2},{1,3},{2,0},{3,1},{4,6},{5,7},{6,4},{7,5},{8,10},{9,11},{10,... | collective-permute-start | bytes 884744 | tf_op jit(solution)/shard_map/ppermute | solution.py:40
  31.4 33.4 %collective-permute-start.7 = (bf16[64,2048]{1,0:T(8,128)(2,1)S(1)}, bf16[64,2048]{1,0:T(8,128)(2,1)S(1)}, u32[]{:S(2)}, u32[]{:S(2)}) collective-permute-start(bf16[64,2048]{1,0:T(8,128)(2,1)S(1)} %slice.8), channel_id=1, source_target_pairs={{0,1},{1,0},{2,3},{3,2},{4,5},{5,4},{6,7},{7,6},{8,9},{9,8},{10,11... | collective-permute-start | bytes 786440 | tf_op jit(solution)/shard_map/ppermute | solution.py:40
  44.1 20.8 %collective-permute-start.8 = (bf16[64,2048]{1,0:T(8,128)(2,1)S(1)}, bf16[64,2048]{1,0:T(8,128)(2,1)S(1)}, u32[]{:S(2)}, u32[]{:S(2)}) collective-permute-start(bf16[64,2048]{1,0:T(8,128)(2,1)S(1)} %slice.7), channel_id=1, source_target_pairs={{0,1},{1,0},{2,3},{3,2},{4,5},{5,4},{6,7},{7,6},{8,9},{9,8},{10,11... | collective-permute-start | bytes 786440 | tf_op jit(solution)/shard_map/ppermute | solution.py:40
  45.3 19.5 %collective-permute-start.6 = (bf16[3,128,128]{2,1,0:T(8,128)(2,1)S(1)}, bf16[3,128,128]{2,1,0:T(8,128)(2,1)S(1)}, u32[]{:S(2)}, u32[]{:S(2)}) collective-permute-start(bf16[3,128,128]{2,1,0:T(8,128)(2,1)S(1)} %get-tuple-element.78), channel_id=1, source_target_pairs={{0,3},{1,2},{2,1},{3,0},{4,7},{5,6},{6,5},{7,4},{8,11},{9,10},{10,... | collective-permute-start | bytes 294920 | tf_op jit(solution)/shard_map/ppermute | solution.py:40
  55.9 8.9 %collective-permute-start.5 = (bf16[3,128,128]{2,1,0:T(8,128)(2,1)S(1)}, bf16[3,128,128]{2,1,0:T(8,128)(2,1)S(1)}, u32[]{:S(2)}, u32[]{:S(2)}) collective-permute-start(bf16[3,128,128]{2,1,0:T(8,128)(2,1)S(1)} %get-tuple-element.76), channel_id=1, source_target_pairs={{0,2},{1,3},{2,0},{3,1},{4,6},{5,7},{6,4},{7,5},{8,10},{9,11},{10,... | collective-permute-start | bytes 294920 | tf_op jit(solution)/shard_map/ppermute | solution.py:40
  67.6 3.1 %collective-permute-start.9 = (bf16[256,2048]{1,0:T(8,128)(2,1)S(1)}, bf16[256,2048]{1,0:T(8,128)(2,1)S(1)}, u32[]{:S(2)}, u32[]{:S(2)}) collective-permute-start(bf16[256,2048]{1,0:T(8,128)(2,1)S(1)} %get-tuple-element.89), channel_id=1, source_target_pairs={{0,4},{4,0},{1,5},{5,1},{2,6},{6,2},{3,7},{7,3},{8,12},{12,8},{9,1... | collective-permute-start | bytes 3145736 | tf_op jit(solution)/shard_map/ppermute | solution.py:40
  71.0 9.2 %collective-permute-start.10 = (bf16[64,2048]{1,0:T(8,128)(2,1)S(1)}, bf16[64,2048]{1,0:T(8,128)(2,1)S(1)}, u32[]{:S(2)}, u32[]{:S(2)}) collective-permute-start(bf16[64,2048]{1,0:T(8,128)(2,1)S(1)} %get-tuple-element.101), channel_id=1, source_target_pairs={{0,8},{8,0},{16,24},{24,16},{1,9},{9,1},{17,25},{25,17},{2,10},{10... | collective-permute-start | bytes 786440 | tf_op jit(solution)/shard_map/ppermute | solution.py:40
  72.5 14.0 %collective-permute-start.11 = (bf16[64,2048]{1,0:T(8,128)(2,1)S(1)}, bf16[64,2048]{1,0:T(8,128)(2,1)S(1)}, u32[]{:S(2)}, u32[]{:S(2)}) collective-permute-start(bf16[64,2048]{1,0:T(8,128)(2,1)S(1)} %get-tuple-element.102), channel_id=1, source_target_pairs={{0,16},{8,24},{16,0},{24,8},{1,17},{9,25},{17,1},{25,9},{2,18},{10... | collective-permute-start | bytes 786440 | tf_op jit(solution)/shard_map/ppermute | solution.py:40
  74.0 12.5 %collective-permute-start.12 = (bf16[64,2048]{1,0:T(8,128)(2,1)S(1)}, bf16[64,2048]{1,0:T(8,128)(2,1)S(1)}, u32[]{:S(2)}, u32[]{:S(2)}) collective-permute-start(bf16[64,2048]{1,0:T(8,128)(2,1)S(1)} %get-tuple-element.103), channel_id=1, source_target_pairs={{0,24},{8,16},{16,8},{24,0},{1,25},{9,17},{17,9},{25,1},{2,26},{10... | collective-permute-start | bytes 786440 | tf_op jit(solution)/shard_map/ppermute | solution.py:40
  74.5 29.6 %collective-permute-start.16 = (bf16[3,128,512]{2,1,0:T(8,128)(2,1)S(1)}, bf16[3,128,512]{2,1,0:T(8,128)(2,1)S(1)}, u32[]{:S(2)}, u32[]{:S(2)}) collective-permute-start(bf16[3,128,512]{2,1,0:T(8,128)(2,1)S(1)} %get-tuple-element.104), channel_id=1, source_target_pairs={{0,2},{1,3},{2,0},{3,1},{4,6},{5,7},{6,4},{7,5},{8,10},{9,11},{10,... | collective-permute-start | bytes 1179656 | tf_op jit(solution)/shard_map/ppermute | solution.py:40
  76.0 28.2 %collective-permute-start.17 = (bf16[3,128,512]{2,1,0:T(8,128)(2,1)S(1)}, bf16[3,128,512]{2,1,0:T(8,128)(2,1)S(1)}, u32[]{:S(2)}, u32[]{:S(2)}) collective-permute-start(bf16[3,128,512]{2,1,0:T(8,128)(2,1)S(1)} %get-tuple-element.105), channel_id=1, source_target_pairs={{0,3},{1,2},{2,1},{3,0},{4,7},{5,6},{6,5},{7,4},{8,11},{9,10},{10,... | collective-permute-start | bytes 1179656 | tf_op jit(solution)/shard_map/ppermute | solution.py:40
  86.7 9.3 %collective-permute-start.13 = (bf16[64,2048]{1,0:T(8,128)(2,1)S(1)}, bf16[64,2048]{1,0:T(8,128)(2,1)S(1)}, u32[]{:S(2)}, u32[]{:S(2)}) collective-permute-start(bf16[64,2048]{1,0:T(8,128)(2,1)S(1)} %scene_mean.1.refs_0_), channel_id=1, source_target_pairs={{0,8},{8,0},{16,24},{24,16},{1,9},{9,1},{17,25},{25,17},{2,10},{10... | collective-permute-start | bytes 786440 | tf_op jit(solution)/shard_map/ppermute | solution.py:40
  88.0 13.1 %collective-permute-start.15 = (bf16[64,2048]{1,0:T(8,128)(2,1)S(1)}, bf16[64,2048]{1,0:T(8,128)(2,1)S(1)}, u32[]{:S(2)}, u32[]{:S(2)}) collective-permute-start(bf16[64,2048]{1,0:T(8,128)(2,1)S(1)} %scene_mean.1.refs_0_), channel_id=1, source_target_pairs={{0,24},{8,16},{16,8},{24,0},{1,25},{9,17},{17,9},{25,1},{2,26},{10... | collective-permute-start | bytes 786440 | tf_op jit(solution)/shard_map/ppermute | solution.py:40
  89.8 12.7 %collective-permute-start.14 = (bf16[64,2048]{1,0:T(8,128)(2,1)S(1)}, bf16[64,2048]{1,0:T(8,128)(2,1)S(1)}, u32[]{:S(2)}, u32[]{:S(2)}) collective-permute-start(bf16[64,2048]{1,0:T(8,128)(2,1)S(1)} %scene_mean.1.refs_0_), channel_id=1, source_target_pairs={{0,16},{8,24},{16,0},{24,8},{1,17},{9,25},{17,1},{25,9},{2,18},{10... | collective-permute-start | bytes 786440 | tf_op jit(solution)/shard_map/ppermute | solution.py:40
  96.0 15.4 %collective-permute-start.22 = (bf16[3,128,512]{2,1,0:T(8,128)(2,1)S(1)}, bf16[3,128,512]{2,1,0:T(8,128)(2,1)S(1)}, u32[]{:S(2)}, u32[]{:S(2)}) collective-permute-start(bf16[3,128,512]{2,1,0:T(8,128)(2,1)S(1)} %get-tuple-element.111), channel_id=1, source_target_pairs={{0,1},{1,0},{2,3},{3,2},{4,5},{5,4},{6,7},{7,6},{8,9},{9,8},{10,11... | collective-permute-start | bytes 1179656 | tf_op jit(solution)/shard_map/ppermute | solution.py:40
  104.2 2.7 %collective-permute-start.18 = (bf16[64,2048]{1,0:T(8,128)(2,1)S(1)}, bf16[64,2048]{1,0:T(8,128)(2,1)S(1)}, u32[]{:S(2)}, u32[]{:S(2)}) collective-permute-start(bf16[64,2048]{1,0:T(8,128)(2,1)S(1)} %scene_mean.1.refs_0_), channel_id=1, source_target_pairs={{0,4},{4,0},{1,5},{5,1},{2,6},{6,2},{3,7},{7,3},{8,12},{12,8},{9,1... | collective-permute-start | bytes 786440 | tf_op jit(solution)/shard_map/ppermute | solution.py:40
  104.2 2.7 %collective-permute-start.19 = (bf16[64,2048]{1,0:T(8,128)(2,1)S(1)}, bf16[64,2048]{1,0:T(8,128)(2,1)S(1)}, u32[]{:S(2)}, u32[]{:S(2)}) collective-permute-start(bf16[64,2048]{1,0:T(8,128)(2,1)S(1)} %collective-permute-done.13.refs_1_), channel_id=1, source_target_pairs={{0,4},{4,0},{1,5},{5,1},{2,6},{6,2},{3,7},{7,3},{8,12},{12,8},{9,1... | collective-permute-start | bytes 786440 | tf_op jit(solution)/shard_map/ppermute | solution.py:40
  104.7 2.2 %collective-permute-start.20 = (bf16[64,2048]{1,0:T(8,128)(2,1)S(1)}, bf16[64,2048]{1,0:T(8,128)(2,1)S(1)}, u32[]{:S(2)}, u32[]{:S(2)}) collective-permute-start(bf16[64,2048]{1,0:T(8,128)(2,1)S(1)} %collective-permute-done.14.refs_2_), channel_id=1, source_target_pairs={{0,4},{4,0},{1,5},{5,1},{2,6},{6,2},{3,7},{7,3},{8,12},{12,8},{9,1... | collective-permute-start | bytes 786440 | tf_op jit(solution)/shard_map/ppermute | solution.py:40
  104.7 2.1 %collective-permute-start.21 = (bf16[64,2048]{1,0:T(8,128)(2,1)S(1)}, bf16[64,2048]{1,0:T(8,128)(2,1)S(1)}, u32[]{:S(2)}, u32[]{:S(2)}) collective-permute-start(bf16[64,2048]{1,0:T(8,128)(2,1)S(1)} %collective-permute-done.15.refs_3_), channel_id=1, source_target_pairs={{0,4},{4,0},{1,5},{5,1},{2,6},{6,2},{3,7},{7,3},{8,12},{12,8},{9,1... | collective-permute-start | bytes 786440 | tf_op jit(solution)/shard_map/ppermute | solution.py:40

commit v5 on v4

--- a/solution.py
+++ b/solution.py
@@ -206,43 +206,57 @@
     return whole(backward_early_kernel, shapes, (*pieces, grad, *saved), "backward_early", 0, 8)
 
 
-def backward_kernel(own, near, far2a, far3a, far2b, far3b, early_ref, late_ref, *refs):
-    saved, done, backs = (refs[:3], refs[3:6]), refs[6:9], refs[9:]
+def backward_kernel(meta, own, near, far2a, far3a, far2b, far3b, early_ref, corner0, corner1, w_ref, *refs):
+    saved, done, backs, late_ref = (refs[:3], refs[3:6]), refs[6:9], refs[9:13], refs[13]
     rows = own.shape[1]
     early, total = early_ref.shape[0], 4 * rows
-    for n in range(own.shape[2] // HDIM):
+    heads = own.shape[2] // HDIM
+    sums = {}
+
+    def head_span(n, span, grad):
         group, h = divmod(n, EARLY)
         query, key, value = head_of(((own, near, far2a, far3a), (own, near, far2b, far3b))[group], group, h)
         weight_ref, inverse_ref, out_ref = saved[group]
         here = slice(h * HDIM, (h + 1) * HDIM)
         cols = slice(n * HDIM, (n + 1) * HDIM)
-        if group == 0:
-            spans = ((slice(early, total), late_ref[:, cols]),)
-            grad_key, grad_value = done[1][:, here], done[2][:, here]
+        grad_query, add_key, add_value = span_gradients(
+            query[span], key, value, grad, weight_ref[h, :, span], inverse_ref[h, :, span], out_ref[here, span]
+        )
+        for k in range(span.start // rows, span.stop // rows):
+            at = k * rows - span.start
+            backs[k][0, :, cols] = grad_query[at : at + rows]
+        grad_key, grad_value = sums.get(n, (0.0, 0.0))
+        sums[n] = (grad_key + add_key, grad_value + add_value)
+
+    for n in range(EARLY, heads):
+        head_span(n, slice(0, 2 * rows), early_ref[: 2 * rows, n * HDIM : (n + 1) * HDIM])
+    corner = jnp.concatenate([corner0[...], corner1[...]], axis=0)
+    live = token_pos((rows, 1), 0, meta[Z], early) < meta[COUNT]
+    tile = 2 * HDIM
+    for i in range(w_ref.shape[0] // tile):
+        part = slice(i * tile, (i + 1) * tile)
+        late_ref[:, part] = jnp.where(live, dot(corner, w_ref[part, :], 1, 1), 0.0).astype(bf16)
+    for n in range(heads):
+        cols = slice(n * HDIM, (n + 1) * HDIM)
+        if n < EARLY:
+            sums[n] = (done[1][:, cols], done[2][:, cols])
             for k in range(early // rows):
-                backs[k][0, :, cols] = done[0][k * rows : (k + 1) * rows, here]
+                backs[k][0, :, cols] = done[0][k * rows : (k + 1) * rows, cols]
+            head_span(n, slice(early, total), late_ref[:, cols])
         else:
-            grad = jnp.concatenate([early_ref[:, cols], late_ref[:, cols]], axis=0)
-            spans = [(slice(t, t + 2 * rows), grad[t : t + 2 * rows]) for t in (0, 2 * rows)]
-            grad_key = grad_value = 0.0
-        for span, grad in spans:
-            grad_query, add_key, add_value = span_gradients(
-                query[span], key, value, grad, weight_ref[h, :, span], inverse_ref[h, :, span], out_ref[here, span]
-            )
-            for k in range(span.start // rows, span.stop // rows):
-                at = k * rows - span.start
-                backs[k][0, :, cols] = grad_query[at : at + rows]
-            grad_key += add_key
-            grad_value += add_value
+            grad = jnp.concatenate([early_ref[2 * rows :, cols], late_ref[:, cols]], axis=0)
+            head_span(n, slice(2 * rows, total), grad)
         for k in range(4):
             mine = slice(k * rows, (k + 1) * rows)
-            backs[k][1, :, cols] = grad_key[mine].astype(bf16)
-            backs[k][2, :, cols] = grad_value[mine].astype(bf16)
-
-
-def backward(pieces, grads, saved, done):
+            backs[k][1, :, cols] = sums[n][0][mine].astype(bf16)
+            backs[k][2, :, cols] = sums[n][1][mine].astype(bf16)
+
+
+def backward(meta, pieces, grad, corners, weight, saved, done):
     shapes = [sds(pieces[0].shape, bf16)] * 4
-    return whole(backward_kernel, shapes, (*pieces, *grads, *saved, *done), "attend_backward", 0, 8)
+    operands = (meta, *pieces, grad, *corners, weight, *saved, *done)
+    scratch = [pltpu.VMEM((pieces[0].shape[1], weight.shape[0]), bf16)]
+    return whole(backward_kernel, shapes, operands, "attend_backward", 1, 10, scratch)
 
 
 LINE = HDIM // 8
@@ -417,9 +431,9 @@
 
     *saved_b, out, keep = weight_halves(meta, (own, piece1, piece2b, piece3b), bias, heads_a, grads)
     recv = swap(out, "core", 2, 1)
-    grad_late = grad_attn(meta, after(grads[3:], out), out_weight, 3 * BLOCK)
+    corners = after(grads[3:], out)
     pieces = (own, piece1, piece2a, piece3a, piece2b, piece3b)
-    own0, *backs = backward(pieces, (grad_early, grad_late), (*saved_a, *saved_b), early)
+    own0, *backs = backward(meta, pieces, grad_early, corners, out_weight, (*saved_a, *saved_b), early)
     own_part, *sends = add_parts(after(keep, own0), recv)
     recvs = [swap(x, "chips", 4, j + 1) for j, x in enumerate(sends)]
     back3, back2 = send(backs[2], 3), send(backs[1], 2)

time: 114 us -> 114 us (level)
    pallas_call x8 -> x7, Pallas kernels: 13.3 us -> 13 us  [whole(): pl.pallas_call(kernel, out_shape=out_shape, in_specs=[pl.BlockSpec(memory...]
where the time goes in v5:
time: 114 us; the launch traced here: 113 us
  waiting for transfers between devices  59.3 us (52%)
  starting transfers between devices  28.7 us (25%)
  Pallas kernels  19.1 us (17%)
  local copies, waits for them, and re-layouts  4.21 us (4%)
  between operations  1.45 us (1%)
    ppermute x23, waiting for transfers between devices, swap(): return lax.ppermute(x, axis, [(i, i ^ flip) for i in range(size)])  59.3 us
    ppermute x23, starting transfers between devices, swap(): return lax.ppermute(x, axis, [(i, i ^ flip) for i in range(size)])  28.7 us
    pallas_call x7, Pallas kernels, whole(): pl.pallas_call(kernel, out_shape=out_shape, in_specs=[pl.BlockSpec(memory...  13 us
    pallas_call x3, Pallas kernels, join(): pl.pallas_call(kernel, out_shape=shapes, in_specs=[pl.BlockSpec(memory_sp...  5.04 us
    unnamed x10, local copies, waits for them, and re-layouts  4.17 us
  transfers between devices with their start and end apart: 23, of which 12 were waited for; matrix products, arithmetic and copies ran while one was open for 0% of the time, Pallas kernels for 13%

profile of v5, /device:TPU:0, one launch (start us, length us, event | category | flops | bytes accessed | tf_op | source)
XLA Modules:
  0.0 112.9 jit_solution(10522128378636106262)
XLA Ops:
  0.6 0.0 copy-start
  0.6 3.1 %collective-permute-start.1 = (bf16[128,2048]{1,0:T(8,128)(2,1)}, bf16[128,2048]{1,0:T(8,128)(2,1)S(1)}, u32[]{:S(2)}, u32[]{:S(2)}) collective-permute-start(bf16[128,2048]{1,0:T(8,128)(2,1)} %grad_ref.1), channel_id=1, source_target_pairs={{0,1},{1,0},{2,3},{3,2},{4,5},{5,4},{6,7},{7,6},{8,9},{9,8},{10,11... | collective-permute-start | bytes 1572872 | tf_op jit(solution)/shard_map/ppermute | solution.py:40
  3.7 2.6 %collective-permute-start.2 = (bf16[128,2048]{1,0:T(8,128)(2,1)}, bf16[128,2048]{1,0:T(8,128)(2,1)S(1)}, u32[]{:S(2)}, u32[]{:S(2)}) collective-permute-start(bf16[128,2048]{1,0:T(8,128)(2,1)} %grad_ref.1), channel_id=1, source_target_pairs={{0,2},{1,3},{2,0},{3,1},{4,6},{5,7},{6,4},{7,5},{8,10},{9,11},{10,... | collective-permute-start | bytes 1572872 | tf_op jit(solution)/shard_map/ppermute | solution.py:40
  7.0 0.1 pad_add_fusion.meta
  7.1 1.0 copy-done.1
  8.1 1.0 copy-done.2
  9.1 1.0 copy-done.3
  10.2 1.0 copy-done.4
  11.2 1.1 pack_heads.1
  12.3 0.5 collective-permute-start
  12.8 15.0 %collective-permute-done.1.refs_1_ = bf16[128,2048]{1,0:T(8,128)(2,1)S(1)} collective-permute-done((bf16[128,2048]{1,0:T(8,128)(2,1)}, bf16[128,2048]{1,0:T(8,128)(2,1)S(1)}, u32[]{:S(2)}, u32[]{:S(2)}) %collective-permute-start.1) | collective-permute-done | bytes 524320 | tf_op jit(solution)/shard_map/ppermute | solution.py:40
  27.8 3.6 %collective-permute-start.4 = (bf16[3,128,384]{2,1,0:T(8,128)(2,1)S(1)}, bf16[3,128,384]{2,1,0:T(8,128)(2,1)S(1)}, u32[]{:S(2)}, u32[]{:S(2)}) collective-permute-start(bf16[3,128,384]{2,1,0:T(8,128)(2,1)S(1)} %get-tuple-element.67), channel_id=1, source_target_pairs={{0,3},{1,2},{2,1},{3,0},{4,7},{5,6},{6,5},{7,4},{8,11},{9,10},{10,... | collective-permute-start | bytes 884744 | tf_op jit(solution)/shard_map/ppermute | solution.py:40
  31.4 0.0 collective-permute-done.2.refs_2_
  31.4 0.0 collective-permute-start.3
  31.4 2.1 %collective-permute-start.7 = (bf16[64,2048]{1,0:T(8,128)(2,1)S(1)}, bf16[64,2048]{1,0:T(8,128)(2,1)S(1)}, u32[]{:S(2)}, u32[]{:S(2)}) collective-permute-start(bf16[64,2048]{1,0:T(8,128)(2,1)S(1)} %slice.8), channel_id=1, source_target_pairs={{0,1},{1,0},{2,3},{3,2},{4,5},{5,4},{6,7},{7,6},{8,9},{9,8},{10,11... | collective-permute-start | bytes 786440 | tf_op jit(solution)/shard_map/ppermute | solution.py:40
  33.5 0.0 copy-done
  33.5 1.5 %grad_attn.1.refs_4_.early_ref = bf16[384,512]{1,0:T(8,128)(2,1)S(1)} custom-call(s32[4]{0:T(128)S(1)} %pad_add_fusion.meta, bf16[128,2048]{1,0:T(8,128)(2,1)S(1)} %get-tuple-element.63.refs_0_, bf16[128,2048]{1,0:T(8,128)(2,1)S(1)} %collective-permute-done.1.refs_1_, bf16[128,2048]{1,0:T(8,128)(2,1)S(1)} %collective-permute-done.2.refs_2_, ...), custom_call_target="tpu_custom_call" | custom-call | bytes 1024 | tf_op jit(solution)/shard_map/grad_attn/pallas_call | solution.py:55
  35.0 9.0 %collective-permute-done.p1.refs_1_.near = bf16[3,128,512]{2,1,0:T(8,128)(2,1)S(1)} collective-permute-done((bf16[3,128,512]{2,1,0:T(8,128)(2,1)S(1)}, bf16[3,128,512]{2,1,0:T(8,128)(2,1)S(1)}, u32[]{:S(2)}, u32[]{:S(2)}) %collective-permute-start) | collective-permute-done | bytes 393248 | tf_op jit(solution)/shard_map/ppermute | solution.py:40
  44.1 0.1 collective-permute-start.8
  44.2 1.2 %collective-permute-done.4.p3.refs_3_.far3a = bf16[3,128,384]{2,1,0:T(8,128)(2,1)S(1)} collective-permute-done((bf16[3,128,384]{2,1,0:T(8,128)(2,1)S(1)}, bf16[3,128,384]{2,1,0:T(8,128)(2,1)S(1)}, u32[]{:S(2)}, u32[]{:S(2)}) %collective-permute-start.4) | collective-permute-done | bytes 294944 | tf_op jit(solution)/shard_map/ppermute | solution.py:40
  45.3 3.0 %collective-permute-start.6 = (bf16[3,128,128]{2,1,0:T(8,128)(2,1)S(1)}, bf16[3,128,128]{2,1,0:T(8,128)(2,1)S(1)}, u32[]{:S(2)}, u32[]{:S(2)}) collective-permute-start(bf16[3,128,128]{2,1,0:T(8,128)(2,1)S(1)} %get-tuple-element.78), channel_id=1, source_target_pairs={{0,3},{1,2},{2,1},{3,0},{4,7},{5,6},{6,5},{7,4},{8,11},{9,10},{10,... | collective-permute-start | bytes 294920 | tf_op jit(solution)/shard_map/ppermute | solution.py:40
  48.3 7.6 %collective-permute-done.3.p2.refs_2_.far2a = bf16[3,128,384]{2,1,0:T(8,128)(2,1)S(1)} collective-permute-done((bf16[3,128,384]{2,1,0:T(8,128)(2,1)S(1)}, bf16[3,128,384]{2,1,0:T(8,128)(2,1)S(1)}, u32[]{:S(2)}, u32[]{:S(2)}) %collective-permute-start.3) | collective-permute-done | bytes 294944 | tf_op jit(solution)/shard_map/ppermute | solution.py:40
  55.9 0.0 collective-permute-start.5
  55.9 3.3 %attend_forward.1 = (bf16[3,512,512]{2,1,0:T(8,128)(2,1)S(1)}, f32[3,1,512]{2,1,0:T(1,128)S(1)}, f32[384,512]{1,0:T(8,128)S(1)}, bf16[384,512]{1,0:T(8,128)(2,1)S(1)}, f32[512,512]{1,0:T(8,128)S(1)}) custom-call(s32[4]{0:T(128)S(1)} %pad_add_fusion.meta, bf16[3,128,512]{2,1,0:T(8,128)(2,1)S(1)} %get-tuple-element.61.p0.refs_0_.own, ...), custom_call_target="tpu_custom_call" | custom-call | bytes 1024 | tf_op jit(solution)/shard_map/attend_forward/pallas_call | solution.py:55
  59.3 2.3 %backward_early.1 = (bf16[384,384]{1,0:T(8,128)(2,1)S(1)}, f32[512,384]{1,0:T(8,128)S(1)}, f32[512,384]{1,0:T(8,128)S(1)}) custom-call(bf16[3,128,512]{2,1,0:T(8,128)(2,1)S(1)} %get-tuple-element.61.p0.refs_0_.own, bf16[3,128,512]{2,1,0:T(8,128)(2,1)S(1)} %collective-permute-done.p1.refs_1_.near, ...), custom_call_target="tpu_custom_call" | custom-call | bytes 1024 | tf_op jit(solution)/shard_map/backward_early/pallas_call | solution.py:55
  61.6 3.3 %collective-permute-done.6.p3.far3b = bf16[3,128,128]{2,1,0:T(8,128)(2,1)S(1)} collective-permute-done((bf16[3,128,128]{2,1,0:T(8,128)(2,1)S(1)}, bf16[3,128,128]{2,1,0:T(8,128)(2,1)S(1)}, u32[]{:S(2)}, u32[]{:S(2)}) %collective-permute-start.6) | collective-permute-done | bytes 98336 | tf_op jit(solution)/shard_map/ppermute | solution.py:40
  64.8 0.0 collective-permute-done.5.p2.far2b
  64.8 0.0 collective-permute-done.7.refs_3_.corner0
  64.8 0.0 collective-permute-done.8.refs_4_.corner1
  64.9 2.7 %weight_halves.1 = (bf16[1,512,512]{2,1,0:T(8,128)(2,1)S(1)}, f32[1,1,512]{2,1,0:T(1,128)S(1)}, f32[128,512]{1,0:T(8,128)S(1)}, bf16[256,2048]{1,0:T(8,128)(2,1)S(1)}, f32[256,2048]{1,0:T(8,128)S(1)}) custom-call(s32[4]{0:T(128)S(1)} %pad_add_fusion.meta, bf16[3,128,512]{2,1,0:T(8,128)(2,1)S(1)} %get-tuple-element.61.p0.refs_0_.own, ...), custom_call_target="tpu_custom_call" | custom-call | bytes 1024 | tf_op jit(solution)/shard_map/weight_halves/pallas_call | solution.py:55
  67.5 0.1 collective-permute-start.9
  67.6 2.9 %attend_backward.1 = (bf16[3,128,512]{2,1,0:T(8,128)(2,1)S(1)}, bf16[3,128,512]{2,1,0:T(8,128)(2,1)S(1)}, bf16[3,128,512]{2,1,0:T(8,128)(2,1)S(1)}, bf16[3,128,512]{2,1,0:T(8,128)(2,1)S(1)}) custom-call(s32[4]{0:T(128)S(1)} %pad_add_fusion.meta, bf16[3,128,512]{2,1,0:T(8,128)(2,1)S(1)} %get-tuple-element.61.p0.refs_0_.own, ...), custom_call_target="tpu_custom_call" | custom-call | bytes 1024 | tf_op jit(solution)/shard_map/attend_backward/pallas_call | solution.py:55
  70.5 0.0 collective-permute-done.9.recv_ref
  70.5 0.2 add_parts.1
  70.7 1.6 %collective-permute-start.10 = (bf16[64,2048]{1,0:T(8,128)(2,1)S(1)}, bf16[64,2048]{1,0:T(8,128)(2,1)S(1)}, u32[]{:S(2)}, u32[]{:S(2)}) collective-permute-start(bf16[64,2048]{1,0:T(8,128)(2,1)S(1)} %get-tuple-element.101), channel_id=1, source_target_pairs={{0,8},{8,0},{16,24},{24,16},{1,9},{9,1},{17,25},{25,17},{2,10},{10... | collective-permute-start | bytes 786440 | tf_op jit(solution)/shard_map/ppermute | solution.py:40
  72.2 1.5 %collective-permute-start.11 = (bf16[64,2048]{1,0:T(8,128)(2,1)S(1)}, bf16[64,2048]{1,0:T(8,128)(2,1)S(1)}, u32[]{:S(2)}, u32[]{:S(2)}) collective-permute-start(bf16[64,2048]{1,0:T(8,128)(2,1)S(1)} %get-tuple-element.102), channel_id=1, source_target_pairs={{0,16},{8,24},{16,0},{24,8},{1,17},{9,25},{17,1},{25,9},{2,18},{10... | collective-permute-start | bytes 786440 | tf_op jit(solution)/shard_map/ppermute | solution.py:40
  73.8 0.5 collective-permute-start.12
  74.2 1.5 %collective-permute-start.16 = (bf16[3,128,512]{2,1,0:T(8,128)(2,1)S(1)}, bf16[3,128,512]{2,1,0:T(8,128)(2,1)S(1)}, u32[]{:S(2)}, u32[]{:S(2)}) collective-permute-start(bf16[3,128,512]{2,1,0:T(8,128)(2,1)S(1)} %get-tuple-element.104), channel_id=1, source_target_pairs={{0,2},{1,3},{2,0},{3,1},{4,6},{5,7},{6,4},{7,5},{8,10},{9,11},{10,... | collective-permute-start | bytes 1179656 | tf_op jit(solution)/shard_map/ppermute | solution.py:40
  75.7 2.5 %collective-permute-start.17 = (bf16[3,128,512]{2,1,0:T(8,128)(2,1)S(1)}, bf16[3,128,512]{2,1,0:T(8,128)(2,1)S(1)}, u32[]{:S(2)}, u32[]{:S(2)}) collective-permute-start(bf16[3,128,512]{2,1,0:T(8,128)(2,1)S(1)} %get-tuple-element.105), channel_id=1, source_target_pairs={{0,3},{1,2},{2,1},{3,0},{4,7},{5,6},{6,5},{7,4},{8,11},{9,10},{10,... | collective-permute-start | bytes 1179656 | tf_op jit(solution)/shard_map/ppermute | solution.py:40
  78.2 1.7 %collective-permute-done.10.r1 = bf16[64,2048]{1,0:T(8,128)(2,1)S(1)} collective-permute-done((bf16[64,2048]{1,0:T(8,128)(2,1)S(1)}, bf16[64,2048]{1,0:T(8,128)(2,1)S(1)}, u32[]{:S(2)}, u32[]{:S(2)}) %collective-permute-start.10) | collective-permute-done | bytes 262176 | tf_op jit(solution)/shard_map/ppermute | solution.py:40
  79.8 6.4 %collective-permute-done.11.r2 = bf16[64,2048]{1,0:T(8,128)(2,1)S(1)} collective-permute-done((bf16[64,2048]{1,0:T(8,128)(2,1)S(1)}, bf16[64,2048]{1,0:T(8,128)(2,1)S(1)}, u32[]{:S(2)}, u32[]{:S(2)}) %collective-permute-start.11) | collective-permute-done | bytes 262176 | tf_op jit(solution)/shard_map/ppermute | solution.py:40
  86.3 0.0 collective-permute-done.12.r3
  86.3 0.1 scene_mean.1.refs_0_
  86.4 1.3 %collective-permute-start.13 = (bf16[64,2048]{1,0:T(8,128)(2,1)S(1)}, bf16[64,2048]{1,0:T(8,128)(2,1)S(1)}, u32[]{:S(2)}, u32[]{:S(2)}) collective-permute-start(bf16[64,2048]{1,0:T(8,128)(2,1)S(1)} %scene_mean.1.refs_0_), channel_id=1, source_target_pairs={{0,8},{8,0},{16,24},{24,16},{1,9},{9,1},{17,25},{25,17},{2,10},{10... | collective-permute-start | bytes 786440 | tf_op jit(solution)/shard_map/ppermute | solution.py:40
  87.7 1.8 %collective-permute-start.15 = (bf16[64,2048]{1,0:T(8,128)(2,1)S(1)}, bf16[64,2048]{1,0:T(8,128)(2,1)S(1)}, u32[]{:S(2)}, u32[]{:S(2)}) collective-permute-start(bf16[64,2048]{1,0:T(8,128)(2,1)S(1)} %scene_mean.1.refs_0_), channel_id=1, source_target_pairs={{0,24},{8,16},{16,8},{24,0},{1,25},{9,17},{17,9},{25,1},{2,26},{10... | collective-permute-start | bytes 786440 | tf_op jit(solution)/shard_map/ppermute | solution.py:40
  89.5 0.5 collective-permute-start.14
  90.0 5.8 %collective-permute-done.13.refs_1_ = bf16[64,2048]{1,0:T(8,128)(2,1)S(1)} collective-permute-done((bf16[64,2048]{1,0:T(8,128)(2,1)S(1)}, bf16[64,2048]{1,0:T(8,128)(2,1)S(1)}, u32[]{:S(2)}, u32[]{:S(2)}) %collective-permute-start.13) | collective-permute-done | bytes 262176 | tf_op jit(solution)/shard_map/ppermute | solution.py:40
  95.7 1.6 %collective-permute-start.22 = (bf16[3,128,512]{2,1,0:T(8,128)(2,1)S(1)}, bf16[3,128,512]{2,1,0:T(8,128)(2,1)S(1)}, u32[]{:S(2)}, u32[]{:S(2)}) collective-permute-start(bf16[3,128,512]{2,1,0:T(8,128)(2,1)S(1)} %get-tuple-element.111), channel_id=1, source_target_pairs={{0,1},{1,0},{2,3},{3,2},{4,5},{5,4},{6,7},{7,6},{8,9},{9,8},{10,11... | collective-permute-start | bytes 1179656 | tf_op jit(solution)/shard_map/ppermute | solution.py:40
  97.3 3.4 %collective-permute-done.15.refs_3_ = bf16[64,2048]{1,0:T(8,128)(2,1)S(1)} collective-permute-done((bf16[64,2048]{1,0:T(8,128)(2,1)S(1)}, bf16[64,2048]{1,0:T(8,128)(2,1)S(1)}, u32[]{:S(2)}, u32[]{:S(2)}) %collective-permute-start.15) | collective-permute-done | bytes 262176 | tf_op jit(solution)/shard_map/ppermute | solution.py:40
  100.8 1.4 %collective-permute-done.14.refs_2_ = bf16[64,2048]{1,0:T(8,128)(2,1)S(1)} collective-permute-done((bf16[64,2048]{1,0:T(8,128)(2,1)S(1)}, bf16[64,2048]{1,0:T(8,128)(2,1)S(1)}, u32[]{:S(2)}, u32[]{:S(2)}) %collective-permute-start.14) | collective-permute-done | bytes 262176 | tf_op jit(solution)/shard_map/ppermute | solution.py:40
  102.1 1.6 %join_weight.1.refs_8_ = bf16[512,2048]{1,0:T(8,128)(2,1)} custom-call(s32[4]{0:T(128)S(1)} %pad_add_fusion.meta, bf16[64,2048]{1,0:T(8,128)(2,1)S(1)} %scene_mean.1.refs_0_, bf16[64,2048]{1,0:T(8,128)(2,1)S(1)} %collective-permute-done.13.refs_1_, bf16[64,2048]{1,0:T(8,128)(2,1)S(1)} %collective-permute-done.14.refs_2_, ...), custom_call_target="tpu_custom_call" | custom-call | bytes 1024 | tf_op jit(solution)/shard_map/join_weight/pallas_call | solution.py:363
  103.8 0.1 collective-permute-done.16.back2
  103.9 0.0 collective-permute-done.17.back3
  103.9 0.0 collective-permute-start.18
  103.9 0.5 collective-permute-start.19
  104.4 0.1 collective-permute-start.20
  104.4 0.5 collective-permute-start.21
  104.9 1.6 %join_heads.1 = (bf16[128,2048]{1,0:T(8,128)(2,1)}, bf16[128,2048]{1,0:T(8,128)(2,1)}, bf16[128,2048]{1,0:T(8,128)(2,1)}) custom-call(s32[4]{0:T(128)S(1)} %pad_add_fusion.meta, bf16[3,128,512]{2,1,0:T(8,128)(2,1)S(1)} %get-tuple-element.98.own, bf16[3,128,512]{2,1,0:T(8,128)(2,1)S(1)} %collective-permute-done.16.back2, ...), custom_call_target="tpu_custom_call" | custom-call | bytes 1024 | tf_op jit(solution)/shard_map/join_heads/pallas_call | solution.py:363
  106.5 0.0 collective-permute-done.18.refs_0_
  106.5 0.0 collective-permute-done.19.refs_1_
  106.5 0.0 collective-permute-done.20.refs_2_
  106.5 0.0 collective-permute-done.21.refs_3_
  106.6 4.5 %collective-permute-done.22.refs_4_ = bf16[3,128,512]{2,1,0:T(8,128)(2,1)S(1)} collective-permute-done((bf16[3,128,512]{2,1,0:T(8,128)(2,1)S(1)}, bf16[3,128,512]{2,1,0:T(8,128)(2,1)S(1)}, u32[]{:S(2)}, u32[]{:S(2)}) %collective-permute-start.22) | collective-permute-done | bytes 393248 | tf_op jit(solution)/shard_map/ppermute | solution.py:40
  111.1 1.8 %join_last.1 = (bf16[128,2048]{1,0:T(8,128)(2,1)}, bf16[128,2048]{1,0:T(8,128)(2,1)}, bf16[128,2048]{1,0:T(8,128)(2,1)}, bf16[512,2048]{1,0:T(8,128)(2,1)}) custom-call(s32[4]{0:T(128)S(1)} %pad_add_fusion.meta, bf16[64,2048]{1,0:T(8,128)(2,1)S(1)} %collective-permute-done.18.refs_0_, ...), custom_call_target="tpu_custom_call", output_to_operand_aliasing={{0}: (6, {}), {1}: (7, {}), {2}: (8, {}), {3}: (9, {})} | custom-call | bytes 1024 | tf_op jit(solution)/shard_map/join_last/pallas_call | solution.py:363
  (6 shorter events, 0.0 us)
Async XLA Ops:
  0.6 32.9 %copy-start = (bf16[512,2048]{1,0:T(8,128)(2,1)S(1)}, bf16[512,2048]{1,0:T(8,128)(2,1)}, u32[]{:S(2)}) copy-start(bf16[512,2048]{1,0:T(8,128)(2,1)} %w_ref.1) | copy-start | bytes 6291460
  0.6 27.2 %collective-permute-start.1 = (bf16[128,2048]{1,0:T(8,128)(2,1)}, bf16[128,2048]{1,0:T(8,128)(2,1)S(1)}, u32[]{:S(2)}, u32[]{:S(2)}) collective-permute-start(bf16[128,2048]{1,0:T(8,128)(2,1)} %grad_ref.1), channel_id=1, source_target_pairs={{0,1},{1,0},{2,3},{3,2},{4,5},{5,4},{6,7},{7,6},{8,9},{9,8},{10,11... | collective-permute-start | bytes 1572872 | tf_op jit(solution)/shard_map/ppermute | solution.py:40
  3.7 27.7 %collective-permute-start.2 = (bf16[128,2048]{1,0:T(8,128)(2,1)}, bf16[128,2048]{1,0:T(8,128)(2,1)S(1)}, u32[]{:S(2)}, u32[]{:S(2)}) collective-permute-start(bf16[128,2048]{1,0:T(8,128)(2,1)} %grad_ref.1), channel_id=1, source_target_pairs={{0,2},{1,3},{2,0},{3,1},{4,6},{5,7},{6,4},{7,5},{8,10},{9,11},{10,... | collective-permute-start | bytes 1572872 | tf_op jit(solution)/shard_map/ppermute | solution.py:40
  7.0 1.0 copy-start.1
  8.1 1.0 copy-start.2
  9.1 1.0 copy-start.3
  10.2 1.0 copy-start.4
  12.3 31.8 %collective-permute-start = (bf16[3,128,512]{2,1,0:T(8,128)(2,1)S(1)}, bf16[3,128,512]{2,1,0:T(8,128)(2,1)S(1)}, u32[]{:S(2)}, u32[]{:S(2)}) collective-permute-start(bf16[3,128,512]{2,1,0:T(8,128)(2,1)S(1)} %get-tuple-element.62), channel_id=1, source_target_pairs={{0,1},{1,0},{2,3},{3,2},{4,5},{5,4},{6,7},{7,6},{8,9},{9,8},{10,11... | collective-permute-start | bytes 1179656 | tf_op jit(solution)/shard_map/ppermute | solution.py:40
  27.8 17.5 %collective-permute-start.4 = (bf16[3,128,384]{2,1,0:T(8,128)(2,1)S(1)}, bf16[3,128,384]{2,1,0:T(8,128)(2,1)S(1)}, u32[]{:S(2)}, u32[]{:S(2)}) collective-permute-start(bf16[3,128,384]{2,1,0:T(8,128)(2,1)S(1)} %get-tuple-element.67), channel_id=1, source_target_pairs={{0,3},{1,2},{2,1},{3,0},{4,7},{5,6},{6,5},{7,4},{8,11},{9,10},{10,... | collective-permute-start | bytes 884744 | tf_op jit(solution)/shard_map/ppermute | solution.py:40
  31.4 24.5 %collective-permute-start.3 = (bf16[3,128,384]{2,1,0:T(8,128)(2,1)S(1)}, bf16[3,128,384]{2,1,0:T(8,128)(2,1)S(1)}, u32[]{:S(2)}, u32[]{:S(2)}) collective-permute-start(bf16[3,128,384]{2,1,0:T(8,128)(2,1)S(1)} %get-tuple-element.65), channel_id=1, source_target_pairs={{0,2},{1,3},{2,0},{3,1},{4,6},{5,7},{6,4},{7,5},{8,10},{9,11},{10,... | collective-permute-start | bytes 884744 | tf_op jit(solution)/shard_map/ppermute | solution.py:40
  31.4 33.4 %collective-permute-start.7 = (bf16[64,2048]{1,0:T(8,128)(2,1)S(1)}, bf16[64,2048]{1,0:T(8,128)(2,1)S(1)}, u32[]{:S(2)}, u32[]{:S(2)}) collective-permute-start(bf16[64,2048]{1,0:T(8,128)(2,1)S(1)} %slice.8), channel_id=1, source_target_pairs={{0,1},{1,0},{2,3},{3,2},{4,5},{5,4},{6,7},{7,6},{8,9},{9,8},{10,11... | collective-permute-start | bytes 786440 | tf_op jit(solution)/shard_map/ppermute | solution.py:40
  44.1 20.8 %collective-permute-start.8 = (bf16[64,2048]{1,0:T(8,128)(2,1)S(1)}, bf16[64,2048]{1,0:T(8,128)(2,1)S(1)}, u32[]{:S(2)}, u32[]{:S(2)}) collective-permute-start(bf16[64,2048]{1,0:T(8,128)(2,1)S(1)} %slice.7), channel_id=1, source_target_pairs={{0,1},{1,0},{2,3},{3,2},{4,5},{5,4},{6,7},{7,6},{8,9},{9,8},{10,11... | collective-permute-start | bytes 786440 | tf_op jit(solution)/shard_map/ppermute | solution.py:40
  45.3 19.5 %collective-permute-start.6 = (bf16[3,128,128]{2,1,0:T(8,128)(2,1)S(1)}, bf16[3,128,128]{2,1,0:T(8,128)(2,1)S(1)}, u32[]{:S(2)}, u32[]{:S(2)}) collective-permute-start(bf16[3,128,128]{2,1,0:T(8,128)(2,1)S(1)} %get-tuple-element.78), channel_id=1, source_target_pairs={{0,3},{1,2},{2,1},{3,0},{4,7},{5,6},{6,5},{7,4},{8,11},{9,10},{10,... | collective-permute-start | bytes 294920 | tf_op jit(solution)/shard_map/ppermute | solution.py:40
  55.9 8.9 %collective-permute-start.5 = (bf16[3,128,128]{2,1,0:T(8,128)(2,1)S(1)}, bf16[3,128,128]{2,1,0:T(8,128)(2,1)S(1)}, u32[]{:S(2)}, u32[]{:S(2)}) collective-permute-start(bf16[3,128,128]{2,1,0:T(8,128)(2,1)S(1)} %get-tuple-element.76), channel_id=1, source_target_pairs={{0,2},{1,3},{2,0},{3,1},{4,6},{5,7},{6,4},{7,5},{8,10},{9,11},{10,... | collective-permute-start | bytes 294920 | tf_op jit(solution)/shard_map/ppermute | solution.py:40
  67.5 2.9 %collective-permute-start.9 = (bf16[256,2048]{1,0:T(8,128)(2,1)S(1)}, bf16[256,2048]{1,0:T(8,128)(2,1)S(1)}, u32[]{:S(2)}, u32[]{:S(2)}) collective-permute-start(bf16[256,2048]{1,0:T(8,128)(2,1)S(1)} %get-tuple-element.89), channel_id=1, source_target_pairs={{0,4},{4,0},{1,5},{5,1},{2,6},{6,2},{3,7},{7,3},{8,12},{12,8},{9,1... | collective-permute-start | bytes 3145736 | tf_op jit(solution)/shard_map/ppermute | solution.py:40
  70.7 9.2 %collective-permute-start.10 = (bf16[64,2048]{1,0:T(8,128)(2,1)S(1)}, bf16[64,2048]{1,0:T(8,128)(2,1)S(1)}, u32[]{:S(2)}, u32[]{:S(2)}) collective-permute-start(bf16[64,2048]{1,0:T(8,128)(2,1)S(1)} %get-tuple-element.101), channel_id=1, source_target_pairs={{0,8},{8,0},{16,24},{24,16},{1,9},{9,1},{17,25},{25,17},{2,10},{10... | collective-permute-start | bytes 786440 | tf_op jit(solution)/shard_map/ppermute | solution.py:40
  72.2 14.0 %collective-permute-start.11 = (bf16[64,2048]{1,0:T(8,128)(2,1)S(1)}, bf16[64,2048]{1,0:T(8,128)(2,1)S(1)}, u32[]{:S(2)}, u32[]{:S(2)}) collective-permute-start(bf16[64,2048]{1,0:T(8,128)(2,1)S(1)} %get-tuple-element.102), channel_id=1, source_target_pairs={{0,16},{8,24},{16,0},{24,8},{1,17},{9,25},{17,1},{25,9},{2,18},{10... | collective-permute-start | bytes 786440 | tf_op jit(solution)/shard_map/ppermute | solution.py:40
  73.8 12.5 %collective-permute-start.12 = (bf16[64,2048]{1,0:T(8,128)(2,1)S(1)}, bf16[64,2048]{1,0:T(8,128)(2,1)S(1)}, u32[]{:S(2)}, u32[]{:S(2)}) collective-permute-start(bf16[64,2048]{1,0:T(8,128)(2,1)S(1)} %get-tuple-element.103), channel_id=1, source_target_pairs={{0,24},{8,16},{16,8},{24,0},{1,25},{9,17},{17,9},{25,1},{2,26},{10... | collective-permute-start | bytes 786440 | tf_op jit(solution)/shard_map/ppermute | solution.py:40
  74.2 29.6 %collective-permute-start.16 = (bf16[3,128,512]{2,1,0:T(8,128)(2,1)S(1)}, bf16[3,128,512]{2,1,0:T(8,128)(2,1)S(1)}, u32[]{:S(2)}, u32[]{:S(2)}) collective-permute-start(bf16[3,128,512]{2,1,0:T(8,128)(2,1)S(1)} %get-tuple-element.104), channel_id=1, source_target_pairs={{0,2},{1,3},{2,0},{3,1},{4,6},{5,7},{6,4},{7,5},{8,10},{9,11},{10,... | collective-permute-start | bytes 1179656 | tf_op jit(solution)/shard_map/ppermute | solution.py:40
  75.7 28.2 %collective-permute-start.17 = (bf16[3,128,512]{2,1,0:T(8,128)(2,1)S(1)}, bf16[3,128,512]{2,1,0:T(8,128)(2,1)S(1)}, u32[]{:S(2)}, u32[]{:S(2)}) collective-permute-start(bf16[3,128,512]{2,1,0:T(8,128)(2,1)S(1)} %get-tuple-element.105), channel_id=1, source_target_pairs={{0,3},{1,2},{2,1},{3,0},{4,7},{5,6},{6,5},{7,4},{8,11},{9,10},{10,... | collective-permute-start | bytes 1179656 | tf_op jit(solution)/shard_map/ppermute | solution.py:40
  86.4 9.3 %collective-permute-start.13 = (bf16[64,2048]{1,0:T(8,128)(2,1)S(1)}, bf16[64,2048]{1,0:T(8,128)(2,1)S(1)}, u32[]{:S(2)}, u32[]{:S(2)}) collective-permute-start(bf16[64,2048]{1,0:T(8,128)(2,1)S(1)} %scene_mean.1.refs_0_), channel_id=1, source_target_pairs={{0,8},{8,0},{16,24},{24,16},{1,9},{9,1},{17,25},{25,17},{2,10},{10... | collective-permute-start | bytes 786440 | tf_op jit(solution)/shard_map/ppermute | solution.py:40
  87.7 13.0 %collective-permute-start.15 = (bf16[64,2048]{1,0:T(8,128)(2,1)S(1)}, bf16[64,2048]{1,0:T(8,128)(2,1)S(1)}, u32[]{:S(2)}, u32[]{:S(2)}) collective-permute-start(bf16[64,2048]{1,0:T(8,128)(2,1)S(1)} %scene_mean.1.refs_0_), channel_id=1, source_target_pairs={{0,24},{8,16},{16,8},{24,0},{1,25},{9,17},{17,9},{25,1},{2,26},{10... | collective-permute-start | bytes 786440 | tf_op jit(solution)/shard_map/ppermute | solution.py:40
  89.5 12.6 %collective-permute-start.14 = (bf16[64,2048]{1,0:T(8,128)(2,1)S(1)}, bf16[64,2048]{1,0:T(8,128)(2,1)S(1)}, u32[]{:S(2)}, u32[]{:S(2)}) collective-permute-start(bf16[64,2048]{1,0:T(8,128)(2,1)S(1)} %scene_mean.1.refs_0_), channel_id=1, source_target_pairs={{0,16},{8,24},{16,0},{24,8},{1,17},{9,25},{17,1},{25,9},{2,18},{10... | collective-permute-start | bytes 786440 | tf_op jit(solution)/shard_map/ppermute | solution.py:40
  95.7 15.4 %collective-permute-start.22 = (bf16[3,128,512]{2,1,0:T(8,128)(2,1)S(1)}, bf16[3,128,512]{2,1,0:T(8,128)(2,1)S(1)}, u32[]{:S(2)}, u32[]{:S(2)}) collective-permute-start(bf16[3,128,512]{2,1,0:T(8,128)(2,1)S(1)} %get-tuple-element.111), channel_id=1, source_target_pairs={{0,1},{1,0},{2,3},{3,2},{4,5},{5,4},{6,7},{7,6},{8,9},{9,8},{10,11... | collective-permute-start | bytes 1179656 | tf_op jit(solution)/shard_map/ppermute | solution.py:40
  103.9 2.7 %collective-permute-start.18 = (bf16[64,2048]{1,0:T(8,128)(2,1)S(1)}, bf16[64,2048]{1,0:T(8,128)(2,1)S(1)}, u32[]{:S(2)}, u32[]{:S(2)}) collective-permute-start(bf16[64,2048]{1,0:T(8,128)(2,1)S(1)} %scene_mean.1.refs_0_), channel_id=1, source_target_pairs={{0,4},{4,0},{1,5},{5,1},{2,6},{6,2},{3,7},{7,3},{8,12},{12,8},{9,1... | collective-permute-start | bytes 786440 | tf_op jit(solution)/shard_map/ppermute | solution.py:40
  103.9 2.7 %collective-permute-start.19 = (bf16[64,2048]{1,0:T(8,128)(2,1)S(1)}, bf16[64,2048]{1,0:T(8,128)(2,1)S(1)}, u32[]{:S(2)}, u32[]{:S(2)}) collective-permute-start(bf16[64,2048]{1,0:T(8,128)(2,1)S(1)} %collective-permute-done.13.refs_1_), channel_id=1, source_target_pairs={{0,4},{4,0},{1,5},{5,1},{2,6},{6,2},{3,7},{7,3},{8,12},{12,8},{9,1... | collective-permute-start | bytes 786440 | tf_op jit(solution)/shard_map/ppermute | solution.py:40
  104.4 2.2 %collective-permute-start.20 = (bf16[64,2048]{1,0:T(8,128)(2,1)S(1)}, bf16[64,2048]{1,0:T(8,128)(2,1)S(1)}, u32[]{:S(2)}, u32[]{:S(2)}) collective-permute-start(bf16[64,2048]{1,0:T(8,128)(2,1)S(1)} %collective-permute-done.14.refs_2_), channel_id=1, source_target_pairs={{0,4},{4,0},{1,5},{5,1},{2,6},{6,2},{3,7},{7,3},{8,12},{12,8},{9,1... | collective-permute-start | bytes 786440 | tf_op jit(solution)/shard_map/ppermute | solution.py:40
  104.4 2.1 %collective-permute-start.21 = (bf16[64,2048]{1,0:T(8,128)(2,1)S(1)}, bf16[64,2048]{1,0:T(8,128)(2,1)S(1)}, u32[]{:S(2)}, u32[]{:S(2)}) collective-permute-start(bf16[64,2048]{1,0:T(8,128)(2,1)S(1)} %collective-permute-done.15.refs_3_), channel_id=1, source_target_pairs={{0,4},{4,0},{1,5},{5,1},{2,6},{6,2},{3,7},{7,3},{8,12},{12,8},{9,1... | collective-permute-start | bytes 786440 | tf_op jit(solution)/shard_map/ppermute | solution.py:40

commit v6 on v5

--- a/solution.py
+++ b/solution.py
@@ -65,10 +65,10 @@
     )(*operands)
 
 
-def pack_kernel(meta, q_ref, k_ref, v_ref, grad_ref, mine_ref, *refs):
+def pack_kernel(meta, q_ref, k_ref, v_ref, *refs):
     *outs, sems = refs
     width = outs[0].shape[2]
-    copies = [pltpu.make_async_copy(grad_ref, mine_ref, sems.at[3 * len(outs)])]
+    copies = []
     for n, out_ref in enumerate(outs):
         k, first = (n, 0) if n < 2 else (n // 2 + 1, n % 2 * EARLY * HDIM)
         start = pl.multiple_of((meta[Z] ^ k) * width + first, 128)
@@ -78,21 +78,28 @@
     run_all(copies)
 
 
-def pack(meta, queries, keys_in, values, grad):
+def pack(meta, queries, keys_in, values):
     rows, width = queries.shape
     part, early = width // 4, EARLY * HDIM
     shapes = [sds((3, rows, n), bf16) for n in (part, part, early, part - early, early, part - early)]
-    shapes = [sds(grad.shape, bf16)] + shapes
     return pl.pallas_call(
         pack_kernel,
         out_shape=shapes,
-        in_specs=[pl.BlockSpec(memory_space=pltpu.SMEM)] + [pl.BlockSpec(memory_space=pl.ANY)] * 4,
+        in_specs=[pl.BlockSpec(memory_space=pltpu.SMEM)] + [pl.BlockSpec(memory_space=pl.ANY)] * 3,
         out_specs=[pl.BlockSpec(memory_space=pltpu.VMEM)] * len(shapes),
         scratch_shapes=[pltpu.SemaphoreType.DMA((3 * len(shapes),))],
         compiler_params=params(),
         cost_estimate=NO_COST,
         name="pack_heads",
-    )(meta, queries, keys_in, values, grad)
+    )(meta, queries, keys_in, values)
+
+
+def hold_kernel(in_ref, out_ref):
+    out_ref[...] = in_ref[...]
+
+
+def hold(x):
+    return whole(hold_kernel, sds(x.shape, x.dtype), (x,), "hold")
 
 
 def token_pos(shape, dim, z, start=0):
@@ -413,13 +420,14 @@
 
     across = send(out_grad, 2)
     beside = send(out_grad, 1)
-    mine, own, near1, far2a, far2b, far3a, far3b = pack(meta, queries, keys_in, values, out_grad)
+    own, near1, far2a, far2b, far3a, far3b = pack(meta, queries, keys_in, values)
     piece1 = send(near1, 1)
     piece3a = send(far3a, 3, beside)
     piece2a = send(far2a, 2, across)
     piece3b = send(far3b, 3, piece3a)
     piece2b = send(far2b, 2, piece2a)
     half = across.shape[0] // 2
+    mine = hold(after(out_grad, across))
     grad_early = grad_attn(meta, (mine, beside, across), out_weight, 0)
     corners = [send(across[:half], 1), send(after(across, piece1, grad_early)[half:], 1)]
 

time: 114 us -> 114 us (level)
    pallas_call x7 -> x8, Pallas kernels: 13 us -> 13.1 us  [whole(): pl.pallas_call(kernel, out_shape=out_shape, in_specs=[pl.BlockSpec(memory...]
where the time goes in v6:
time: 114 us; the launch traced here: 113 us
  waiting for transfers between devices  59.4 us (52%)
  starting transfers between devices  28.7 us (25%)
  Pallas kernels  19.2 us (17%)
  local copies, waits for them, and re-layouts  4.21 us (4%)
  between operations  1.45 us (1%)
    ppermute x23, waiting for transfers between devices, swap(): return lax.ppermute(x, axis, [(i, i ^ flip) for i in range(size)])  59.4 us
    ppermute x23, starting transfers between devices, swap(): return lax.ppermute(x, axis, [(i, i ^ flip) for i in range(size)])  28.7 us
    pallas_call x8, Pallas kernels, whole(): pl.pallas_call(kernel, out_shape=out_shape, in_specs=[pl.BlockSpec(memory...  13.1 us
    pallas_call x3, Pallas kernels, join(): pl.pallas_call(kernel, out_shape=shapes, in_specs=[pl.BlockSpec(memory_sp...  5.04 us
    unnamed x10, local copies, waits for them, and re-layouts  4.17 us
  transfers between devices with their start and end apart: 23, of which 12 were waited for; matrix products, arithmetic and copies ran while one was open for 0% of the time, Pallas kernels for 13%

profile of v6, /device:TPU:0, one launch (start us, length us, event | category | flops | bytes accessed | tf_op | source)
XLA Modules:
  0.0 112.9 jit_solution(11418897385336051741)
XLA Ops:
  0.6 0.0 copy-start
  0.6 3.1 %collective-permute-start.2 = (bf16[128,2048]{1,0:T(8,128)(2,1)}, bf16[128,2048]{1,0:T(8,128)(2,1)S(1)}, u32[]{:S(2)}, u32[]{:S(2)}) collective-permute-start(bf16[128,2048]{1,0:T(8,128)(2,1)} %in_ref), channel_id=1, source_target_pairs={{0,1},{1,0},{2,3},{3,2},{4,5},{5,4},{6,7},{7,6},{8,9},{9,8},{10,11... | collective-permute-start | bytes 1572872 | tf_op jit(solution)/shard_map/ppermute | solution.py:40
  3.7 2.6 %collective-permute-start.1 = (bf16[128,2048]{1,0:T(8,128)(2,1)}, bf16[128,2048]{1,0:T(8,128)(2,1)S(1)}, u32[]{:S(2)}, u32[]{:S(2)}) collective-permute-start(bf16[128,2048]{1,0:T(8,128)(2,1)} %in_ref), channel_id=1, source_target_pairs={{0,2},{1,3},{2,0},{3,1},{4,6},{5,7},{6,4},{7,5},{8,10},{9,11},{10,... | collective-permute-start | bytes 1572872 | tf_op jit(solution)/shard_map/ppermute | solution.py:40
  7.0 0.1 pad_add_fusion.meta
  7.1 1.0 copy-done.1
  8.1 1.0 copy-done.2
  9.1 1.0 copy-done.3
  10.2 1.0 pack_heads.1
  11.2 0.5 collective-permute-start
  11.7 16.1 %collective-permute-done.2.refs_1_ = bf16[128,2048]{1,0:T(8,128)(2,1)S(1)} collective-permute-done((bf16[128,2048]{1,0:T(8,128)(2,1)}, bf16[128,2048]{1,0:T(8,128)(2,1)S(1)}, u32[]{:S(2)}, u32[]{:S(2)}) %collective-permute-start.2) | collective-permute-done | bytes 524320 | tf_op jit(solution)/shard_map/ppermute | solution.py:40
  27.8 3.6 %collective-permute-start.4 = (bf16[3,128,384]{2,1,0:T(8,128)(2,1)S(1)}, bf16[3,128,384]{2,1,0:T(8,128)(2,1)S(1)}, u32[]{:S(2)}, u32[]{:S(2)}) collective-permute-start(bf16[3,128,384]{2,1,0:T(8,128)(2,1)S(1)} %get-tuple-element.67), channel_id=1, source_target_pairs={{0,3},{1,2},{2,1},{3,0},{4,7},{5,6},{6,5},{7,4},{8,11},{9,10},{10,... | collective-permute-start | bytes 884744 | tf_op jit(solution)/shard_map/ppermute | solution.py:40
  31.4 0.0 collective-permute-done.1.refs_2_
  31.4 0.0 collective-permute-start.3
  31.4 2.1 %collective-permute-start.7 = (bf16[64,2048]{1,0:T(8,128)(2,1)S(1)}, bf16[64,2048]{1,0:T(8,128)(2,1)S(1)}, u32[]{:S(2)}, u32[]{:S(2)}) collective-permute-start(bf16[64,2048]{1,0:T(8,128)(2,1)S(1)} %slice.8), channel_id=1, source_target_pairs={{0,1},{1,0},{2,3},{3,2},{4,5},{5,4},{6,7},{7,6},{8,9},{9,8},{10,11... | collective-permute-start | bytes 786440 | tf_op jit(solution)/shard_map/ppermute | solution.py:40
  33.5 1.0 copy-done.4
  34.6 0.0 copy-done
  34.6 1.5 %grad_attn.1.refs_4_.early_ref = bf16[384,512]{1,0:T(8,128)(2,1)S(1)} custom-call(s32[4]{0:T(128)S(1)} %pad_add_fusion.meta, bf16[128,2048]{1,0:T(8,128)(2,1)S(1)} %hold.1.refs_0_, bf16[128,2048]{1,0:T(8,128)(2,1)S(1)} %collective-permute-done.2.refs_1_, bf16[128,2048]{1,0:T(8,128)(2,1)S(1)} %collective-permute-done.1.refs_2_, bf16[512,2048]{1,0:T(8,128)(2,1)S(1)} %copy-done), custom_call_target="tpu_custom_call" | custom-call | bytes 1024 | tf_op jit(solution)/shard_map/grad_attn/pallas_call | solution.py:55
  36.1 7.9 %collective-permute-done.p1.refs_1_.near = bf16[3,128,512]{2,1,0:T(8,128)(2,1)S(1)} collective-permute-done((bf16[3,128,512]{2,1,0:T(8,128)(2,1)S(1)}, bf16[3,128,512]{2,1,0:T(8,128)(2,1)S(1)}, u32[]{:S(2)}, u32[]{:S(2)}) %collective-permute-start) | collective-permute-done | bytes 393248 | tf_op jit(solution)/shard_map/ppermute | solution.py:40
  44.1 0.1 collective-permute-start.8
  44.2 1.2 %collective-permute-done.4.p3.refs_3_.far3a = bf16[3,128,384]{2,1,0:T(8,128)(2,1)S(1)} collective-permute-done((bf16[3,128,384]{2,1,0:T(8,128)(2,1)S(1)}, bf16[3,128,384]{2,1,0:T(8,128)(2,1)S(1)}, u32[]{:S(2)}, u32[]{:S(2)}) %collective-permute-start.4) | collective-permute-done | bytes 294944 | tf_op jit(solution)/shard_map/ppermute | solution.py:40
  45.3 3.0 %collective-permute-start.6 = (bf16[3,128,128]{2,1,0:T(8,128)(2,1)S(1)}, bf16[3,128,128]{2,1,0:T(8,128)(2,1)S(1)}, u32[]{:S(2)}, u32[]{:S(2)}) collective-permute-start(bf16[3,128,128]{2,1,0:T(8,128)(2,1)S(1)} %get-tuple-element.78), channel_id=1, source_target_pairs={{0,3},{1,2},{2,1},{3,0},{4,7},{5,6},{6,5},{7,4},{8,11},{9,10},{10,... | collective-permute-start | bytes 294920 | tf_op jit(solution)/shard_map/ppermute | solution.py:40
  48.3 7.6 %collective-permute-done.3.p2.refs_2_.far2a = bf16[3,128,384]{2,1,0:T(8,128)(2,1)S(1)} collective-permute-done((bf16[3,128,384]{2,1,0:T(8,128)(2,1)S(1)}, bf16[3,128,384]{2,1,0:T(8,128)(2,1)S(1)}, u32[]{:S(2)}, u32[]{:S(2)}) %collective-permute-start.3) | collective-permute-done | bytes 294944 | tf_op jit(solution)/shard_map/ppermute | solution.py:40
  55.9 0.0 collective-permute-start.5
  55.9 3.3 %attend_forward.1 = (bf16[3,512,512]{2,1,0:T(8,128)(2,1)S(1)}, f32[3,1,512]{2,1,0:T(1,128)S(1)}, f32[384,512]{1,0:T(8,128)S(1)}, bf16[384,512]{1,0:T(8,128)(2,1)S(1)}, f32[512,512]{1,0:T(8,128)S(1)}) custom-call(s32[4]{0:T(128)S(1)} %pad_add_fusion.meta, bf16[3,128,512]{2,1,0:T(8,128)(2,1)S(1)} %get-tuple-element.61.p0.refs_0_.own, ...), custom_call_target="tpu_custom_call" | custom-call | bytes 1024 | tf_op jit(solution)/shard_map/attend_forward/pallas_call | solution.py:55
  59.3 2.3 %backward_early.1 = (bf16[384,384]{1,0:T(8,128)(2,1)S(1)}, f32[512,384]{1,0:T(8,128)S(1)}, f32[512,384]{1,0:T(8,128)S(1)}) custom-call(bf16[3,128,512]{2,1,0:T(8,128)(2,1)S(1)} %get-tuple-element.61.p0.refs_0_.own, bf16[3,128,512]{2,1,0:T(8,128)(2,1)S(1)} %collective-permute-done.p1.refs_1_.near, ...), custom_call_target="tpu_custom_call" | custom-call | bytes 1024 | tf_op jit(solution)/shard_map/backward_early/pallas_call | solution.py:55
  61.6 3.3 %collective-permute-done.6.p3.far3b = bf16[3,128,128]{2,1,0:T(8,128)(2,1)S(1)} collective-permute-done((bf16[3,128,128]{2,1,0:T(8,128)(2,1)S(1)}, bf16[3,128,128]{2,1,0:T(8,128)(2,1)S(1)}, u32[]{:S(2)}, u32[]{:S(2)}) %collective-permute-start.6) | collective-permute-done | bytes 98336 | tf_op jit(solution)/shard_map/ppermute | solution.py:40
  64.8 0.0 collective-permute-done.5.p2.far2b
  64.8 0.0 collective-permute-done.7.refs_3_.corner0
  64.8 0.0 collective-permute-done.8.refs_4_.corner1
  64.9 2.7 %weight_halves.1 = (bf16[1,512,512]{2,1,0:T(8,128)(2,1)S(1)}, f32[1,1,512]{2,1,0:T(1,128)S(1)}, f32[128,512]{1,0:T(8,128)S(1)}, bf16[256,2048]{1,0:T(8,128)(2,1)S(1)}, f32[256,2048]{1,0:T(8,128)S(1)}) custom-call(s32[4]{0:T(128)S(1)} %pad_add_fusion.meta, bf16[3,128,512]{2,1,0:T(8,128)(2,1)S(1)} %get-tuple-element.61.p0.refs_0_.own, ...), custom_call_target="tpu_custom_call" | custom-call | bytes 1024 | tf_op jit(solution)/shard_map/weight_halves/pallas_call | solution.py:55
  67.5 0.1 collective-permute-start.9
  67.6 2.8 %attend_backward.1 = (bf16[3,128,512]{2,1,0:T(8,128)(2,1)S(1)}, bf16[3,128,512]{2,1,0:T(8,128)(2,1)S(1)}, bf16[3,128,512]{2,1,0:T(8,128)(2,1)S(1)}, bf16[3,128,512]{2,1,0:T(8,128)(2,1)S(1)}) custom-call(s32[4]{0:T(128)S(1)} %pad_add_fusion.meta, bf16[3,128,512]{2,1,0:T(8,128)(2,1)S(1)} %get-tuple-element.61.p0.refs_0_.own, ...), custom_call_target="tpu_custom_call" | custom-call | bytes 1024 | tf_op jit(solution)/shard_map/attend_backward/pallas_call | solution.py:55
  70.5 0.0 collective-permute-done.9.recv_ref
  70.5 0.3 add_parts.1
  70.7 1.6 %collective-permute-start.10 = (bf16[64,2048]{1,0:T(8,128)(2,1)S(1)}, bf16[64,2048]{1,0:T(8,128)(2,1)S(1)}, u32[]{:S(2)}, u32[]{:S(2)}) collective-permute-start(bf16[64,2048]{1,0:T(8,128)(2,1)S(1)} %get-tuple-element.101), channel_id=1, source_target_pairs={{0,8},{8,0},{16,24},{24,16},{1,9},{9,1},{17,25},{25,17},{2,10},{10... | collective-permute-start | bytes 786440 | tf_op jit(solution)/shard_map/ppermute | solution.py:40
  72.3 1.5 %collective-permute-start.11 = (bf16[64,2048]{1,0:T(8,128)(2,1)S(1)}, bf16[64,2048]{1,0:T(8,128)(2,1)S(1)}, u32[]{:S(2)}, u32[]{:S(2)}) collective-permute-start(bf16[64,2048]{1,0:T(8,128)(2,1)S(1)} %get-tuple-element.102), channel_id=1, source_target_pairs={{0,16},{8,24},{16,0},{24,8},{1,17},{9,25},{17,1},{25,9},{2,18},{10... | collective-permute-start | bytes 786440 | tf_op jit(solution)/shard_map/ppermute | solution.py:40
  73.8 0.5 collective-permute-start.12
  74.3 1.5 %collective-permute-start.16 = (bf16[3,128,512]{2,1,0:T(8,128)(2,1)S(1)}, bf16[3,128,512]{2,1,0:T(8,128)(2,1)S(1)}, u32[]{:S(2)}, u32[]{:S(2)}) collective-permute-start(bf16[3,128,512]{2,1,0:T(8,128)(2,1)S(1)} %get-tuple-element.104), channel_id=1, source_target_pairs={{0,2},{1,3},{2,0},{3,1},{4,6},{5,7},{6,4},{7,5},{8,10},{9,11},{10,... | collective-permute-start | bytes 1179656 | tf_op jit(solution)/shard_map/ppermute | solution.py:40
  75.8 2.5 %collective-permute-start.17 = (bf16[3,128,512]{2,1,0:T(8,128)(2,1)S(1)}, bf16[3,128,512]{2,1,0:T(8,128)(2,1)S(1)}, u32[]{:S(2)}, u32[]{:S(2)}) collective-permute-start(bf16[3,128,512]{2,1,0:T(8,128)(2,1)S(1)} %get-tuple-element.105), channel_id=1, source_target_pairs={{0,3},{1,2},{2,1},{3,0},{4,7},{5,6},{6,5},{7,4},{8,11},{9,10},{10,... | collective-permute-start | bytes 1179656 | tf_op jit(solution)/shard_map/ppermute | solution.py:40
  78.3 1.7 %collective-permute-done.10.r1 = bf16[64,2048]{1,0:T(8,128)(2,1)S(1)} collective-permute-done((bf16[64,2048]{1,0:T(8,128)(2,1)S(1)}, bf16[64,2048]{1,0:T(8,128)(2,1)S(1)}, u32[]{:S(2)}, u32[]{:S(2)}) %collective-permute-start.10) | collective-permute-done | bytes 262176 | tf_op jit(solution)/shard_map/ppermute | solution.py:40
  79.9 6.4 %collective-permute-done.11.r2 = bf16[64,2048]{1,0:T(8,128)(2,1)S(1)} collective-permute-done((bf16[64,2048]{1,0:T(8,128)(2,1)S(1)}, bf16[64,2048]{1,0:T(8,128)(2,1)S(1)}, u32[]{:S(2)}, u32[]{:S(2)}) %collective-permute-start.11) | collective-permute-done | bytes 262176 | tf_op jit(solution)/shard_map/ppermute | solution.py:40
  86.3 0.0 collective-permute-done.12.r3
  86.3 0.1 scene_mean.1.refs_0_
  86.5 1.3 %collective-permute-start.13 = (bf16[64,2048]{1,0:T(8,128)(2,1)S(1)}, bf16[64,2048]{1,0:T(8,128)(2,1)S(1)}, u32[]{:S(2)}, u32[]{:S(2)}) collective-permute-start(bf16[64,2048]{1,0:T(8,128)(2,1)S(1)} %scene_mean.1.refs_0_), channel_id=1, source_target_pairs={{0,8},{8,0},{16,24},{24,16},{1,9},{9,1},{17,25},{25,17},{2,10},{10... | collective-permute-start | bytes 786440 | tf_op jit(solution)/shard_map/ppermute | solution.py:40
  87.8 1.8 %collective-permute-start.15 = (bf16[64,2048]{1,0:T(8,128)(2,1)S(1)}, bf16[64,2048]{1,0:T(8,128)(2,1)S(1)}, u32[]{:S(2)}, u32[]{:S(2)}) collective-permute-start(bf16[64,2048]{1,0:T(8,128)(2,1)S(1)} %scene_mean.1.refs_0_), channel_id=1, source_target_pairs={{0,24},{8,16},{16,8},{24,0},{1,25},{9,17},{17,9},{25,1},{2,26},{10... | collective-permute-start | bytes 786440 | tf_op jit(solution)/shard_map/ppermute | solution.py:40
  89.5 0.5 collective-permute-start.14
  90.0 5.8 %collective-permute-done.13.refs_1_ = bf16[64,2048]{1,0:T(8,128)(2,1)S(1)} collective-permute-done((bf16[64,2048]{1,0:T(8,128)(2,1)S(1)}, bf16[64,2048]{1,0:T(8,128)(2,1)S(1)}, u32[]{:S(2)}, u32[]{:S(2)}) %collective-permute-start.13) | collective-permute-done | bytes 262176 | tf_op jit(solution)/shard_map/ppermute | solution.py:40
  95.8 1.6 %collective-permute-start.22 = (bf16[3,128,512]{2,1,0:T(8,128)(2,1)S(1)}, bf16[3,128,512]{2,1,0:T(8,128)(2,1)S(1)}, u32[]{:S(2)}, u32[]{:S(2)}) collective-permute-start(bf16[3,128,512]{2,1,0:T(8,128)(2,1)S(1)} %get-tuple-element.111), channel_id=1, source_target_pairs={{0,1},{1,0},{2,3},{3,2},{4,5},{5,4},{6,7},{7,6},{8,9},{9,8},{10,11... | collective-permute-start | bytes 1179656 | tf_op jit(solution)/shard_map/ppermute | solution.py:40
  97.4 3.4 %collective-permute-done.15.refs_3_ = bf16[64,2048]{1,0:T(8,128)(2,1)S(1)} collective-permute-done((bf16[64,2048]{1,0:T(8,128)(2,1)S(1)}, bf16[64,2048]{1,0:T(8,128)(2,1)S(1)}, u32[]{:S(2)}, u32[]{:S(2)}) %collective-permute-start.15) | collective-permute-done | bytes 262176 | tf_op jit(solution)/shard_map/ppermute | solution.py:40
  100.8 1.4 %collective-permute-done.14.refs_2_ = bf16[64,2048]{1,0:T(8,128)(2,1)S(1)} collective-permute-done((bf16[64,2048]{1,0:T(8,128)(2,1)S(1)}, bf16[64,2048]{1,0:T(8,128)(2,1)S(1)}, u32[]{:S(2)}, u32[]{:S(2)}) %collective-permute-start.14) | collective-permute-done | bytes 262176 | tf_op jit(solution)/shard_map/ppermute | solution.py:40
  102.2 1.6 %join_weight.1.refs_8_ = bf16[512,2048]{1,0:T(8,128)(2,1)} custom-call(s32[4]{0:T(128)S(1)} %pad_add_fusion.meta, bf16[64,2048]{1,0:T(8,128)(2,1)S(1)} %scene_mean.1.refs_0_, bf16[64,2048]{1,0:T(8,128)(2,1)S(1)} %collective-permute-done.13.refs_1_, bf16[64,2048]{1,0:T(8,128)(2,1)S(1)} %collective-permute-done.14.refs_2_, ...), custom_call_target="tpu_custom_call" | custom-call | bytes 1024 | tf_op jit(solution)/shard_map/join_weight/pallas_call | solution.py:370
  103.8 0.1 collective-permute-done.16.back2
  103.9 0.0 collective-permute-done.17.back3
  103.9 0.0 collective-permute-start.18
  103.9 0.5 collective-permute-start.19
  104.4 0.0 collective-permute-start.20
  104.5 0.5 collective-permute-start.21
  105.0 1.6 %join_heads.1 = (bf16[128,2048]{1,0:T(8,128)(2,1)}, bf16[128,2048]{1,0:T(8,128)(2,1)}, bf16[128,2048]{1,0:T(8,128)(2,1)}) custom-call(s32[4]{0:T(128)S(1)} %pad_add_fusion.meta, bf16[3,128,512]{2,1,0:T(8,128)(2,1)S(1)} %get-tuple-element.98.own, bf16[3,128,512]{2,1,0:T(8,128)(2,1)S(1)} %collective-permute-done.16.back2, ...), custom_call_target="tpu_custom_call" | custom-call | bytes 1024 | tf_op jit(solution)/shard_map/join_heads/pallas_call | solution.py:370
  106.6 0.0 collective-permute-done.18.refs_0_
  106.6 0.0 collective-permute-done.19.refs_1_
  106.6 0.0 collective-permute-done.20.refs_2_
  106.6 0.0 collective-permute-done.21.refs_3_
  106.6 4.5 %collective-permute-done.22.refs_4_ = bf16[3,128,512]{2,1,0:T(8,128)(2,1)S(1)} collective-permute-done((bf16[3,128,512]{2,1,0:T(8,128)(2,1)S(1)}, bf16[3,128,512]{2,1,0:T(8,128)(2,1)S(1)}, u32[]{:S(2)}, u32[]{:S(2)}) %collective-permute-start.22) | collective-permute-done | bytes 393248 | tf_op jit(solution)/shard_map/ppermute | solution.py:40
  111.1 1.8 %join_last.1 = (bf16[128,2048]{1,0:T(8,128)(2,1)}, bf16[128,2048]{1,0:T(8,128)(2,1)}, bf16[128,2048]{1,0:T(8,128)(2,1)}, bf16[512,2048]{1,0:T(8,128)(2,1)}) custom-call(s32[4]{0:T(128)S(1)} %pad_add_fusion.meta, bf16[64,2048]{1,0:T(8,128)(2,1)S(1)} %collective-permute-done.18.refs_0_, ...), custom_call_target="tpu_custom_call", output_to_operand_aliasing={{0}: (6, {}), {1}: (7, {}), {2}: (8, {}), {3}: (9, {})} | custom-call | bytes 1024 | tf_op jit(solution)/shard_map/join_last/pallas_call | solution.py:370
  (7 shorter events, 0.1 us)
Async XLA Ops:
  0.6 33.9 %copy-start = (bf16[512,2048]{1,0:T(8,128)(2,1)S(1)}, bf16[512,2048]{1,0:T(8,128)(2,1)}, u32[]{:S(2)}) copy-start(bf16[512,2048]{1,0:T(8,128)(2,1)} %w_ref.1) | copy-start | bytes 6291460
  0.6 27.2 %collective-permute-start.2 = (bf16[128,2048]{1,0:T(8,128)(2,1)}, bf16[128,2048]{1,0:T(8,128)(2,1)S(1)}, u32[]{:S(2)}, u32[]{:S(2)}) collective-permute-start(bf16[128,2048]{1,0:T(8,128)(2,1)} %in_ref), channel_id=1, source_target_pairs={{0,1},{1,0},{2,3},{3,2},{4,5},{5,4},{6,7},{7,6},{8,9},{9,8},{10,11... | collective-permute-start | bytes 1572872 | tf_op jit(solution)/shard_map/ppermute | solution.py:40
  3.7 27.7 %collective-permute-start.1 = (bf16[128,2048]{1,0:T(8,128)(2,1)}, bf16[128,2048]{1,0:T(8,128)(2,1)S(1)}, u32[]{:S(2)}, u32[]{:S(2)}) collective-permute-start(bf16[128,2048]{1,0:T(8,128)(2,1)} %in_ref), channel_id=1, source_target_pairs={{0,2},{1,3},{2,0},{3,1},{4,6},{5,7},{6,4},{7,5},{8,10},{9,11},{10,... | collective-permute-start | bytes 1572872 | tf_op jit(solution)/shard_map/ppermute | solution.py:40
  7.0 1.0 copy-start.1
  8.1 1.0 copy-start.2
  9.1 1.0 copy-start.3
  11.2 32.9 %collective-permute-start = (bf16[3,128,512]{2,1,0:T(8,128)(2,1)S(1)}, bf16[3,128,512]{2,1,0:T(8,128)(2,1)S(1)}, u32[]{:S(2)}, u32[]{:S(2)}) collective-permute-start(bf16[3,128,512]{2,1,0:T(8,128)(2,1)S(1)} %get-tuple-element.62), channel_id=1, source_target_pairs={{0,1},{1,0},{2,3},{3,2},{4,5},{5,4},{6,7},{7,6},{8,9},{9,8},{10,11... | collective-permute-start | bytes 1179656 | tf_op jit(solution)/shard_map/ppermute | solution.py:40
  27.8 17.5 %collective-permute-start.4 = (bf16[3,128,384]{2,1,0:T(8,128)(2,1)S(1)}, bf16[3,128,384]{2,1,0:T(8,128)(2,1)S(1)}, u32[]{:S(2)}, u32[]{:S(2)}) collective-permute-start(bf16[3,128,384]{2,1,0:T(8,128)(2,1)S(1)} %get-tuple-element.67), channel_id=1, source_target_pairs={{0,3},{1,2},{2,1},{3,0},{4,7},{5,6},{6,5},{7,4},{8,11},{9,10},{10,... | collective-permute-start | bytes 884744 | tf_op jit(solution)/shard_map/ppermute | solution.py:40
  31.4 24.5 %collective-permute-start.3 = (bf16[3,128,384]{2,1,0:T(8,128)(2,1)S(1)}, bf16[3,128,384]{2,1,0:T(8,128)(2,1)S(1)}, u32[]{:S(2)}, u32[]{:S(2)}) collective-permute-start(bf16[3,128,384]{2,1,0:T(8,128)(2,1)S(1)} %get-tuple-element.65), channel_id=1, source_target_pairs={{0,2},{1,3},{2,0},{3,1},{4,6},{5,7},{6,4},{7,5},{8,10},{9,11},{10,... | collective-permute-start | bytes 884744 | tf_op jit(solution)/shard_map/ppermute | solution.py:40
  31.4 33.4 %collective-permute-start.7 = (bf16[64,2048]{1,0:T(8,128)(2,1)S(1)}, bf16[64,2048]{1,0:T(8,128)(2,1)S(1)}, u32[]{:S(2)}, u32[]{:S(2)}) collective-permute-start(bf16[64,2048]{1,0:T(8,128)(2,1)S(1)} %slice.8), channel_id=1, source_target_pairs={{0,1},{1,0},{2,3},{3,2},{4,5},{5,4},{6,7},{7,6},{8,9},{9,8},{10,11... | collective-permute-start | bytes 786440 | tf_op jit(solution)/shard_map/ppermute | solution.py:40
  33.5 1.0 copy-start.4
  44.1 20.8 %collective-permute-start.8 = (bf16[64,2048]{1,0:T(8,128)(2,1)S(1)}, bf16[64,2048]{1,0:T(8,128)(2,1)S(1)}, u32[]{:S(2)}, u32[]{:S(2)}) collective-permute-start(bf16[64,2048]{1,0:T(8,128)(2,1)S(1)} %slice.7), channel_id=1, source_target_pairs={{0,1},{1,0},{2,3},{3,2},{4,5},{5,4},{6,7},{7,6},{8,9},{9,8},{10,11... | collective-permute-start | bytes 786440 | tf_op jit(solution)/shard_map/ppermute | solution.py:40
  45.3 19.5 %collective-permute-start.6 = (bf16[3,128,128]{2,1,0:T(8,128)(2,1)S(1)}, bf16[3,128,128]{2,1,0:T(8,128)(2,1)S(1)}, u32[]{:S(2)}, u32[]{:S(2)}) collective-permute-start(bf16[3,128,128]{2,1,0:T(8,128)(2,1)S(1)} %get-tuple-element.78), channel_id=1, source_target_pairs={{0,3},{1,2},{2,1},{3,0},{4,7},{5,6},{6,5},{7,4},{8,11},{9,10},{10,... | collective-permute-start | bytes 294920 | tf_op jit(solution)/shard_map/ppermute | solution.py:40
  55.9 8.9 %collective-permute-start.5 = (bf16[3,128,128]{2,1,0:T(8,128)(2,1)S(1)}, bf16[3,128,128]{2,1,0:T(8,128)(2,1)S(1)}, u32[]{:S(2)}, u32[]{:S(2)}) collective-permute-start(bf16[3,128,128]{2,1,0:T(8,128)(2,1)S(1)} %get-tuple-element.76), channel_id=1, source_target_pairs={{0,2},{1,3},{2,0},{3,1},{4,6},{5,7},{6,4},{7,5},{8,10},{9,11},{10,... | collective-permute-start | bytes 294920 | tf_op jit(solution)/shard_map/ppermute | solution.py:40
  67.5 2.9 %collective-permute-start.9 = (bf16[256,2048]{1,0:T(8,128)(2,1)S(1)}, bf16[256,2048]{1,0:T(8,128)(2,1)S(1)}, u32[]{:S(2)}, u32[]{:S(2)}) collective-permute-start(bf16[256,2048]{1,0:T(8,128)(2,1)S(1)} %get-tuple-element.89), channel_id=1, source_target_pairs={{0,4},{4,0},{1,5},{5,1},{2,6},{6,2},{3,7},{7,3},{8,12},{12,8},{9,1... | collective-permute-start | bytes 3145736 | tf_op jit(solution)/shard_map/ppermute | solution.py:40
  70.7 9.2 %collective-permute-start.10 = (bf16[64,2048]{1,0:T(8,128)(2,1)S(1)}, bf16[64,2048]{1,0:T(8,128)(2,1)S(1)}, u32[]{:S(2)}, u32[]{:S(2)}) collective-permute-start(bf16[64,2048]{1,0:T(8,128)(2,1)S(1)} %get-tuple-element.101), channel_id=1, source_target_pairs={{0,8},{8,0},{16,24},{24,16},{1,9},{9,1},{17,25},{25,17},{2,10},{10... | collective-permute-start | bytes 786440 | tf_op jit(solution)/shard_map/ppermute | solution.py:40
  72.3 14.0 %collective-permute-start.11 = (bf16[64,2048]{1,0:T(8,128)(2,1)S(1)}, bf16[64,2048]{1,0:T(8,128)(2,1)S(1)}, u32[]{:S(2)}, u32[]{:S(2)}) collective-permute-start(bf16[64,2048]{1,0:T(8,128)(2,1)S(1)} %get-tuple-element.102), channel_id=1, source_target_pairs={{0,16},{8,24},{16,0},{24,8},{1,17},{9,25},{17,1},{25,9},{2,18},{10... | collective-permute-start | bytes 786440 | tf_op jit(solution)/shard_map/ppermute | solution.py:40
  73.8 12.5 %collective-permute-start.12 = (bf16[64,2048]{1,0:T(8,128)(2,1)S(1)}, bf16[64,2048]{1,0:T(8,128)(2,1)S(1)}, u32[]{:S(2)}, u32[]{:S(2)}) collective-permute-start(bf16[64,2048]{1,0:T(8,128)(2,1)S(1)} %get-tuple-element.103), channel_id=1, source_target_pairs={{0,24},{8,16},{16,8},{24,0},{1,25},{9,17},{17,9},{25,1},{2,26},{10... | collective-permute-start | bytes 786440 | tf_op jit(solution)/shard_map/ppermute | solution.py:40
  74.3 29.6 %collective-permute-start.16 = (bf16[3,128,512]{2,1,0:T(8,128)(2,1)S(1)}, bf16[3,128,512]{2,1,0:T(8,128)(2,1)S(1)}, u32[]{:S(2)}, u32[]{:S(2)}) collective-permute-start(bf16[3,128,512]{2,1,0:T(8,128)(2,1)S(1)} %get-tuple-element.104), channel_id=1, source_target_pairs={{0,2},{1,3},{2,0},{3,1},{4,6},{5,7},{6,4},{7,5},{8,10},{9,11},{10,... | collective-permute-start | bytes 1179656 | tf_op jit(solution)/shard_map/ppermute | solution.py:40
  75.8 28.2 %collective-permute-start.17 = (bf16[3,128,512]{2,1,0:T(8,128)(2,1)S(1)}, bf16[3,128,512]{2,1,0:T(8,128)(2,1)S(1)}, u32[]{:S(2)}, u32[]{:S(2)}) collective-permute-start(bf16[3,128,512]{2,1,0:T(8,128)(2,1)S(1)} %get-tuple-element.105), channel_id=1, source_target_pairs={{0,3},{1,2},{2,1},{3,0},{4,7},{5,6},{6,5},{7,4},{8,11},{9,10},{10,... | collective-permute-start | bytes 1179656 | tf_op jit(solution)/shard_map/ppermute | solution.py:40
  86.5 9.3 %collective-permute-start.13 = (bf16[64,2048]{1,0:T(8,128)(2,1)S(1)}, bf16[64,2048]{1,0:T(8,128)(2,1)S(1)}, u32[]{:S(2)}, u32[]{:S(2)}) collective-permute-start(bf16[64,2048]{1,0:T(8,128)(2,1)S(1)} %scene_mean.1.refs_0_), channel_id=1, source_target_pairs={{0,8},{8,0},{16,24},{24,16},{1,9},{9,1},{17,25},{25,17},{2,10},{10... | collective-permute-start | bytes 786440 | tf_op jit(solution)/shard_map/ppermute | solution.py:40
  87.8 13.0 %collective-permute-start.15 = (bf16[64,2048]{1,0:T(8,128)(2,1)S(1)}, bf16[64,2048]{1,0:T(8,128)(2,1)S(1)}, u32[]{:S(2)}, u32[]{:S(2)}) collective-permute-start(bf16[64,2048]{1,0:T(8,128)(2,1)S(1)} %scene_mean.1.refs_0_), channel_id=1, source_target_pairs={{0,24},{8,16},{16,8},{24,0},{1,25},{9,17},{17,9},{25,1},{2,26},{10... | collective-permute-start | bytes 786440 | tf_op jit(solution)/shard_map/ppermute | solution.py:40
  89.5 12.6 %collective-permute-start.14 = (bf16[64,2048]{1,0:T(8,128)(2,1)S(1)}, bf16[64,2048]{1,0:T(8,128)(2,1)S(1)}, u32[]{:S(2)}, u32[]{:S(2)}) collective-permute-start(bf16[64,2048]{1,0:T(8,128)(2,1)S(1)} %scene_mean.1.refs_0_), channel_id=1, source_target_pairs={{0,16},{8,24},{16,0},{24,8},{1,17},{9,25},{17,1},{25,9},{2,18},{10... | collective-permute-start | bytes 786440 | tf_op jit(solution)/shard_map/ppermute | solution.py:40
  95.8 15.4 %collective-permute-start.22 = (bf16[3,128,512]{2,1,0:T(8,128)(2,1)S(1)}, bf16[3,128,512]{2,1,0:T(8,128)(2,1)S(1)}, u32[]{:S(2)}, u32[]{:S(2)}) collective-permute-start(bf16[3,128,512]{2,1,0:T(8,128)(2,1)S(1)} %get-tuple-element.111), channel_id=1, source_target_pairs={{0,1},{1,0},{2,3},{3,2},{4,5},{5,4},{6,7},{7,6},{8,9},{9,8},{10,11... | collective-permute-start | bytes 1179656 | tf_op jit(solution)/shard_map/ppermute | solution.py:40
  103.9 2.7 %collective-permute-start.18 = (bf16[64,2048]{1,0:T(8,128)(2,1)S(1)}, bf16[64,2048]{1,0:T(8,128)(2,1)S(1)}, u32[]{:S(2)}, u32[]{:S(2)}) collective-permute-start(bf16[64,2048]{1,0:T(8,128)(2,1)S(1)} %scene_mean.1.refs_0_), channel_id=1, source_target_pairs={{0,4},{4,0},{1,5},{5,1},{2,6},{6,2},{3,7},{7,3},{8,12},{12,8},{9,1... | collective-permute-start | bytes 786440 | tf_op jit(solution)/shard_map/ppermute | solution.py:40
  103.9 2.7 %collective-permute-start.19 = (bf16[64,2048]{1,0:T(8,128)(2,1)S(1)}, bf16[64,2048]{1,0:T(8,128)(2,1)S(1)}, u32[]{:S(2)}, u32[]{:S(2)}) collective-permute-start(bf16[64,2048]{1,0:T(8,128)(2,1)S(1)} %collective-permute-done.13.refs_1_), channel_id=1, source_target_pairs={{0,4},{4,0},{1,5},{5,1},{2,6},{6,2},{3,7},{7,3},{8,12},{12,8},{9,1... | collective-permute-start | bytes 786440 | tf_op jit(solution)/shard_map/ppermute | solution.py:40
  104.4 2.2 %collective-permute-start.20 = (bf16[64,2048]{1,0:T(8,128)(2,1)S(1)}, bf16[64,2048]{1,0:T(8,128)(2,1)S(1)}, u32[]{:S(2)}, u32[]{:S(2)}) collective-permute-start(bf16[64,2048]{1,0:T(8,128)(2,1)S(1)} %collective-permute-done.14.refs_2_), channel_id=1, source_target_pairs={{0,4},{4,0},{1,5},{5,1},{2,6},{6,2},{3,7},{7,3},{8,12},{12,8},{9,1... | collective-permute-start | bytes 786440 | tf_op jit(solution)/shard_map/ppermute | solution.py:40
  104.5 2.1 %collective-permute-start.21 = (bf16[64,2048]{1,0:T(8,128)(2,1)S(1)}, bf16[64,2048]{1,0:T(8,128)(2,1)S(1)}, u32[]{:S(2)}, u32[]{:S(2)}) collective-permute-start(bf16[64,2048]{1,0:T(8,128)(2,1)S(1)} %collective-permute-done.15.refs_3_), channel_id=1, source_target_pairs={{0,4},{4,0},{1,5},{5,1},{2,6},{6,2},{3,7},{7,3},{8,12},{12,8},{9,1... | collective-permute-start | bytes 786440 | tf_op jit(solution)/shard_map/ppermute | solution.py:40

commit v7 on v6

--- a/solution.py
+++ b/solution.py
@@ -444,12 +444,12 @@
     own0, *backs = backward(meta, pieces, grad_early, corners, out_weight, (*saved_a, *saved_b), early)
     own_part, *sends = add_parts(after(keep, own0), recv)
     recvs = [swap(x, "chips", 4, j + 1) for j, x in enumerate(sends)]
-    back3, back2 = send(backs[2], 3), send(backs[1], 2)
+    back2, back3 = send(backs[1], 2), send(backs[2], 3)
     done = total_of(own_part, recvs, 1.0 / 8)
     near = [done] + [swap(done, "chips", 4, j) for j in (1, 2, 3)]
     back1 = send(backs[0], 1, near[1])
     weight = join_weight(meta, near)
-    weight, *near, back2, back3 = lax.optimization_barrier((weight, *near, back2, back3))
+    weight, *near, back3, back2 = lax.optimization_barrier((weight, *near, back3, back2))
     far = [swap(x, "core", 2, 1) for x in near]
     heads = join_heads(meta, own0, back2, back3)
     return tuple(join_last(meta, far, back1, (*heads, weight)))

time: 114 us -> 116 us (1.018)
  waiting for transfers between devices: 59.4 us -> 63.2 us
    ppermute x23, waiting for transfers between devices: 59.4 us -> 63.2 us  [swap(): return lax.ppermute(x, axis, [(i, i ^ flip) for i in range(size)])]
  transfers between devices with their start and end apart: 23 -> 23, of which waited for: 12 -> 11; matrix products, arithmetic and copies ran while one was open for 0% -> 0% of each run, Pallas kernels for 13% -> 12%
where the time goes in v7:
time: 116 us
  waiting for transfers between devices  63.2 us (54%)
  starting transfers between devices  27.8 us (24%)
  Pallas kernels  19.2 us (17%)
  local copies, waits for them, and re-layouts  4.21 us (4%)
  between operations  1.47 us (1%)
    ppermute x23, waiting for transfers between devices, swap(): return lax.ppermute(x, axis, [(i, i ^ flip) for i in range(size)])  63.2 us
    ppermute x23, starting transfers between devices, swap(): return lax.ppermute(x, axis, [(i, i ^ flip) for i in range(size)])  27.8 us
    pallas_call x8, Pallas kernels, whole(): pl.pallas_call(kernel, out_shape=out_shape, in_specs=[pl.BlockSpec(memory...  13.1 us
    pallas_call x3, Pallas kernels, join(): pl.pallas_call(kernel, out_shape=shapes, in_specs=[pl.BlockSpec(memory_sp...  5.05 us
    unnamed x10, local copies, waits for them, and re-layouts  4.17 us
  transfers between devices with their start and end apart: 23, of which 11 were waited for; matrix products, arithmetic and copies ran while one was open for 0% of the time, Pallas kernels for 12%

profile of v7, /device:TPU:0, one launch (start us, length us, event | category | flops | bytes accessed | tf_op | source)
XLA Modules:
  0.0 115.9 jit_solution(3590758356431969592)
XLA Ops:
  0.6 0.0 copy-start
  0.6 3.1 %collective-permute-start.2 = (bf16[128,2048]{1,0:T(8,128)(2,1)}, bf16[128,2048]{1,0:T(8,128)(2,1)S(1)}, u32[]{:S(2)}, u32[]{:S(2)}) collective-permute-start(bf16[128,2048]{1,0:T(8,128)(2,1)} %in_ref), channel_id=1, source_target_pairs={{0,1},{1,0},{2,3},{3,2},{4,5},{5,4},{6,7},{7,6},{8,9},{9,8},{10,11... | collective-permute-start | bytes 1572872 | tf_op jit(solution)/shard_map/ppermute | solution.py:40
  3.7 2.6 %collective-permute-start.1 = (bf16[128,2048]{1,0:T(8,128)(2,1)}, bf16[128,2048]{1,0:T(8,128)(2,1)S(1)}, u32[]{:S(2)}, u32[]{:S(2)}) collective-permute-start(bf16[128,2048]{1,0:T(8,128)(2,1)} %in_ref), channel_id=1, source_target_pairs={{0,2},{1,3},{2,0},{3,1},{4,6},{5,7},{6,4},{7,5},{8,10},{9,11},{10,... | collective-permute-start | bytes 1572872 | tf_op jit(solution)/shard_map/ppermute | solution.py:40
  7.0 0.1 pad_add_fusion.meta
  7.1 1.0 copy-done.1
  8.1 1.0 copy-done.2
  9.1 1.0 copy-done.3
  10.2 1.0 pack_heads.1
  11.2 0.5 collective-permute-start
  11.7 16.1 %collective-permute-done.2.refs_1_ = bf16[128,2048]{1,0:T(8,128)(2,1)S(1)} collective-permute-done((bf16[128,2048]{1,0:T(8,128)(2,1)}, bf16[128,2048]{1,0:T(8,128)(2,1)S(1)}, u32[]{:S(2)}, u32[]{:S(2)}) %collective-permute-start.2) | collective-permute-done | bytes 524320 | tf_op jit(solution)/shard_map/ppermute | solution.py:40
  27.8 3.6 %collective-permute-start.4 = (bf16[3,128,384]{2,1,0:T(8,128)(2,1)S(1)}, bf16[3,128,384]{2,1,0:T(8,128)(2,1)S(1)}, u32[]{:S(2)}, u32[]{:S(2)}) collective-permute-start(bf16[3,128,384]{2,1,0:T(8,128)(2,1)S(1)} %get-tuple-element.67), channel_id=1, source_target_pairs={{0,3},{1,2},{2,1},{3,0},{4,7},{5,6},{6,5},{7,4},{8,11},{9,10},{10,... | collective-permute-start | bytes 884744 | tf_op jit(solution)/shard_map/ppermute | solution.py:40
  31.4 0.0 collective-permute-done.1.refs_2_
  31.4 0.0 collective-permute-start.3
  31.4 2.1 %collective-permute-start.7 = (bf16[64,2048]{1,0:T(8,128)(2,1)S(1)}, bf16[64,2048]{1,0:T(8,128)(2,1)S(1)}, u32[]{:S(2)}, u32[]{:S(2)}) collective-permute-start(bf16[64,2048]{1,0:T(8,128)(2,1)S(1)} %slice.8), channel_id=1, source_target_pairs={{0,1},{1,0},{2,3},{3,2},{4,5},{5,4},{6,7},{7,6},{8,9},{9,8},{10,11... | collective-permute-start | bytes 786440 | tf_op jit(solution)/shard_map/ppermute | solution.py:40
  33.5 1.0 copy-done.4
  34.6 0.0 copy-done
  34.6 1.5 %grad_attn.1.refs_4_.early_ref = bf16[384,512]{1,0:T(8,128)(2,1)S(1)} custom-call(s32[4]{0:T(128)S(1)} %pad_add_fusion.meta, bf16[128,2048]{1,0:T(8,128)(2,1)S(1)} %hold.1.refs_0_, bf16[128,2048]{1,0:T(8,128)(2,1)S(1)} %collective-permute-done.2.refs_1_, bf16[128,2048]{1,0:T(8,128)(2,1)S(1)} %collective-permute-done.1.refs_2_, bf16[512,2048]{1,0:T(8,128)(2,1)S(1)} %copy-done), custom_call_target="tpu_custom_call" | custom-call | bytes 1024 | tf_op jit(solution)/shard_map/grad_attn/pallas_call | solution.py:55
  36.1 7.9 %collective-permute-done.p1.refs_1_.near = bf16[3,128,512]{2,1,0:T(8,128)(2,1)S(1)} collective-permute-done((bf16[3,128,512]{2,1,0:T(8,128)(2,1)S(1)}, bf16[3,128,512]{2,1,0:T(8,128)(2,1)S(1)}, u32[]{:S(2)}, u32[]{:S(2)}) %collective-permute-start) | collective-permute-done | bytes 393248 | tf_op jit(solution)/shard_map/ppermute | solution.py:40
  44.1 0.1 collective-permute-start.8
  44.2 1.2 %collective-permute-done.4.p3.refs_3_.far3a = bf16[3,128,384]{2,1,0:T(8,128)(2,1)S(1)} collective-permute-done((bf16[3,128,384]{2,1,0:T(8,128)(2,1)S(1)}, bf16[3,128,384]{2,1,0:T(8,128)(2,1)S(1)}, u32[]{:S(2)}, u32[]{:S(2)}) %collective-permute-start.4) | collective-permute-done | bytes 294944 | tf_op jit(solution)/shard_map/ppermute | solution.py:40
  45.3 3.0 %collective-permute-start.6 = (bf16[3,128,128]{2,1,0:T(8,128)(2,1)S(1)}, bf16[3,128,128]{2,1,0:T(8,128)(2,1)S(1)}, u32[]{:S(2)}, u32[]{:S(2)}) collective-permute-start(bf16[3,128,128]{2,1,0:T(8,128)(2,1)S(1)} %get-tuple-element.78), channel_id=1, source_target_pairs={{0,3},{1,2},{2,1},{3,0},{4,7},{5,6},{6,5},{7,4},{8,11},{9,10},{10,... | collective-permute-start | bytes 294920 | tf_op jit(solution)/shard_map/ppermute | solution.py:40
  48.3 7.6 %collective-permute-done.3.p2.refs_2_.far2a = bf16[3,128,384]{2,1,0:T(8,128)(2,1)S(1)} collective-permute-done((bf16[3,128,384]{2,1,0:T(8,128)(2,1)S(1)}, bf16[3,128,384]{2,1,0:T(8,128)(2,1)S(1)}, u32[]{:S(2)}, u32[]{:S(2)}) %collective-permute-start.3) | collective-permute-done | bytes 294944 | tf_op jit(solution)/shard_map/ppermute | solution.py:40
  55.9 0.0 collective-permute-start.5
  55.9 3.3 %attend_forward.1 = (bf16[3,512,512]{2,1,0:T(8,128)(2,1)S(1)}, f32[3,1,512]{2,1,0:T(1,128)S(1)}, f32[384,512]{1,0:T(8,128)S(1)}, bf16[384,512]{1,0:T(8,128)(2,1)S(1)}, f32[512,512]{1,0:T(8,128)S(1)}) custom-call(s32[4]{0:T(128)S(1)} %pad_add_fusion.meta, bf16[3,128,512]{2,1,0:T(8,128)(2,1)S(1)} %get-tuple-element.61.p0.refs_0_.own, ...), custom_call_target="tpu_custom_call" | custom-call | bytes 1024 | tf_op jit(solution)/shard_map/attend_forward/pallas_call | solution.py:55
  59.3 2.3 %backward_early.1 = (bf16[384,384]{1,0:T(8,128)(2,1)S(1)}, f32[512,384]{1,0:T(8,128)S(1)}, f32[512,384]{1,0:T(8,128)S(1)}) custom-call(bf16[3,128,512]{2,1,0:T(8,128)(2,1)S(1)} %get-tuple-element.61.p0.refs_0_.own, bf16[3,128,512]{2,1,0:T(8,128)(2,1)S(1)} %collective-permute-done.p1.refs_1_.near, ...), custom_call_target="tpu_custom_call" | custom-call | bytes 1024 | tf_op jit(solution)/shard_map/backward_early/pallas_call | solution.py:55
  61.6 3.3 %collective-permute-done.6.p3.far3b = bf16[3,128,128]{2,1,0:T(8,128)(2,1)S(1)} collective-permute-done((bf16[3,128,128]{2,1,0:T(8,128)(2,1)S(1)}, bf16[3,128,128]{2,1,0:T(8,128)(2,1)S(1)}, u32[]{:S(2)}, u32[]{:S(2)}) %collective-permute-start.6) | collective-permute-done | bytes 98336 | tf_op jit(solution)/shard_map/ppermute | solution.py:40
  64.8 0.0 collective-permute-done.5.p2.far2b
  64.8 0.0 collective-permute-done.7.refs_3_.corner0
  64.8 0.0 collective-permute-done.8.refs_4_.corner1
  64.9 2.7 %weight_halves.1 = (bf16[1,512,512]{2,1,0:T(8,128)(2,1)S(1)}, f32[1,1,512]{2,1,0:T(1,128)S(1)}, f32[128,512]{1,0:T(8,128)S(1)}, bf16[256,2048]{1,0:T(8,128)(2,1)S(1)}, f32[256,2048]{1,0:T(8,128)S(1)}) custom-call(s32[4]{0:T(128)S(1)} %pad_add_fusion.meta, bf16[3,128,512]{2,1,0:T(8,128)(2,1)S(1)} %get-tuple-element.61.p0.refs_0_.own, ...), custom_call_target="tpu_custom_call" | custom-call | bytes 1024 | tf_op jit(solution)/shard_map/weight_halves/pallas_call | solution.py:55
  67.5 0.1 collective-permute-start.9
  67.6 2.8 %attend_backward.1 = (bf16[3,128,512]{2,1,0:T(8,128)(2,1)S(1)}, bf16[3,128,512]{2,1,0:T(8,128)(2,1)S(1)}, bf16[3,128,512]{2,1,0:T(8,128)(2,1)S(1)}, bf16[3,128,512]{2,1,0:T(8,128)(2,1)S(1)}) custom-call(s32[4]{0:T(128)S(1)} %pad_add_fusion.meta, bf16[3,128,512]{2,1,0:T(8,128)(2,1)S(1)} %get-tuple-element.61.p0.refs_0_.own, ...), custom_call_target="tpu_custom_call" | custom-call | bytes 1024 | tf_op jit(solution)/shard_map/attend_backward/pallas_call | solution.py:55
  70.5 0.0 collective-permute-done.9.recv_ref
  70.5 0.3 add_parts.1
  70.7 1.6 %collective-permute-start.10 = (bf16[64,2048]{1,0:T(8,128)(2,1)S(1)}, bf16[64,2048]{1,0:T(8,128)(2,1)S(1)}, u32[]{:S(2)}, u32[]{:S(2)}) collective-permute-start(bf16[64,2048]{1,0:T(8,128)(2,1)S(1)} %get-tuple-element.101), channel_id=1, source_target_pairs={{0,8},{8,0},{16,24},{24,16},{1,9},{9,1},{17,25},{25,17},{2,10},{10... | collective-permute-start | bytes 786440 | tf_op jit(solution)/shard_map/ppermute | solution.py:40
  72.3 1.5 %collective-permute-start.11 = (bf16[64,2048]{1,0:T(8,128)(2,1)S(1)}, bf16[64,2048]{1,0:T(8,128)(2,1)S(1)}, u32[]{:S(2)}, u32[]{:S(2)}) collective-permute-start(bf16[64,2048]{1,0:T(8,128)(2,1)S(1)} %get-tuple-element.102), channel_id=1, source_target_pairs={{0,16},{8,24},{16,0},{24,8},{1,17},{9,25},{17,1},{25,9},{2,18},{10... | collective-permute-start | bytes 786440 | tf_op jit(solution)/shard_map/ppermute | solution.py:40
  73.8 0.5 collective-permute-start.12
  74.3 2.8 %collective-permute-start.16 = (bf16[3,128,512]{2,1,0:T(8,128)(2,1)S(1)}, bf16[3,128,512]{2,1,0:T(8,128)(2,1)S(1)}, u32[]{:S(2)}, u32[]{:S(2)}) collective-permute-start(bf16[3,128,512]{2,1,0:T(8,128)(2,1)S(1)} %get-tuple-element.104), channel_id=1, source_target_pairs={{0,3},{1,2},{2,1},{3,0},{4,7},{5,6},{6,5},{7,4},{8,11},{9,10},{10,... | collective-permute-start | bytes 1179656 | tf_op jit(solution)/shard_map/ppermute | solution.py:40
  77.1 0.2 collective-permute-start.17
  77.4 2.6 %collective-permute-done.10.r1 = bf16[64,2048]{1,0:T(8,128)(2,1)S(1)} collective-permute-done((bf16[64,2048]{1,0:T(8,128)(2,1)S(1)}, bf16[64,2048]{1,0:T(8,128)(2,1)S(1)}, u32[]{:S(2)}, u32[]{:S(2)}) %collective-permute-start.10) | collective-permute-done | bytes 262176 | tf_op jit(solution)/shard_map/ppermute | solution.py:40
  79.9 6.4 %collective-permute-done.11.r2 = bf16[64,2048]{1,0:T(8,128)(2,1)S(1)} collective-permute-done((bf16[64,2048]{1,0:T(8,128)(2,1)S(1)}, bf16[64,2048]{1,0:T(8,128)(2,1)S(1)}, u32[]{:S(2)}, u32[]{:S(2)}) %collective-permute-start.11) | collective-permute-done | bytes 262176 | tf_op jit(solution)/shard_map/ppermute | solution.py:40
  86.3 0.0 collective-permute-done.12.r3
  86.3 0.1 scene_mean.1.refs_0_
  86.5 1.3 %collective-permute-start.13 = (bf16[64,2048]{1,0:T(8,128)(2,1)S(1)}, bf16[64,2048]{1,0:T(8,128)(2,1)S(1)}, u32[]{:S(2)}, u32[]{:S(2)}) collective-permute-start(bf16[64,2048]{1,0:T(8,128)(2,1)S(1)} %scene_mean.1.refs_0_), channel_id=1, source_target_pairs={{0,8},{8,0},{16,24},{24,16},{1,9},{9,1},{17,25},{25,17},{2,10},{10... | collective-permute-start | bytes 786440 | tf_op jit(solution)/shard_map/ppermute | solution.py:40
  87.8 1.8 %collective-permute-start.15 = (bf16[64,2048]{1,0:T(8,128)(2,1)S(1)}, bf16[64,2048]{1,0:T(8,128)(2,1)S(1)}, u32[]{:S(2)}, u32[]{:S(2)}) collective-permute-start(bf16[64,2048]{1,0:T(8,128)(2,1)S(1)} %scene_mean.1.refs_0_), channel_id=1, source_target_pairs={{0,24},{8,16},{16,8},{24,0},{1,25},{9,17},{17,9},{25,1},{2,26},{10... | collective-permute-start | bytes 786440 | tf_op jit(solution)/shard_map/ppermute | solution.py:40
  89.5 0.5 collective-permute-start.14
  90.0 5.8 %collective-permute-done.13.refs_1_ = bf16[64,2048]{1,0:T(8,128)(2,1)S(1)} collective-permute-done((bf16[64,2048]{1,0:T(8,128)(2,1)S(1)}, bf16[64,2048]{1,0:T(8,128)(2,1)S(1)}, u32[]{:S(2)}, u32[]{:S(2)}) %collective-permute-start.13) | collective-permute-done | bytes 262176 | tf_op jit(solution)/shard_map/ppermute | solution.py:40
  95.8 1.6 %collective-permute-start.22 = (bf16[3,128,512]{2,1,0:T(8,128)(2,1)S(1)}, bf16[3,128,512]{2,1,0:T(8,128)(2,1)S(1)}, u32[]{:S(2)}, u32[]{:S(2)}) collective-permute-start(bf16[3,128,512]{2,1,0:T(8,128)(2,1)S(1)} %get-tuple-element.111), channel_id=1, source_target_pairs={{0,1},{1,0},{2,3},{3,2},{4,5},{5,4},{6,7},{7,6},{8,9},{9,8},{10,11... | collective-permute-start | bytes 1179656 | tf_op jit(solution)/shard_map/ppermute | solution.py:40
  97.4 3.4 %collective-permute-done.15.refs_3_ = bf16[64,2048]{1,0:T(8,128)(2,1)S(1)} collective-permute-done((bf16[64,2048]{1,0:T(8,128)(2,1)S(1)}, bf16[64,2048]{1,0:T(8,128)(2,1)S(1)}, u32[]{:S(2)}, u32[]{:S(2)}) %collective-permute-start.15) | collective-permute-done | bytes 262176 | tf_op jit(solution)/shard_map/ppermute | solution.py:40
  100.8 1.4 %collective-permute-done.14.refs_2_ = bf16[64,2048]{1,0:T(8,128)(2,1)S(1)} collective-permute-done((bf16[64,2048]{1,0:T(8,128)(2,1)S(1)}, bf16[64,2048]{1,0:T(8,128)(2,1)S(1)}, u32[]{:S(2)}, u32[]{:S(2)}) %collective-permute-start.14) | collective-permute-done | bytes 262176 | tf_op jit(solution)/shard_map/ppermute | solution.py:40
  102.2 1.6 %join_weight.1.refs_8_ = bf16[512,2048]{1,0:T(8,128)(2,1)} custom-call(s32[4]{0:T(128)S(1)} %pad_add_fusion.meta, bf16[64,2048]{1,0:T(8,128)(2,1)S(1)} %scene_mean.1.refs_0_, bf16[64,2048]{1,0:T(8,128)(2,1)S(1)} %collective-permute-done.13.refs_1_, bf16[64,2048]{1,0:T(8,128)(2,1)S(1)} %collective-permute-done.14.refs_2_, ...), custom_call_target="tpu_custom_call" | custom-call | bytes 1024 | tf_op jit(solution)/shard_map/join_weight/pallas_call | solution.py:370
  103.8 0.0 collective-permute-done.16.back3
  103.8 7.6 %collective-permute-done.17.back2 = bf16[3,128,512]{2,1,0:T(8,128)(2,1)S(1)} collective-permute-done((bf16[3,128,512]{2,1,0:T(8,128)(2,1)S(1)}, bf16[3,128,512]{2,1,0:T(8,128)(2,1)S(1)}, u32[]{:S(2)}, u32[]{:S(2)}) %collective-permute-start.17) | collective-permute-done | bytes 393248 | tf_op jit(solution)/shard_map/ppermute | solution.py:40
  111.4 0.0 collective-permute-start.18
  111.4 0.5 collective-permute-start.19
  111.9 0.0 collective-permute-start.20
  111.9 0.5 collective-permute-start.21
  112.4 1.6 %join_heads.1 = (bf16[128,2048]{1,0:T(8,128)(2,1)}, bf16[128,2048]{1,0:T(8,128)(2,1)}, bf16[128,2048]{1,0:T(8,128)(2,1)}) custom-call(s32[4]{0:T(128)S(1)} %pad_add_fusion.meta, bf16[3,128,512]{2,1,0:T(8,128)(2,1)S(1)} %get-tuple-element.98.own, bf16[3,128,512]{2,1,0:T(8,128)(2,1)S(1)} %collective-permute-done.17.back2, ...), custom_call_target="tpu_custom_call" | custom-call | bytes 1024 | tf_op jit(solution)/shard_map/join_heads/pallas_call | solution.py:370
  114.0 0.0 collective-permute-done.18.refs_0_
  114.0 0.0 collective-permute-done.19.refs_1_
  114.1 0.0 collective-permute-done.20.refs_2_
  114.1 0.0 collective-permute-done.21.refs_3_
  114.1 0.0 collective-permute-done.22.refs_4_
  114.1 1.8 %join_last.1 = (bf16[128,2048]{1,0:T(8,128)(2,1)}, bf16[128,2048]{1,0:T(8,128)(2,1)}, bf16[128,2048]{1,0:T(8,128)(2,1)}, bf16[512,2048]{1,0:T(8,128)(2,1)}) custom-call(s32[4]{0:T(128)S(1)} %pad_add_fusion.meta, bf16[64,2048]{1,0:T(8,128)(2,1)S(1)} %collective-permute-done.18.refs_0_, ...), custom_call_target="tpu_custom_call", output_to_operand_aliasing={{0}: (6, {}), {1}: (7, {}), {2}: (8, {}), {3}: (9, {})} | custom-call | bytes 1024 | tf_op jit(solution)/shard_map/join_last/pallas_call | solution.py:370
  (7 shorter events, 0.1 us)
Async XLA Ops:
  0.6 33.9 %copy-start = (bf16[512,2048]{1,0:T(8,128)(2,1)S(1)}, bf16[512,2048]{1,0:T(8,128)(2,1)}, u32[]{:S(2)}) copy-start(bf16[512,2048]{1,0:T(8,128)(2,1)} %w_ref.1) | copy-start | bytes 6291460
  0.6 27.2 %collective-permute-start.2 = (bf16[128,2048]{1,0:T(8,128)(2,1)}, bf16[128,2048]{1,0:T(8,128)(2,1)S(1)}, u32[]{:S(2)}, u32[]{:S(2)}) collective-permute-start(bf16[128,2048]{1,0:T(8,128)(2,1)} %in_ref), channel_id=1, source_target_pairs={{0,1},{1,0},{2,3},{3,2},{4,5},{5,4},{6,7},{7,6},{8,9},{9,8},{10,11... | collective-permute-start | bytes 1572872 | tf_op jit(solution)/shard_map/ppermute | solution.py:40
  3.7 27.7 %collective-permute-start.1 = (bf16[128,2048]{1,0:T(8,128)(2,1)}, bf16[128,2048]{1,0:T(8,128)(2,1)S(1)}, u32[]{:S(2)}, u32[]{:S(2)}) collective-permute-start(bf16[128,2048]{1,0:T(8,128)(2,1)} %in_ref), channel_id=1, source_target_pairs={{0,2},{1,3},{2,0},{3,1},{4,6},{5,7},{6,4},{7,5},{8,10},{9,11},{10,... | collective-permute-start | bytes 1572872 | tf_op jit(solution)/shard_map/ppermute | solution.py:40
  7.0 1.0 copy-start.1
  8.1 1.0 copy-start.2
  9.1 1.0 copy-start.3
  11.2 32.9 %collective-permute-start = (bf16[3,128,512]{2,1,0:T(8,128)(2,1)S(1)}, bf16[3,128,512]{2,1,0:T(8,128)(2,1)S(1)}, u32[]{:S(2)}, u32[]{:S(2)}) collective-permute-start(bf16[3,128,512]{2,1,0:T(8,128)(2,1)S(1)} %get-tuple-element.62), channel_id=1, source_target_pairs={{0,1},{1,0},{2,3},{3,2},{4,5},{5,4},{6,7},{7,6},{8,9},{9,8},{10,11... | collective-permute-start | bytes 1179656 | tf_op jit(solution)/shard_map/ppermute | solution.py:40
  27.8 17.5 %collective-permute-start.4 = (bf16[3,128,384]{2,1,0:T(8,128)(2,1)S(1)}, bf16[3,128,384]{2,1,0:T(8,128)(2,1)S(1)}, u32[]{:S(2)}, u32[]{:S(2)}) collective-permute-start(bf16[3,128,384]{2,1,0:T(8,128)(2,1)S(1)} %get-tuple-element.67), channel_id=1, source_target_pairs={{0,3},{1,2},{2,1},{3,0},{4,7},{5,6},{6,5},{7,4},{8,11},{9,10},{10,... | collective-permute-start | bytes 884744 | tf_op jit(solution)/shard_map/ppermute | solution.py:40
  31.4 24.5 %collective-permute-start.3 = (bf16[3,128,384]{2,1,0:T(8,128)(2,1)S(1)}, bf16[3,128,384]{2,1,0:T(8,128)(2,1)S(1)}, u32[]{:S(2)}, u32[]{:S(2)}) collective-permute-start(bf16[3,128,384]{2,1,0:T(8,128)(2,1)S(1)} %get-tuple-element.65), channel_id=1, source_target_pairs={{0,2},{1,3},{2,0},{3,1},{4,6},{5,7},{6,4},{7,5},{8,10},{9,11},{10,... | collective-permute-start | bytes 884744 | tf_op jit(solution)/shard_map/ppermute | solution.py:40
  31.4 33.4 %collective-permute-start.7 = (bf16[64,2048]{1,0:T(8,128)(2,1)S(1)}, bf16[64,2048]{1,0:T(8,128)(2,1)S(1)}, u32[]{:S(2)}, u32[]{:S(2)}) collective-permute-start(bf16[64,2048]{1,0:T(8,128)(2,1)S(1)} %slice.8), channel_id=1, source_target_pairs={{0,1},{1,0},{2,3},{3,2},{4,5},{5,4},{6,7},{7,6},{8,9},{9,8},{10,11... | collective-permute-start | bytes 786440 | tf_op jit(solution)/shard_map/ppermute | solution.py:40
  33.5 1.0 copy-start.4
  44.1 20.8 %collective-permute-start.8 = (bf16[64,2048]{1,0:T(8,128)(2,1)S(1)}, bf16[64,2048]{1,0:T(8,128)(2,1)S(1)}, u32[]{:S(2)}, u32[]{:S(2)}) collective-permute-start(bf16[64,2048]{1,0:T(8,128)(2,1)S(1)} %slice.7), channel_id=1, source_target_pairs={{0,1},{1,0},{2,3},{3,2},{4,5},{5,4},{6,7},{7,6},{8,9},{9,8},{10,11... | collective-permute-start | bytes 786440 | tf_op jit(solution)/shard_map/ppermute | solution.py:40
  45.3 19.5 %collective-permute-start.6 = (bf16[3,128,128]{2,1,0:T(8,128)(2,1)S(1)}, bf16[3,128,128]{2,1,0:T(8,128)(2,1)S(1)}, u32[]{:S(2)}, u32[]{:S(2)}) collective-permute-start(bf16[3,128,128]{2,1,0:T(8,128)(2,1)S(1)} %get-tuple-element.78), channel_id=1, source_target_pairs={{0,3},{1,2},{2,1},{3,0},{4,7},{5,6},{6,5},{7,4},{8,11},{9,10},{10,... | collective-permute-start | bytes 294920 | tf_op jit(solution)/shard_map/ppermute | solution.py:40
  55.9 8.9 %collective-permute-start.5 = (bf16[3,128,128]{2,1,0:T(8,128)(2,1)S(1)}, bf16[3,128,128]{2,1,0:T(8,128)(2,1)S(1)}, u32[]{:S(2)}, u32[]{:S(2)}) collective-permute-start(bf16[3,128,128]{2,1,0:T(8,128)(2,1)S(1)} %get-tuple-element.76), channel_id=1, source_target_pairs={{0,2},{1,3},{2,0},{3,1},{4,6},{5,7},{6,4},{7,5},{8,10},{9,11},{10,... | collective-permute-start | bytes 294920 | tf_op jit(solution)/shard_map/ppermute | solution.py:40
  67.5 2.9 %collective-permute-start.9 = (bf16[256,2048]{1,0:T(8,128)(2,1)S(1)}, bf16[256,2048]{1,0:T(8,128)(2,1)S(1)}, u32[]{:S(2)}, u32[]{:S(2)}) collective-permute-start(bf16[256,2048]{1,0:T(8,128)(2,1)S(1)} %get-tuple-element.89), channel_id=1, source_target_pairs={{0,4},{4,0},{1,5},{5,1},{2,6},{6,2},{3,7},{7,3},{8,12},{12,8},{9,1... | collective-permute-start | bytes 3145736 | tf_op jit(solution)/shard_map/ppermute | solution.py:40
  70.7 9.2 %collective-permute-start.10 = (bf16[64,2048]{1,0:T(8,128)(2,1)S(1)}, bf16[64,2048]{1,0:T(8,128)(2,1)S(1)}, u32[]{:S(2)}, u32[]{:S(2)}) collective-permute-start(bf16[64,2048]{1,0:T(8,128)(2,1)S(1)} %get-tuple-element.101), channel_id=1, source_target_pairs={{0,8},{8,0},{16,24},{24,16},{1,9},{9,1},{17,25},{25,17},{2,10},{10... | collective-permute-start | bytes 786440 | tf_op jit(solution)/shard_map/ppermute | solution.py:40
  72.3 14.0 %collective-permute-start.11 = (bf16[64,2048]{1,0:T(8,128)(2,1)S(1)}, bf16[64,2048]{1,0:T(8,128)(2,1)S(1)}, u32[]{:S(2)}, u32[]{:S(2)}) collective-permute-start(bf16[64,2048]{1,0:T(8,128)(2,1)S(1)} %get-tuple-element.102), channel_id=1, source_target_pairs={{0,16},{8,24},{16,0},{24,8},{1,17},{9,25},{17,1},{25,9},{2,18},{10... | collective-permute-start | bytes 786440 | tf_op jit(solution)/shard_map/ppermute | solution.py:40
  73.8 12.5 %collective-permute-start.12 = (bf16[64,2048]{1,0:T(8,128)(2,1)S(1)}, bf16[64,2048]{1,0:T(8,128)(2,1)S(1)}, u32[]{:S(2)}, u32[]{:S(2)}) collective-permute-start(bf16[64,2048]{1,0:T(8,128)(2,1)S(1)} %get-tuple-element.103), channel_id=1, source_target_pairs={{0,24},{8,16},{16,8},{24,0},{1,25},{9,17},{17,9},{25,1},{2,26},{10... | collective-permute-start | bytes 786440 | tf_op jit(solution)/shard_map/ppermute | solution.py:40
  74.3 29.5 %collective-permute-start.16 = (bf16[3,128,512]{2,1,0:T(8,128)(2,1)S(1)}, bf16[3,128,512]{2,1,0:T(8,128)(2,1)S(1)}, u32[]{:S(2)}, u32[]{:S(2)}) collective-permute-start(bf16[3,128,512]{2,1,0:T(8,128)(2,1)S(1)} %get-tuple-element.104), channel_id=1, source_target_pairs={{0,3},{1,2},{2,1},{3,0},{4,7},{5,6},{6,5},{7,4},{8,11},{9,10},{10,... | collective-permute-start | bytes 1179656 | tf_op jit(solution)/shard_map/ppermute | solution.py:40
  77.1 34.3 %collective-permute-start.17 = (bf16[3,128,512]{2,1,0:T(8,128)(2,1)S(1)}, bf16[3,128,512]{2,1,0:T(8,128)(2,1)S(1)}, u32[]{:S(2)}, u32[]{:S(2)}) collective-permute-start(bf16[3,128,512]{2,1,0:T(8,128)(2,1)S(1)} %get-tuple-element.105), channel_id=1, source_target_pairs={{0,2},{1,3},{2,0},{3,1},{4,6},{5,7},{6,4},{7,5},{8,10},{9,11},{10,... | collective-permute-start | bytes 1179656 | tf_op jit(solution)/shard_map/ppermute | solution.py:40
  86.5 9.3 %collective-permute-start.13 = (bf16[64,2048]{1,0:T(8,128)(2,1)S(1)}, bf16[64,2048]{1,0:T(8,128)(2,1)S(1)}, u32[]{:S(2)}, u32[]{:S(2)}) collective-permute-start(bf16[64,2048]{1,0:T(8,128)(2,1)S(1)} %scene_mean.1.refs_0_), channel_id=1, source_target_pairs={{0,8},{8,0},{16,24},{24,16},{1,9},{9,1},{17,25},{25,17},{2,10},{10... | collective-permute-start | bytes 786440 | tf_op jit(solution)/shard_map/ppermute | solution.py:40
  87.8 13.0 %collective-permute-start.15 = (bf16[64,2048]{1,0:T(8,128)(2,1)S(1)}, bf16[64,2048]{1,0:T(8,128)(2,1)S(1)}, u32[]{:S(2)}, u32[]{:S(2)}) collective-permute-start(bf16[64,2048]{1,0:T(8,128)(2,1)S(1)} %scene_mean.1.refs_0_), channel_id=1, source_target_pairs={{0,24},{8,16},{16,8},{24,0},{1,25},{9,17},{17,9},{25,1},{2,26},{10... | collective-permute-start | bytes 786440 | tf_op jit(solution)/shard_map/ppermute | solution.py:40
  89.5 12.6 %collective-permute-start.14 = (bf16[64,2048]{1,0:T(8,128)(2,1)S(1)}, bf16[64,2048]{1,0:T(8,128)(2,1)S(1)}, u32[]{:S(2)}, u32[]{:S(2)}) collective-permute-start(bf16[64,2048]{1,0:T(8,128)(2,1)S(1)} %scene_mean.1.refs_0_), channel_id=1, source_target_pairs={{0,16},{8,24},{16,0},{24,8},{1,17},{9,25},{17,1},{25,9},{2,18},{10... | collective-permute-start | bytes 786440 | tf_op jit(solution)/shard_map/ppermute | solution.py:40
  95.8 18.3 %collective-permute-start.22 = (bf16[3,128,512]{2,1,0:T(8,128)(2,1)S(1)}, bf16[3,128,512]{2,1,0:T(8,128)(2,1)S(1)}, u32[]{:S(2)}, u32[]{:S(2)}) collective-permute-start(bf16[3,128,512]{2,1,0:T(8,128)(2,1)S(1)} %get-tuple-element.111), channel_id=1, source_target_pairs={{0,1},{1,0},{2,3},{3,2},{4,5},{5,4},{6,7},{7,6},{8,9},{9,8},{10,11... | collective-permute-start | bytes 1179656 | tf_op jit(solution)/shard_map/ppermute | solution.py:40
  111.4 2.7 %collective-permute-start.18 = (bf16[64,2048]{1,0:T(8,128)(2,1)S(1)}, bf16[64,2048]{1,0:T(8,128)(2,1)S(1)}, u32[]{:S(2)}, u32[]{:S(2)}) collective-permute-start(bf16[64,2048]{1,0:T(8,128)(2,1)S(1)} %scene_mean.1.refs_0_), channel_id=1, source_target_pairs={{0,4},{4,0},{1,5},{5,1},{2,6},{6,2},{3,7},{7,3},{8,12},{12,8},{9,1... | collective-permute-start | bytes 786440 | tf_op jit(solution)/shard_map/ppermute | solution.py:40
  111.4 2.7 %collective-permute-start.19 = (bf16[64,2048]{1,0:T(8,128)(2,1)S(1)}, bf16[64,2048]{1,0:T(8,128)(2,1)S(1)}, u32[]{:S(2)}, u32[]{:S(2)}) collective-permute-start(bf16[64,2048]{1,0:T(8,128)(2,1)S(1)} %collective-permute-done.13.refs_1_), channel_id=1, source_target_pairs={{0,4},{4,0},{1,5},{5,1},{2,6},{6,2},{3,7},{7,3},{8,12},{12,8},{9,1... | collective-permute-start | bytes 786440 | tf_op jit(solution)/shard_map/ppermute | solution.py:40
  111.9 2.2 %collective-permute-start.20 = (bf16[64,2048]{1,0:T(8,128)(2,1)S(1)}, bf16[64,2048]{1,0:T(8,128)(2,1)S(1)}, u32[]{:S(2)}, u32[]{:S(2)}) collective-permute-start(bf16[64,2048]{1,0:T(8,128)(2,1)S(1)} %collective-permute-done.14.refs_2_), channel_id=1, source_target_pairs={{0,4},{4,0},{1,5},{5,1},{2,6},{6,2},{3,7},{7,3},{8,12},{12,8},{9,1... | collective-permute-start | bytes 786440 | tf_op jit(solution)/shard_map/ppermute | solution.py:40
  111.9 2.2 %collective-permute-start.21 = (bf16[64,2048]{1,0:T(8,128)(2,1)S(1)}, bf16[64,2048]{1,0:T(8,128)(2,1)S(1)}, u32[]{:S(2)}, u32[]{:S(2)}) collective-permute-start(bf16[64,2048]{1,0:T(8,128)(2,1)S(1)} %collective-permute-done.15.refs_3_), channel_id=1, source_target_pairs={{0,4},{4,0},{1,5},{5,1},{2,6},{6,2},{3,7},{7,3},{8,12},{12,8},{9,1... | collective-permute-start | bytes 786440 | tf_op jit(solution)/shard_map/ppermute | solution.py:40

commit v8 on v6

--- a/solution.py
+++ b/solution.py
@@ -426,7 +426,7 @@
     piece2a = send(far2a, 2, across)
     piece3b = send(far3b, 3, piece3a)
     piece2b = send(far2b, 2, piece2a)
-    half = across.shape[0] // 2
+    half = across.shape[0] * 5 // 8
     mine = hold(after(out_grad, across))
     grad_early = grad_attn(meta, (mine, beside, across), out_weight, 0)
     corners = [send(across[:half], 1), send(after(across, piece1, grad_early)[half:], 1)]

time: 114 us -> 114 us (level)
  no operation moved by 1% of the time
where the time goes in v8:
time: 114 us; the launch traced here: 113 us
  waiting for transfers between devices  59.4 us (52%)
  starting transfers between devices  28.7 us (25%)
  Pallas kernels  19.2 us (17%)
  local copies, waits for them, and re-layouts  4.21 us (4%)
  between operations  1.45 us (1%)
    ppermute x23, waiting for transfers between devices, swap(): return lax.ppermute(x, axis, [(i, i ^ flip) for i in range(size)])  59.4 us
    ppermute x23, starting transfers between devices, swap(): return lax.ppermute(x, axis, [(i, i ^ flip) for i in range(size)])  28.7 us
    pallas_call x8, Pallas kernels, whole(): pl.pallas_call(kernel, out_shape=out_shape, in_specs=[pl.BlockSpec(memory...  13.1 us
    pallas_call x3, Pallas kernels, join(): pl.pallas_call(kernel, out_shape=shapes, in_specs=[pl.BlockSpec(memory_sp...  5.04 us
    unnamed x10, local copies, waits for them, and re-layouts  4.17 us
  transfers between devices with their start and end apart: 23, of which 12 were waited for; matrix products, arithmetic and copies ran while one was open for 0% of the time, Pallas kernels for 13%

profile of v8, /device:TPU:0, one launch (start us, length us, event | category | flops | bytes accessed | tf_op | source)
XLA Modules:
  0.0 112.9 jit_solution(11801481543675086713)
XLA Ops:
  0.6 0.0 copy-start
  0.6 3.1 %collective-permute-start.2 = (bf16[128,2048]{1,0:T(8,128)(2,1)}, bf16[128,2048]{1,0:T(8,128)(2,1)S(1)}, u32[]{:S(2)}, u32[]{:S(2)}) collective-permute-start(bf16[128,2048]{1,0:T(8,128)(2,1)} %in_ref), channel_id=1, source_target_pairs={{0,1},{1,0},{2,3},{3,2},{4,5},{5,4},{6,7},{7,6},{8,9},{9,8},{10,11... | collective-permute-start | bytes 1572872 | tf_op jit(solution)/shard_map/ppermute | solution.py:40
  3.7 2.6 %collective-permute-start.1 = (bf16[128,2048]{1,0:T(8,128)(2,1)}, bf16[128,2048]{1,0:T(8,128)(2,1)S(1)}, u32[]{:S(2)}, u32[]{:S(2)}) collective-permute-start(bf16[128,2048]{1,0:T(8,128)(2,1)} %in_ref), channel_id=1, source_target_pairs={{0,2},{1,3},{2,0},{3,1},{4,6},{5,7},{6,4},{7,5},{8,10},{9,11},{10,... | collective-permute-start | bytes 1572872 | tf_op jit(solution)/shard_map/ppermute | solution.py:40
  7.0 0.1 pad_add_fusion.meta
  7.1 1.0 copy-done.1
  8.1 1.0 copy-done.2
  9.1 1.0 copy-done.3
  10.2 1.0 pack_heads.1
  11.2 0.5 collective-permute-start
  11.7 16.1 %collective-permute-done.2.refs_1_ = bf16[128,2048]{1,0:T(8,128)(2,1)S(1)} collective-permute-done((bf16[128,2048]{1,0:T(8,128)(2,1)}, bf16[128,2048]{1,0:T(8,128)(2,1)S(1)}, u32[]{:S(2)}, u32[]{:S(2)}) %collective-permute-start.2) | collective-permute-done | bytes 524320 | tf_op jit(solution)/shard_map/ppermute | solution.py:40
  27.8 3.6 %collective-permute-start.4 = (bf16[3,128,384]{2,1,0:T(8,128)(2,1)S(1)}, bf16[3,128,384]{2,1,0:T(8,128)(2,1)S(1)}, u32[]{:S(2)}, u32[]{:S(2)}) collective-permute-start(bf16[3,128,384]{2,1,0:T(8,128)(2,1)S(1)} %get-tuple-element.67), channel_id=1, source_target_pairs={{0,3},{1,2},{2,1},{3,0},{4,7},{5,6},{6,5},{7,4},{8,11},{9,10},{10,... | collective-permute-start | bytes 884744 | tf_op jit(solution)/shard_map/ppermute | solution.py:40
  31.4 0.0 collective-permute-done.1.refs_2_
  31.4 0.0 collective-permute-start.3
  31.4 2.1 %collective-permute-start.7 = (bf16[80,2048]{1,0:T(8,128)(2,1)S(1)}, bf16[80,2048]{1,0:T(8,128)(2,1)S(1)}, u32[]{:S(2)}, u32[]{:S(2)}) collective-permute-start(bf16[80,2048]{1,0:T(8,128)(2,1)S(1)} %slice.8), channel_id=1, source_target_pairs={{0,1},{1,0},{2,3},{3,2},{4,5},{5,4},{6,7},{7,6},{8,9},{9,8},{10,11... | collective-permute-start | bytes 983048 | tf_op jit(solution)/shard_map/ppermute | solution.py:40
  33.5 1.0 copy-done.4
  34.6 0.0 copy-done
  34.6 1.6 %grad_attn.1.refs_4_.early_ref = bf16[384,512]{1,0:T(8,128)(2,1)S(1)} custom-call(s32[4]{0:T(128)S(1)} %pad_add_fusion.meta, bf16[128,2048]{1,0:T(8,128)(2,1)S(1)} %hold.1.refs_0_, bf16[128,2048]{1,0:T(8,128)(2,1)S(1)} %collective-permute-done.2.refs_1_, bf16[128,2048]{1,0:T(8,128)(2,1)S(1)} %collective-permute-done.1.refs_2_, bf16[512,2048]{1,0:T(8,128)(2,1)S(1)} %copy-done), custom_call_target="tpu_custom_call" | custom-call | bytes 1024 | tf_op jit(solution)/shard_map/grad_attn/pallas_call | solution.py:55
  36.1 7.9 %collective-permute-done.p1.refs_1_.near = bf16[3,128,512]{2,1,0:T(8,128)(2,1)S(1)} collective-permute-done((bf16[3,128,512]{2,1,0:T(8,128)(2,1)S(1)}, bf16[3,128,512]{2,1,0:T(8,128)(2,1)S(1)}, u32[]{:S(2)}, u32[]{:S(2)}) %collective-permute-start) | collective-permute-done | bytes 393248 | tf_op jit(solution)/shard_map/ppermute | solution.py:40
  44.1 0.1 collective-permute-start.8
  44.2 1.2 %collective-permute-done.4.p3.refs_3_.far3a = bf16[3,128,384]{2,1,0:T(8,128)(2,1)S(1)} collective-permute-done((bf16[3,128,384]{2,1,0:T(8,128)(2,1)S(1)}, bf16[3,128,384]{2,1,0:T(8,128)(2,1)S(1)}, u32[]{:S(2)}, u32[]{:S(2)}) %collective-permute-start.4) | collective-permute-done | bytes 294944 | tf_op jit(solution)/shard_map/ppermute | solution.py:40
  45.3 3.0 %collective-permute-start.6 = (bf16[3,128,128]{2,1,0:T(8,128)(2,1)S(1)}, bf16[3,128,128]{2,1,0:T(8,128)(2,1)S(1)}, u32[]{:S(2)}, u32[]{:S(2)}) collective-permute-start(bf16[3,128,128]{2,1,0:T(8,128)(2,1)S(1)} %get-tuple-element.78), channel_id=1, source_target_pairs={{0,3},{1,2},{2,1},{3,0},{4,7},{5,6},{6,5},{7,4},{8,11},{9,10},{10,... | collective-permute-start | bytes 294920 | tf_op jit(solution)/shard_map/ppermute | solution.py:40
  48.3 7.6 %collective-permute-done.3.p2.refs_2_.far2a = bf16[3,128,384]{2,1,0:T(8,128)(2,1)S(1)} collective-permute-done((bf16[3,128,384]{2,1,0:T(8,128)(2,1)S(1)}, bf16[3,128,384]{2,1,0:T(8,128)(2,1)S(1)}, u32[]{:S(2)}, u32[]{:S(2)}) %collective-permute-start.3) | collective-permute-done | bytes 294944 | tf_op jit(solution)/shard_map/ppermute | solution.py:40
  55.9 0.0 collective-permute-start.5
  55.9 3.3 %attend_forward.1 = (bf16[3,512,512]{2,1,0:T(8,128)(2,1)S(1)}, f32[3,1,512]{2,1,0:T(1,128)S(1)}, f32[384,512]{1,0:T(8,128)S(1)}, bf16[384,512]{1,0:T(8,128)(2,1)S(1)}, f32[512,512]{1,0:T(8,128)S(1)}) custom-call(s32[4]{0:T(128)S(1)} %pad_add_fusion.meta, bf16[3,128,512]{2,1,0:T(8,128)(2,1)S(1)} %get-tuple-element.61.p0.refs_0_.own, ...), custom_call_target="tpu_custom_call" | custom-call | bytes 1024 | tf_op jit(solution)/shard_map/attend_forward/pallas_call | solution.py:55
  59.3 2.3 %backward_early.1 = (bf16[384,384]{1,0:T(8,128)(2,1)S(1)}, f32[512,384]{1,0:T(8,128)S(1)}, f32[512,384]{1,0:T(8,128)S(1)}) custom-call(bf16[3,128,512]{2,1,0:T(8,128)(2,1)S(1)} %get-tuple-element.61.p0.refs_0_.own, bf16[3,128,512]{2,1,0:T(8,128)(2,1)S(1)} %collective-permute-done.p1.refs_1_.near, ...), custom_call_target="tpu_custom_call" | custom-call | bytes 1024 | tf_op jit(solution)/shard_map/backward_early/pallas_call | solution.py:55
  61.6 3.3 %collective-permute-done.6.p3.far3b = bf16[3,128,128]{2,1,0:T(8,128)(2,1)S(1)} collective-permute-done((bf16[3,128,128]{2,1,0:T(8,128)(2,1)S(1)}, bf16[3,128,128]{2,1,0:T(8,128)(2,1)S(1)}, u32[]{:S(2)}, u32[]{:S(2)}) %collective-permute-start.6) | collective-permute-done | bytes 98336 | tf_op jit(solution)/shard_map/ppermute | solution.py:40
  64.8 0.0 collective-permute-done.5.p2.far2b
  64.8 0.0 collective-permute-done.8.refs_4_.corner1
  64.8 0.0 collective-permute-done.7.refs_3_.corner0
  64.9 2.7 %weight_halves.1 = (bf16[1,512,512]{2,1,0:T(8,128)(2,1)S(1)}, f32[1,1,512]{2,1,0:T(1,128)S(1)}, f32[128,512]{1,0:T(8,128)S(1)}, bf16[256,2048]{1,0:T(8,128)(2,1)S(1)}, f32[256,2048]{1,0:T(8,128)S(1)}) custom-call(s32[4]{0:T(128)S(1)} %pad_add_fusion.meta, bf16[3,128,512]{2,1,0:T(8,128)(2,1)S(1)} %get-tuple-element.61.p0.refs_0_.own, ...), custom_call_target="tpu_custom_call" | custom-call | bytes 1024 | tf_op jit(solution)/shard_map/weight_halves/pallas_call | solution.py:55
  67.5 0.1 collective-permute-start.9
  67.6 2.9 %attend_backward.1 = (bf16[3,128,512]{2,1,0:T(8,128)(2,1)S(1)}, bf16[3,128,512]{2,1,0:T(8,128)(2,1)S(1)}, bf16[3,128,512]{2,1,0:T(8,128)(2,1)S(1)}, bf16[3,128,512]{2,1,0:T(8,128)(2,1)S(1)}) custom-call(s32[4]{0:T(128)S(1)} %pad_add_fusion.meta, bf16[3,128,512]{2,1,0:T(8,128)(2,1)S(1)} %get-tuple-element.61.p0.refs_0_.own, ...), custom_call_target="tpu_custom_call" | custom-call | bytes 1024 | tf_op jit(solution)/shard_map/attend_backward/pallas_call | solution.py:55
  70.5 0.0 collective-permute-done.9.recv_ref
  70.5 0.2 add_parts.1
  70.7 1.6 %collective-permute-start.10 = (bf16[64,2048]{1,0:T(8,128)(2,1)S(1)}, bf16[64,2048]{1,0:T(8,128)(2,1)S(1)}, u32[]{:S(2)}, u32[]{:S(2)}) collective-permute-start(bf16[64,2048]{1,0:T(8,128)(2,1)S(1)} %get-tuple-element.101), channel_id=1, source_target_pairs={{0,8},{8,0},{16,24},{24,16},{1,9},{9,1},{17,25},{25,17},{2,10},{10... | collective-permute-start | bytes 786440 | tf_op jit(solution)/shard_map/ppermute | solution.py:40
  72.3 1.5 %collective-permute-start.11 = (bf16[64,2048]{1,0:T(8,128)(2,1)S(1)}, bf16[64,2048]{1,0:T(8,128)(2,1)S(1)}, u32[]{:S(2)}, u32[]{:S(2)}) collective-permute-start(bf16[64,2048]{1,0:T(8,128)(2,1)S(1)} %get-tuple-element.102), channel_id=1, source_target_pairs={{0,16},{8,24},{16,0},{24,8},{1,17},{9,25},{17,1},{25,9},{2,18},{10... | collective-permute-start | bytes 786440 | tf_op jit(solution)/shard_map/ppermute | solution.py:40
  73.8 0.5 collective-permute-start.12
  74.3 1.5 %collective-permute-start.16 = (bf16[3,128,512]{2,1,0:T(8,128)(2,1)S(1)}, bf16[3,128,512]{2,1,0:T(8,128)(2,1)S(1)}, u32[]{:S(2)}, u32[]{:S(2)}) collective-permute-start(bf16[3,128,512]{2,1,0:T(8,128)(2,1)S(1)} %get-tuple-element.104), channel_id=1, source_target_pairs={{0,2},{1,3},{2,0},{3,1},{4,6},{5,7},{6,4},{7,5},{8,10},{9,11},{10,... | collective-permute-start | bytes 1179656 | tf_op jit(solution)/shard_map/ppermute | solution.py:40
  75.8 2.5 %collective-permute-start.17 = (bf16[3,128,512]{2,1,0:T(8,128)(2,1)S(1)}, bf16[3,128,512]{2,1,0:T(8,128)(2,1)S(1)}, u32[]{:S(2)}, u32[]{:S(2)}) collective-permute-start(bf16[3,128,512]{2,1,0:T(8,128)(2,1)S(1)} %get-tuple-element.105), channel_id=1, source_target_pairs={{0,3},{1,2},{2,1},{3,0},{4,7},{5,6},{6,5},{7,4},{8,11},{9,10},{10,... | collective-permute-start | bytes 1179656 | tf_op jit(solution)/shard_map/ppermute | solution.py:40
  78.2 1.7 %collective-permute-done.10.r1 = bf16[64,2048]{1,0:T(8,128)(2,1)S(1)} collective-permute-done((bf16[64,2048]{1,0:T(8,128)(2,1)S(1)}, bf16[64,2048]{1,0:T(8,128)(2,1)S(1)}, u32[]{:S(2)}, u32[]{:S(2)}) %collective-permute-start.10) | collective-permute-done | bytes 262176 | tf_op jit(solution)/shard_map/ppermute | solution.py:40
  79.9 6.4 %collective-permute-done.11.r2 = bf16[64,2048]{1,0:T(8,128)(2,1)S(1)} collective-permute-done((bf16[64,2048]{1,0:T(8,128)(2,1)S(1)}, bf16[64,2048]{1,0:T(8,128)(2,1)S(1)}, u32[]{:S(2)}, u32[]{:S(2)}) %collective-permute-start.11) | collective-permute-done | bytes 262176 | tf_op jit(solution)/shard_map/ppermute | solution.py:40
  86.3 0.0 collective-permute-done.12.r3
  86.3 0.1 scene_mean.1.refs_0_
  86.5 1.3 %collective-permute-start.13 = (bf16[64,2048]{1,0:T(8,128)(2,1)S(1)}, bf16[64,2048]{1,0:T(8,128)(2,1)S(1)}, u32[]{:S(2)}, u32[]{:S(2)}) collective-permute-start(bf16[64,2048]{1,0:T(8,128)(2,1)S(1)} %scene_mean.1.refs_0_), channel_id=1, source_target_pairs={{0,8},{8,0},{16,24},{24,16},{1,9},{9,1},{17,25},{25,17},{2,10},{10... | collective-permute-start | bytes 786440 | tf_op jit(solution)/shard_map/ppermute | solution.py:40
  87.8 1.8 %collective-permute-start.15 = (bf16[64,2048]{1,0:T(8,128)(2,1)S(1)}, bf16[64,2048]{1,0:T(8,128)(2,1)S(1)}, u32[]{:S(2)}, u32[]{:S(2)}) collective-permute-start(bf16[64,2048]{1,0:T(8,128)(2,1)S(1)} %scene_mean.1.refs_0_), channel_id=1, source_target_pairs={{0,24},{8,16},{16,8},{24,0},{1,25},{9,17},{17,9},{25,1},{2,26},{10... | collective-permute-start | bytes 786440 | tf_op jit(solution)/shard_map/ppermute | solution.py:40
  89.5 0.5 collective-permute-start.14
  90.0 5.8 %collective-permute-done.13.refs_1_ = bf16[64,2048]{1,0:T(8,128)(2,1)S(1)} collective-permute-done((bf16[64,2048]{1,0:T(8,128)(2,1)S(1)}, bf16[64,2048]{1,0:T(8,128)(2,1)S(1)}, u32[]{:S(2)}, u32[]{:S(2)}) %collective-permute-start.13) | collective-permute-done | bytes 262176 | tf_op jit(solution)/shard_map/ppermute | solution.py:40
  95.8 1.6 %collective-permute-start.22 = (bf16[3,128,512]{2,1,0:T(8,128)(2,1)S(1)}, bf16[3,128,512]{2,1,0:T(8,128)(2,1)S(1)}, u32[]{:S(2)}, u32[]{:S(2)}) collective-permute-start(bf16[3,128,512]{2,1,0:T(8,128)(2,1)S(1)} %get-tuple-element.111), channel_id=1, source_target_pairs={{0,1},{1,0},{2,3},{3,2},{4,5},{5,4},{6,7},{7,6},{8,9},{9,8},{10,11... | collective-permute-start | bytes 1179656 | tf_op jit(solution)/shard_map/ppermute | solution.py:40
  97.4 3.4 %collective-permute-done.15.refs_3_ = bf16[64,2048]{1,0:T(8,128)(2,1)S(1)} collective-permute-done((bf16[64,2048]{1,0:T(8,128)(2,1)S(1)}, bf16[64,2048]{1,0:T(8,128)(2,1)S(1)}, u32[]{:S(2)}, u32[]{:S(2)}) %collective-permute-start.15) | collective-permute-done | bytes 262176 | tf_op jit(solution)/shard_map/ppermute | solution.py:40
  100.8 1.4 %collective-permute-done.14.refs_2_ = bf16[64,2048]{1,0:T(8,128)(2,1)S(1)} collective-permute-done((bf16[64,2048]{1,0:T(8,128)(2,1)S(1)}, bf16[64,2048]{1,0:T(8,128)(2,1)S(1)}, u32[]{:S(2)}, u32[]{:S(2)}) %collective-permute-start.14) | collective-permute-done | bytes 262176 | tf_op jit(solution)/shard_map/ppermute | solution.py:40
  102.1 1.6 %join_weight.1.refs_8_ = bf16[512,2048]{1,0:T(8,128)(2,1)} custom-call(s32[4]{0:T(128)S(1)} %pad_add_fusion.meta, bf16[64,2048]{1,0:T(8,128)(2,1)S(1)} %scene_mean.1.refs_0_, bf16[64,2048]{1,0:T(8,128)(2,1)S(1)} %collective-permute-done.13.refs_1_, bf16[64,2048]{1,0:T(8,128)(2,1)S(1)} %collective-permute-done.14.refs_2_, ...), custom_call_target="tpu_custom_call" | custom-call | bytes 1024 | tf_op jit(solution)/shard_map/join_weight/pallas_call | solution.py:370
  103.8 0.1 collective-permute-done.16.back2
  103.9 0.0 collective-permute-done.17.back3
  103.9 0.0 collective-permute-start.18
  103.9 0.5 collective-permute-start.19
  104.4 0.0 collective-permute-start.20
  104.5 0.5 collective-permute-start.21
  104.9 1.6 %join_heads.1 = (bf16[128,2048]{1,0:T(8,128)(2,1)}, bf16[128,2048]{1,0:T(8,128)(2,1)}, bf16[128,2048]{1,0:T(8,128)(2,1)}) custom-call(s32[4]{0:T(128)S(1)} %pad_add_fusion.meta, bf16[3,128,512]{2,1,0:T(8,128)(2,1)S(1)} %get-tuple-element.98.own, bf16[3,128,512]{2,1,0:T(8,128)(2,1)S(1)} %collective-permute-done.16.back2, ...), custom_call_target="tpu_custom_call" | custom-call | bytes 1024 | tf_op jit(solution)/shard_map/join_heads/pallas_call | solution.py:370
  106.6 0.0 collective-permute-done.18.refs_0_
  106.6 0.0 collective-permute-done.19.refs_1_
  106.6 0.0 collective-permute-done.20.refs_2_
  106.6 0.0 collective-permute-done.21.refs_3_
  106.6 4.5 %collective-permute-done.22.refs_4_ = bf16[3,128,512]{2,1,0:T(8,128)(2,1)S(1)} collective-permute-done((bf16[3,128,512]{2,1,0:T(8,128)(2,1)S(1)}, bf16[3,128,512]{2,1,0:T(8,128)(2,1)S(1)}, u32[]{:S(2)}, u32[]{:S(2)}) %collective-permute-start.22) | collective-permute-done | bytes 393248 | tf_op jit(solution)/shard_map/ppermute | solution.py:40
  111.1 1.8 %join_last.1 = (bf16[128,2048]{1,0:T(8,128)(2,1)}, bf16[128,2048]{1,0:T(8,128)(2,1)}, bf16[128,2048]{1,0:T(8,128)(2,1)}, bf16[512,2048]{1,0:T(8,128)(2,1)}) custom-call(s32[4]{0:T(128)S(1)} %pad_add_fusion.meta, bf16[64,2048]{1,0:T(8,128)(2,1)S(1)} %collective-permute-done.18.refs_0_, ...), custom_call_target="tpu_custom_call", output_to_operand_aliasing={{0}: (6, {}), {1}: (7, {}), {2}: (8, {}), {3}: (9, {})} | custom-call | bytes 1024 | tf_op jit(solution)/shard_map/join_last/pallas_call | solution.py:370
  (7 shorter events, 0.1 us)
Async XLA Ops:
  0.6 33.9 %copy-start = (bf16[512,2048]{1,0:T(8,128)(2,1)S(1)}, bf16[512,2048]{1,0:T(8,128)(2,1)}, u32[]{:S(2)}) copy-start(bf16[512,2048]{1,0:T(8,128)(2,1)} %w_ref.1) | copy-start | bytes 6291460
  0.6 27.2 %collective-permute-start.2 = (bf16[128,2048]{1,0:T(8,128)(2,1)}, bf16[128,2048]{1,0:T(8,128)(2,1)S(1)}, u32[]{:S(2)}, u32[]{:S(2)}) collective-permute-start(bf16[128,2048]{1,0:T(8,128)(2,1)} %in_ref), channel_id=1, source_target_pairs={{0,1},{1,0},{2,3},{3,2},{4,5},{5,4},{6,7},{7,6},{8,9},{9,8},{10,11... | collective-permute-start | bytes 1572872 | tf_op jit(solution)/shard_map/ppermute | solution.py:40
  3.7 27.7 %collective-permute-start.1 = (bf16[128,2048]{1,0:T(8,128)(2,1)}, bf16[128,2048]{1,0:T(8,128)(2,1)S(1)}, u32[]{:S(2)}, u32[]{:S(2)}) collective-permute-start(bf16[128,2048]{1,0:T(8,128)(2,1)} %in_ref), channel_id=1, source_target_pairs={{0,2},{1,3},{2,0},{3,1},{4,6},{5,7},{6,4},{7,5},{8,10},{9,11},{10,... | collective-permute-start | bytes 1572872 | tf_op jit(solution)/shard_map/ppermute | solution.py:40
  7.0 1.0 copy-start.1
  8.1 1.0 copy-start.2
  9.1 1.0 copy-start.3
  11.2 32.9 %collective-permute-start = (bf16[3,128,512]{2,1,0:T(8,128)(2,1)S(1)}, bf16[3,128,512]{2,1,0:T(8,128)(2,1)S(1)}, u32[]{:S(2)}, u32[]{:S(2)}) collective-permute-start(bf16[3,128,512]{2,1,0:T(8,128)(2,1)S(1)} %get-tuple-element.62), channel_id=1, source_target_pairs={{0,1},{1,0},{2,3},{3,2},{4,5},{5,4},{6,7},{7,6},{8,9},{9,8},{10,11... | collective-permute-start | bytes 1179656 | tf_op jit(solution)/shard_map/ppermute | solution.py:40
  27.8 17.5 %collective-permute-start.4 = (bf16[3,128,384]{2,1,0:T(8,128)(2,1)S(1)}, bf16[3,128,384]{2,1,0:T(8,128)(2,1)S(1)}, u32[]{:S(2)}, u32[]{:S(2)}) collective-permute-start(bf16[3,128,384]{2,1,0:T(8,128)(2,1)S(1)} %get-tuple-element.67), channel_id=1, source_target_pairs={{0,3},{1,2},{2,1},{3,0},{4,7},{5,6},{6,5},{7,4},{8,11},{9,10},{10,... | collective-permute-start | bytes 884744 | tf_op jit(solution)/shard_map/ppermute | solution.py:40
  31.4 24.5 %collective-permute-start.3 = (bf16[3,128,384]{2,1,0:T(8,128)(2,1)S(1)}, bf16[3,128,384]{2,1,0:T(8,128)(2,1)S(1)}, u32[]{:S(2)}, u32[]{:S(2)}) collective-permute-start(bf16[3,128,384]{2,1,0:T(8,128)(2,1)S(1)} %get-tuple-element.65), channel_id=1, source_target_pairs={{0,2},{1,3},{2,0},{3,1},{4,6},{5,7},{6,4},{7,5},{8,10},{9,11},{10,... | collective-permute-start | bytes 884744 | tf_op jit(solution)/shard_map/ppermute | solution.py:40
  31.4 33.4 %collective-permute-start.7 = (bf16[80,2048]{1,0:T(8,128)(2,1)S(1)}, bf16[80,2048]{1,0:T(8,128)(2,1)S(1)}, u32[]{:S(2)}, u32[]{:S(2)}) collective-permute-start(bf16[80,2048]{1,0:T(8,128)(2,1)S(1)} %slice.8), channel_id=1, source_target_pairs={{0,1},{1,0},{2,3},{3,2},{4,5},{5,4},{6,7},{7,6},{8,9},{9,8},{10,11... | collective-permute-start | bytes 983048 | tf_op jit(solution)/shard_map/ppermute | solution.py:40
  33.5 1.0 copy-start.4
  44.1 20.8 %collective-permute-start.8 = (bf16[48,2048]{1,0:T(8,128)(2,1)S(1)}, bf16[48,2048]{1,0:T(8,128)(2,1)S(1)}, u32[]{:S(2)}, u32[]{:S(2)}) collective-permute-start(bf16[48,2048]{1,0:T(8,128)(2,1)S(1)} %slice.7), channel_id=1, source_target_pairs={{0,1},{1,0},{2,3},{3,2},{4,5},{5,4},{6,7},{7,6},{8,9},{9,8},{10,11... | collective-permute-start | bytes 589832 | tf_op jit(solution)/shard_map/ppermute | solution.py:40
  45.3 19.5 %collective-permute-start.6 = (bf16[3,128,128]{2,1,0:T(8,128)(2,1)S(1)}, bf16[3,128,128]{2,1,0:T(8,128)(2,1)S(1)}, u32[]{:S(2)}, u32[]{:S(2)}) collective-permute-start(bf16[3,128,128]{2,1,0:T(8,128)(2,1)S(1)} %get-tuple-element.78), channel_id=1, source_target_pairs={{0,3},{1,2},{2,1},{3,0},{4,7},{5,6},{6,5},{7,4},{8,11},{9,10},{10,... | collective-permute-start | bytes 294920 | tf_op jit(solution)/shard_map/ppermute | solution.py:40
  55.9 8.9 %collective-permute-start.5 = (bf16[3,128,128]{2,1,0:T(8,128)(2,1)S(1)}, bf16[3,128,128]{2,1,0:T(8,128)(2,1)S(1)}, u32[]{:S(2)}, u32[]{:S(2)}) collective-permute-start(bf16[3,128,128]{2,1,0:T(8,128)(2,1)S(1)} %get-tuple-element.76), channel_id=1, source_target_pairs={{0,2},{1,3},{2,0},{3,1},{4,6},{5,7},{6,4},{7,5},{8,10},{9,11},{10,... | collective-permute-start | bytes 294920 | tf_op jit(solution)/shard_map/ppermute | solution.py:40
  67.5 3.0 %collective-permute-start.9 = (bf16[256,2048]{1,0:T(8,128)(2,1)S(1)}, bf16[256,2048]{1,0:T(8,128)(2,1)S(1)}, u32[]{:S(2)}, u32[]{:S(2)}) collective-permute-start(bf16[256,2048]{1,0:T(8,128)(2,1)S(1)} %get-tuple-element.89), channel_id=1, source_target_pairs={{0,4},{4,0},{1,5},{5,1},{2,6},{6,2},{3,7},{7,3},{8,12},{12,8},{9,1... | collective-permute-start | bytes 3145736 | tf_op jit(solution)/shard_map/ppermute | solution.py:40
  70.7 9.2 %collective-permute-start.10 = (bf16[64,2048]{1,0:T(8,128)(2,1)S(1)}, bf16[64,2048]{1,0:T(8,128)(2,1)S(1)}, u32[]{:S(2)}, u32[]{:S(2)}) collective-permute-start(bf16[64,2048]{1,0:T(8,128)(2,1)S(1)} %get-tuple-element.101), channel_id=1, source_target_pairs={{0,8},{8,0},{16,24},{24,16},{1,9},{9,1},{17,25},{25,17},{2,10},{10... | collective-permute-start | bytes 786440 | tf_op jit(solution)/shard_map/ppermute | solution.py:40
  72.3 14.0 %collective-permute-start.11 = (bf16[64,2048]{1,0:T(8,128)(2,1)S(1)}, bf16[64,2048]{1,0:T(8,128)(2,1)S(1)}, u32[]{:S(2)}, u32[]{:S(2)}) collective-permute-start(bf16[64,2048]{1,0:T(8,128)(2,1)S(1)} %get-tuple-element.102), channel_id=1, source_target_pairs={{0,16},{8,24},{16,0},{24,8},{1,17},{9,25},{17,1},{25,9},{2,18},{10... | collective-permute-start | bytes 786440 | tf_op jit(solution)/shard_map/ppermute | solution.py:40
  73.8 12.5 %collective-permute-start.12 = (bf16[64,2048]{1,0:T(8,128)(2,1)S(1)}, bf16[64,2048]{1,0:T(8,128)(2,1)S(1)}, u32[]{:S(2)}, u32[]{:S(2)}) collective-permute-start(bf16[64,2048]{1,0:T(8,128)(2,1)S(1)} %get-tuple-element.103), channel_id=1, source_target_pairs={{0,24},{8,16},{16,8},{24,0},{1,25},{9,17},{17,9},{25,1},{2,26},{10... | collective-permute-start | bytes 786440 | tf_op jit(solution)/shard_map/ppermute | solution.py:40
  74.3 29.6 %collective-permute-start.16 = (bf16[3,128,512]{2,1,0:T(8,128)(2,1)S(1)}, bf16[3,128,512]{2,1,0:T(8,128)(2,1)S(1)}, u32[]{:S(2)}, u32[]{:S(2)}) collective-permute-start(bf16[3,128,512]{2,1,0:T(8,128)(2,1)S(1)} %get-tuple-element.104), channel_id=1, source_target_pairs={{0,2},{1,3},{2,0},{3,1},{4,6},{5,7},{6,4},{7,5},{8,10},{9,11},{10,... | collective-permute-start | bytes 1179656 | tf_op jit(solution)/shard_map/ppermute | solution.py:40
  75.8 28.2 %collective-permute-start.17 = (bf16[3,128,512]{2,1,0:T(8,128)(2,1)S(1)}, bf16[3,128,512]{2,1,0:T(8,128)(2,1)S(1)}, u32[]{:S(2)}, u32[]{:S(2)}) collective-permute-start(bf16[3,128,512]{2,1,0:T(8,128)(2,1)S(1)} %get-tuple-element.105), channel_id=1, source_target_pairs={{0,3},{1,2},{2,1},{3,0},{4,7},{5,6},{6,5},{7,4},{8,11},{9,10},{10,... | collective-permute-start | bytes 1179656 | tf_op jit(solution)/shard_map/ppermute | solution.py:40
  86.5 9.3 %collective-permute-start.13 = (bf16[64,2048]{1,0:T(8,128)(2,1)S(1)}, bf16[64,2048]{1,0:T(8,128)(2,1)S(1)}, u32[]{:S(2)}, u32[]{:S(2)}) collective-permute-start(bf16[64,2048]{1,0:T(8,128)(2,1)S(1)} %scene_mean.1.refs_0_), channel_id=1, source_target_pairs={{0,8},{8,0},{16,24},{24,16},{1,9},{9,1},{17,25},{25,17},{2,10},{10... | collective-permute-start | bytes 786440 | tf_op jit(solution)/shard_map/ppermute | solution.py:40
  87.8 13.0 %collective-permute-start.15 = (bf16[64,2048]{1,0:T(8,128)(2,1)S(1)}, bf16[64,2048]{1,0:T(8,128)(2,1)S(1)}, u32[]{:S(2)}, u32[]{:S(2)}) collective-permute-start(bf16[64,2048]{1,0:T(8,128)(2,1)S(1)} %scene_mean.1.refs_0_), channel_id=1, source_target_pairs={{0,24},{8,16},{16,8},{24,0},{1,25},{9,17},{17,9},{25,1},{2,26},{10... | collective-permute-start | bytes 786440 | tf_op jit(solution)/shard_map/ppermute | solution.py:40
  89.5 12.6 %collective-permute-start.14 = (bf16[64,2048]{1,0:T(8,128)(2,1)S(1)}, bf16[64,2048]{1,0:T(8,128)(2,1)S(1)}, u32[]{:S(2)}, u32[]{:S(2)}) collective-permute-start(bf16[64,2048]{1,0:T(8,128)(2,1)S(1)} %scene_mean.1.refs_0_), channel_id=1, source_target_pairs={{0,16},{8,24},{16,0},{24,8},{1,17},{9,25},{17,1},{25,9},{2,18},{10... | collective-permute-start | bytes 786440 | tf_op jit(solution)/shard_map/ppermute | solution.py:40
  95.8 15.4 %collective-permute-start.22 = (bf16[3,128,512]{2,1,0:T(8,128)(2,1)S(1)}, bf16[3,128,512]{2,1,0:T(8,128)(2,1)S(1)}, u32[]{:S(2)}, u32[]{:S(2)}) collective-permute-start(bf16[3,128,512]{2,1,0:T(8,128)(2,1)S(1)} %get-tuple-element.111), channel_id=1, source_target_pairs={{0,1},{1,0},{2,3},{3,2},{4,5},{5,4},{6,7},{7,6},{8,9},{9,8},{10,11... | collective-permute-start | bytes 1179656 | tf_op jit(solution)/shard_map/ppermute | solution.py:40
  103.9 2.7 %collective-permute-start.18 = (bf16[64,2048]{1,0:T(8,128)(2,1)S(1)}, bf16[64,2048]{1,0:T(8,128)(2,1)S(1)}, u32[]{:S(2)}, u32[]{:S(2)}) collective-permute-start(bf16[64,2048]{1,0:T(8,128)(2,1)S(1)} %scene_mean.1.refs_0_), channel_id=1, source_target_pairs={{0,4},{4,0},{1,5},{5,1},{2,6},{6,2},{3,7},{7,3},{8,12},{12,8},{9,1... | collective-permute-start | bytes 786440 | tf_op jit(solution)/shard_map/ppermute | solution.py:40
  103.9 2.7 %collective-permute-start.19 = (bf16[64,2048]{1,0:T(8,128)(2,1)S(1)}, bf16[64,2048]{1,0:T(8,128)(2,1)S(1)}, u32[]{:S(2)}, u32[]{:S(2)}) collective-permute-start(bf16[64,2048]{1,0:T(8,128)(2,1)S(1)} %collective-permute-done.13.refs_1_), channel_id=1, source_target_pairs={{0,4},{4,0},{1,5},{5,1},{2,6},{6,2},{3,7},{7,3},{8,12},{12,8},{9,1... | collective-permute-start | bytes 786440 | tf_op jit(solution)/shard_map/ppermute | solution.py:40
  104.4 2.2 %collective-permute-start.20 = (bf16[64,2048]{1,0:T(8,128)(2,1)S(1)}, bf16[64,2048]{1,0:T(8,128)(2,1)S(1)}, u32[]{:S(2)}, u32[]{:S(2)}) collective-permute-start(bf16[64,2048]{1,0:T(8,128)(2,1)S(1)} %collective-permute-done.14.refs_2_), channel_id=1, source_target_pairs={{0,4},{4,0},{1,5},{5,1},{2,6},{6,2},{3,7},{7,3},{8,12},{12,8},{9,1... | collective-permute-start | bytes 786440 | tf_op jit(solution)/shard_map/ppermute | solution.py:40
  104.5 2.1 %collective-permute-start.21 = (bf16[64,2048]{1,0:T(8,128)(2,1)S(1)}, bf16[64,2048]{1,0:T(8,128)(2,1)S(1)}, u32[]{:S(2)}, u32[]{:S(2)}) collective-permute-start(bf16[64,2048]{1,0:T(8,128)(2,1)S(1)} %collective-permute-done.15.refs_3_), channel_id=1, source_target_pairs={{0,4},{4,0},{1,5},{5,1},{2,6},{6,2},{3,7},{7,3},{8,12},{12,8},{9,1... | collective-permute-start | bytes 786440 | tf_op jit(solution)/shard_map/ppermute | solution.py:40
